TPU v7x, 32 devices: a whole 2x2x4 slice. The times are simulated.
32 devices in a mesh: dp: 8 (over y, x, core), tensor: 4 (over z).
Axes of the slice: x: 2, y: 2, z: 4, core: 2. Of those that a mesh axis runs over, the one named last changes fastest.
Arguments:
- context: bfloat16 [512, 180, 768], P(('dp', 'tensor')), may hold values from -6 to 6
- stream: bfloat16 [512, 180, 768], P(('dp', 'tensor')), may hold values from -6 to 6
- out_weight: bfloat16 [768, 768], replicated, may hold values from -0.21875 to 0.21875
- gain: float32 [768], replicated, may hold values from 0.5 to 1.5
- bias: float32 [768], replicated, may hold values from -3 to 3
- proj_weight: bfloat16 [768, 128], replicated, may hold values from -0.21875 to 0.21875
- query_states: bfloat16 [8, 32, 768], P('dp'), may hold values from -6 to 6
- passage_len: int32 [512], P(('dp', 'tensor')), may hold values from 45 to 180, as said below
- passage_dest: int32 [512], P(('dp', 'tensor')), may hold values from 0 to 511, as said below
- teacher_states: bfloat16 [512, 212, 1024], P(('dp', 'tensor')), may hold values from -6 to 6
- teacher_query: bfloat16 [1024, 1024], P(None, 'tensor'), may hold values from -0.1875 to 0.1875
- teacher_key: bfloat16 [1024, 1024], P(None, 'tensor'), may hold values from -0.1875 to 0.1875
Outputs:
- loss: float32 [], replicated
- grad_out: float32 [768, 768], replicated
- grad_proj: float32 [768, 128], replicated
- grad_gain: float32 [768], replicated
- grad_bias: float32 [768], replicated
- grad_context: bfloat16 [512, 180, 768], P(('dp', 'tensor'))
Inputs may be any that keep to these rules, and one draw needn't show every extreme that they name: `passage_dest`: A permutation of the pair positions. Passage rows form runs of 16 (run a = i * 4 + t), and so do pair positions; run a sends exactly 16 / 8 of its rows into each pair run j * 4 + t, for every j. `passage_len`: every run of 16 passage rows holds one passage of full length.
All inputs are finite; a program needn't handle non-finite values.
Results may differ from a plain program's by a relative error of at most 0.011.
Values may be sent and summed in bfloat16 or wider, within the bound.
No kernel may reach another device: no remote copies, remote signals or barrier semaphores. Data moves between devices by JAX's collectives and lax.ppermute only.
A program may use at most 192 MiB of HBM per device.

v0:
```python
import functools
import math

import jax
import jax.numpy as jnp
from jax import lax
from jax.experimental import pallas as pl
from jax.experimental.pallas import tpu as pltpu
from jax.sharding import PartitionSpec as P

sharpness = 0.05
softcap = 10.0
epsilon = 1e-06
CORES = 2
VMEM_LIMIT = 56 * 1024 * 1024

F32 = jnp.float32
BF16 = jnp.bfloat16
VMEM = pl.BlockSpec(memory_space=pltpu.VMEM)
SMEM = pl.BlockSpec(memory_space=pltpu.SMEM)
ANY = pl.BlockSpec(memory_space=pl.ANY)


def up(n, m):
    return -(-n // m) * m


def dot(a, b, ca, cb):
    return lax.dot_general(a, b, (((ca,), (cb,)), ((), ())), preferred_element_type=F32)


def split_rows(rows, most):
    return max(n for n in range(16, most + 1, 16) if rows % n == 0)


def params(**kw):
    return pltpu.CompilerParams(vmem_limit_bytes=VMEM_LIMIT, **kw)


def cost(flops, nbytes):
    return pl.CostEstimate(flops=int(flops), bytes_accessed=int(nbytes), transcendentals=0)


def forward_kernel(x_ref, str_ref, wo_ref, gain_ref, bias_ref, wp_ref, after_ref, normed_ref, emb_ref, inv_ref, prod_s, hid_s):
    rows, width = x_ref.shape
    sub = split_rows(rows, 256)
    gain, bias = gain_ref[...], bias_ref[...]
    for b in range(0, rows, sub):
        prod_s[b : b + sub] = dot(x_ref[b : b + sub], wo_ref[...], 1, 0)
        for c in range(b, b + sub, 16):
            summed = prod_s[c : c + 16] + str_ref[c : c + 16].astype(F32)
            centred = summed - jnp.mean(summed, axis=-1, keepdims=True)
            inverse = lax.rsqrt(jnp.mean(centred * centred, axis=-1, keepdims=True) + epsilon)
            normed = centred * inverse
            normed_ref[c : c + 16] = normed.astype(BF16)
            inv_ref[c : c + 16] = jnp.broadcast_to(inverse, (16, inv_ref.shape[1]))
            hid_s[c : c + 16] = (normed * gain + bias).astype(BF16)
        emb_ref[b : b + sub] = dot(hid_s[b : b + sub], wp_ref[...], 1, 0)


def student_forward(x, stream, out_weight, gain, bias, proj_weight, after):
    total, width = x.shape
    emb = proj_weight.shape[1]
    rows = split_rows(total, 720)
    block = lambda last: pl.BlockSpec((rows, last), lambda s: (s, 0))
    whole = lambda a: pl.BlockSpec(a.shape, lambda s: (0,) * a.ndim)
    return pl.pallas_call(
        forward_kernel,
        grid=(total // rows,),
        in_specs=[block(width), block(width)] + [whole(a) for a in (out_weight, gain, bias, proj_weight)] + [ANY],
        out_specs=[block(width), block(emb), block(128)],
        out_shape=[
            jax.ShapeDtypeStruct((total, width), BF16),
            jax.ShapeDtypeStruct((total, emb), F32),
            jax.ShapeDtypeStruct((total, 128), F32),
        ],
        scratch_shapes=[pltpu.VMEM((rows, width), F32), pltpu.VMEM((rows, width), BF16)],
        compiler_params=params(),
        cost_estimate=cost(2 * total * width * (width + emb), 8 * total * width),
        name="student_forward",
    )(x, stream, out_weight, gain, bias, proj_weight, after)


def teacher_kernel(parts, count, tokens, order_ref, rows_ref, states_ref, wq_ref, wk_ref, after_ref, *rest):
    pieces, out_ref = rest[:parts], rest[parts]
    w_s, own_s, q_s, g_s, key_s, e_s, map_s, q_sem, key_sem, w_sem, own_sem = rest[parts + 1 :]
    depth = q_s.shape[1]
    slices = w_s.shape[0] // 2
    part_rows = pieces[0].shape[1]
    total = key_s.shape[0]
    seq = total // count
    blocks = key_sem.shape[0]
    rows = total // blocks
    first = count * tokens
    own = [
        pltpu.make_async_copy(wq_ref, own_s.at[0], own_sem.at[0]),
        pltpu.make_async_copy(wk_ref, own_s.at[1], own_sem.at[1]),
    ]
    queries = pltpu.make_async_copy(states_ref.at[pl.ds(0, first)], q_s, q_sem)
    gathered = [
        pltpu.make_async_copy(
            pieces[a],
            w_s.at[:, pl.ds(pl.multiple_of(rows_ref[a] * part_rows, part_rows), part_rows), :],
            w_sem.at[a],
        )
        for a in range(parts)
    ]
    keys = [
        pltpu.make_async_copy(
            states_ref.at[pl.ds(first + b * rows, rows)], key_s.at[pl.ds(b * rows, rows)], key_sem.at[b]
        )
        for b in range(blocks)
    ]
    queries.start()
    for copy in own + gathered + keys:
        copy.start()
    queries.wait()
    for copy in own:
        copy.wait()
    q = q_s[...]
    mixed = dot(dot(q, own_s[0], 1, 0).astype(BF16), own_s[1], 1, 1)
    for copy in gathered:
        copy.wait()
    for k in range(slices):
        mixed = mixed + dot(dot(q, w_s[2 * k], 1, 0).astype(BF16), w_s[2 * k + 1], 1, 1)
    for v in range(depth // 128):
        g_s[v] = mixed[:, v * 128 : (v + 1) * 128]
        for p in range(count):
            q_s[p * tokens : (p + 1) * tokens, v * 128 : (v + 1) * 128] = g_s[
                v, pl.ds(p, tokens, stride=count), :
            ].astype(BF16)
    mixed = q_s[...]
    scale = 1.0 / (math.sqrt(depth) * softcap)
    side = 128 // tokens
    pair = lax.broadcasted_iota(jnp.int32, (rows, 128), 0) % count
    for b in range(blocks):
        keys[b].wait()
        raw = dot(key_s[b * rows : (b + 1) * rows], mixed, 1, 1)
        mine = raw[:, :128]
        for v in range(1, count // side):
            mine = jnp.where(pair >= v * side, raw[:, v * 128 : (v + 1) * 128], mine)
        e_s[b * rows : (b + 1) * rows] = jnp.exp(softcap * jnp.tanh(mine * scale))
    lane = lax.broadcasted_iota(jnp.int32, (seq, 128), 1) // tokens
    filler = jnp.zeros((up(seq, 128) - seq, 128), F32)
    for g in range(count // side):
        both = e_s[pl.ds(g * side, seq, stride=count), :]
        for v in range(1, side):
            both = jnp.where(lane == v, e_s[pl.ds(g * side + v, seq, stride=count), :], both)
        turned = jnp.concatenate([both, filler], axis=0).T
        for v in range(side):
            map_s[g * side + v] = turned[v * tokens : (v + 1) * tokens, :seq].astype(BF16)
    for n in range(count):
        out_ref[n] = map_s[order_ref[n]]


def teacher_maps(order, rows, states, wq, wk, after, pieces, count, tokens):
    total, depth = states.shape
    keys = total - count * tokens
    heads = wq.shape[1]
    parts = len(pieces)
    slices = pieces[0].shape[0]
    blocks = keys // split_rows(keys, 720)
    return pl.pallas_call(
        functools.partial(teacher_kernel, parts, count, tokens),
        in_specs=[SMEM, SMEM] + [ANY] * (4 + parts),
        out_specs=VMEM,
        out_shape=jax.ShapeDtypeStruct((count, tokens, keys // count), BF16),
        scratch_shapes=[
            pltpu.VMEM((slices, depth, heads), BF16),
            pltpu.VMEM((2, depth, heads), BF16),
            pltpu.VMEM((count * tokens, depth), BF16),
            pltpu.VMEM((depth // 128, count * tokens, 128), F32),
            pltpu.VMEM((keys, depth), BF16),
            pltpu.VMEM((keys, 128), F32),
            pltpu.VMEM((count, tokens, keys // count), BF16),
            pltpu.SemaphoreType.DMA,
            pltpu.SemaphoreType.DMA((blocks,)),
            pltpu.SemaphoreType.DMA((parts,)),
            pltpu.SemaphoreType.DMA((2,)),
        ],
        compiler_params=params(),
        cost_estimate=cost(8 * count * tokens * depth * depth, 2 * states.size + 4 * depth * depth),
        name="teacher_maps",
    )(order, rows, states, wq, wk, after, *pieces)


def score_rows(tokens, count, per, group_queries, qidx_ref, midx_ref, len_ref, maps_ref, payload_ref, emb_ref, wp_ref,
               qs_s, qunit_s, qdir_s, qlen_s, qg_s, dir_s, un_s, up_s, eg_s, l_s):
    total, emb = emb_ref.shape
    seq = total // count
    sub = split_rows(total, 128)
    each = group_queries * tokens
    for k in range(payload_ref.shape[0]):
        qs_s[k * each : (k + 1) * each] = payload_ref[k, :each]
    qe = dot(qs_s[...], wp_ref[...], 1, 0)
    length = jnp.sqrt(jnp.sum(qe * qe, axis=-1, keepdims=True) + epsilon)
    qdir = qe / length
    qdir_s[...] = qdir
    qlen_s[...] = jnp.broadcast_to(length, qlen_s.shape)
    qunit_s[...] = qdir.astype(BF16).reshape(qunit_s.shape)
    qg_s[...] = jnp.zeros_like(qg_s)
    for b in range(0, total, sub):
        e = emb_ref[b : b + sub]
        dir_s[b : b + sub] = e / jnp.sqrt(jnp.sum(e * e, axis=-1, keepdims=True) + epsilon)
    spread = jnp.zeros((tokens, 1), F32)
    sums = []
    for r in range(count):
        units = dir_s[pl.ds(r, seq, stride=count), :].astype(BF16)
        q = qunit_s[qidx_ref[r]]
        logits = dot(q, units, 1, 1) / sharpness
        valid = lax.broadcasted_iota(jnp.int32, logits.shape, 1) < len_ref[r]
        student = jnp.where(valid, jnp.exp(logits), 0.0)
        student_total = jnp.sum(student, axis=-1, keepdims=True)
        teacher = maps_ref[midx_ref[r]].astype(F32)
        teacher_log = jnp.log(teacher)
        teacher = jnp.where(valid, teacher, 0.0)
        teacher_total = jnp.sum(teacher, axis=-1, keepdims=True)
        student_prob = student / student_total
        teacher_prob = teacher / teacher_total
        gap = (teacher_log - jnp.log(teacher_total)) - (logits - jnp.log(student_total))
        spread += jnp.sum(jnp.where(valid, teacher_prob * gap, 0.0), axis=-1, keepdims=True)
        slope = ((student_prob - teacher_prob) / (tokens * sharpness)).astype(BF16)
        up_s[pl.ds(r, seq, stride=count), :] = dot(slope, q, 0, 0).astype(BF16).astype(F32)
        un_s[r] = dot(slope, units, 1, 0)
    for r in range(count):
        qg_s[qidx_ref[r]] += un_s[r]
    l_s[...] = jnp.broadcast_to(spread, l_s.shape)
    for b in range(0, total, sub):
        e = emb_ref[b : b + sub]
        upstream = up_s[b : b + sub]
        length = jnp.sqrt(jnp.sum(e * e, axis=-1, keepdims=True) + epsilon)
        direction = dir_s[b : b + sub]
        eg = (upstream - direction * jnp.sum(direction * upstream, axis=-1, keepdims=True)) / length
        eg_s[b : b + sub] = eg.astype(BF16)


def backward_kernel(
    tokens, count, per, group_queries,
    qidx_ref, midx_ref, len_ref, core_ref,
    maps_ref, payload_ref, emb_ref, x_ref, normed_ref, inv_ref, gain_ref, bias_ref, wp_ref, wpt_ref,
    sg_ref, send_ref, keep_ref,
    qs_s, qunit_s, qdir_s, qlen_s, qg_s, dir_s, un_s, up_s, eg_s, l_s,
    hg_s, wo_s, nt_s, s_s, right_s,
):
    step = pl.program_id(0)
    rows, width = x_ref.shape
    sub = split_rows(rows, 256)
    gain = gain_ref[...]

    @pl.when(step == 0)
    def _():
        score_rows(tokens, count, per, group_queries, qidx_ref, midx_ref, len_ref, maps_ref, payload_ref, emb_ref,
                   wp_ref, qs_s, qunit_s, qdir_s, qlen_s, qg_s, dir_s, un_s, up_s, eg_s, l_s)
        wo_s[...] = jnp.zeros_like(wo_s)
        nt_s[...] = jnp.zeros_like(nt_s)
        s_s[...] = jnp.zeros_like(s_s)

    base = pl.multiple_of(step * rows, 16)
    for b in range(0, rows, sub):
        hg_s[b : b + sub] = dot(eg_s[pl.ds(base + b, sub)], wp_ref[...], 1, 1)
        for c in range(b, b + sub, 16):
            scaled = hg_s[c : c + 16] * gain
            normed = normed_ref[c : c + 16].astype(F32)
            mean = jnp.mean(scaled, axis=-1, keepdims=True)
            along = jnp.mean(scaled * normed, axis=-1, keepdims=True)
            sg_ref[c : c + 16] = (inv_ref[c : c + 16, :1] * (scaled - mean - normed * along)).astype(BF16)
    eg = eg_s[pl.ds(base, rows)]
    wo_s[...] += dot(x_ref[...], sg_ref[...], 0, 0)
    nt_s[...] += dot(eg, normed_ref[...], 0, 0)
    s_s[...] += dot(eg, jnp.ones((rows, 128), BF16), 0, 0)

    @pl.when(step == pl.num_programs(0) - 1)
    def _():
        qg = qg_s[...].reshape(qdir_s.shape)
        qdir = qdir_s[...]
        qeg = (qg - qdir * jnp.sum(qdir * qg, axis=-1, keepdims=True)) / qlen_s[:, :1]
        high = qeg.astype(BF16)
        low = (qeg - high.astype(F32)).astype(BF16)
        qs = qs_s[...]
        proj_query = dot(high, qs, 0, 0) + dot(low, qs, 0, 0)
        nt = nt_s[...]
        s = s_s[:, :1]
        wpt = wpt_ref[...].astype(F32)
        proj = nt * gain + s * bias_ref[...] + proj_query
        gain_row = jnp.sum(wpt * nt, axis=0, keepdims=True)
        bias_row = jnp.sum(wpt * s, axis=0, keepdims=True)
        index = lax.broadcasted_iota(jnp.int32, (tokens, width), 0)
        top = jnp.where(index == 0, gain_row, jnp.where(index == 1, bias_row, 0.0))
        spread = jnp.broadcast_to(l_s[:, :1], (tokens, width))
        rest_rows = jnp.zeros((128 - 2 * tokens, width), F32)
        right_s[...] = jnp.concatenate([proj, top, spread, rest_rows], axis=0).T
        half = width // CORES
        chunk = send_ref.shape[1]
        for ref, which in ((send_ref, 1 - core_ref[0]), (keep_ref, core_ref[0])):
            start = pl.multiple_of(which * half, half)
            left = wo_s[pl.ds(start, half)].astype(BF16)
            right = right_s[pl.ds(start, half)].astype(BF16)
            for c in range(half // chunk):
                ref[c, :, :width] = left[c * chunk : (c + 1) * chunk]
                ref[c, :, width:] = right[c * chunk : (c + 1) * chunk]


def student_backward(
    qidx, midx, lens, core, maps, payload, embeds, x, normed, inverse, gain, bias, wp, wpt,
    count, tokens, group_queries, chunk,
):
    total, width = x.shape
    emb = wp.shape[1]
    rows = split_rows(total, 720)
    dests = payload.shape[0]
    per = count // dests
    chunks = width // CORES // chunk
    block = lambda last: pl.BlockSpec((rows, last), lambda s, *_: (s, 0))
    whole = lambda a: pl.BlockSpec(a.shape, lambda s, *_: (0,) * a.ndim)
    full = pl.BlockSpec((chunks, chunk, width + emb + 128), lambda s, *_: (0, 0, 0))
    queries = dests * group_queries
    return pl.pallas_call(
        functools.partial(backward_kernel, tokens, count, per, group_queries),
        grid_spec=pltpu.PrefetchScalarGridSpec(
            num_scalar_prefetch=4,
            grid=(total // rows,),
            in_specs=[whole(maps), whole(payload), whole(embeds), block(width), block(width), block(128)]
            + [whole(a) for a in (gain, bias, wp, wpt)],
            out_specs=[block(width), full, full],
            scratch_shapes=[
                pltpu.VMEM((queries * tokens, width), BF16),
                pltpu.VMEM((queries, tokens, emb), BF16),
                pltpu.VMEM((queries * tokens, emb), F32),
                pltpu.VMEM((queries * tokens, 128), F32),
                pltpu.VMEM((queries, tokens, emb), F32),
                pltpu.VMEM((total, emb), F32),
                pltpu.VMEM((count, tokens, emb), F32),
                pltpu.VMEM((total, emb), F32),
                pltpu.VMEM((total, emb), BF16),
                pltpu.VMEM((tokens, 128), F32),
                pltpu.VMEM((rows, width), F32),
                pltpu.VMEM((width, width), F32),
                pltpu.VMEM((emb, width), F32),
                pltpu.VMEM((emb, 128), F32),
                pltpu.VMEM((width, emb + 128), F32),
            ],
        ),
        out_shape=[
            jax.ShapeDtypeStruct((total, width), BF16),
            jax.ShapeDtypeStruct((chunks, chunk, width + emb + 128), BF16),
            jax.ShapeDtypeStruct((chunks, chunk, width + emb + 128), BF16),
        ],
        compiler_params=params(),
        cost_estimate=cost(2 * total * width * (width + 2 * emb), 8 * total * width),
        name="student_backward",
    )(qidx, midx, lens, core, maps, payload, embeds, x, normed, inverse, gain, bias, wp, wpt)


def context_kernel(sg_ref, wo_ref, after_ref, out_ref):
    out_ref[...] = dot(sg_ref[...], wo_ref[...], 1, 1).astype(BF16)


def context_grad(sg, out_weight, after):
    total, width = sg.shape
    rows = split_rows(total, 720)
    block = pl.BlockSpec((rows, width), lambda s: (s, 0))
    return pl.pallas_call(
        context_kernel,
        grid=(total // rows,),
        in_specs=[block, pl.BlockSpec(out_weight.shape, lambda s: (0, 0)), ANY],
        out_specs=block,
        out_shape=jax.ShapeDtypeStruct(sg.shape, BF16),
        compiler_params=params(),
        cost_estimate=cost(2 * total * width * width, 4 * total * width),
        name="context_grad",
    )(sg, out_weight, after)


def split_sum_kernel(inputs, outputs, after, index_ref, *rest):
    ins, outs, total_s = rest[:inputs], rest[inputs + after : inputs + after + outputs], rest[-1]
    total = ins[0][...].astype(F32)
    for ref in ins[1:]:
        total = total + ref[...].astype(F32)
    total_s[...] = total.astype(BF16).reshape(total_s.shape)
    for k in range(outputs):
        outs[k][...] = total_s[index_ref[k]].reshape(outs[k].shape)


def split_sum(arrays, index, name, after=()):
    outputs = index.shape[0]
    shape = arrays[0].shape
    lead = shape[0] // outputs
    out = shape[1:] if lead == 1 else (lead,) + shape[1:]
    return pl.pallas_call(
        functools.partial(split_sum_kernel, len(arrays), outputs, len(after)),
        in_specs=[SMEM] + [VMEM] * len(arrays) + [ANY] * len(after),
        out_specs=[VMEM] * outputs,
        out_shape=[jax.ShapeDtypeStruct(out, BF16)] * outputs,
        scratch_shapes=[pltpu.VMEM((outputs, lead) + shape[1:], BF16)],
        compiler_params=params(),
        name=name,
    )(index, *arrays, *after)


def sum_kernel(*refs):
    total = refs[0][...].astype(F32)
    for ref in refs[1:-1]:
        total = total + ref[...].astype(F32)
    refs[-1][...] = total.astype(BF16)


def plain_sum(arrays, name):
    return pl.pallas_call(
        sum_kernel,
        in_specs=[VMEM] * len(arrays),
        out_specs=VMEM,
        out_shape=jax.ShapeDtypeStruct(arrays[0].shape, BF16),
        compiler_params=params(),
        name=name,
    )(*arrays)


def unpack_kernel(parts, width, emb, tokens, scale, index_ref, *rest):
    ins = rest[:parts]
    wo_ref, proj_ref, gain_ref, bias_ref, loss_ref, small_s = rest[parts:]
    per = ins[0].shape[0]
    for a in range(parts):
        for k in range(per):
            c = index_ref[a * per + k]
            value = ins[a][k].astype(F32)
            wo_ref[c] = value[:, :width]
            proj_ref[c] = value[:, width : width + emb]
            small_s[c] = value[:, width + emb :]
    turned = small_s[...].reshape(width, 128).T
    gain_ref[...] = turned[0:1]
    bias_ref[...] = turned[1:2]
    loss_ref[0] = jnp.sum(turned[tokens : 2 * tokens, 0:1]) * scale


def unpack(arrays, index, width, emb, tokens, scale):
    parts = len(arrays)
    per, chunk, _ = arrays[0].shape
    chunks = parts * per
    return pl.pallas_call(
        functools.partial(unpack_kernel, parts, width, emb, tokens, scale),
        in_specs=[SMEM] + [VMEM] * parts,
        out_specs=[VMEM] * 4 + [SMEM],
        out_shape=[jax.ShapeDtypeStruct((chunks, chunk, n), F32) for n in (width, emb)]
        + [jax.ShapeDtypeStruct((1, width), F32)] * 2
        + [jax.ShapeDtypeStruct((1,), F32)],
        scratch_shapes=[pltpu.VMEM((chunks, chunk, 128), F32)],
        compiler_params=params(),
        name="unpack",
    )(index, *arrays)


def local(
    context,
    stream,
    out_weight,
    gain,
    bias,
    proj_weight,
    query_states,
    passage_len,
    passage_dest,
    teacher_states,
    teacher_query,
    teacher_key,
):
    dp = lax.axis_size("dp")
    nt = lax.axis_size("tensor")
    chips = dp // CORES
    me = lax.axis_index("dp")
    chip, core = me // CORES, me % CORES
    mt = lax.axis_index("tensor")
    count, seq, width = context.shape
    emb = proj_weight.shape[1]
    group_queries, tokens, _ = query_states.shape
    depth, heads = teacher_query.shape
    per = count // dp
    per_query = count * nt // group_queries

    def flat(a):
        return a.transpose(1, 0, 2).reshape(-1, a.shape[2])

    def shift_chip(x, k):
        return lax.ppermute(
            x, "dp", [(c * CORES + o, (c + k) % chips * CORES + o) for c in range(chips) for o in range(CORES)]
        )

    def swap_core(x):
        return lax.ppermute(x, "dp", [(d, d ^ 1) for d in range(dp)])

    def shift_t(x, k):
        return lax.ppermute(x, "tensor", [(t, (t + k) % nt) for t in range(nt)])

    part = depth // dp
    mine = jnp.stack(
        [lax.dynamic_slice_in_dim(w, me * part, part, 0) for w in (teacher_query, teacher_key)]
    )
    along = jnp.concatenate([shift_t(mine, k) for k in range(1, nt)], axis=0)
    plane = [along] + [shift_chip(along, k) for k in range(1, chips)]
    pieces = plane + [swap_core(x) for x in plane]
    shifts = jnp.arange(chips, dtype=jnp.int32)
    behind = (chip - shifts) % chips
    piece_rows = jnp.concatenate([behind * CORES + core, behind * CORES + 1 - core]).astype(jnp.int32)

    dest_group = passage_dest // (count * nt)
    rows = jnp.arange(count, dtype=jnp.int32)
    rank = jnp.sum(
        (dest_group[:, None] == dest_group[None, :]) & (rows[None, :] < rows[:, None]), axis=1, dtype=jnp.int32
    )
    place = dest_group * per + rank
    positions = jnp.sum(
        jnp.where(place[:, None] == rows[None, :], (passage_dest % count)[:, None], 0), axis=0
    )
    queries = query_states.reshape(group_queries * tokens, width)
    extra = jnp.pad(positions.astype(BF16)[None, :], ((0, 15), (0, width - count)))
    payload = jnp.concatenate([queries, extra], axis=0)
    payload = lax.all_to_all(
        jnp.broadcast_to(payload[None], (dp,) + payload.shape), "dp", split_axis=0, concat_axis=0, tiled=True
    )
    told = payload[:, group_queries * tokens, :count].astype(jnp.int32)
    order = lax.dynamic_slice_in_dim(told, me * per, per, 1).reshape(-1)
    midx = place.astype(jnp.int32)
    qidx = (passage_dest // per_query).astype(jnp.int32)

    gain2, bias2 = gain.reshape(1, width), bias.reshape(1, width)
    x = flat(context)
    normed, embeds, inverse = student_forward(x, flat(stream), out_weight, gain2, bias2, proj_weight, along)
    maps = teacher_maps(
        order, piece_rows, flat(teacher_states), teacher_query, teacher_key, inverse, pieces, count, tokens
    )
    maps = lax.all_to_all(maps, "dp", split_axis=0, concat_axis=0, tiled=True)
    chunk = width // (CORES * chips * nt)
    sg, send, keep = student_backward(
        qidx, midx, passage_len, core.astype(jnp.int32).reshape(1), maps, payload,
        embeds, x, normed, inverse, gain2, bias2, proj_weight, proj_weight.T,
        count, tokens, group_queries, chunk,
    )

    ahead = ((chip + shifts) % chips).astype(jnp.int32)
    t_shifts = jnp.arange(nt, dtype=jnp.int32)
    t_ahead = ((mt + t_shifts) % nt).astype(jnp.int32)
    parts = split_sum([keep, swap_core(send)], ahead, "sum_cores")
    grad_context = context_grad(sg, out_weight, parts[0])
    parts = [parts[0]] + [shift_chip(parts[k], k) for k in range(1, chips)]
    parts = split_sum(parts, t_ahead, "sum_plane", (grad_context,))
    parts = [parts[0]] + [shift_t(parts[k], k) for k in range(1, nt)]
    total = plain_sum(parts, "sum_tensor")
    line = jnp.stack([total] + [shift_t(total, k) for k in range(1, nt)])
    plane = [line] + [shift_chip(line, k) for k in range(1, chips)]
    arrays = plane + [swap_core(x) for x in plane]
    t_behind = (mt - t_shifts) % nt
    base = jnp.concatenate([core * chips + behind, (1 - core) * chips + behind]) * nt
    index = (base[:, None] + t_behind[None, :]).reshape(-1).astype(jnp.int32)
    grad_out, grad_proj, grad_gain, grad_bias, loss = unpack(
        arrays, index, width, emb, tokens, 1.0 / (count * dp * nt * tokens)
    )
    return (
        loss.reshape(()),
        grad_out.reshape(width, width),
        grad_proj.reshape(width, emb),
        grad_gain.reshape(width),
        grad_bias.reshape(width),
        grad_context.reshape(seq, count, width).transpose(1, 0, 2),
    )


def solution(mesh):
    return jax.shard_map(
        local,
        mesh=mesh,
        in_specs=(
            P(("dp", "tensor"), None, None),
            P(("dp", "tensor"), None, None),
            P(),
            P(),
            P(),
            P(),
            P("dp", None, None),
            P(("dp", "tensor")),
            P(("dp", "tensor")),
            P(("dp", "tensor"), None, None),
            P(None, "tensor"),
            P(None, "tensor"),
        ),
        out_specs=(P(), P(), P(), P(), P(), P(("dp", "tensor"), None, None)),
        check_vma=False,
    )
```

profile of v0, /device:TPU:0, one launch (start us, length us, event | category | flops | bytes accessed | tf_op | source)
XLA Modules:
  0.0 160.3 jit_solution(11249795515285523971)
XLA Ops:
  1.5 3.1 %collective-permute-start = (bf16[2,128,256]{2,1,0:T(8,128)(2,1)S(1)}, bf16[2,128,256]{2,1,0:T(8,128)(2,1)S(1)}, u32[]{:S(2)}, u32[]{:S(2)}) collective-permute-start(bf16[2,128,256]{2,1,0:T(8,128)(2,1)S(1)} %pad_maximum_fusion.1), channel_id=1, source_target_pairs={{0,1},{1,2},{2,3},{3,0},{4,5},{5,6},{6,7},{7,4},{8,9},{9,10},{10,1... | collective-permute-start | bytes 393224 | tf_op jit(solution)/shard_map/ppermute | solution.py:491
  4.6 2.6 %collective-permute-start.1 = (bf16[2,128,256]{2,1,0:T(8,128)(2,1)S(1)}, bf16[2,128,256]{2,1,0:T(8,128)(2,1)S(1)}, u32[]{:S(2)}, u32[]{:S(2)}) collective-permute-start(bf16[2,128,256]{2,1,0:T(8,128)(2,1)S(1)} %pad_maximum_fusion.1), channel_id=1, source_target_pairs={{0,2},{1,3},{2,0},{3,1},{4,6},{5,7},{6,4},{7,5},{8,10},{9,11},{10,... | collective-permute-start | bytes 393224 | tf_op jit(solution)/shard_map/ppermute | solution.py:491
  9.5 1.6 collective-permute-done
  11.1 4.8 %collective-permute-done.1 = bf16[2,128,256]{2,1,0:T(8,128)(2,1)S(1)} collective-permute-done((bf16[2,128,256]{2,1,0:T(8,128)(2,1)S(1)}, bf16[2,128,256]{2,1,0:T(8,128)(2,1)S(1)}, u32[]{:S(2)}, u32[]{:S(2)}) %collective-permute-start.1) | collective-permute-done | bytes 131104 | tf_op jit(solution)/shard_map/ppermute | solution.py:491
  22.1 3.5 %all-to-all-start = ((bf16[8,48,768]{2,1,0:T(8,128)(2,1)}), bf16[8,48,768]{2,1,0:T(8,128)(2,1)S(1)}, u32[]{:S(2)}, u32[]{:S(2)}) async-start(bf16[8,48,768]{2,1,0:T(8,128)(2,1)} %broadcast_in_dim.16), calls=%async_computation | async-start | bytes 1179648 | tf_op jit(solution)/shard_map/all_to_all | solution.py:516
  26.1 2.8 %collective-permute-done.3.rest_1_ = bf16[6,128,256]{2,1,0:T(8,128)(2,1)S(1)} collective-permute-done((bf16[6,128,256]{2,1,0:T(8,128)(2,1)S(1)}, bf16[6,128,256]{2,1,0:T(8,128)(2,1)S(1)}, u32[]{:S(2)}, u32[]{:S(2)}) %collective-permute-start.3) | collective-permute-done | bytes 393248 | tf_op jit(solution)/shard_map/ppermute | solution.py:483
  28.9 7.4 %collective-permute-done.4.rest_2_ = bf16[6,128,256]{2,1,0:T(8,128)(2,1)S(1)} collective-permute-done((bf16[6,128,256]{2,1,0:T(8,128)(2,1)S(1)}, bf16[6,128,256]{2,1,0:T(8,128)(2,1)S(1)}, u32[]{:S(2)}, u32[]{:S(2)}) %collective-permute-start.4) | collective-permute-done | bytes 393248 | tf_op jit(solution)/shard_map/ppermute | solution.py:483
  40.6 12.5 %student_forward.1 = (bf16[2880,768]{1,0:T(8,128)(2,1)}, f32[2880,128]{1,0:T(8,128)}, f32[2880,128]{1,0:T(8,128)}) custom-call(bf16[2880,768]{1,0:T(8,128)(2,1)} %bitcast.37, bf16[2880,768]{1,0:T(8,128)(2,1)} %bitcast.36, bf16[768,768]{1,0:T(8,128)(2,1)} %wo_ref.3, f32[1,768]{1,0:T(1,128)} %reshape.108.gain_ref, f32[1,768]{1,0:T(1,128)} %reshape.109.bias_ref, ...), custom_call_target="tpu_custom_call" | custom-call | flops 3963617280 | bytes 17694720 | tf_op jit(solution)/shard_map/student_forward/pallas_call | solution.py:67
  54.9 13.9 %teacher_maps.1 = bf16[16,32,180]{2,1,0:T(8,128)(2,1)} custom-call(s32[16]{0:T(128)} %reshape.104.order_ref, s32[8]{0:T(128)} %pad_add_fusion.rows_ref, bf16[3392,1024]{1,0:T(8,128)(2,1)} %bitcast.35, bf16[1024,256]{1,0:T(8,128)(2,1)} %wq_ref.1, bf16[1024,256]{1,0:T(8,128)(2,1)} %wk_ref.1, f32[2880,128]{1,0:T(8,128)} %get-tuple-element.25.after_ref.inv_ref, ...), custom_call_target="tpu_custom_call" | custom-call | flops 4294967296 | bytes 11141120 | tf_op jit(solution)/shard_map/teacher_maps/pallas_call | solution.py:163
  68.8 3.7 %all-to-all-start.1 = ((bf16[16,32,180]{2,1,0:T(8,128)(2,1)}), bf16[16,32,180]{2,1,0:T(8,128)(2,1)S(1)}, u32[]{:S(2)}, u32[]{:S(2)}) async-start(bf16[16,32,180]{2,1,0:T(8,128)(2,1)} %teacher_maps.1), calls=%async_computation.1 | async-start | bytes 524288 | tf_op jit(solution)/shard_map/all_to_all | solution.py:530
  73.3 6.1 %all-to-all-done.1.maps_ref = bf16[16,32,180]{2,1,0:T(8,128)(2,1)S(1)} async-done(((bf16[16,32,180]{2,1,0:T(8,128)(2,1)}), bf16[16,32,180]{2,1,0:T(8,128)(2,1)S(1)}, u32[]{:S(2)}, u32[]{:S(2)}) %all-to-all-start.1) | async-done | bytes 184352 | tf_op jit(solution)/shard_map/all_to_all | solution.py:530
  80.1 21.9 %student_backward.1 = (bf16[2880,768]{1,0:T(8,128)(2,1)}, bf16[16,24,1024]{2,1,0:T(8,128)(2,1)}, bf16[16,24,1024]{2,1,0:T(8,128)(2,1)}) custom-call(s32[16]{0:T(128)} %copy-done.25, s32[16]{0:T(128)} %copy-done.26, s32[16]{0:T(128)} %len_ref.1, s32[1]{0:T(128)} %bitcast.core_ref, bf16[16,32,180]{2,1,0:T(8,128)(2,1)} %copy-done.3, ...), custom_call_target="tpu_custom_call" | custom-call | flops 4529848320 | bytes 17694720 | tf_op jit(solution)/shard_map/student_backward/pallas_call | solution.py:317
  105.4 2.7 %sum_cores.1 = (bf16[4,24,1024]{2,1,0:T(8,128)(2,1)}, bf16[4,24,1024]{2,1,0:T(8,128)(2,1)}, bf16[4,24,1024]{2,1,0:T(8,128)(2,1)}, bf16[4,24,1024]{2,1,0:T(8,128)(2,1)}) custom-call(s32[4]{0:T(128)} %and_select_fusion.2.index_ref, bf16[16,24,1024]{2,1,0:T(8,128)(2,1)} %get-tuple-element.28.rest_0_, bf16[16,24,1024]{2,1,0:T(8,128)(2,1)} %copy-done), custom_call_target="tpu_custom_call" | custom-call | tf_op jit(solution)/shard_map/sum_cores/pallas_call | solution.py:389
  109.2 2.5 %collective-permute-start.13 = (bf16[4,24,1024]{2,1,0:T(8,128)(2,1)}, bf16[4,24,1024]{2,1,0:T(8,128)(2,1)S(1)}, u32[]{:S(2)}, u32[]{:S(2)}) collective-permute-start(bf16[4,24,1024]{2,1,0:T(8,128)(2,1)} %get-tuple-element.33), channel_id=1, source_target_pairs={{0,24},{4,28},{8,0},{12,4},{16,8},{20,12},{24,16},{28,20},{1,25},{... | collective-permute-start | bytes 589832 | tf_op jit(solution)/shard_map/ppermute | solution.py:483
  111.7 7.5 %context_grad.1.rest_4_ = bf16[2880,768]{1,0:T(8,128)(2,1)} custom-call(bf16[2880,768]{1,0:T(8,128)(2,1)} %get-tuple-element.34.sg_ref, bf16[768,768]{1,0:T(8,128)(2,1)} %wo_ref.3, bf16[4,24,1024]{2,1,0:T(8,128)(2,1)} %get-tuple-element.30.after_ref.rest_0_), custom_call_target="tpu_custom_call" | custom-call | flops 3397386240 | bytes 8847360 | tf_op jit(solution)/shard_map/context_grad/pallas_call | solution.py:362
  121.1 2.1 %sum_plane.1 = (bf16[24,1024]{1,0:T(8,128)(2,1)}, bf16[24,1024]{1,0:T(8,128)(2,1)}, bf16[24,1024]{1,0:T(8,128)(2,1)}, bf16[24,1024]{1,0:T(8,128)(2,1)}) custom-call(s32[4]{0:T(128)} %and_select_fusion.3.index_ref, bf16[4,24,1024]{2,1,0:T(8,128)(2,1)} %get-tuple-element.30.after_ref.rest_0_, bf16[4,24,1024]{2,1,0:T(8,128)(2,1)} %copy-done.4, ...), custom_call_target="tpu_custom_call" | custom-call | tf_op jit(solution)/shard_map/sum_plane/pallas_call | solution.py:389
  123.1 3.5 %collective-permute-start.14 = (bf16[24,1024]{1,0:T(8,128)(2,1)}, bf16[24,1024]{1,0:T(8,128)(2,1)S(1)}, u32[]{:S(2)}, u32[]{:S(2)}) collective-permute-start(bf16[24,1024]{1,0:T(8,128)(2,1)} %get-tuple-element.36), channel_id=1, source_target_pairs={{0,1},{1,2},{2,3},{3,0},{4,5},{5,6},{6,7},{7,4},{8,9},{9,10},{10,1... | collective-permute-start | bytes 147464 | tf_op jit(solution)/shard_map/ppermute | solution.py:491
  129.8 2.3 %collective-permute-done.15.refs_2_ = bf16[24,1024]{1,0:T(8,128)(2,1)S(1)} collective-permute-done((bf16[24,1024]{1,0:T(8,128)(2,1)}, bf16[24,1024]{1,0:T(8,128)(2,1)S(1)}, u32[]{:S(2)}, u32[]{:S(2)}) %collective-permute-start.15) | collective-permute-done | bytes 49184 | tf_op jit(solution)/shard_map/ppermute | solution.py:491
  135.3 2.5 %collective-permute-start.18 = (bf16[24,1024]{1,0:T(8,128)(2,1)}, bf16[24,1024]{1,0:T(8,128)(2,1)S(1)}, u32[]{:S(2)}, u32[]{:S(2)}) collective-permute-start(bf16[24,1024]{1,0:T(8,128)(2,1)} %sum_tensor.1), channel_id=1, source_target_pairs={{0,2},{1,3},{2,0},{3,1},{4,6},{5,7},{6,4},{7,5},{8,10},{9,11},{10,... | collective-permute-start | bytes 147464 | tf_op jit(solution)/shard_map/ppermute | solution.py:491
  138.9 1.9 %collective-permute-done.17 = bf16[24,1024]{1,0:T(8,128)(2,1)S(1)} collective-permute-done((bf16[24,1024]{1,0:T(8,128)(2,1)}, bf16[24,1024]{1,0:T(8,128)(2,1)S(1)}, u32[]{:S(2)}, u32[]{:S(2)}) %collective-permute-start.17) | collective-permute-done | bytes 49184 | tf_op jit(solution)/shard_map/ppermute | solution.py:491
  142.9 1.6 collective-permute-start.20
  146.9 2.7 %collective-permute-done.20.rest_1_ = bf16[4,24,1024]{2,1,0:T(8,128)(2,1)S(1)} collective-permute-done((bf16[4,24,1024]{2,1,0:T(8,128)(2,1)S(1)}, bf16[4,24,1024]{2,1,0:T(8,128)(2,1)S(1)}, u32[]{:S(2)}, u32[]{:S(2)}) %collective-permute-start.20) | collective-permute-done | bytes 196640 | tf_op jit(solution)/shard_map/ppermute | solution.py:483
  149.7 2.0 %collective-permute-done.21.rest_2_ = bf16[4,24,1024]{2,1,0:T(8,128)(2,1)S(1)} collective-permute-done((bf16[4,24,1024]{2,1,0:T(8,128)(2,1)S(1)}, bf16[4,24,1024]{2,1,0:T(8,128)(2,1)S(1)}, u32[]{:S(2)}, u32[]{:S(2)}) %collective-permute-start.21) | collective-permute-done | bytes 196640 | tf_op jit(solution)/shard_map/ppermute | solution.py:483
  154.5 3.3 %unpack.1 = (f32[32,24,768]{2,1,0:T(8,128)}, f32[32,24,128]{2,1,0:T(8,128)}, f32[1,768]{1,0:T(1,128)}, f32[1,768]{1,0:T(1,128)}, f32[1]{0:T(128)}) custom-call(s32[32]{0:T(128)} %add.110.index_ref, bf16[4,24,1024]{2,1,0:T(8,128)(2,1)} %copy-done.1, bf16[4,24,1024]{2,1,0:T(8,128)(2,1)} %copy-done.8, bf16[4,24,1024]{2,1,0:T(8,128)(2,1)} %copy-done.9, ...), custom_call_target="tpu_custom_call" | custom-call | tf_op jit(solution)/shard_map/unpack/pallas_call | solution.py:439
  (126 shorter events, 41.2 us)
Async XLA Ops:
  1.5 9.5 %collective-permute-start = (bf16[2,128,256]{2,1,0:T(8,128)(2,1)S(1)}, bf16[2,128,256]{2,1,0:T(8,128)(2,1)S(1)}, u32[]{:S(2)}, u32[]{:S(2)}) collective-permute-start(bf16[2,128,256]{2,1,0:T(8,128)(2,1)S(1)} %pad_maximum_fusion.1), channel_id=1, source_target_pairs={{0,1},{1,2},{2,3},{3,0},{4,5},{5,6},{6,7},{7,4},{8,9},{9,10},{10,1... | collective-permute-start | bytes 393224 | tf_op jit(solution)/shard_map/ppermute | solution.py:491
  4.6 11.2 %collective-permute-start.1 = (bf16[2,128,256]{2,1,0:T(8,128)(2,1)S(1)}, bf16[2,128,256]{2,1,0:T(8,128)(2,1)S(1)}, u32[]{:S(2)}, u32[]{:S(2)}) collective-permute-start(bf16[2,128,256]{2,1,0:T(8,128)(2,1)S(1)} %pad_maximum_fusion.1), channel_id=1, source_target_pairs={{0,2},{1,3},{2,0},{3,1},{4,6},{5,7},{6,4},{7,5},{8,10},{9,11},{10,... | collective-permute-start | bytes 393224 | tf_op jit(solution)/shard_map/ppermute | solution.py:491
  7.2 8.7 %collective-permute-start.2 = (bf16[2,128,256]{2,1,0:T(8,128)(2,1)S(1)}, bf16[2,128,256]{2,1,0:T(8,128)(2,1)S(1)}, u32[]{:S(2)}, u32[]{:S(2)}) collective-permute-start(bf16[2,128,256]{2,1,0:T(8,128)(2,1)S(1)} %pad_maximum_fusion.1), channel_id=1, source_target_pairs={{0,3},{1,0},{2,1},{3,2},{4,7},{5,4},{6,5},{7,6},{8,11},{9,8},{10,9... | collective-permute-start | bytes 393224 | tf_op jit(solution)/shard_map/ppermute | solution.py:491
  15.9 13.0 %collective-permute-start.3 = (bf16[6,128,256]{2,1,0:T(8,128)(2,1)S(1)}, bf16[6,128,256]{2,1,0:T(8,128)(2,1)S(1)}, u32[]{:S(2)}, u32[]{:S(2)}) collective-permute-start(bf16[6,128,256]{2,1,0:T(8,128)(2,1)S(1)} %constant_dynamic-update-slice_fusion.after_ref.rest_0_), channel_id=1, source_target_pairs={{0,8},{4,12},{8,16},{12,20},{16,24},{20,28},{24,0},{28,4},{1,9},{5... | collective-permute-start | bytes 1179656 | tf_op jit(solution)/shard_map/ppermute | solution.py:483
  17.5 18.9 %collective-permute-start.4 = (bf16[6,128,256]{2,1,0:T(8,128)(2,1)S(1)}, bf16[6,128,256]{2,1,0:T(8,128)(2,1)S(1)}, u32[]{:S(2)}, u32[]{:S(2)}) collective-permute-start(bf16[6,128,256]{2,1,0:T(8,128)(2,1)S(1)} %constant_dynamic-update-slice_fusion.after_ref.rest_0_), channel_id=1, source_target_pairs={{0,16},{4,20},{8,24},{12,28},{16,0},{20,4},{24,8},{28,12},{1,17},{... | collective-permute-start | bytes 1179656 | tf_op jit(solution)/shard_map/ppermute | solution.py:483
  19.0 18.4 %collective-permute-start.5 = (bf16[6,128,256]{2,1,0:T(8,128)(2,1)S(1)}, bf16[6,128,256]{2,1,0:T(8,128)(2,1)S(1)}, u32[]{:S(2)}, u32[]{:S(2)}) collective-permute-start(bf16[6,128,256]{2,1,0:T(8,128)(2,1)S(1)} %constant_dynamic-update-slice_fusion.after_ref.rest_0_), channel_id=1, source_target_pairs={{0,24},{4,28},{8,0},{12,4},{16,8},{20,12},{24,16},{28,20},{1,25},{... | collective-permute-start | bytes 1179656 | tf_op jit(solution)/shard_map/ppermute | solution.py:483
  22.1 31.0 %all-to-all-start = ((bf16[8,48,768]{2,1,0:T(8,128)(2,1)}), bf16[8,48,768]{2,1,0:T(8,128)(2,1)S(1)}, u32[]{:S(2)}, u32[]{:S(2)}) async-start(bf16[8,48,768]{2,1,0:T(8,128)(2,1)} %broadcast_in_dim.16), calls=%async_computation | async-start | bytes 1179648 | tf_op jit(solution)/shard_map/all_to_all | solution.py:516
  25.7 28.2 %collective-permute-start.6 = (bf16[6,128,256]{2,1,0:T(8,128)(2,1)S(1)}, bf16[6,128,256]{2,1,0:T(8,128)(2,1)S(1)}, u32[]{:S(2)}, u32[]{:S(2)}) collective-permute-start(bf16[6,128,256]{2,1,0:T(8,128)(2,1)S(1)} %constant_dynamic-update-slice_fusion.after_ref.rest_0_), channel_id=1, source_target_pairs={{0,4},{4,0},{8,12},{12,8},{16,20},{20,16},{24,28},{28,24},{1,5},{5... | collective-permute-start | bytes 1179656 | tf_op jit(solution)/shard_map/ppermute | solution.py:488
  28.9 25.0 %collective-permute-start.7 = (bf16[6,128,256]{2,1,0:T(8,128)(2,1)S(1)}, bf16[6,128,256]{2,1,0:T(8,128)(2,1)S(1)}, u32[]{:S(2)}, u32[]{:S(2)}) collective-permute-start(bf16[6,128,256]{2,1,0:T(8,128)(2,1)S(1)} %collective-permute-done.3.rest_1_), channel_id=1, source_target_pairs={{0,4},{4,0},{8,12},{12,8},{16,20},{20,16},{24,28},{28,24},{1,5},{5... | collective-permute-start | bytes 1179656 | tf_op jit(solution)/shard_map/ppermute | solution.py:488
  36.3 17.5 %collective-permute-start.8 = (bf16[6,128,256]{2,1,0:T(8,128)(2,1)S(1)}, bf16[6,128,256]{2,1,0:T(8,128)(2,1)S(1)}, u32[]{:S(2)}, u32[]{:S(2)}) collective-permute-start(bf16[6,128,256]{2,1,0:T(8,128)(2,1)S(1)} %collective-permute-done.4.rest_2_), channel_id=1, source_target_pairs={{0,4},{4,0},{8,12},{12,8},{16,20},{20,16},{24,28},{28,24},{1,5},{5... | collective-permute-start | bytes 1179656 | tf_op jit(solution)/shard_map/ppermute | solution.py:488
  37.4 16.5 %collective-permute-start.9 = (bf16[6,128,256]{2,1,0:T(8,128)(2,1)S(1)}, bf16[6,128,256]{2,1,0:T(8,128)(2,1)}, u32[]{:S(2)}, u32[]{:S(2)}) collective-permute-start(bf16[6,128,256]{2,1,0:T(8,128)(2,1)S(1)} %collective-permute-done.5.rest_3_), channel_id=1, source_target_pairs={{0,4},{4,0},{8,12},{12,8},{16,20},{20,16},{24,28},{28,24},{1,5},{5... | collective-permute-start | bytes 1179656 | tf_op jit(solution)/shard_map/ppermute | solution.py:488
  68.8 10.6 %all-to-all-start.1 = ((bf16[16,32,180]{2,1,0:T(8,128)(2,1)}), bf16[16,32,180]{2,1,0:T(8,128)(2,1)S(1)}, u32[]{:S(2)}, u32[]{:S(2)}) async-start(bf16[16,32,180]{2,1,0:T(8,128)(2,1)} %teacher_maps.1), calls=%async_computation.1 | async-start | bytes 524288 | tf_op jit(solution)/shard_map/all_to_all | solution.py:530
  108.1 11.2 %collective-permute-start.11 = (bf16[4,24,1024]{2,1,0:T(8,128)(2,1)}, bf16[4,24,1024]{2,1,0:T(8,128)(2,1)S(1)}, u32[]{:S(2)}, u32[]{:S(2)}) collective-permute-start(bf16[4,24,1024]{2,1,0:T(8,128)(2,1)} %get-tuple-element.31), channel_id=1, source_target_pairs={{0,8},{4,12},{8,16},{12,20},{16,24},{20,28},{24,0},{28,4},{1,9},{5... | collective-permute-start | bytes 589832 | tf_op jit(solution)/shard_map/ppermute | solution.py:483
  108.6 11.1 %collective-permute-start.12 = (bf16[4,24,1024]{2,1,0:T(8,128)(2,1)}, bf16[4,24,1024]{2,1,0:T(8,128)(2,1)S(1)}, u32[]{:S(2)}, u32[]{:S(2)}) collective-permute-start(bf16[4,24,1024]{2,1,0:T(8,128)(2,1)} %get-tuple-element.32), channel_id=1, source_target_pairs={{0,16},{4,20},{8,24},{12,28},{16,0},{20,4},{24,8},{28,12},{1,17},{... | collective-permute-start | bytes 589832 | tf_op jit(solution)/shard_map/ppermute | solution.py:483
  109.2 10.5 %collective-permute-start.13 = (bf16[4,24,1024]{2,1,0:T(8,128)(2,1)}, bf16[4,24,1024]{2,1,0:T(8,128)(2,1)S(1)}, u32[]{:S(2)}, u32[]{:S(2)}) collective-permute-start(bf16[4,24,1024]{2,1,0:T(8,128)(2,1)} %get-tuple-element.33), channel_id=1, source_target_pairs={{0,24},{4,28},{8,0},{12,4},{16,8},{20,12},{24,16},{28,20},{1,25},{... | collective-permute-start | bytes 589832 | tf_op jit(solution)/shard_map/ppermute | solution.py:483
  123.1 6.7 %collective-permute-start.14 = (bf16[24,1024]{1,0:T(8,128)(2,1)}, bf16[24,1024]{1,0:T(8,128)(2,1)S(1)}, u32[]{:S(2)}, u32[]{:S(2)}) collective-permute-start(bf16[24,1024]{1,0:T(8,128)(2,1)} %get-tuple-element.36), channel_id=1, source_target_pairs={{0,1},{1,2},{2,3},{3,0},{4,5},{5,6},{6,7},{7,4},{8,9},{9,10},{10,1... | collective-permute-start | bytes 147464 | tf_op jit(solution)/shard_map/ppermute | solution.py:491
  126.6 5.6 %collective-permute-start.15 = (bf16[24,1024]{1,0:T(8,128)(2,1)}, bf16[24,1024]{1,0:T(8,128)(2,1)S(1)}, u32[]{:S(2)}, u32[]{:S(2)}) collective-permute-start(bf16[24,1024]{1,0:T(8,128)(2,1)} %get-tuple-element.37), channel_id=1, source_target_pairs={{0,2},{1,3},{2,0},{3,1},{4,6},{5,7},{6,4},{7,5},{8,10},{9,11},{10,... | collective-permute-start | bytes 147464 | tf_op jit(solution)/shard_map/ppermute | solution.py:491
  127.8 4.7 %collective-permute-start.16 = (bf16[24,1024]{1,0:T(8,128)(2,1)}, bf16[24,1024]{1,0:T(8,128)(2,1)S(1)}, u32[]{:S(2)}, u32[]{:S(2)}) collective-permute-start(bf16[24,1024]{1,0:T(8,128)(2,1)} %get-tuple-element.38), channel_id=1, source_target_pairs={{0,3},{1,0},{2,1},{3,2},{4,7},{5,4},{6,5},{7,6},{8,11},{9,8},{10,9... | collective-permute-start | bytes 147464 | tf_op jit(solution)/shard_map/ppermute | solution.py:491
  134.6 6.2 %collective-permute-start.17 = (bf16[24,1024]{1,0:T(8,128)(2,1)}, bf16[24,1024]{1,0:T(8,128)(2,1)S(1)}, u32[]{:S(2)}, u32[]{:S(2)}) collective-permute-start(bf16[24,1024]{1,0:T(8,128)(2,1)} %sum_tensor.1), channel_id=1, source_target_pairs={{0,1},{1,2},{2,3},{3,0},{4,5},{5,6},{6,7},{7,4},{8,9},{9,10},{10,1... | collective-permute-start | bytes 147464 | tf_op jit(solution)/shard_map/ppermute | solution.py:491
  135.3 6.3 %collective-permute-start.18 = (bf16[24,1024]{1,0:T(8,128)(2,1)}, bf16[24,1024]{1,0:T(8,128)(2,1)S(1)}, u32[]{:S(2)}, u32[]{:S(2)}) collective-permute-start(bf16[24,1024]{1,0:T(8,128)(2,1)} %sum_tensor.1), channel_id=1, source_target_pairs={{0,2},{1,3},{2,0},{3,1},{4,6},{5,7},{6,4},{7,5},{8,10},{9,11},{10,... | collective-permute-start | bytes 147464 | tf_op jit(solution)/shard_map/ppermute | solution.py:491
  142.9 6.7 %collective-permute-start.20 = (bf16[4,24,1024]{2,1,0:T(8,128)(2,1)S(1)}, bf16[4,24,1024]{2,1,0:T(8,128)(2,1)S(1)}, u32[]{:S(2)}, u32[]{:S(2)}) collective-permute-start(bf16[4,24,1024]{2,1,0:T(8,128)(2,1)S(1)} %pad_maximum_fusion.rest_0_), channel_id=1, source_target_pairs={{0,8},{4,12},{8,16},{12,20},{16,24},{20,28},{24,0},{28,4},{1,9},{5... | collective-permute-start | bytes 589832 | tf_op jit(solution)/shard_map/ppermute | solution.py:483
  144.5 7.1 %collective-permute-start.21 = (bf16[4,24,1024]{2,1,0:T(8,128)(2,1)S(1)}, bf16[4,24,1024]{2,1,0:T(8,128)(2,1)S(1)}, u32[]{:S(2)}, u32[]{:S(2)}) collective-permute-start(bf16[4,24,1024]{2,1,0:T(8,128)(2,1)S(1)} %pad_maximum_fusion.rest_0_), channel_id=1, source_target_pairs={{0,16},{4,20},{8,24},{12,28},{16,0},{20,4},{24,8},{28,12},{1,17},{... | collective-permute-start | bytes 589832 | tf_op jit(solution)/shard_map/ppermute | solution.py:483
  145.9 5.8 %collective-permute-start.22 = (bf16[4,24,1024]{2,1,0:T(8,128)(2,1)S(1)}, bf16[4,24,1024]{2,1,0:T(8,128)(2,1)S(1)}, u32[]{:S(2)}, u32[]{:S(2)}) collective-permute-start(bf16[4,24,1024]{2,1,0:T(8,128)(2,1)S(1)} %pad_maximum_fusion.rest_0_), channel_id=1, source_target_pairs={{0,24},{4,28},{8,0},{12,4},{16,8},{20,12},{24,16},{28,20},{1,25},{... | collective-permute-start | bytes 589832 | tf_op jit(solution)/shard_map/ppermute | solution.py:483
  146.9 5.9 %collective-permute-start.23 = (bf16[4,24,1024]{2,1,0:T(8,128)(2,1)S(1)}, bf16[4,24,1024]{2,1,0:T(8,128)(2,1)S(1)}, u32[]{:S(2)}, u32[]{:S(2)}) collective-permute-start(bf16[4,24,1024]{2,1,0:T(8,128)(2,1)S(1)} %pad_maximum_fusion.rest_0_), channel_id=1, source_target_pairs={{0,4},{4,0},{8,12},{12,8},{16,20},{20,16},{24,28},{28,24},{1,5},{5... | collective-permute-start | bytes 589832 | tf_op jit(solution)/shard_map/ppermute | solution.py:488
  (32 other events, 246.0 us)
where the time goes:
time: 161 us; the launch traced here: 160 us
  Pallas kernels  65.2 us (40%)
  waiting for transfers between devices  37.6 us (23%)
  starting transfers between devices  37.4 us (23%)
  local copies, waits for them, and re-layouts  12 us (7%)
  other arithmetic  7.18 us (4%)
    pallas_call x1, Pallas kernels, student_backward(): pl.pallas_call(functools.partial(backward_kernel, tokens, count, per, gro...  21.9 us
    ppermute x9, starting transfers between devices, shift_t(): return lax.ppermute(x, 'tensor', [(t, (t + k) % nt) for t in range(nt)])  17.1 us
    ppermute x9, waiting for transfers between devices, shift_chip(): lax.ppermute(x, 'dp', [(c * CORES + o, (c + k) % chips * CORES + o) for c...  16.5 us
    pallas_call x1, Pallas kernels, teacher_maps(): pl.pallas_call(functools.partial(teacher_kernel, parts, count, tokens), i...  13.9 us
    ppermute x9, waiting for transfers between devices, shift_t(): return lax.ppermute(x, 'tensor', [(t, (t + k) % nt) for t in range(nt)])  13 us
    pallas_call x1, Pallas kernels, student_forward(): pl.pallas_call(forward_kernel, grid=(total // rows,), in_specs=[block(wid...  12.5 us
    ppermute x9, starting transfers between devices, shift_chip(): lax.ppermute(x, 'dp', [(c * CORES + o, (c + k) % chips * CORES + o) for c...  12 us
    pallas_call x1, Pallas kernels, context_grad(): pl.pallas_call(context_kernel, grid=(total // rows,), in_specs=[block, pl...  7.52 us
  transfers between devices with their start and end apart: 29, of which 18 were waited for; matrix products, arithmetic and copies ran while one was open for 6% of the time, Pallas kernels for 12%

commit v1 on v0

v1 whole, which is shorter than its diff:
```python
import functools
import math

import jax
import jax.numpy as jnp
from jax import lax
from jax.experimental import pallas as pl
from jax.experimental.pallas import tpu as pltpu
from jax.sharding import PartitionSpec as P

sharpness = 0.05
softcap = 10.0
epsilon = 1e-06
CORES = 2
VMEM_LIMIT = 56 * 1024 * 1024
SMALL_LIMIT = 14 * 1024 * 1024

F32 = jnp.float32
BF16 = jnp.bfloat16
VMEM = pl.BlockSpec(memory_space=pltpu.VMEM)
SMEM = pl.BlockSpec(memory_space=pltpu.SMEM)
ANY = pl.BlockSpec(memory_space=pl.ANY)
TOKEN = jax.ShapeDtypeStruct((8, 128), F32)


def up(n, m):
    return -(-n // m) * m


def dot(a, b, ca, cb):
    return lax.dot_general(a, b, (((ca,), (cb,)), ((), ())), preferred_element_type=F32)


def split_rows(rows, most):
    return max(n for n in range(16, most + 1, 16) if rows % n == 0)


def params(**kw):
    return pltpu.CompilerParams(vmem_limit_bytes=VMEM_LIMIT, **kw)


def cost(flops, nbytes):
    return pl.CostEstimate(flops=int(flops), bytes_accessed=int(nbytes), transcendentals=0)


def forward_kernel(x_ref, str_ref, wo_ref, gain_ref, bias_ref, wp_ref, normed_ref, emb_ref, inv_ref, prod_s, hid_s):
    rows, width = x_ref.shape
    sub = split_rows(rows, 256)
    gain, bias = gain_ref[...], bias_ref[...]
    for b in range(0, rows, sub):
        prod_s[b : b + sub] = dot(x_ref[b : b + sub], wo_ref[...], 1, 0)
        for c in range(b, b + sub, 16):
            summed = prod_s[c : c + 16] + str_ref[c : c + 16].astype(F32)
            centred = summed - jnp.mean(summed, axis=-1, keepdims=True)
            inverse = lax.rsqrt(jnp.mean(centred * centred, axis=-1, keepdims=True) + epsilon)
            normed = centred * inverse
            normed_ref[c : c + 16] = normed.astype(BF16)
            inv_ref[c : c + 16] = jnp.broadcast_to(inverse, (16, inv_ref.shape[1]))
            hid_s[c : c + 16] = (normed * gain + bias).astype(BF16)
        emb_ref[b : b + sub] = dot(hid_s[b : b + sub], wp_ref[...], 1, 0)


def student_forward(x, stream, out_weight, gain, bias, proj_weight):
    total, width = x.shape
    emb = proj_weight.shape[1]
    rows = split_rows(total, 720)
    block = lambda last: pl.BlockSpec((rows, last), lambda s: (s, 0))
    whole = lambda a: pl.BlockSpec(a.shape, lambda s: (0,) * a.ndim)
    return pl.pallas_call(
        forward_kernel,
        grid=(total // rows,),
        in_specs=[block(width), block(width)] + [whole(a) for a in (out_weight, gain, bias, proj_weight)],
        out_specs=[block(width), block(emb), block(128)],
        out_shape=[
            jax.ShapeDtypeStruct((total, width), BF16),
            jax.ShapeDtypeStruct((total, emb), F32),
            jax.ShapeDtypeStruct((total, 128), F32),
        ],
        scratch_shapes=[pltpu.VMEM((rows, width), F32), pltpu.VMEM((rows, width), BF16)],
        compiler_params=params(),
        cost_estimate=cost(2 * total * width * (width + emb), 8 * total * width),
        name="student_forward",
    )(x, stream, out_weight, gain, bias, proj_weight)


def teacher_kernel(parts, count, tokens, order_ref, rows_ref, states_ref, wq_ref, wk_ref, *rest):
    pieces, out_ref, token_ref = rest[:parts], rest[parts], rest[parts + 1]
    w_s, own_s, q_s, g_s, key_s, e_s, map_s, q_sem, key_sem, w_sem, own_sem = rest[parts + 2 :]
    depth = q_s.shape[1]
    slices = w_s.shape[1]
    part_rows = pieces[0].shape[2]
    total = key_s.shape[0]
    seq = total // count
    blocks = key_sem.shape[0]
    rows = total // blocks
    first = count * tokens
    own = [
        pltpu.make_async_copy(wq_ref, own_s.at[0], own_sem.at[0]),
        pltpu.make_async_copy(wk_ref, own_s.at[1], own_sem.at[1]),
    ]
    queries = pltpu.make_async_copy(states_ref.at[pl.ds(0, first)], q_s, q_sem)
    gathered = []
    chips = pieces[0].shape[0]
    for a in range(parts):
        for c in range(chips):
            start = pl.multiple_of(rows_ref[a // 2 * chips + c] * part_rows, part_rows)
            gathered.append(
                pltpu.make_async_copy(
                    pieces[a].at[c], w_s.at[a % 2, :, pl.ds(start, part_rows), :], w_sem.at[a * chips + c]
                )
            )
    keys = [
        pltpu.make_async_copy(
            states_ref.at[pl.ds(first + b * rows, rows)], key_s.at[pl.ds(b * rows, rows)], key_sem.at[b]
        )
        for b in range(blocks)
    ]
    queries.start()
    for copy in own + gathered + keys:
        copy.start()
    queries.wait()
    for copy in own:
        copy.wait()
    q = q_s[...]
    mixed = dot(dot(q, own_s[0], 1, 0).astype(BF16), own_s[1], 1, 1)
    for copy in gathered:
        copy.wait()
    for k in range(slices):
        mixed = mixed + dot(dot(q, w_s[0, k], 1, 0).astype(BF16), w_s[1, k], 1, 1)
    for v in range(depth // 128):
        g_s[v] = mixed[:, v * 128 : (v + 1) * 128]
        for p in range(count):
            q_s[p * tokens : (p + 1) * tokens, v * 128 : (v + 1) * 128] = g_s[
                v, pl.ds(p, tokens, stride=count), :
            ].astype(BF16)
    mixed = q_s[...]
    scale = 1.0 / (math.sqrt(depth) * softcap)
    side = 128 // tokens
    pair = lax.broadcasted_iota(jnp.int32, (rows, 128), 0) % count
    for b in range(blocks):
        keys[b].wait()
        raw = dot(key_s[b * rows : (b + 1) * rows], mixed, 1, 1)
        mine = raw[:, :128]
        for v in range(1, count // side):
            mine = jnp.where(pair >= v * side, raw[:, v * 128 : (v + 1) * 128], mine)
        e_s[b * rows : (b + 1) * rows] = jnp.exp(softcap * jnp.tanh(mine * scale))
    lane = lax.broadcasted_iota(jnp.int32, (seq, 128), 1) // tokens
    filler = jnp.zeros((up(seq, 128) - seq, 128), F32)
    for g in range(count // side):
        both = e_s[pl.ds(g * side, seq, stride=count), :]
        for v in range(1, side):
            both = jnp.where(lane == v, e_s[pl.ds(g * side + v, seq, stride=count), :], both)
        turned = jnp.concatenate([both, filler], axis=0).T
        for v in range(side):
            map_s[g * side + v] = turned[v * tokens : (v + 1) * tokens, :seq].astype(BF16)
    for n in range(count):
        out_ref[n] = map_s[order_ref[n]]
    token_ref[...] = jnp.zeros_like(token_ref)


def teacher_maps(order, rows, states, wq, wk, pieces, count, tokens):
    total, depth = states.shape
    keys = total - count * tokens
    heads = wq.shape[1]
    parts = len(pieces)
    chips, slices = pieces[0].shape[:2]
    blocks = keys // split_rows(keys, 720)
    return pl.pallas_call(
        functools.partial(teacher_kernel, parts, count, tokens),
        in_specs=[SMEM, SMEM] + [ANY] * (3 + parts),
        out_specs=[VMEM, VMEM],
        out_shape=[jax.ShapeDtypeStruct((count, tokens, keys // count), BF16), TOKEN],
        scratch_shapes=[
            pltpu.VMEM((2, slices, depth, heads), BF16),
            pltpu.VMEM((2, depth, heads), BF16),
            pltpu.VMEM((count * tokens, depth), BF16),
            pltpu.VMEM((depth // 128, count * tokens, 128), F32),
            pltpu.VMEM((keys, depth), BF16),
            pltpu.VMEM((keys, 128), F32),
            pltpu.VMEM((count, tokens, keys // count), BF16),
            pltpu.SemaphoreType.DMA,
            pltpu.SemaphoreType.DMA((blocks,)),
            pltpu.SemaphoreType.DMA((parts * chips,)),
            pltpu.SemaphoreType.DMA((2,)),
        ],
        compiler_params=params(),
        cost_estimate=cost(8 * count * tokens * depth * depth, 2 * states.size + 4 * depth * depth),
        name="teacher_maps",
    )(order, rows, states, wq, wk, *pieces)


def scores_kernel(tokens, count, group_queries, qidx_ref, len_ref, payload_ref, emb_ref, wp_ref, after_ref,
                  prob_ref, log_ref, units_ref, qunit_ref, qdir_ref, qlen_ref, qs_s, dir_s):
    total, emb = emb_ref.shape
    seq = total // count
    sub = split_rows(total, 128)
    each = group_queries * tokens
    for k in range(payload_ref.shape[0]):
        qs_s[k * each : (k + 1) * each] = payload_ref[k, :each]
    qe = dot(qs_s[...], wp_ref[...], 1, 0)
    length = jnp.sqrt(jnp.sum(qe * qe, axis=-1, keepdims=True) + epsilon)
    qdir = qe / length
    qdir_ref[...] = qdir
    qlen_ref[...] = jnp.broadcast_to(length, qlen_ref.shape)
    qunit_ref[...] = qdir.astype(BF16).reshape(qunit_ref.shape)
    for b in range(0, total, sub):
        e = emb_ref[b : b + sub]
        dir_s[b : b + sub] = e / jnp.sqrt(jnp.sum(e * e, axis=-1, keepdims=True) + epsilon)
    for r in range(count):
        units = dir_s[pl.ds(r, seq, stride=count), :].astype(BF16)
        units_ref[r] = units
        logits = dot(qunit_ref[qidx_ref[r]], units, 1, 1) / sharpness
        valid = lax.broadcasted_iota(jnp.int32, logits.shape, 1) < len_ref[r]
        student = jnp.where(valid, jnp.exp(logits), 0.0)
        student_total = jnp.sum(student, axis=-1, keepdims=True)
        prob_ref[r] = student / student_total
        log_ref[r] = logits - jnp.log(student_total)


def student_scores(qidx, lens, payload, embeds, wp, after, count, tokens, group_queries):
    total, emb = embeds.shape
    seq = total // count
    queries = payload.shape[0] * group_queries
    return pl.pallas_call(
        functools.partial(scores_kernel, tokens, count, group_queries),
        in_specs=[SMEM, SMEM, VMEM, VMEM, VMEM, ANY],
        out_specs=[VMEM] * 6,
        out_shape=[
            jax.ShapeDtypeStruct((count, tokens, seq), F32),
            jax.ShapeDtypeStruct((count, tokens, seq), F32),
            jax.ShapeDtypeStruct((count, seq, emb), BF16),
            jax.ShapeDtypeStruct((queries, tokens, emb), BF16),
            jax.ShapeDtypeStruct((queries * tokens, emb), F32),
            jax.ShapeDtypeStruct((queries * tokens, 128), F32),
        ],
        scratch_shapes=[pltpu.VMEM((queries * tokens, payload.shape[2]), BF16), pltpu.VMEM((total, emb), F32)],
        compiler_params=params(),
        cost_estimate=cost(1e9, 4 * total * emb),
        name="student_scores",
    )(qidx, lens, payload, embeds, wp, after)


def two_parts(a, b):
    high = a.astype(BF16)
    low = (a - high.astype(F32)).astype(BF16)
    return dot(high, b, 1, 0) + dot(low, b, 1, 0)


def backward_kernel(
    tokens, count, blocks, group_queries,
    qidx_ref, midx_ref, len_ref, core_ref,
    maps_in, prob_in, log_in, units_in, qunit_in, emb_in, x_in, normed_in, inv_in, payload_in,
    qdir_ref, qlen_ref, gain_ref, bias_ref, wp_ref, wpt_ref,
    sg_out, send_ref, keep_ref,
    maps_s, prob_s, log_s, units_s, qunit_s, emb_s, x_s, normed_s, inv_s, payload_s,
    up_s, eg_s, mean_s, along_s, un_s, qg_s, hg_s, sg_s, wo_s, nt_s, right_s,
    first_sem, block_sem, out_sem, last_sem,
):
    total, width = x_s.shape
    emb = emb_s.shape[1]
    seq = total // count
    rows = total // blocks
    sub = split_rows(rows, 256)
    thin = split_rows(total, 128)
    step = split_rows(sub, 48)
    first = [
        pltpu.make_async_copy(src, dst, first_sem.at[n])
        for n, (src, dst) in enumerate(
            (
                (qunit_in, qunit_s), (maps_in, maps_s), (prob_in, prob_s), (log_in, log_s), (units_in, units_s),
                (emb_in, emb_s), (inv_in, inv_s),
            )
        )
    ]
    loads = [
        [
            pltpu.make_async_copy(src.at[pl.ds(b * rows, rows)], dst.at[pl.ds(b * rows, rows)], block_sem.at[2 * b + n])
            for n, (src, dst) in enumerate(((normed_in, normed_s), (x_in, x_s)))
        ]
        for b in range(blocks)
    ]
    last = pltpu.make_async_copy(payload_in, payload_s, last_sem)
    for copy in first:
        copy.start()
    for pair in loads:
        for copy in pair:
            copy.start()
    last.start()
    gain, bias = gain_ref[...], bias_ref[...]
    gain_w = two_parts(gain, wp_ref[...])
    bias_w = two_parts(bias, wp_ref[...])
    qg_s[...] = jnp.zeros_like(qg_s)
    for copy in first:
        copy.wait()

    spread = jnp.zeros((tokens, 1), F32)
    for r in range(count):
        teacher = maps_s[midx_ref[r]].astype(F32)
        valid = lax.broadcasted_iota(jnp.int32, teacher.shape, 1) < len_ref[r]
        teacher_log = jnp.log(teacher)
        teacher = jnp.where(valid, teacher, 0.0)
        teacher_total = jnp.sum(teacher, axis=-1, keepdims=True)
        teacher_prob = teacher / teacher_total
        gap = (teacher_log - jnp.log(teacher_total)) - log_s[r]
        spread += jnp.sum(jnp.where(valid, teacher_prob * gap, 0.0), axis=-1, keepdims=True)
        slope = ((prob_s[r] - teacher_prob) / (tokens * sharpness)).astype(BF16)
        up_s[pl.ds(r, seq, stride=count), :] = dot(slope, qunit_s[qidx_ref[r]], 0, 0).astype(BF16).astype(F32)
        un_s[r] = dot(slope, units_s[r], 1, 0)
    for r in range(count):
        qg_s[qidx_ref[r]] += un_s[r]
    total_eg = jnp.zeros((1, emb), F32)
    for b in range(0, total, thin):
        e = emb_s[b : b + thin]
        upstream = up_s[b : b + thin]
        length = jnp.sqrt(jnp.sum(e * e, axis=-1, keepdims=True) + epsilon)
        direction = e / length
        eg = (upstream - direction * jnp.sum(direction * upstream, axis=-1, keepdims=True)) / length
        eg = eg.astype(BF16)
        eg_s[b : b + thin] = eg
        eg = eg.astype(F32)
        total_eg += jnp.sum(eg, axis=0, keepdims=True)
        inverse = inv_s[b : b + thin]
        mean_s[b : b + thin] = inverse * (jnp.sum(eg * gain_w, axis=-1, keepdims=True) / width)
        along_s[b : b + thin] = inverse * (jnp.sum(eg * (e - bias_w), axis=-1, keepdims=True) / width)

    def wide(b):
        hg_s[...] = dot(eg_s[b : b + sub], wp_ref[...], 1, 1)
        for c in range(b, b + sub, step):
            inverse, mean, along = inv_s[c : c + step], mean_s[c : c + step], along_s[c : c + step]
            for v in range(0, width, 128):
                scaled = hg_s[c - b : c - b + step, v : v + 128] * gain[:, v : v + 128]
                normed = normed_s[c : c + step, v : v + 128].astype(F32)
                sg_s[c : c + step, v : v + 128] = (inverse * scaled - mean - normed * along).astype(BF16)

    def products(b, part, parts):
        span = width // parts
        x = x_s[b * rows : (b + 1) * rows, part * span : (part + 1) * span]
        value = dot(x, sg_s[b * rows : (b + 1) * rows], 0, 0)
        if b == 0:
            wo_s[part * span : (part + 1) * span] = value
        else:
            wo_s[part * span : (part + 1) * span] += value

    parts = rows // sub if width % (rows // sub * 128) == 0 else 1
    stores = []
    for b in range(blocks):
        for copy in loads[b]:
            copy.wait()
        for n in range(rows // sub):
            wide(b * rows + n * sub)
            if b > 0 and n < parts:
                products(b - 1, n, parts)
        stores.append(
            pltpu.make_async_copy(
                sg_s.at[pl.ds(b * rows, rows)], sg_out.at[pl.ds(b * rows, rows)], out_sem.at[b]
            )
        )
        stores[-1].start()
        value = dot(eg_s[b * rows : (b + 1) * rows], normed_s[b * rows : (b + 1) * rows], 0, 0)
        if b == 0:
            nt_s[...] = value
        else:
            nt_s[...] += value
    for n in range(parts):
        products(blocks - 1, n, parts)

    last.wait()
    qg = qg_s[...].reshape(qdir_ref.shape)
    qdir = qdir_ref[...]
    qeg = (qg - qdir * jnp.sum(qdir * qg, axis=-1, keepdims=True)) / qlen_ref[:, :1]
    high = qeg.astype(BF16)
    low = (qeg - high.astype(F32)).astype(BF16)
    each = group_queries * tokens
    proj_query = jnp.zeros((emb, width), F32)
    for k in range(payload_s.shape[0]):
        qs = payload_s[k, :each]
        part = slice(k * each, (k + 1) * each)
        proj_query = proj_query + (dot(high[part], qs, 0, 0) + dot(low[part], qs, 0, 0))
    nt = nt_s[...]
    s = jnp.broadcast_to(total_eg, (emb, emb)).T[:, :1]
    wpt = wpt_ref[...].astype(F32)
    proj = nt * gain + s * bias + proj_query
    gain_row = jnp.sum(wpt * nt, axis=0, keepdims=True)
    bias_row = jnp.sum(wpt * s, axis=0, keepdims=True)
    index = lax.broadcasted_iota(jnp.int32, (tokens, width), 0)
    top = jnp.where(index == 0, gain_row, jnp.where(index == 1, bias_row, 0.0))
    rest_rows = jnp.zeros((128 - 2 * tokens, width), F32)
    right_s[...] = jnp.concatenate([proj, top, jnp.broadcast_to(spread, (tokens, width)), rest_rows], axis=0).T
    half = width // CORES
    chunk = send_ref.shape[1]
    for ref, which in ((send_ref, 1 - core_ref[0]), (keep_ref, core_ref[0])):
        start = pl.multiple_of(which * half, half)
        left = wo_s[pl.ds(start, half)].astype(BF16)
        right = right_s[pl.ds(start, half)].astype(BF16)
        for c in range(half // chunk):
            ref[c, :, :width] = left[c * chunk : (c + 1) * chunk]
            ref[c, :, width:] = right[c * chunk : (c + 1) * chunk]
    for copy in stores:
        copy.wait()


def student_backward(
    qidx, midx, lens, core, maps, scores, payload, embeds, x, normed, inverse, gain, bias, wp, wpt,
    count, tokens, group_queries, chunk,
):
    total, width = x.shape
    emb = wp.shape[1]
    blocks = total // split_rows(total, 720)
    sub = split_rows(total // blocks, 256)
    chunks = width // CORES // chunk
    prob, log, units, qunit, qdir, qlen = scores
    manual = [maps, prob, log, units, qunit, embeds, x, normed, inverse, payload]
    packed = jax.ShapeDtypeStruct((chunks, chunk, width + emb + 128), BF16)
    return pl.pallas_call(
        functools.partial(backward_kernel, tokens, count, blocks, group_queries),
        in_specs=[SMEM] * 4 + [ANY] * len(manual) + [VMEM] * 6,
        out_specs=[ANY, VMEM, VMEM],
        scratch_shapes=[pltpu.VMEM(a.shape, a.dtype) for a in manual]
        + [
            pltpu.VMEM((total, emb), F32),
            pltpu.VMEM((total, emb), BF16),
            pltpu.VMEM((total, 128), F32),
            pltpu.VMEM((total, 128), F32),
            pltpu.VMEM((count, tokens, emb), F32),
            pltpu.VMEM(qunit.shape, F32),
            pltpu.VMEM((sub, width), F32),
            pltpu.VMEM((total, width), BF16),
            pltpu.VMEM((width, width), F32),
            pltpu.VMEM((emb, width), F32),
            pltpu.VMEM((width, emb + 128), F32),
            pltpu.SemaphoreType.DMA((7,)),
            pltpu.SemaphoreType.DMA((2 * blocks,)),
            pltpu.SemaphoreType.DMA((blocks,)),
            pltpu.SemaphoreType.DMA,
        ],
        out_shape=[jax.ShapeDtypeStruct((total, width), BF16), packed, packed],
        compiler_params=params(),
        cost_estimate=cost(2 * total * width * (width + 2 * emb), 8 * total * width),
        name="student_backward",
    )(qidx, midx, lens, core, *manual, qdir, qlen, gain, bias, wp, wpt)


def context_kernel(sg_ref, wo_ref, after_ref, out_ref, token_ref):
    token_ref[...] = jnp.zeros_like(token_ref)
    out_ref[...] = dot(sg_ref[...], wo_ref[...], 1, 1).astype(BF16)


def context_grad(sg, out_weight, after):
    total, width = sg.shape
    rows = split_rows(total, 720)
    block = pl.BlockSpec((rows, width), lambda s: (s, 0))
    return pl.pallas_call(
        context_kernel,
        grid=(total // rows,),
        in_specs=[block, pl.BlockSpec(out_weight.shape, lambda s: (0, 0)), ANY],
        out_specs=[block, pl.BlockSpec(TOKEN.shape, lambda s: (0, 0))],
        out_shape=[jax.ShapeDtypeStruct(sg.shape, BF16), TOKEN],
        compiler_params=params(),
        cost_estimate=cost(2 * total * width * width, 4 * total * width),
        name="context_grad",
    )(sg, out_weight, after)


def sum_kernel(inputs, lead, *refs):
    total = None
    for ref in refs[:inputs]:
        for value in [ref[n] for n in range(ref.shape[0])] if lead else [ref[...]]:
            total = value.astype(F32) if total is None else total + value.astype(F32)
    total = total.astype(BF16)
    out = refs[-2]
    refs[-1][...] = jnp.zeros_like(refs[-1])
    if len(out.shape) > len(total.shape):
        for n in range(out.shape[0]):
            out[n] = total
    else:
        out[...] = total


def summed(arrays, name, lead=False, copies=0, after=()):
    shape = arrays[0].shape[1:] if lead else arrays[0].shape
    return pl.pallas_call(
        functools.partial(sum_kernel, len(arrays), lead),
        in_specs=[VMEM] * len(arrays) + [ANY] * len(after),
        out_specs=[VMEM, VMEM],
        out_shape=[jax.ShapeDtypeStruct(((copies,) if copies else ()) + shape, BF16), TOKEN],
        compiler_params=pltpu.CompilerParams(vmem_limit_bytes=SMALL_LIMIT),
        name=name,
    )(*arrays, *after)


def unpack_kernel(parts, width, emb, tokens, scale, index_ref, *rest):
    ins = rest[:parts]
    wo_ref, proj_ref, gain_ref, bias_ref, loss_ref, small_s = rest[parts:]
    per = ins[0].shape[0]
    for a in range(parts):
        for k in range(per):
            c = index_ref[a * per + k]
            value = ins[a][k].astype(F32)
            wo_ref[c] = value[:, :width]
            proj_ref[c] = value[:, width : width + emb]
            small_s[c] = value[:, width + emb :]
    turned = small_s[...].reshape(width, 128).T
    for v in range(width // 128):
        gain_ref[v : v + 1] = turned[0:1, v * 128 : (v + 1) * 128]
        bias_ref[v : v + 1] = turned[1:2, v * 128 : (v + 1) * 128]
    loss_ref[0] = jnp.sum(turned[tokens : 2 * tokens, 0:1]) * scale


def unpack(arrays, index, width, emb, tokens, scale):
    parts = len(arrays)
    per, chunk, _ = arrays[0].shape
    chunks = parts * per
    return pl.pallas_call(
        functools.partial(unpack_kernel, parts, width, emb, tokens, scale),
        in_specs=[SMEM] + [VMEM] * parts,
        out_specs=[VMEM] * 4 + [SMEM],
        out_shape=[jax.ShapeDtypeStruct((chunks, chunk, n), F32) for n in (width, emb)]
        + [jax.ShapeDtypeStruct((width // 128, 128), F32)] * 2
        + [jax.ShapeDtypeStruct((1,), F32)],
        scratch_shapes=[pltpu.VMEM((chunks, chunk, 128), F32)],
        compiler_params=pltpu.CompilerParams(vmem_limit_bytes=SMALL_LIMIT),
        name="unpack",
    )(index, *arrays)


def local(
    context,
    stream,
    out_weight,
    gain,
    bias,
    proj_weight,
    query_states,
    passage_len,
    passage_dest,
    teacher_states,
    teacher_query,
    teacher_key,
):
    dp = lax.axis_size("dp")
    nt = lax.axis_size("tensor")
    chips = dp // CORES
    me = lax.axis_index("dp")
    chip, core = me // CORES, me % CORES
    mt = lax.axis_index("tensor")
    count, seq, width = context.shape
    emb = proj_weight.shape[1]
    group_queries, tokens, _ = query_states.shape
    depth, heads = teacher_query.shape
    per = count // dp
    per_query = count * nt // group_queries

    def flat(a):
        return a.transpose(1, 0, 2).reshape(-1, a.shape[2])

    def shift_chip(x, k):
        return lax.ppermute(
            x, "dp", [(c * CORES + o, (c + k) % chips * CORES + o) for c in range(chips) for o in range(CORES)]
        )

    def swap_core(x):
        return lax.ppermute(x, "dp", [(d, d ^ 1) for d in range(dp)])

    def shift_t(x, k):
        return lax.ppermute(x, "tensor", [(t, (t + k) % nt) for t in range(nt)])

    chip_groups = [[c * CORES + o for c in range(chips)] for o in range(CORES)]

    def exchange_chips(x):
        return lax.all_to_all(x, "dp", split_axis=0, concat_axis=0, tiled=True, axis_index_groups=chip_groups)

    def exchange_t(x):
        return lax.all_to_all(x, "tensor", split_axis=0, concat_axis=0, tiled=True)

    part = depth // dp
    plane = []
    for w in (teacher_query, teacher_key):
        mine = lax.dynamic_slice_in_dim(w, me * part, part, 0)
        along = jnp.stack([shift_t(mine, k) for k in range(1, nt)])
        plane.append(exchange_chips(jnp.broadcast_to(along[None], (chips,) + along.shape)))
    shifts = jnp.arange(chips, dtype=jnp.int32)
    piece_rows = jnp.concatenate([shifts * CORES + core, shifts * CORES + 1 - core]).astype(jnp.int32)

    dest_group = passage_dest // (count * nt)
    rows = jnp.arange(count, dtype=jnp.int32)
    rank = jnp.sum(
        (dest_group[:, None] == dest_group[None, :]) & (rows[None, :] < rows[:, None]), axis=1, dtype=jnp.int32
    )
    place = dest_group * per + rank
    positions = jnp.sum(
        jnp.where(place[:, None] == rows[None, :], (passage_dest % count)[:, None], 0), axis=0
    )
    queries = query_states.reshape(group_queries * tokens, width)
    extra = jnp.pad(positions.astype(BF16)[None, :], ((0, 15), (0, width - count)))
    payload = jnp.concatenate([queries, extra], axis=0)
    payload = lax.all_to_all(
        jnp.broadcast_to(payload[None], (dp,) + payload.shape), "dp", split_axis=0, concat_axis=0, tiled=True
    )
    told = payload[:, group_queries * tokens, :count].astype(jnp.int32)
    order = lax.dynamic_slice_in_dim(told, me * per, per, 1).reshape(-1)
    midx = place.astype(jnp.int32)
    qidx = (passage_dest // per_query).astype(jnp.int32)

    gain2, bias2 = gain.reshape(1, width), bias.reshape(1, width)
    x = flat(context)
    normed, embeds, inverse = student_forward(x, flat(stream), out_weight, gain2, bias2, proj_weight)
    plane[0], plane[1], normed, embeds, inverse = lax.optimization_barrier(
        (plane[0], plane[1], normed, embeds, inverse)
    )
    pieces = plane + [swap_core(a) for a in plane]
    maps, token = teacher_maps(
        order, piece_rows, flat(teacher_states), teacher_query, teacher_key, pieces, count, tokens
    )
    maps = lax.all_to_all(maps, "dp", split_axis=0, concat_axis=0, tiled=True)
    scores = student_scores(qidx, passage_len, payload, embeds, proj_weight, token, count, tokens, group_queries)
    chunk = width // (CORES * chips * nt)
    sg, send, keep = student_backward(
        qidx, midx, passage_len, core.astype(jnp.int32).reshape(1), maps, scores, payload,
        embeds, x, normed, inverse, gain2, bias2, proj_weight, proj_weight.T,
        count, tokens, group_queries, chunk,
    )

    parts, token = summed([keep, swap_core(send)], "sum_cores")
    grad_context, token = context_grad(sg, out_weight, token)
    parts = exchange_chips(parts.reshape(chips, nt, chunk, -1))
    parts, _ = summed([parts], "sum_plane", lead=True, after=(token,))
    parts, _ = summed([exchange_t(parts)], "sum_tensor", lead=True, copies=nt)
    line = exchange_t(parts)
    plane = [line] + [shift_chip(line, k) for k in range(1, chips)]
    arrays = plane + [swap_core(a) for a in plane]
    behind = (chip - shifts) % chips
    base = jnp.concatenate([core * chips + behind, (1 - core) * chips + behind]) * nt
    index = (base[:, None] + jnp.arange(nt)[None, :]).reshape(-1).astype(jnp.int32)
    grad_out, grad_proj, grad_gain, grad_bias, loss = unpack(
        arrays, index, width, emb, tokens, 1.0 / (count * dp * nt * tokens)
    )
    return (
        loss.reshape(()),
        grad_out.reshape(width, width),
        grad_proj.reshape(width, emb),
        grad_gain.reshape(width),
        grad_bias.reshape(width),
        grad_context.reshape(seq, count, width).transpose(1, 0, 2),
    )


def solution(mesh):
    return jax.shard_map(
        local,
        mesh=mesh,
        in_specs=(
            P(("dp", "tensor"), None, None),
            P(("dp", "tensor"), None, None),
            P(),
            P(),
            P(),
            P(),
            P("dp", None, None),
            P(("dp", "tensor")),
            P(("dp", "tensor")),
            P(("dp", "tensor"), None, None),
            P(None, "tensor"),
            P(None, "tensor"),
        ),
        out_specs=(P(), P(), P(), P(), P(), P(("dp", "tensor"), None, None)),
        check_vma=False,
    )
```

time: 161 us -> 171 us (1.062)
  blocking collectives: 0 us -> 9.77 us
  other arithmetic: 7.18 us -> 1.82 us
  waiting for transfers between devices: 37.6 us -> 41.8 us
  Pallas kernels: 65.2 us -> 67.7 us
    all_to_all x0 -> x4, starting transfers between devices: none -> 14.1 us  [the longest x3 10.7 us: exchange_chips(): lax.all_to_all(x, 'dp', split_axis=0, concat_axis=0, tiled=True, axis_ind...]
    all_to_all x0 -> x4, waiting for transfers between devices: none -> 11.5 us  [the longest x1 6.18 us: exchange_t(): return lax.all_to_all(x, 'tensor', split_axis=0, concat_axis=0, tiled=True)]
    ppermute x9 -> x3, waiting for transfers between devices: 16.5 us -> 6.05 us  [shift_chip(): lax.ppermute(x, 'dp', [(c * CORES + o, (c + k) % chips * CORES + o) for c...]
    all_to_all x1, waiting for transfers between devices: 0.01 us -> 9.88 us  [local(): lax.all_to_all(jnp.broadcast_to(payload[None], (dp,) + payload.shape), 'd...]
    all_to_all x0 -> x1, blocking collectives: none -> 9.77 us  [exchange_t(): return lax.all_to_all(x, 'tensor', split_axis=0, concat_axis=0, tiled=True)]
    ppermute x9 -> x3, starting transfers between devices: 12 us -> 3.49 us  [shift_chip(): lax.ppermute(x, 'dp', [(c * CORES + o, (c + k) % chips * CORES + o) for c...]
    ppermute x9 -> x6, starting transfers between devices: 17.1 us -> 9.86 us  [shift_t(): return lax.ppermute(x, 'tensor', [(t, (t + k) % nt) for t in range(nt)])]
    all_to_all x1, waiting for transfers between devices: 6.08 us -> 1.56 us  [local(): maps = lax.all_to_all(maps, 'dp', split_axis=0, concat_axis=0, tiled=True)]
  transfers between devices with their start and end apart: 29 -> 22, of which waited for: 18 -> 13; matrix products, arithmetic and copies ran while one was open for 6% -> 4% of each run, Pallas kernels for 12% -> 14%
where the time goes in v1:
time: 171 us; the launch traced here: 170 us
  Pallas kernels  67.7 us (40%)
  waiting for transfers between devices  41.8 us (24%)
  starting transfers between devices  36.3 us (21%)
  local copies, waits for them, and re-layouts  11.3 us (7%)
  blocking collectives  9.77 us (6%)
  other arithmetic  1.82 us (1%)
    pallas_call x1, Pallas kernels, student_backward(): pl.pallas_call(functools.partial(backward_kernel, tokens, count, blocks,...  24.6 us
    pallas_call x1, Pallas kernels, teacher_maps(): pl.pallas_call(functools.partial(teacher_kernel, parts, count, tokens), i...  14.1 us
    pallas_call x1, Pallas kernels, student_forward(): pl.pallas_call(forward_kernel, grid=(total // rows,), in_specs=[block(wid...  12.5 us
    all_to_all x3, starting transfers between devices, exchange_chips(): lax.all_to_all(x, 'dp', split_axis=0, concat_axis=0, tiled=True, axis_ind...  10.7 us
    all_to_all x1, waiting for transfers between devices, local(): lax.all_to_all(jnp.broadcast_to(payload[None], (dp,) + payload.shape), 'd...  9.88 us
    ppermute x6, starting transfers between devices, shift_t(): return lax.ppermute(x, 'tensor', [(t, (t + k) % nt) for t in range(nt)])  9.86 us
    all_to_all x1, blocking collectives, exchange_t(): return lax.all_to_all(x, 'tensor', split_axis=0, concat_axis=0, tiled=True)  9.77 us
    ppermute x6, waiting for transfers between devices, shift_t(): return lax.ppermute(x, 'tensor', [(t, (t + k) % nt) for t in range(nt)])  9.32 us
  transfers between devices with their start and end apart: 22, of which 13 were waited for; matrix products, arithmetic and copies ran while one was open for 4% of the time, Pallas kernels for 14%

profile of v1, /device:TPU:0, one launch (start us, length us, event | category | flops | bytes accessed | tf_op | source)
XLA Modules:
  0.0 169.8 jit_solution(11227743758228528744)
XLA Ops:
  1.5 5.0 %collective-permute-start.2 = (bf16[128,256]{1,0:T(8,128)(2,1)S(1)}, bf16[128,256]{1,0:T(8,128)(2,1)S(1)}, u32[]{:S(2)}, u32[]{:S(2)}) collective-permute-start(bf16[128,256]{1,0:T(8,128)(2,1)S(1)} %constant_dynamic-slice_fusion.1), channel_id=1, source_target_pairs={{0,3},{1,0},{2,1},{3,2},{4,7},{5,4},{6,5},{7,6},{8,11},{9,8},{10,9... | collective-permute-start | bytes 196616 | tf_op jit(solution)/shard_map/ppermute | solution.py:565
  9.1 4.0 %collective-permute-done.1 = bf16[128,256]{1,0:T(8,128)(2,1)S(1)} collective-permute-done((bf16[128,256]{1,0:T(8,128)(2,1)S(1)}, bf16[128,256]{1,0:T(8,128)(2,1)S(1)}, u32[]{:S(2)}, u32[]{:S(2)}) %collective-permute-start.1) | collective-permute-done | bytes 65568 | tf_op jit(solution)/shard_map/ppermute | solution.py:565
  14.0 3.7 %all-to-all-start.1 = ((bf16[4,3,128,256]{3,2,1,0:T(8,128)(2,1)}), bf16[4,3,128,256]{3,2,1,0:T(8,128)(2,1)S(1)}, u32[]{:S(2)}, u32[]{:S(2)}) async-start(bf16[4,3,128,256]{3,2,1,0:T(8,128)(2,1)} %broadcast_in_dim.17), calls=%async_computation.1 | async-start | bytes 1572864 | tf_op jit(solution)/shard_map/all_to_all | solution.py:570
  18.6 1.9 %collective-permute-start.5 = (bf16[128,256]{1,0:T(8,128)(2,1)S(1)}, bf16[128,256]{1,0:T(8,128)(2,1)S(1)}, u32[]{:S(2)}, u32[]{:S(2)}) collective-permute-start(bf16[128,256]{1,0:T(8,128)(2,1)S(1)} %constant_dynamic-slice_fusion), channel_id=1, source_target_pairs={{0,3},{1,0},{2,1},{3,2},{4,7},{5,4},{6,5},{7,6},{8,11},{9,8},{10,9... | collective-permute-start | bytes 196616 | tf_op jit(solution)/shard_map/ppermute | solution.py:565
  20.5 1.9 %collective-permute-start.3 = (bf16[128,256]{1,0:T(8,128)(2,1)S(1)}, bf16[128,256]{1,0:T(8,128)(2,1)S(1)}, u32[]{:S(2)}, u32[]{:S(2)}) collective-permute-start(bf16[128,256]{1,0:T(8,128)(2,1)S(1)} %constant_dynamic-slice_fusion), channel_id=1, source_target_pairs={{0,1},{1,2},{2,3},{3,0},{4,5},{5,6},{6,7},{7,4},{8,9},{9,10},{10,1... | collective-permute-start | bytes 196616 | tf_op jit(solution)/shard_map/ppermute | solution.py:565
  23.2 3.9 %collective-permute-done.4 = bf16[128,256]{1,0:T(8,128)(2,1)S(1)} collective-permute-done((bf16[128,256]{1,0:T(8,128)(2,1)S(1)}, bf16[128,256]{1,0:T(8,128)(2,1)S(1)}, u32[]{:S(2)}, u32[]{:S(2)}) %collective-permute-start.4) | collective-permute-done | bytes 65568 | tf_op jit(solution)/shard_map/ppermute | solution.py:565
  29.6 3.5 %all-to-all-start.2 = ((bf16[4,3,128,256]{3,2,1,0:T(8,128)(2,1)}), bf16[4,3,128,256]{3,2,1,0:T(8,128)(2,1)S(1)}, u32[]{:S(2)}, u32[]{:S(2)}) async-start(bf16[4,3,128,256]{3,2,1,0:T(8,128)(2,1)} %broadcast_in_dim.18), calls=%async_computation.2 | async-start | bytes 1572864 | tf_op jit(solution)/shard_map/all_to_all | solution.py:570
  34.4 12.5 %student_forward.1 = (bf16[2880,768]{1,0:T(8,128)(2,1)}, f32[2880,128]{1,0:T(8,128)}, f32[2880,128]{1,0:T(8,128)}) custom-call(bf16[2880,768]{1,0:T(8,128)(2,1)} %bitcast.39, bf16[2880,768]{1,0:T(8,128)(2,1)} %bitcast.38, bf16[768,768]{1,0:T(8,128)(2,1)} %wo_ref.3, f32[1,768]{1,0:T(1,128)} %reshape.98.gain_ref, f32[1,768]{1,0:T(1,128)} %reshape.99.bias_ref, ...), custom_call_target="tpu_custom_call" | custom-call | flops 3963617280 | bytes 17694720 | tf_op jit(solution)/shard_map/student_forward/pallas_call | solution.py:69
  48.4 4.1 %all-to-all-start = ((bf16[8,48,768]{2,1,0:T(8,128)(2,1)}), bf16[8,48,768]{2,1,0:T(8,128)(2,1)S(1)}, u32[]{:S(2)}, u32[]{:S(2)}) async-start(bf16[8,48,768]{2,1,0:T(8,128)(2,1)} %broadcast_in_dim.16), calls=%async_computation | async-start | bytes 1179648 | tf_op jit(solution)/shard_map/all_to_all | solution.py:596
  53.1 9.9 %all-to-all-done.payload_ref.payload_in = bf16[8,48,768]{2,1,0:T(8,128)(2,1)S(1)} async-done(((bf16[8,48,768]{2,1,0:T(8,128)(2,1)}), bf16[8,48,768]{2,1,0:T(8,128)(2,1)S(1)}, u32[]{:S(2)}, u32[]{:S(2)}) %all-to-all-start) | async-done | bytes 589856 | tf_op jit(solution)/shard_map/all_to_all | solution.py:596
  64.7 14.1 %teacher_maps.1 = (bf16[16,32,180]{2,1,0:T(8,128)(2,1)}, f32[8,128]{1,0:T(8,128)}) custom-call(s32[16]{0:T(128)} %reshape.94.order_ref, s32[8]{0:T(128)} %pad_add_fusion.rows_ref, bf16[3392,1024]{1,0:T(8,128)(2,1)} %bitcast.37, bf16[1024,256]{1,0:T(8,128)(2,1)} %wq_ref.1, bf16[1024,256]{1,0:T(8,128)(2,1)} %wk_ref.1, bf16[4,3,128,256]{3,2,1,0:T(8,128)(2,1)} %copy-done.3, ...), custom_call_target="tpu_custom_call" | custom-call | flops 4294967296 | bytes 11141120 | tf_op jit(solution)/shard_map/teacher_maps/pallas_call | solution.py:168
  78.8 3.6 %all-to-all-start.3 = ((bf16[16,32,180]{2,1,0:T(8,128)(2,1)}), bf16[16,32,180]{2,1,0:T(8,128)(2,1)S(1)}, u32[]{:S(2)}, u32[]{:S(2)}) async-start(bf16[16,32,180]{2,1,0:T(8,128)(2,1)} %get-tuple-element.41), calls=%async_computation.3 | async-start | bytes 524288 | tf_op jit(solution)/shard_map/all_to_all | solution.py:614
  83.2 4.3 %student_scores.1 = (f32[16,32,180]{2,1,0:T(8,128)}, f32[16,32,180]{2,1,0:T(8,128)}, bf16[16,180,128]{2,1,0:T(8,128)(2,1)}, bf16[8,32,128]{2,1,0:T(8,128)(2,1)}, f32[256,128]{1,0:T(8,128)}, /*index=5*/f32[256,128]{1,0:T(8,128)}) custom-call(s32[16]{0:T(128)} %copy-done.12, s32[16]{0:T(128)} %len_ref.3, bf16[8,48,768]{2,1,0:T(8,128)(2,1)} %copy-done.5, ...), custom_call_target="tpu_custom_call" | custom-call | flops 1000000000 | bytes 1474560 | tf_op jit(solution)/shard_map/student_scores/pallas_call | solution.py:224
  89.8 24.6 %student_backward.1 = (bf16[2880,768]{1,0:T(8,128)(2,1)}, bf16[16,24,1024]{2,1,0:T(8,128)(2,1)}, bf16[16,24,1024]{2,1,0:T(8,128)(2,1)}) custom-call(s32[16]{0:T(128)} %copy-done.12, s32[16]{0:T(128)} %copy-done.13, s32[16]{0:T(128)} %len_ref.3, s32[1]{0:T(128)} %bitcast.core_ref, bf16[16,32,180]{2,1,0:T(8,128)(2,1)} %copy-done.6, ...), custom_call_target="tpu_custom_call" | custom-call | flops 4529848320 | bytes 17694720 | tf_op jit(solution)/shard_map/student_backward/pallas_call | solution.py:414
  114.4 2.5 %collective-permute-done.8.refs_1_ = bf16[16,24,1024]{2,1,0:T(8,128)(2,1)S(1)} collective-permute-done((bf16[16,24,1024]{2,1,0:T(8,128)(2,1)}, bf16[16,24,1024]{2,1,0:T(8,128)(2,1)S(1)}, u32[]{:S(2)}, u32[]{:S(2)}) %collective-permute-start.8) | collective-permute-done | bytes 786464 | tf_op jit(solution)/shard_map/ppermute | solution.py:562
  119.7 3.5 %all-to-all-start.4 = ((bf16[4,4,24,1024]{3,2,1,0:T(8,128)(2,1)}), bf16[4,4,24,1024]{3,2,1,0:T(8,128)(2,1)S(1)}, u32[]{:S(2)}, u32[]{:S(2)}) async-start(bf16[4,4,24,1024]{3,2,1,0:T(8,128)(2,1)} %bitcast.16), calls=%async_computation.4 | async-start | bytes 1572864 | tf_op jit(solution)/shard_map/all_to_all | solution.py:570
  123.2 7.5 %context_grad.1 = (bf16[2880,768]{1,0:T(8,128)(2,1)}, f32[8,128]{1,0:T(8,128)}) custom-call(bf16[2880,768]{1,0:T(8,128)(2,1)} %get-tuple-element.55.sg_ref, bf16[768,768]{1,0:T(8,128)(2,1)} %wo_ref.3, f32[8,128]{1,0:T(8,128)} %copy-done.2), custom_call_target="tpu_custom_call" | custom-call | flops 3397386240 | bytes 8847360 | tf_op jit(solution)/shard_map/context_grad/pallas_call | solution.py:452
  130.7 3.8 %all-to-all-done.4.refs_0_ = bf16[4,4,24,1024]{3,2,1,0:T(8,128)(2,1)S(1)} async-done(((bf16[4,4,24,1024]{3,2,1,0:T(8,128)(2,1)}), bf16[4,4,24,1024]{3,2,1,0:T(8,128)(2,1)S(1)}, u32[]{:S(2)}, u32[]{:S(2)}) %all-to-all-start.4) | async-done | bytes 786464 | tf_op jit(solution)/shard_map/all_to_all | solution.py:570
  135.9 9.8 %all_to_all.35.refs_0_ = bf16[4,24,1024]{2,1,0:T(8,128)(2,1)S(1)} all-to-all(bf16[4,24,1024]{2,1,0:T(8,128)(2,1)S(1)} %get-tuple-element.58), channel_id=1, replica_groups=mesh['dp'=8,'tensor'=4] {'tensor'}, dimensions={0} | all-to-all | bytes 393216 | tf_op jit(solution)/shard_map/all_to_all | solution.py:573
  146.4 3.4 %all-to-all-start.6 = ((bf16[4,24,1024]{2,1,0:T(8,128)(2,1)}), bf16[4,24,1024]{2,1,0:T(8,128)(2,1)S(1)}, u32[]{:S(2)}, u32[]{:S(2)}) async-start(bf16[4,24,1024]{2,1,0:T(8,128)(2,1)} %get-tuple-element.59), calls=%async_computation.6 | async-start | bytes 393216 | tf_op jit(solution)/shard_map/all_to_all | solution.py:573
  149.8 6.2 %all-to-all-done.6.rest_0_ = bf16[4,24,1024]{2,1,0:T(8,128)(2,1)S(1)} async-done(((bf16[4,24,1024]{2,1,0:T(8,128)(2,1)}), bf16[4,24,1024]{2,1,0:T(8,128)(2,1)S(1)}, u32[]{:S(2)}, u32[]{:S(2)}) %all-to-all-start.6) | async-done | bytes 196640 | tf_op jit(solution)/shard_map/all_to_all | solution.py:573
  159.6 2.9 %collective-permute-done.11.rest_3_ = bf16[4,24,1024]{2,1,0:T(8,128)(2,1)S(1)} collective-permute-done((bf16[4,24,1024]{2,1,0:T(8,128)(2,1)S(1)}, bf16[4,24,1024]{2,1,0:T(8,128)(2,1)S(1)}, u32[]{:S(2)}, u32[]{:S(2)}) %collective-permute-start.11) | collective-permute-done | bytes 196640 | tf_op jit(solution)/shard_map/ppermute | solution.py:557
  162.4 3.2 %collective-permute-done.10.rest_2_ = bf16[4,24,1024]{2,1,0:T(8,128)(2,1)S(1)} collective-permute-done((bf16[4,24,1024]{2,1,0:T(8,128)(2,1)S(1)}, bf16[4,24,1024]{2,1,0:T(8,128)(2,1)S(1)}, u32[]{:S(2)}, u32[]{:S(2)}) %collective-permute-start.10) | collective-permute-done | bytes 196640 | tf_op jit(solution)/shard_map/ppermute | solution.py:557
  167.3 2.3 %unpack.1 = (f32[32,24,768]{2,1,0:T(8,128)}, f32[32,24,128]{2,1,0:T(8,128)}, f32[6,128]{1,0:T(8,128)}, f32[6,128]{1,0:T(8,128)}, f32[1]{0:T(128)}) custom-call(s32[32]{0:T(128)S(1)} %add.85.index_ref, bf16[4,24,1024]{2,1,0:T(8,128)(2,1)S(1)} %all-to-all-done.6.rest_0_, bf16[4,24,1024]{2,1,0:T(8,128)(2,1)S(1)} %collective-permute-done.9.rest_1_, ...), custom_call_target="tpu_custom_call" | custom-call | tf_op jit(solution)/shard_map/unpack/pallas_call | solution.py:513
  (84 shorter events, 26.8 us)
Async XLA Ops:
  0.6 32.5 %copy-start.9 = (f32[768]{0:T(1024)S(1)}, f32[768]{0:T(1024)}, u32[]{:S(2)}) copy-start(f32[768]{0:T(1024)} %param.15) | copy-start | bytes 9220
  0.6 33.1 %copy-start.10 = (f32[768]{0:T(1024)S(1)}, f32[768]{0:T(1024)}, u32[]{:S(2)}) copy-start(f32[768]{0:T(1024)} %param.16) | copy-start | bytes 9220
  1.5 7.5 %collective-permute-start.2 = (bf16[128,256]{1,0:T(8,128)(2,1)S(1)}, bf16[128,256]{1,0:T(8,128)(2,1)S(1)}, u32[]{:S(2)}, u32[]{:S(2)}) collective-permute-start(bf16[128,256]{1,0:T(8,128)(2,1)S(1)} %constant_dynamic-slice_fusion.1), channel_id=1, source_target_pairs={{0,3},{1,0},{2,1},{3,2},{4,7},{5,4},{6,5},{7,6},{8,11},{9,8},{10,9... | collective-permute-start | bytes 196616 | tf_op jit(solution)/shard_map/ppermute | solution.py:565
  6.6 6.5 %collective-permute-start.1 = (bf16[128,256]{1,0:T(8,128)(2,1)S(1)}, bf16[128,256]{1,0:T(8,128)(2,1)S(1)}, u32[]{:S(2)}, u32[]{:S(2)}) collective-permute-start(bf16[128,256]{1,0:T(8,128)(2,1)S(1)} %constant_dynamic-slice_fusion.1), channel_id=1, source_target_pairs={{0,2},{1,3},{2,0},{3,1},{4,6},{5,7},{6,4},{7,5},{8,10},{9,11},{10,... | collective-permute-start | bytes 196616 | tf_op jit(solution)/shard_map/ppermute | solution.py:565
  6.6 6.5 %collective-permute-start = (bf16[128,256]{1,0:T(8,128)(2,1)S(1)}, bf16[128,256]{1,0:T(8,128)(2,1)S(1)}, u32[]{:S(2)}, u32[]{:S(2)}) collective-permute-start(bf16[128,256]{1,0:T(8,128)(2,1)S(1)} %constant_dynamic-slice_fusion.1), channel_id=1, source_target_pairs={{0,1},{1,2},{2,3},{3,0},{4,5},{5,6},{6,7},{7,4},{8,9},{9,10},{10,1... | collective-permute-start | bytes 196616 | tf_op jit(solution)/shard_map/ppermute | solution.py:565
  14.0 14.6 %all-to-all-start.1 = ((bf16[4,3,128,256]{3,2,1,0:T(8,128)(2,1)}), bf16[4,3,128,256]{3,2,1,0:T(8,128)(2,1)S(1)}, u32[]{:S(2)}, u32[]{:S(2)}) async-start(bf16[4,3,128,256]{3,2,1,0:T(8,128)(2,1)} %broadcast_in_dim.17), calls=%async_computation.1 | async-start | bytes 1572864 | tf_op jit(solution)/shard_map/all_to_all | solution.py:570
  18.6 4.6 %collective-permute-start.5 = (bf16[128,256]{1,0:T(8,128)(2,1)S(1)}, bf16[128,256]{1,0:T(8,128)(2,1)S(1)}, u32[]{:S(2)}, u32[]{:S(2)}) collective-permute-start(bf16[128,256]{1,0:T(8,128)(2,1)S(1)} %constant_dynamic-slice_fusion), channel_id=1, source_target_pairs={{0,3},{1,0},{2,1},{3,2},{4,7},{5,4},{6,5},{7,6},{8,11},{9,8},{10,9... | collective-permute-start | bytes 196616 | tf_op jit(solution)/shard_map/ppermute | solution.py:565
  20.5 6.6 %collective-permute-start.4 = (bf16[128,256]{1,0:T(8,128)(2,1)S(1)}, bf16[128,256]{1,0:T(8,128)(2,1)S(1)}, u32[]{:S(2)}, u32[]{:S(2)}) collective-permute-start(bf16[128,256]{1,0:T(8,128)(2,1)S(1)} %constant_dynamic-slice_fusion), channel_id=1, source_target_pairs={{0,2},{1,3},{2,0},{3,1},{4,6},{5,7},{6,4},{7,5},{8,10},{9,11},{10,... | collective-permute-start | bytes 196616 | tf_op jit(solution)/shard_map/ppermute | solution.py:565
  20.5 6.6 %collective-permute-start.3 = (bf16[128,256]{1,0:T(8,128)(2,1)S(1)}, bf16[128,256]{1,0:T(8,128)(2,1)S(1)}, u32[]{:S(2)}, u32[]{:S(2)}) collective-permute-start(bf16[128,256]{1,0:T(8,128)(2,1)S(1)} %constant_dynamic-slice_fusion), channel_id=1, source_target_pairs={{0,1},{1,2},{2,3},{3,0},{4,5},{5,6},{6,7},{7,4},{8,9},{9,10},{10,1... | collective-permute-start | bytes 196616 | tf_op jit(solution)/shard_map/ppermute | solution.py:565
  29.6 17.3 %all-to-all-start.2 = ((bf16[4,3,128,256]{3,2,1,0:T(8,128)(2,1)}), bf16[4,3,128,256]{3,2,1,0:T(8,128)(2,1)S(1)}, u32[]{:S(2)}, u32[]{:S(2)}) async-start(bf16[4,3,128,256]{3,2,1,0:T(8,128)(2,1)} %broadcast_in_dim.18), calls=%async_computation.2 | async-start | bytes 1572864 | tf_op jit(solution)/shard_map/all_to_all | solution.py:570
  46.9 16.8 %collective-permute-start.6 = (bf16[4,3,128,256]{3,2,1,0:T(8,128)(2,1)S(1)}, bf16[4,3,128,256]{3,2,1,0:T(8,128)(2,1)S(1)}, u32[]{:S(2)}, u32[]{:S(2)}) collective-permute-start(bf16[4,3,128,256]{3,2,1,0:T(8,128)(2,1)S(1)} %all-to-all-done.1.rest_0_), channel_id=1, source_target_pairs={{0,4},{4,0},{8,12},{12,8},{16,20},{20,16},{24,28},{28,24},{1,5},{5... | collective-permute-start | bytes 2359304 | tf_op jit(solution)/shard_map/ppermute | solution.py:562
  47.0 16.8 %collective-permute-start.7 = (bf16[4,3,128,256]{3,2,1,0:T(8,128)(2,1)S(1)}, bf16[4,3,128,256]{3,2,1,0:T(8,128)(2,1)}, u32[]{:S(2)}, u32[]{:S(2)}) collective-permute-start(bf16[4,3,128,256]{3,2,1,0:T(8,128)(2,1)S(1)} %all-to-all-done.2.rest_1_), channel_id=1, source_target_pairs={{0,4},{4,0},{8,12},{12,8},{16,20},{20,16},{24,28},{28,24},{1,5},{5... | collective-permute-start | bytes 2359304 | tf_op jit(solution)/shard_map/ppermute | solution.py:562
  48.4 14.6 %all-to-all-start = ((bf16[8,48,768]{2,1,0:T(8,128)(2,1)}), bf16[8,48,768]{2,1,0:T(8,128)(2,1)S(1)}, u32[]{:S(2)}, u32[]{:S(2)}) async-start(bf16[8,48,768]{2,1,0:T(8,128)(2,1)} %broadcast_in_dim.16), calls=%async_computation | async-start | bytes 1179648 | tf_op jit(solution)/shard_map/all_to_all | solution.py:596
  78.8 10.3 %all-to-all-start.3 = ((bf16[16,32,180]{2,1,0:T(8,128)(2,1)}), bf16[16,32,180]{2,1,0:T(8,128)(2,1)S(1)}, u32[]{:S(2)}, u32[]{:S(2)}) async-start(bf16[16,32,180]{2,1,0:T(8,128)(2,1)} %get-tuple-element.41), calls=%async_computation.3 | async-start | bytes 524288 | tf_op jit(solution)/shard_map/all_to_all | solution.py:614
  114.3 2.6 %collective-permute-start.8 = (bf16[16,24,1024]{2,1,0:T(8,128)(2,1)}, bf16[16,24,1024]{2,1,0:T(8,128)(2,1)S(1)}, u32[]{:S(2)}, u32[]{:S(2)}) collective-permute-start(bf16[16,24,1024]{2,1,0:T(8,128)(2,1)} %get-tuple-element.53), channel_id=1, source_target_pairs={{0,4},{4,0},{8,12},{12,8},{16,20},{20,16},{24,28},{28,24},{1,5},{5... | collective-permute-start | bytes 2359304 | tf_op jit(solution)/shard_map/ppermute | solution.py:562
  119.7 14.9 %all-to-all-start.4 = ((bf16[4,4,24,1024]{3,2,1,0:T(8,128)(2,1)}), bf16[4,4,24,1024]{3,2,1,0:T(8,128)(2,1)S(1)}, u32[]{:S(2)}, u32[]{:S(2)}) async-start(bf16[4,4,24,1024]{3,2,1,0:T(8,128)(2,1)} %bitcast.16), calls=%async_computation.4 | async-start | bytes 1572864 | tf_op jit(solution)/shard_map/all_to_all | solution.py:570
  146.4 9.6 %all-to-all-start.6 = ((bf16[4,24,1024]{2,1,0:T(8,128)(2,1)}), bf16[4,24,1024]{2,1,0:T(8,128)(2,1)S(1)}, u32[]{:S(2)}, u32[]{:S(2)}) async-start(bf16[4,24,1024]{2,1,0:T(8,128)(2,1)} %get-tuple-element.59), calls=%async_computation.6 | async-start | bytes 393216 | tf_op jit(solution)/shard_map/all_to_all | solution.py:573
  156.0 6.5 %collective-permute-start.11 = (bf16[4,24,1024]{2,1,0:T(8,128)(2,1)S(1)}, bf16[4,24,1024]{2,1,0:T(8,128)(2,1)S(1)}, u32[]{:S(2)}, u32[]{:S(2)}) collective-permute-start(bf16[4,24,1024]{2,1,0:T(8,128)(2,1)S(1)} %all-to-all-done.6.rest_0_), channel_id=1, source_target_pairs={{0,24},{4,28},{8,0},{12,4},{16,8},{20,12},{24,16},{28,20},{1,25},{... | collective-permute-start | bytes 589832 | tf_op jit(solution)/shard_map/ppermute | solution.py:557
  157.5 8.1 %collective-permute-start.10 = (bf16[4,24,1024]{2,1,0:T(8,128)(2,1)S(1)}, bf16[4,24,1024]{2,1,0:T(8,128)(2,1)S(1)}, u32[]{:S(2)}, u32[]{:S(2)}) collective-permute-start(bf16[4,24,1024]{2,1,0:T(8,128)(2,1)S(1)} %all-to-all-done.6.rest_0_), channel_id=1, source_target_pairs={{0,16},{4,20},{8,24},{12,28},{16,0},{20,4},{24,8},{28,12},{1,17},{... | collective-permute-start | bytes 589832 | tf_op jit(solution)/shard_map/ppermute | solution.py:557
  158.8 6.8 %collective-permute-start.9 = (bf16[4,24,1024]{2,1,0:T(8,128)(2,1)S(1)}, bf16[4,24,1024]{2,1,0:T(8,128)(2,1)S(1)}, u32[]{:S(2)}, u32[]{:S(2)}) collective-permute-start(bf16[4,24,1024]{2,1,0:T(8,128)(2,1)S(1)} %all-to-all-done.6.rest_0_), channel_id=1, source_target_pairs={{0,8},{4,12},{8,16},{12,20},{16,24},{20,28},{24,0},{28,4},{1,9},{5... | collective-permute-start | bytes 589832 | tf_op jit(solution)/shard_map/ppermute | solution.py:557
  159.5 6.7 %collective-permute-start.12 = (bf16[4,24,1024]{2,1,0:T(8,128)(2,1)S(1)}, bf16[4,24,1024]{2,1,0:T(8,128)(2,1)S(1)}, u32[]{:S(2)}, u32[]{:S(2)}) collective-permute-start(bf16[4,24,1024]{2,1,0:T(8,128)(2,1)S(1)} %all-to-all-done.6.rest_0_), channel_id=1, source_target_pairs={{0,4},{4,0},{8,12},{12,8},{16,20},{20,16},{24,28},{28,24},{1,5},{5... | collective-permute-start | bytes 589832 | tf_op jit(solution)/shard_map/ppermute | solution.py:562
  162.4 3.9 %collective-permute-start.15 = (bf16[4,24,1024]{2,1,0:T(8,128)(2,1)S(1)}, bf16[4,24,1024]{2,1,0:T(8,128)(2,1)S(1)}, u32[]{:S(2)}, u32[]{:S(2)}) collective-permute-start(bf16[4,24,1024]{2,1,0:T(8,128)(2,1)S(1)} %collective-permute-done.11.rest_3_), channel_id=1, source_target_pairs={{0,4},{4,0},{8,12},{12,8},{16,20},{20,16},{24,28},{28,24},{1,5},{5... | collective-permute-start | bytes 589832 | tf_op jit(solution)/shard_map/ppermute | solution.py:562
  165.6 1.4 collective-permute-start.14
  165.6 1.7 %collective-permute-start.13 = (bf16[4,24,1024]{2,1,0:T(8,128)(2,1)S(1)}, bf16[4,24,1024]{2,1,0:T(8,128)(2,1)S(1)}, u32[]{:S(2)}, u32[]{:S(2)}) collective-permute-start(bf16[4,24,1024]{2,1,0:T(8,128)(2,1)S(1)} %collective-permute-done.9.rest_1_), channel_id=1, source_target_pairs={{0,4},{4,0},{8,12},{12,8},{16,20},{20,16},{24,28},{28,24},{1,5},{5... | collective-permute-start | bytes 589832 | tf_op jit(solution)/shard_map/ppermute | solution.py:562
  (12 other events, 123.5 us)

commit v2 on v1

--- a/solution.py
+++ b/solution.py
@@ -43,7 +43,7 @@
     return pl.CostEstimate(flops=int(flops), bytes_accessed=int(nbytes), transcendentals=0)
 
 
-def forward_kernel(x_ref, str_ref, wo_ref, gain_ref, bias_ref, wp_ref, normed_ref, emb_ref, inv_ref, prod_s, hid_s):
+def forward_kernel(x_ref, str_ref, wo_ref, gain_ref, bias_ref, wp_ref, normed_ref, emb_ref, inv_ref, turned_ref, prod_s, hid_s):
     rows, width = x_ref.shape
     sub = split_rows(rows, 256)
     gain, bias = gain_ref[...], bias_ref[...]
@@ -58,6 +58,7 @@
             inv_ref[c : c + 16] = jnp.broadcast_to(inverse, (16, inv_ref.shape[1]))
             hid_s[c : c + 16] = (normed * gain + bias).astype(BF16)
         emb_ref[b : b + sub] = dot(hid_s[b : b + sub], wp_ref[...], 1, 0)
+    turned_ref[0] = x_ref[...].T
 
 
 def student_forward(x, stream, out_weight, gain, bias, proj_weight):
@@ -70,11 +71,12 @@
         forward_kernel,
         grid=(total // rows,),
         in_specs=[block(width), block(width)] + [whole(a) for a in (out_weight, gain, bias, proj_weight)],
-        out_specs=[block(width), block(emb), block(128)],
+        out_specs=[block(width), block(emb), block(128), pl.BlockSpec((1, width, rows), lambda s: (s, 0, 0))],
         out_shape=[
             jax.ShapeDtypeStruct((total, width), BF16),
             jax.ShapeDtypeStruct((total, emb), F32),
             jax.ShapeDtypeStruct((total, 128), F32),
+            jax.ShapeDtypeStruct((total // rows, width, rows), BF16),
         ],
         scratch_shapes=[pltpu.VMEM((rows, width), F32), pltpu.VMEM((rows, width), BF16)],
         compiler_params=params(),
@@ -87,8 +89,8 @@
     pieces, out_ref, token_ref = rest[:parts], rest[parts], rest[parts + 1]
     w_s, own_s, q_s, g_s, key_s, e_s, map_s, q_sem, key_sem, w_sem, own_sem = rest[parts + 2 :]
     depth = q_s.shape[1]
-    slices = w_s.shape[1]
-    part_rows = pieces[0].shape[2]
+    slices = w_s.shape[0] // 2
+    part_rows = pieces[0].shape[1]
     total = key_s.shape[0]
     seq = total // count
     blocks = key_sem.shape[0]
@@ -99,16 +101,14 @@
         pltpu.make_async_copy(wk_ref, own_s.at[1], own_sem.at[1]),
     ]
     queries = pltpu.make_async_copy(states_ref.at[pl.ds(0, first)], q_s, q_sem)
-    gathered = []
-    chips = pieces[0].shape[0]
-    for a in range(parts):
-        for c in range(chips):
-            start = pl.multiple_of(rows_ref[a // 2 * chips + c] * part_rows, part_rows)
-            gathered.append(
-                pltpu.make_async_copy(
-                    pieces[a].at[c], w_s.at[a % 2, :, pl.ds(start, part_rows), :], w_sem.at[a * chips + c]
-                )
-            )
+    gathered = [
+        pltpu.make_async_copy(
+            pieces[a],
+            w_s.at[:, pl.ds(pl.multiple_of(rows_ref[a] * part_rows, part_rows), part_rows), :],
+            w_sem.at[a],
+        )
+        for a in range(parts)
+    ]
     keys = [
         pltpu.make_async_copy(
             states_ref.at[pl.ds(first + b * rows, rows)], key_s.at[pl.ds(b * rows, rows)], key_sem.at[b]
@@ -116,17 +116,19 @@
         for b in range(blocks)
     ]
     queries.start()
-    for copy in own + gathered + keys:
+    for copy in own + gathered:
         copy.start()
     queries.wait()
     for copy in own:
         copy.wait()
+    for copy in keys:
+        copy.start()
     q = q_s[...]
     mixed = dot(dot(q, own_s[0], 1, 0).astype(BF16), own_s[1], 1, 1)
     for copy in gathered:
         copy.wait()
     for k in range(slices):
-        mixed = mixed + dot(dot(q, w_s[0, k], 1, 0).astype(BF16), w_s[1, k], 1, 1)
+        mixed = mixed + dot(dot(q, w_s[2 * k], 1, 0).astype(BF16), w_s[2 * k + 1], 1, 1)
     for v in range(depth // 128):
         g_s[v] = mixed[:, v * 128 : (v + 1) * 128]
         for p in range(count):
@@ -163,7 +165,7 @@
     keys = total - count * tokens
     heads = wq.shape[1]
     parts = len(pieces)
-    chips, slices = pieces[0].shape[:2]
+    slices = pieces[0].shape[0]
     blocks = keys // split_rows(keys, 720)
     return pl.pallas_call(
         functools.partial(teacher_kernel, parts, count, tokens),
@@ -171,7 +173,7 @@
         out_specs=[VMEM, VMEM],
         out_shape=[jax.ShapeDtypeStruct((count, tokens, keys // count), BF16), TOKEN],
         scratch_shapes=[
-            pltpu.VMEM((2, slices, depth, heads), BF16),
+            pltpu.VMEM((slices, depth, heads), BF16),
             pltpu.VMEM((2, depth, heads), BF16),
             pltpu.VMEM((count * tokens, depth), BF16),
             pltpu.VMEM((depth // 128, count * tokens, 128), F32),
@@ -180,7 +182,7 @@
             pltpu.VMEM((count, tokens, keys // count), BF16),
             pltpu.SemaphoreType.DMA,
             pltpu.SemaphoreType.DMA((blocks,)),
-            pltpu.SemaphoreType.DMA((parts * chips,)),
+            pltpu.SemaphoreType.DMA((parts,)),
             pltpu.SemaphoreType.DMA((2,)),
         ],
         compiler_params=params(),
@@ -253,10 +255,10 @@
     qdir_ref, qlen_ref, gain_ref, bias_ref, wp_ref, wpt_ref,
     sg_out, send_ref, keep_ref,
     maps_s, prob_s, log_s, units_s, qunit_s, emb_s, x_s, normed_s, inv_s, payload_s,
-    up_s, eg_s, mean_s, along_s, un_s, qg_s, hg_s, sg_s, wo_s, nt_s, right_s,
+    up_s, eg_s, mean_s, along_s, un_s, qg_s, hg_both, sg_s, wo_s, nt_s, right_s,
     first_sem, block_sem, out_sem, last_sem,
 ):
-    total, width = x_s.shape
+    total, width = normed_s.shape
     emb = emb_s.shape[1]
     seq = total // count
     rows = total // blocks
@@ -274,24 +276,26 @@
     ]
     loads = [
         [
-            pltpu.make_async_copy(src.at[pl.ds(b * rows, rows)], dst.at[pl.ds(b * rows, rows)], block_sem.at[2 * b + n])
-            for n, (src, dst) in enumerate(((normed_in, normed_s), (x_in, x_s)))
+            pltpu.make_async_copy(
+                normed_in.at[pl.ds(b * rows, rows)], normed_s.at[pl.ds(b * rows, rows)], block_sem.at[2 * b]
+            ),
+            pltpu.make_async_copy(x_in.at[b], x_s.at[b], block_sem.at[2 * b + 1]),
         ]
         for b in range(blocks)
     ]
     last = pltpu.make_async_copy(payload_in, payload_s, last_sem)
     for copy in first:
         copy.start()
-    for pair in loads:
-        for copy in pair:
-            copy.start()
-    last.start()
     gain, bias = gain_ref[...], bias_ref[...]
     gain_w = two_parts(gain, wp_ref[...])
     bias_w = two_parts(bias, wp_ref[...])
     qg_s[...] = jnp.zeros_like(qg_s)
     for copy in first:
         copy.wait()
+    for pair in loads:
+        for copy in pair:
+            copy.start()
+    last.start()
 
     spread = jnp.zeros((tokens, 1), F32)
     for r in range(count):
@@ -324,7 +328,8 @@
         along_s[b : b + thin] = inverse * (jnp.sum(eg * (e - bias_w), axis=-1, keepdims=True) / width)
 
     def wide(b):
-        hg_s[...] = dot(eg_s[b : b + sub], wp_ref[...], 1, 1)
+        hg_s = hg_both.at[b // sub % 2]
+        hg_s[...] = dot(eg_s[b : b + sub], wpt_ref[...], 1, 0)
         for c in range(b, b + sub, step):
             inverse, mean, along = inv_s[c : c + step], mean_s[c : c + step], along_s[c : c + step]
             for v in range(0, width, 128):
@@ -334,8 +339,7 @@
 
     def products(b, part, parts):
         span = width // parts
-        x = x_s[b * rows : (b + 1) * rows, part * span : (part + 1) * span]
-        value = dot(x, sg_s[b * rows : (b + 1) * rows], 0, 0)
+        value = dot(x_s[b, part * span : (part + 1) * span], sg_s[b * rows : (b + 1) * rows], 1, 0)
         if b == 0:
             wo_s[part * span : (part + 1) * span] = value
         else:
@@ -403,9 +407,9 @@
     qidx, midx, lens, core, maps, scores, payload, embeds, x, normed, inverse, gain, bias, wp, wpt,
     count, tokens, group_queries, chunk,
 ):
-    total, width = x.shape
+    total, width = normed.shape
     emb = wp.shape[1]
-    blocks = total // split_rows(total, 720)
+    blocks = x.shape[0]
     sub = split_rows(total // blocks, 256)
     chunks = width // CORES // chunk
     prob, log, units, qunit, qdir, qlen = scores
@@ -423,7 +427,7 @@
             pltpu.VMEM((total, 128), F32),
             pltpu.VMEM((count, tokens, emb), F32),
             pltpu.VMEM(qunit.shape, F32),
-            pltpu.VMEM((sub, width), F32),
+            pltpu.VMEM((2, sub, width), F32),
             pltpu.VMEM((total, width), BF16),
             pltpu.VMEM((width, width), F32),
             pltpu.VMEM((emb, width), F32),
@@ -461,31 +465,51 @@
     )(sg, out_weight, after)
 
 
-def sum_kernel(inputs, lead, *refs):
-    total = None
-    for ref in refs[:inputs]:
-        for value in [ref[n] for n in range(ref.shape[0])] if lead else [ref[...]]:
-            total = value.astype(F32) if total is None else total + value.astype(F32)
-    total = total.astype(BF16)
-    out = refs[-2]
-    refs[-1][...] = jnp.zeros_like(refs[-1])
-    if len(out.shape) > len(total.shape):
-        for n in range(out.shape[0]):
-            out[n] = total
-    else:
-        out[...] = total
-
-
-def summed(arrays, name, lead=False, copies=0, after=()):
-    shape = arrays[0].shape[1:] if lead else arrays[0].shape
-    return pl.pallas_call(
-        functools.partial(sum_kernel, len(arrays), lead),
-        in_specs=[VMEM] * len(arrays) + [ANY] * len(after),
-        out_specs=[VMEM, VMEM],
-        out_shape=[jax.ShapeDtypeStruct(((copies,) if copies else ()) + shape, BF16), TOKEN],
+def split_sum_kernel(inputs, outputs, after, index_ref, *rest):
+    ins, outs = rest[:inputs], rest[inputs + after : inputs + after + outputs]
+    token_ref, total_s = rest[-2:]
+    total = ins[0][...].astype(F32)
+    for ref in ins[1:]:
+        total = total + ref[...].astype(F32)
+    total_s[...] = total.astype(BF16).reshape(total_s.shape)
+    for k in range(outputs):
+        outs[k][...] = total_s[index_ref[k]].reshape(outs[k].shape)
+    token_ref[...] = jnp.zeros_like(token_ref)
+
+
+def split_sum(arrays, index, name, after=()):
+    outputs = index.shape[0]
+    shape = arrays[0].shape
+    lead = shape[0] // outputs
+    out = shape[1:] if lead == 1 else (lead,) + shape[1:]
+    *parts, token = pl.pallas_call(
+        functools.partial(split_sum_kernel, len(arrays), outputs, len(after)),
+        in_specs=[SMEM] + [VMEM] * len(arrays) + [ANY] * len(after),
+        out_specs=[VMEM] * (outputs + 1),
+        out_shape=[jax.ShapeDtypeStruct(out, BF16)] * outputs + [TOKEN],
+        scratch_shapes=[pltpu.VMEM((outputs, lead) + shape[1:], BF16)],
         compiler_params=pltpu.CompilerParams(vmem_limit_bytes=SMALL_LIMIT),
         name=name,
-    )(*arrays, *after)
+    )(index, *arrays, *after)
+    return parts, token
+
+
+def sum_kernel(*refs):
+    total = refs[0][...].astype(F32)
+    for ref in refs[1:-1]:
+        total = total + ref[...].astype(F32)
+    refs[-1][...] = total.astype(BF16)
+
+
+def plain_sum(arrays, name):
+    return pl.pallas_call(
+        sum_kernel,
+        in_specs=[VMEM] * len(arrays),
+        out_specs=VMEM,
+        out_shape=jax.ShapeDtypeStruct(arrays[0].shape, BF16),
+        compiler_params=pltpu.CompilerParams(vmem_limit_bytes=SMALL_LIMIT),
+        name=name,
+    )(*arrays)
 
 
 def unpack_kernel(parts, width, emb, tokens, scale, index_ref, *rest):
@@ -564,22 +588,15 @@
     def shift_t(x, k):
         return lax.ppermute(x, "tensor", [(t, (t + k) % nt) for t in range(nt)])
 
-    chip_groups = [[c * CORES + o for c in range(chips)] for o in range(CORES)]
-
-    def exchange_chips(x):
-        return lax.all_to_all(x, "dp", split_axis=0, concat_axis=0, tiled=True, axis_index_groups=chip_groups)
-
-    def exchange_t(x):
-        return lax.all_to_all(x, "tensor", split_axis=0, concat_axis=0, tiled=True)
-
     part = depth // dp
-    plane = []
-    for w in (teacher_query, teacher_key):
-        mine = lax.dynamic_slice_in_dim(w, me * part, part, 0)
-        along = jnp.stack([shift_t(mine, k) for k in range(1, nt)])
-        plane.append(exchange_chips(jnp.broadcast_to(along[None], (chips,) + along.shape)))
+    mine = jnp.stack(
+        [lax.dynamic_slice_in_dim(w, me * part, part, 0) for w in (teacher_query, teacher_key)]
+    )
+    along = jnp.concatenate([shift_t(mine, k) for k in range(1, nt)], axis=0)
+    pieces = [along] + [shift_chip(along, k) for k in range(1, chips)]
     shifts = jnp.arange(chips, dtype=jnp.int32)
-    piece_rows = jnp.concatenate([shifts * CORES + core, shifts * CORES + 1 - core]).astype(jnp.int32)
+    behind = (chip - shifts) % chips
+    piece_rows = jnp.concatenate([behind * CORES + core, behind * CORES + 1 - core]).astype(jnp.int32)
 
     dest_group = passage_dest // (count * nt)
     rows = jnp.arange(count, dtype=jnp.int32)
@@ -596,18 +613,18 @@
     payload = lax.all_to_all(
         jnp.broadcast_to(payload[None], (dp,) + payload.shape), "dp", split_axis=0, concat_axis=0, tiled=True
     )
+    midx = place.astype(jnp.int32)
+    qidx = (passage_dest // per_query).astype(jnp.int32)
+
+    gain2, bias2 = gain.reshape(1, width), bias.reshape(1, width)
+    x = flat(context)
+    normed, embeds, inverse, turned = student_forward(x, flat(stream), out_weight, gain2, bias2, proj_weight)
+    pieces[1:], payload, normed, embeds, inverse, turned = lax.optimization_barrier(
+        (pieces[1:], payload, normed, embeds, inverse, turned)
+    )
+    pieces = pieces + [swap_core(a) for a in pieces]
     told = payload[:, group_queries * tokens, :count].astype(jnp.int32)
     order = lax.dynamic_slice_in_dim(told, me * per, per, 1).reshape(-1)
-    midx = place.astype(jnp.int32)
-    qidx = (passage_dest // per_query).astype(jnp.int32)
-
-    gain2, bias2 = gain.reshape(1, width), bias.reshape(1, width)
-    x = flat(context)
-    normed, embeds, inverse = student_forward(x, flat(stream), out_weight, gain2, bias2, proj_weight)
-    plane[0], plane[1], normed, embeds, inverse = lax.optimization_barrier(
-        (plane[0], plane[1], normed, embeds, inverse)
-    )
-    pieces = plane + [swap_core(a) for a in plane]
     maps, token = teacher_maps(
         order, piece_rows, flat(teacher_states), teacher_query, teacher_key, pieces, count, tokens
     )
@@ -616,21 +633,24 @@
     chunk = width // (CORES * chips * nt)
     sg, send, keep = student_backward(
         qidx, midx, passage_len, core.astype(jnp.int32).reshape(1), maps, scores, payload,
-        embeds, x, normed, inverse, gain2, bias2, proj_weight, proj_weight.T,
+        embeds, turned, normed, inverse, gain2, bias2, proj_weight, proj_weight.T,
         count, tokens, group_queries, chunk,
     )
 
-    parts, token = summed([keep, swap_core(send)], "sum_cores")
+    ahead = ((chip + shifts) % chips).astype(jnp.int32)
+    t_shifts = jnp.arange(nt, dtype=jnp.int32)
+    t_ahead = ((mt + t_shifts) % nt).astype(jnp.int32)
+    parts, token = split_sum([keep, swap_core(send)], ahead, "sum_cores")
     grad_context, token = context_grad(sg, out_weight, token)
-    parts = exchange_chips(parts.reshape(chips, nt, chunk, -1))
-    parts, _ = summed([parts], "sum_plane", lead=True, after=(token,))
-    parts, _ = summed([exchange_t(parts)], "sum_tensor", lead=True, copies=nt)
-    line = exchange_t(parts)
+    parts = [parts[0]] + [shift_chip(parts[k], k) for k in range(1, chips)]
+    parts, _ = split_sum(parts, t_ahead, "sum_plane", (token,))
+    parts = [parts[0]] + [shift_t(parts[k], k) for k in range(1, nt)]
+    total = plain_sum(parts, "sum_tensor")
+    line = jnp.stack([total] + [shift_t(total, k) for k in range(1, nt)])
     plane = [line] + [shift_chip(line, k) for k in range(1, chips)]
     arrays = plane + [swap_core(a) for a in plane]
-    behind = (chip - shifts) % chips
     base = jnp.concatenate([core * chips + behind, (1 - core) * chips + behind]) * nt
-    index = (base[:, None] + jnp.arange(nt)[None, :]).reshape(-1).astype(jnp.int32)
+    index = (base[:, None] + ((mt - t_shifts) % nt)[None, :]).reshape(-1).astype(jnp.int32)
     grad_out, grad_proj, grad_gain, grad_bias, loss = unpack(
         arrays, index, width, emb, tokens, 1.0 / (count * dp * nt * tokens)
     )

time: 171 us -> 138 us (0.81)
  waiting for transfers between devices: 41.8 us -> 23.9 us
  blocking collectives: 9.77 us -> 0 us
  Pallas kernels: 67.7 us -> 64.5 us
    all_to_all x4 -> x0, starting transfers between devices: 14.1 us -> none  [the longest x3 10.7 us: exchange_chips(): lax.all_to_all(x, 'dp', split_axis=0, concat_axis=0, tiled=True, axis_ind...]
    all_to_all x4 -> x0, waiting for transfers between devices: 11.5 us -> none  [the longest x1 6.18 us: exchange_t(): return lax.all_to_all(x, 'tensor', split_axis=0, concat_axis=0, tiled=True)]
    all_to_all x1, waiting for transfers between devices: 9.88 us -> 0.01 us  [local(): lax.all_to_all(jnp.broadcast_to(payload[None], (dp,) + payload.shape), 'd...]
    all_to_all x1 -> x0, blocking collectives: 9.77 us -> none  [exchange_t(): return lax.all_to_all(x, 'tensor', split_axis=0, concat_axis=0, tiled=True)]
    ppermute x3 -> x9, starting transfers between devices: 3.49 us -> 12.3 us  [shift_chip(): lax.ppermute(x, 'dp', [(c * CORES + o, (c + k) % chips * CORES + o) for c...]
    ppermute x6 -> x9, starting transfers between devices: 9.86 us -> 14.7 us  [shift_t(): return lax.ppermute(x, 'tensor', [(t, (t + k) % nt) for t in range(nt)])]
    ppermute x3 -> x9, waiting for transfers between devices: 6.05 us -> 9.97 us  [shift_chip(): lax.ppermute(x, 'dp', [(c * CORES + o, (c + k) % chips * CORES + o) for c...]
    pallas_call x1, Pallas kernels: 24.6 us -> 22.3 us  [student_backward(): pl.pallas_call(functools.partial(backward_kernel, tokens, count, blocks,...]
  transfers between devices with their start and end apart: 22 -> 29, of which waited for: 13 -> 16; matrix products, arithmetic and copies ran while one was open for 4% -> 6% of each run, Pallas kernels for 14% -> 18%
where the time goes in v2:
time: 138 us
  Pallas kernels  64.5 us (47%)
  starting transfers between devices  35.6 us (26%)
  waiting for transfers between devices  23.9 us (17%)
  local copies, waits for them, and re-layouts  9.72 us (7%)
  other arithmetic  2.74 us (2%)
    pallas_call x1, Pallas kernels, student_backward(): pl.pallas_call(functools.partial(backward_kernel, tokens, count, blocks,...  22.3 us
    ppermute x9, starting transfers between devices, shift_t(): return lax.ppermute(x, 'tensor', [(t, (t + k) % nt) for t in range(nt)])  14.7 us
    pallas_call x1, Pallas kernels, student_forward(): pl.pallas_call(forward_kernel, grid=(total // rows,), in_specs=[block(wid...  13.2 us
    pallas_call x1, Pallas kernels, teacher_maps(): pl.pallas_call(functools.partial(teacher_kernel, parts, count, tokens), i...  12.6 us
    ppermute x9, starting transfers between devices, shift_chip(): lax.ppermute(x, 'dp', [(c * CORES + o, (c + k) % chips * CORES + o) for c...  12.3 us
    ppermute x9, waiting for transfers between devices, shift_chip(): lax.ppermute(x, 'dp', [(c * CORES + o, (c + k) % chips * CORES + o) for c...  9.97 us
    ppermute x9, waiting for transfers between devices, shift_t(): return lax.ppermute(x, 'tensor', [(t, (t + k) % nt) for t in range(nt)])  7.88 us
    pallas_call x1, Pallas kernels, context_grad(): pl.pallas_call(context_kernel, grid=(total // rows,), in_specs=[block, pl...  7.53 us
  transfers between devices with their start and end apart: 29, of which 16 were waited for; matrix products, arithmetic and copies ran while one was open for 6% of the time, Pallas kernels for 18%

profile of v2, /device:TPU:0, one launch (start us, length us, event | category | flops | bytes accessed | tf_op | source)
XLA Modules:
  0.0 137.6 jit_solution(6368487459109812737)
XLA Ops:
  1.5 3.1 %collective-permute-start = (bf16[2,128,256]{2,1,0:T(8,128)(2,1)S(1)}, bf16[2,128,256]{2,1,0:T(8,128)(2,1)S(1)}, u32[]{:S(2)}, u32[]{:S(2)}) collective-permute-start(bf16[2,128,256]{2,1,0:T(8,128)(2,1)S(1)} %pad_maximum_fusion.1), channel_id=1, source_target_pairs={{0,1},{1,2},{2,3},{3,0},{4,5},{5,6},{6,7},{7,4},{8,9},{9,10},{10,1... | collective-permute-start | bytes 393224 | tf_op jit(solution)/shard_map/ppermute | solution.py:589
  4.6 2.6 %collective-permute-start.1 = (bf16[2,128,256]{2,1,0:T(8,128)(2,1)S(1)}, bf16[2,128,256]{2,1,0:T(8,128)(2,1)S(1)}, u32[]{:S(2)}, u32[]{:S(2)}) collective-permute-start(bf16[2,128,256]{2,1,0:T(8,128)(2,1)S(1)} %pad_maximum_fusion.1), channel_id=1, source_target_pairs={{0,2},{1,3},{2,0},{3,1},{4,6},{5,7},{6,4},{7,5},{8,10},{9,11},{10,... | collective-permute-start | bytes 393224 | tf_op jit(solution)/shard_map/ppermute | solution.py:589
  11.2 3.7 %all-to-all-start = ((bf16[8,48,768]{2,1,0:T(8,128)(2,1)}), bf16[8,48,768]{2,1,0:T(8,128)(2,1)S(1)}, u32[]{:S(2)}, u32[]{:S(2)}) async-start(bf16[8,48,768]{2,1,0:T(8,128)(2,1)} %broadcast_in_dim.16), calls=%async_computation | async-start | bytes 1179648 | tf_op jit(solution)/shard_map/all_to_all | solution.py:613
  15.9 1.5 %collective-permute-start.3 = (bf16[6,128,256]{2,1,0:T(8,128)(2,1)S(1)}, bf16[6,128,256]{2,1,0:T(8,128)(2,1)S(1)}, u32[]{:S(2)}, u32[]{:S(2)}) collective-permute-start(bf16[6,128,256]{2,1,0:T(8,128)(2,1)S(1)} %constant_dynamic-update-slice_fusion.rest_0_), channel_id=1, source_target_pairs={{0,8},{4,12},{8,16},{12,20},{16,24},{20,28},{24,0},{28,4},{1,9},{5... | collective-permute-start | bytes 1179656 | tf_op jit(solution)/shard_map/ppermute | solution.py:581
  17.5 1.5 %collective-permute-start.4 = (bf16[6,128,256]{2,1,0:T(8,128)(2,1)S(1)}, bf16[6,128,256]{2,1,0:T(8,128)(2,1)S(1)}, u32[]{:S(2)}, u32[]{:S(2)}) collective-permute-start(bf16[6,128,256]{2,1,0:T(8,128)(2,1)S(1)} %constant_dynamic-update-slice_fusion.rest_0_), channel_id=1, source_target_pairs={{0,16},{4,20},{8,24},{12,28},{16,0},{20,4},{24,8},{28,12},{1,17},{... | collective-permute-start | bytes 1179656 | tf_op jit(solution)/shard_map/ppermute | solution.py:581
  23.0 13.2 %student_forward.1 = (bf16[2880,768]{1,0:T(8,128)(2,1)}, f32[2880,128]{1,0:T(8,128)}, f32[2880,128]{1,0:T(8,128)}, bf16[4,768,720]{2,1,0:T(8,128)(2,1)}) custom-call(bf16[2880,768]{1,0:T(8,128)(2,1)} %bitcast.37, bf16[2880,768]{1,0:T(8,128)(2,1)} %bitcast.38, bf16[768,768]{1,0:T(8,128)(2,1)} %wo_ref.3, f32[1,768]{1,0:T(1,128)} %reshape.106.gain_ref, ...), custom_call_target="tpu_custom_call" | custom-call | flops 3963617280 | bytes 17694720 | tf_op jit(solution)/shard_map/student_forward/pallas_call | solution.py:70
  36.3 5.1 %collective-permute-done.4.rest_2_ = bf16[6,128,256]{2,1,0:T(8,128)(2,1)S(1)} collective-permute-done((bf16[6,128,256]{2,1,0:T(8,128)(2,1)S(1)}, bf16[6,128,256]{2,1,0:T(8,128)(2,1)S(1)}, u32[]{:S(2)}, u32[]{:S(2)}) %collective-permute-start.4) | collective-permute-done | bytes 393248 | tf_op jit(solution)/shard_map/ppermute | solution.py:581
  45.1 12.6 %teacher_maps.1 = (bf16[16,32,180]{2,1,0:T(8,128)(2,1)}, f32[8,128]{1,0:T(8,128)}) custom-call(s32[16]{0:T(128)} %reshape.108.order_ref, s32[8]{0:T(128)} %pad_add_fusion.rows_ref, bf16[3392,1024]{1,0:T(8,128)(2,1)} %bitcast.36, bf16[1024,256]{1,0:T(8,128)(2,1)} %wq_ref.1, bf16[1024,256]{1,0:T(8,128)(2,1)} %wk_ref.1, bf16[6,128,256]{2,1,0:T(8,128)(2,1)} %copy-done.6, ...), custom_call_target="tpu_custom_call" | custom-call | flops 4294967296 | bytes 11141120 | tf_op jit(solution)/shard_map/teacher_maps/pallas_call | solution.py:170
  57.6 3.6 %all-to-all-start.1 = ((bf16[16,32,180]{2,1,0:T(8,128)(2,1)}), bf16[16,32,180]{2,1,0:T(8,128)(2,1)S(1)}, u32[]{:S(2)}, u32[]{:S(2)}) async-start(bf16[16,32,180]{2,1,0:T(8,128)(2,1)} %get-tuple-element.53), calls=%async_computation.1 | async-start | bytes 524288 | tf_op jit(solution)/shard_map/all_to_all | solution.py:631
  62.1 4.3 %student_scores.1 = (f32[16,32,180]{2,1,0:T(8,128)}, f32[16,32,180]{2,1,0:T(8,128)}, bf16[16,180,128]{2,1,0:T(8,128)(2,1)}, bf16[8,32,128]{2,1,0:T(8,128)(2,1)}, f32[256,128]{1,0:T(8,128)}, /*index=5*/f32[256,128]{1,0:T(8,128)}) custom-call(s32[16]{0:T(128)} %copy-done.13, s32[16]{0:T(128)} %len_ref.3, bf16[8,48,768]{2,1,0:T(8,128)(2,1)} %copy-done.3, ...), custom_call_target="tpu_custom_call" | custom-call | flops 1000000000 | bytes 1474560 | tf_op jit(solution)/shard_map/student_scores/pallas_call | solution.py:226
  66.4 1.6 %all-to-all-done.1.maps_in = bf16[16,32,180]{2,1,0:T(8,128)(2,1)S(1)} async-done(((bf16[16,32,180]{2,1,0:T(8,128)(2,1)}), bf16[16,32,180]{2,1,0:T(8,128)(2,1)S(1)}, u32[]{:S(2)}, u32[]{:S(2)}) %all-to-all-start.1) | async-done | bytes 184352 | tf_op jit(solution)/shard_map/all_to_all | solution.py:631
  68.6 22.3 %student_backward.1 = (bf16[2880,768]{1,0:T(8,128)(2,1)}, bf16[16,24,1024]{2,1,0:T(8,128)(2,1)}, bf16[16,24,1024]{2,1,0:T(8,128)(2,1)}) custom-call(s32[16]{0:T(128)} %copy-done.13, s32[16]{0:T(128)} %copy-done.14, s32[16]{0:T(128)} %len_ref.3, s32[1]{0:T(128)} %bitcast.core_ref, bf16[16,32,180]{2,1,0:T(8,128)(2,1)} %copy-done.4, ...), custom_call_target="tpu_custom_call" | custom-call | flops 4529848320 | bytes 17694720 | tf_op jit(solution)/shard_map/student_backward/pallas_call | solution.py:418
  91.1 2.4 %collective-permute-done.10.rest_1_ = bf16[16,24,1024]{2,1,0:T(8,128)(2,1)S(1)} collective-permute-done((bf16[16,24,1024]{2,1,0:T(8,128)(2,1)}, bf16[16,24,1024]{2,1,0:T(8,128)(2,1)S(1)}, u32[]{:S(2)}, u32[]{:S(2)}) %collective-permute-start.10) | collective-permute-done | bytes 786464 | tf_op jit(solution)/shard_map/ppermute | solution.py:586
  97.9 1.8 %collective-permute-start.13 = (bf16[4,24,1024]{2,1,0:T(8,128)(2,1)S(1)}, bf16[4,24,1024]{2,1,0:T(8,128)(2,1)S(1)}, u32[]{:S(2)}, u32[]{:S(2)}) collective-permute-start(bf16[4,24,1024]{2,1,0:T(8,128)(2,1)S(1)} %get-tuple-element.70), channel_id=1, source_target_pairs={{0,24},{4,28},{8,0},{12,4},{16,8},{20,12},{24,16},{28,20},{1,25},{... | collective-permute-start | bytes 589832 | tf_op jit(solution)/shard_map/ppermute | solution.py:581
  99.7 7.5 %context_grad.1 = (bf16[2880,768]{1,0:T(8,128)(2,1)}, f32[8,128]{1,0:T(8,128)}) custom-call(bf16[2880,768]{1,0:T(8,128)(2,1)} %get-tuple-element.71.sg_ref, bf16[768,768]{1,0:T(8,128)(2,1)} %wo_ref.3, f32[8,128]{1,0:T(8,128)} %copy-done.2), custom_call_target="tpu_custom_call" | custom-call | flops 3397386240 | bytes 8847360 | tf_op jit(solution)/shard_map/context_grad/pallas_call | solution.py:456
  110.7 2.8 %collective-permute-start.16 = (bf16[24,1024]{1,0:T(8,128)(2,1)S(1)}, bf16[24,1024]{1,0:T(8,128)(2,1)S(1)}, u32[]{:S(2)}, u32[]{:S(2)}) collective-permute-start(bf16[24,1024]{1,0:T(8,128)(2,1)S(1)} %get-tuple-element.77), channel_id=1, source_target_pairs={{0,3},{1,0},{2,1},{3,2},{4,7},{5,4},{6,5},{7,6},{8,11},{9,8},{10,9... | collective-permute-start | bytes 147464 | tf_op jit(solution)/shard_map/ppermute | solution.py:589
  113.5 2.2 %collective-permute-done.14.refs_1_ = bf16[24,1024]{1,0:T(8,128)(2,1)S(1)} collective-permute-done((bf16[24,1024]{1,0:T(8,128)(2,1)S(1)}, bf16[24,1024]{1,0:T(8,128)(2,1)S(1)}, u32[]{:S(2)}, u32[]{:S(2)}) %collective-permute-start.14) | collective-permute-done | bytes 49184 | tf_op jit(solution)/shard_map/ppermute | solution.py:589
  118.3 1.8 %collective-permute-start.18 = (bf16[24,1024]{1,0:T(8,128)(2,1)S(1)}, bf16[24,1024]{1,0:T(8,128)(2,1)S(1)}, u32[]{:S(2)}, u32[]{:S(2)}) collective-permute-start(bf16[24,1024]{1,0:T(8,128)(2,1)S(1)} %sum_tensor.1), channel_id=1, source_target_pairs={{0,2},{1,3},{2,0},{3,1},{4,6},{5,7},{6,4},{7,5},{8,10},{9,11},{10,... | collective-permute-start | bytes 147464 | tf_op jit(solution)/shard_map/ppermute | solution.py:589
  120.7 2.1 %collective-permute-done.17 = bf16[24,1024]{1,0:T(8,128)(2,1)S(1)} collective-permute-done((bf16[24,1024]{1,0:T(8,128)(2,1)S(1)}, bf16[24,1024]{1,0:T(8,128)(2,1)S(1)}, u32[]{:S(2)}, u32[]{:S(2)}) %collective-permute-start.17) | collective-permute-done | bytes 49184 | tf_op jit(solution)/shard_map/ppermute | solution.py:589
  125.8 1.5 %collective-permute-start.21 = (bf16[4,24,1024]{2,1,0:T(8,128)(2,1)S(1)}, bf16[4,24,1024]{2,1,0:T(8,128)(2,1)S(1)}, u32[]{:S(2)}, u32[]{:S(2)}) collective-permute-start(bf16[4,24,1024]{2,1,0:T(8,128)(2,1)S(1)} %pad_maximum_fusion.rest_0_), channel_id=1, source_target_pairs={{0,16},{4,20},{8,24},{12,28},{16,0},{20,4},{24,8},{28,12},{1,17},{... | collective-permute-start | bytes 589832 | tf_op jit(solution)/shard_map/ppermute | solution.py:581
  127.3 1.5 %collective-permute-start.22 = (bf16[4,24,1024]{2,1,0:T(8,128)(2,1)S(1)}, bf16[4,24,1024]{2,1,0:T(8,128)(2,1)S(1)}, u32[]{:S(2)}, u32[]{:S(2)}) collective-permute-start(bf16[4,24,1024]{2,1,0:T(8,128)(2,1)S(1)} %pad_maximum_fusion.rest_0_), channel_id=1, source_target_pairs={{0,24},{4,28},{8,0},{12,4},{16,8},{20,12},{24,16},{28,20},{1,25},{... | collective-permute-start | bytes 589832 | tf_op jit(solution)/shard_map/ppermute | solution.py:581
  128.9 2.4 %collective-permute-done.20.rest_1_ = bf16[4,24,1024]{2,1,0:T(8,128)(2,1)S(1)} collective-permute-done((bf16[4,24,1024]{2,1,0:T(8,128)(2,1)S(1)}, bf16[4,24,1024]{2,1,0:T(8,128)(2,1)S(1)}, u32[]{:S(2)}, u32[]{:S(2)}) %collective-permute-start.20) | collective-permute-done | bytes 196640 | tf_op jit(solution)/shard_map/ppermute | solution.py:581
  131.3 2.0 %collective-permute-done.21.rest_2_ = bf16[4,24,1024]{2,1,0:T(8,128)(2,1)S(1)} collective-permute-done((bf16[4,24,1024]{2,1,0:T(8,128)(2,1)S(1)}, bf16[4,24,1024]{2,1,0:T(8,128)(2,1)S(1)}, u32[]{:S(2)}, u32[]{:S(2)}) %collective-permute-start.21) | collective-permute-done | bytes 196640 | tf_op jit(solution)/shard_map/ppermute | solution.py:581
  135.1 2.3 %unpack.1 = (f32[32,24,768]{2,1,0:T(8,128)}, f32[32,24,128]{2,1,0:T(8,128)}, f32[6,128]{1,0:T(8,128)}, f32[6,128]{1,0:T(8,128)}, f32[1]{0:T(128)}) custom-call(s32[32]{0:T(128)S(1)} %add.110.index_ref, bf16[4,24,1024]{2,1,0:T(8,128)(2,1)S(1)} %pad_maximum_fusion.rest_0_, bf16[4,24,1024]{2,1,0:T(8,128)(2,1)S(1)} %collective-permute-done.20.rest_1_, ...), custom_call_target="tpu_custom_call" | custom-call | tf_op jit(solution)/shard_map/unpack/pallas_call | solution.py:537
  (101 shorter events, 30.9 us)
Async XLA Ops:
  1.5 13.4 %collective-permute-start = (bf16[2,128,256]{2,1,0:T(8,128)(2,1)S(1)}, bf16[2,128,256]{2,1,0:T(8,128)(2,1)S(1)}, u32[]{:S(2)}, u32[]{:S(2)}) collective-permute-start(bf16[2,128,256]{2,1,0:T(8,128)(2,1)S(1)} %pad_maximum_fusion.1), channel_id=1, source_target_pairs={{0,1},{1,2},{2,3},{3,0},{4,5},{5,6},{6,7},{7,4},{8,9},{9,10},{10,1... | collective-permute-start | bytes 393224 | tf_op jit(solution)/shard_map/ppermute | solution.py:589
  4.6 11.2 %collective-permute-start.1 = (bf16[2,128,256]{2,1,0:T(8,128)(2,1)S(1)}, bf16[2,128,256]{2,1,0:T(8,128)(2,1)S(1)}, u32[]{:S(2)}, u32[]{:S(2)}) collective-permute-start(bf16[2,128,256]{2,1,0:T(8,128)(2,1)S(1)} %pad_maximum_fusion.1), channel_id=1, source_target_pairs={{0,2},{1,3},{2,0},{3,1},{4,6},{5,7},{6,4},{7,5},{8,10},{9,11},{10,... | collective-permute-start | bytes 393224 | tf_op jit(solution)/shard_map/ppermute | solution.py:589
  7.2 8.7 %collective-permute-start.2 = (bf16[2,128,256]{2,1,0:T(8,128)(2,1)S(1)}, bf16[2,128,256]{2,1,0:T(8,128)(2,1)S(1)}, u32[]{:S(2)}, u32[]{:S(2)}) collective-permute-start(bf16[2,128,256]{2,1,0:T(8,128)(2,1)S(1)} %pad_maximum_fusion.1), channel_id=1, source_target_pairs={{0,3},{1,0},{2,1},{3,2},{4,7},{5,4},{6,5},{7,6},{8,11},{9,8},{10,9... | collective-permute-start | bytes 393224 | tf_op jit(solution)/shard_map/ppermute | solution.py:589
  11.2 25.0 %all-to-all-start = ((bf16[8,48,768]{2,1,0:T(8,128)(2,1)}), bf16[8,48,768]{2,1,0:T(8,128)(2,1)S(1)}, u32[]{:S(2)}, u32[]{:S(2)}) async-start(bf16[8,48,768]{2,1,0:T(8,128)(2,1)} %broadcast_in_dim.16), calls=%async_computation | async-start | bytes 1179648 | tf_op jit(solution)/shard_map/all_to_all | solution.py:613
  15.9 20.4 %collective-permute-start.3 = (bf16[6,128,256]{2,1,0:T(8,128)(2,1)S(1)}, bf16[6,128,256]{2,1,0:T(8,128)(2,1)S(1)}, u32[]{:S(2)}, u32[]{:S(2)}) collective-permute-start(bf16[6,128,256]{2,1,0:T(8,128)(2,1)S(1)} %constant_dynamic-update-slice_fusion.rest_0_), channel_id=1, source_target_pairs={{0,8},{4,12},{8,16},{12,20},{16,24},{20,28},{24,0},{28,4},{1,9},{5... | collective-permute-start | bytes 1179656 | tf_op jit(solution)/shard_map/ppermute | solution.py:581
  17.5 23.9 %collective-permute-start.4 = (bf16[6,128,256]{2,1,0:T(8,128)(2,1)S(1)}, bf16[6,128,256]{2,1,0:T(8,128)(2,1)S(1)}, u32[]{:S(2)}, u32[]{:S(2)}) collective-permute-start(bf16[6,128,256]{2,1,0:T(8,128)(2,1)S(1)} %constant_dynamic-update-slice_fusion.rest_0_), channel_id=1, source_target_pairs={{0,16},{4,20},{8,24},{12,28},{16,0},{20,4},{24,8},{28,12},{1,17},{... | collective-permute-start | bytes 1179656 | tf_op jit(solution)/shard_map/ppermute | solution.py:581
  19.0 22.4 %collective-permute-start.5 = (bf16[6,128,256]{2,1,0:T(8,128)(2,1)S(1)}, bf16[6,128,256]{2,1,0:T(8,128)(2,1)S(1)}, u32[]{:S(2)}, u32[]{:S(2)}) collective-permute-start(bf16[6,128,256]{2,1,0:T(8,128)(2,1)S(1)} %constant_dynamic-update-slice_fusion.rest_0_), channel_id=1, source_target_pairs={{0,24},{4,28},{8,0},{12,4},{16,8},{20,12},{24,16},{28,20},{1,25},{... | collective-permute-start | bytes 1179656 | tf_op jit(solution)/shard_map/ppermute | solution.py:581
  36.2 7.2 %collective-permute-start.6 = (bf16[6,128,256]{2,1,0:T(8,128)(2,1)S(1)}, bf16[6,128,256]{2,1,0:T(8,128)(2,1)S(1)}, u32[]{:S(2)}, u32[]{:S(2)}) collective-permute-start(bf16[6,128,256]{2,1,0:T(8,128)(2,1)S(1)} %constant_dynamic-update-slice_fusion.rest_0_), channel_id=1, source_target_pairs={{0,4},{4,0},{8,12},{12,8},{16,20},{20,16},{24,28},{28,24},{1,5},{5... | collective-permute-start | bytes 1179656 | tf_op jit(solution)/shard_map/ppermute | solution.py:586
  41.4 2.8 %collective-permute-start.8 = (bf16[6,128,256]{2,1,0:T(8,128)(2,1)S(1)}, bf16[6,128,256]{2,1,0:T(8,128)(2,1)S(1)}, u32[]{:S(2)}, u32[]{:S(2)}) collective-permute-start(bf16[6,128,256]{2,1,0:T(8,128)(2,1)S(1)} %collective-permute-done.4.rest_2_), channel_id=1, source_target_pairs={{0,4},{4,0},{8,12},{12,8},{16,20},{20,16},{24,28},{28,24},{1,5},{5... | collective-permute-start | bytes 1179656 | tf_op jit(solution)/shard_map/ppermute | solution.py:586
  57.6 10.3 %all-to-all-start.1 = ((bf16[16,32,180]{2,1,0:T(8,128)(2,1)}), bf16[16,32,180]{2,1,0:T(8,128)(2,1)S(1)}, u32[]{:S(2)}, u32[]{:S(2)}) async-start(bf16[16,32,180]{2,1,0:T(8,128)(2,1)} %get-tuple-element.53), calls=%async_computation.1 | async-start | bytes 524288 | tf_op jit(solution)/shard_map/all_to_all | solution.py:631
  96.3 11.0 %collective-permute-start.11 = (bf16[4,24,1024]{2,1,0:T(8,128)(2,1)S(1)}, bf16[4,24,1024]{2,1,0:T(8,128)(2,1)S(1)}, u32[]{:S(2)}, u32[]{:S(2)}) collective-permute-start(bf16[4,24,1024]{2,1,0:T(8,128)(2,1)S(1)} %get-tuple-element.68), channel_id=1, source_target_pairs={{0,8},{4,12},{8,16},{12,20},{16,24},{20,28},{24,0},{28,4},{1,9},{5... | collective-permute-start | bytes 589832 | tf_op jit(solution)/shard_map/ppermute | solution.py:581
  96.8 10.9 %collective-permute-start.12 = (bf16[4,24,1024]{2,1,0:T(8,128)(2,1)S(1)}, bf16[4,24,1024]{2,1,0:T(8,128)(2,1)S(1)}, u32[]{:S(2)}, u32[]{:S(2)}) collective-permute-start(bf16[4,24,1024]{2,1,0:T(8,128)(2,1)S(1)} %get-tuple-element.69), channel_id=1, source_target_pairs={{0,16},{4,20},{8,24},{12,28},{16,0},{20,4},{24,8},{28,12},{1,17},{... | collective-permute-start | bytes 589832 | tf_op jit(solution)/shard_map/ppermute | solution.py:581
  97.9 9.8 %collective-permute-start.13 = (bf16[4,24,1024]{2,1,0:T(8,128)(2,1)S(1)}, bf16[4,24,1024]{2,1,0:T(8,128)(2,1)S(1)}, u32[]{:S(2)}, u32[]{:S(2)}) collective-permute-start(bf16[4,24,1024]{2,1,0:T(8,128)(2,1)S(1)} %get-tuple-element.70), channel_id=1, source_target_pairs={{0,24},{4,28},{8,0},{12,4},{16,8},{20,12},{24,16},{28,20},{1,25},{... | collective-permute-start | bytes 589832 | tf_op jit(solution)/shard_map/ppermute | solution.py:581
  109.7 6.0 %collective-permute-start.14 = (bf16[24,1024]{1,0:T(8,128)(2,1)S(1)}, bf16[24,1024]{1,0:T(8,128)(2,1)S(1)}, u32[]{:S(2)}, u32[]{:S(2)}) collective-permute-start(bf16[24,1024]{1,0:T(8,128)(2,1)S(1)} %get-tuple-element.75), channel_id=1, source_target_pairs={{0,1},{1,2},{2,3},{3,0},{4,5},{5,6},{6,7},{7,4},{8,9},{9,10},{10,1... | collective-permute-start | bytes 147464 | tf_op jit(solution)/shard_map/ppermute | solution.py:589
  110.4 6.5 %collective-permute-start.15 = (bf16[24,1024]{1,0:T(8,128)(2,1)S(1)}, bf16[24,1024]{1,0:T(8,128)(2,1)S(1)}, u32[]{:S(2)}, u32[]{:S(2)}) collective-permute-start(bf16[24,1024]{1,0:T(8,128)(2,1)S(1)} %get-tuple-element.76), channel_id=1, source_target_pairs={{0,2},{1,3},{2,0},{3,1},{4,6},{5,7},{6,4},{7,5},{8,10},{9,11},{10,... | collective-permute-start | bytes 147464 | tf_op jit(solution)/shard_map/ppermute | solution.py:589
  110.7 6.1 %collective-permute-start.16 = (bf16[24,1024]{1,0:T(8,128)(2,1)S(1)}, bf16[24,1024]{1,0:T(8,128)(2,1)S(1)}, u32[]{:S(2)}, u32[]{:S(2)}) collective-permute-start(bf16[24,1024]{1,0:T(8,128)(2,1)S(1)} %get-tuple-element.77), channel_id=1, source_target_pairs={{0,3},{1,0},{2,1},{3,2},{4,7},{5,4},{6,5},{7,6},{8,11},{9,8},{10,9... | collective-permute-start | bytes 147464 | tf_op jit(solution)/shard_map/ppermute | solution.py:589
  116.9 6.0 %collective-permute-start.17 = (bf16[24,1024]{1,0:T(8,128)(2,1)S(1)}, bf16[24,1024]{1,0:T(8,128)(2,1)S(1)}, u32[]{:S(2)}, u32[]{:S(2)}) collective-permute-start(bf16[24,1024]{1,0:T(8,128)(2,1)S(1)} %sum_tensor.1), channel_id=1, source_target_pairs={{0,1},{1,2},{2,3},{3,0},{4,5},{5,6},{6,7},{7,4},{8,9},{9,10},{10,1... | collective-permute-start | bytes 147464 | tf_op jit(solution)/shard_map/ppermute | solution.py:589
  118.3 5.7 %collective-permute-start.18 = (bf16[24,1024]{1,0:T(8,128)(2,1)S(1)}, bf16[24,1024]{1,0:T(8,128)(2,1)S(1)}, u32[]{:S(2)}, u32[]{:S(2)}) collective-permute-start(bf16[24,1024]{1,0:T(8,128)(2,1)S(1)} %sum_tensor.1), channel_id=1, source_target_pairs={{0,2},{1,3},{2,0},{3,1},{4,6},{5,7},{6,4},{7,5},{8,10},{9,11},{10,... | collective-permute-start | bytes 147464 | tf_op jit(solution)/shard_map/ppermute | solution.py:589
  120.1 4.4 %collective-permute-start.19 = (bf16[24,1024]{1,0:T(8,128)(2,1)S(1)}, bf16[24,1024]{1,0:T(8,128)(2,1)S(1)}, u32[]{:S(2)}, u32[]{:S(2)}) collective-permute-start(bf16[24,1024]{1,0:T(8,128)(2,1)S(1)} %sum_tensor.1), channel_id=1, source_target_pairs={{0,3},{1,0},{2,1},{3,2},{4,7},{5,4},{6,5},{7,6},{8,11},{9,8},{10,9... | collective-permute-start | bytes 147464 | tf_op jit(solution)/shard_map/ppermute | solution.py:589
  124.5 6.9 %collective-permute-start.20 = (bf16[4,24,1024]{2,1,0:T(8,128)(2,1)S(1)}, bf16[4,24,1024]{2,1,0:T(8,128)(2,1)S(1)}, u32[]{:S(2)}, u32[]{:S(2)}) collective-permute-start(bf16[4,24,1024]{2,1,0:T(8,128)(2,1)S(1)} %pad_maximum_fusion.rest_0_), channel_id=1, source_target_pairs={{0,8},{4,12},{8,16},{12,20},{16,24},{20,28},{24,0},{28,4},{1,9},{5... | collective-permute-start | bytes 589832 | tf_op jit(solution)/shard_map/ppermute | solution.py:581
  125.8 7.6 %collective-permute-start.21 = (bf16[4,24,1024]{2,1,0:T(8,128)(2,1)S(1)}, bf16[4,24,1024]{2,1,0:T(8,128)(2,1)S(1)}, u32[]{:S(2)}, u32[]{:S(2)}) collective-permute-start(bf16[4,24,1024]{2,1,0:T(8,128)(2,1)S(1)} %pad_maximum_fusion.rest_0_), channel_id=1, source_target_pairs={{0,16},{4,20},{8,24},{12,28},{16,0},{20,4},{24,8},{28,12},{1,17},{... | collective-permute-start | bytes 589832 | tf_op jit(solution)/shard_map/ppermute | solution.py:581
  127.3 6.1 %collective-permute-start.22 = (bf16[4,24,1024]{2,1,0:T(8,128)(2,1)S(1)}, bf16[4,24,1024]{2,1,0:T(8,128)(2,1)S(1)}, u32[]{:S(2)}, u32[]{:S(2)}) collective-permute-start(bf16[4,24,1024]{2,1,0:T(8,128)(2,1)S(1)} %pad_maximum_fusion.rest_0_), channel_id=1, source_target_pairs={{0,24},{4,28},{8,0},{12,4},{16,8},{20,12},{24,16},{28,20},{1,25},{... | collective-permute-start | bytes 589832 | tf_op jit(solution)/shard_map/ppermute | solution.py:581
  128.9 5.1 %collective-permute-start.23 = (bf16[4,24,1024]{2,1,0:T(8,128)(2,1)S(1)}, bf16[4,24,1024]{2,1,0:T(8,128)(2,1)S(1)}, u32[]{:S(2)}, u32[]{:S(2)}) collective-permute-start(bf16[4,24,1024]{2,1,0:T(8,128)(2,1)S(1)} %pad_maximum_fusion.rest_0_), channel_id=1, source_target_pairs={{0,4},{4,0},{8,12},{12,8},{16,20},{20,16},{24,28},{28,24},{1,5},{5... | collective-permute-start | bytes 589832 | tf_op jit(solution)/shard_map/ppermute | solution.py:586
  131.3 2.7 %collective-permute-start.24 = (bf16[4,24,1024]{2,1,0:T(8,128)(2,1)S(1)}, bf16[4,24,1024]{2,1,0:T(8,128)(2,1)S(1)}, u32[]{:S(2)}, u32[]{:S(2)}) collective-permute-start(bf16[4,24,1024]{2,1,0:T(8,128)(2,1)S(1)} %collective-permute-done.20.rest_1_), channel_id=1, source_target_pairs={{0,4},{4,0},{8,12},{12,8},{16,20},{20,16},{24,28},{28,24},{1,5},{5... | collective-permute-start | bytes 589832 | tf_op jit(solution)/shard_map/ppermute | solution.py:586
  (20 other events, 145.0 us)

commit v3 on v2

--- a/solution.py
+++ b/solution.py
@@ -35,6 +35,10 @@
     return max(n for n in range(16, most + 1, 16) if rows % n == 0)
 
 
+def one_row(ref):
+    return jnp.concatenate([ref[v : v + 1] for v in range(ref.shape[0])], axis=1)
+
+
 def params(**kw):
     return pltpu.CompilerParams(vmem_limit_bytes=VMEM_LIMIT, **kw)
 
@@ -45,8 +49,8 @@
 
 def forward_kernel(x_ref, str_ref, wo_ref, gain_ref, bias_ref, wp_ref, normed_ref, emb_ref, inv_ref, turned_ref, prod_s, hid_s):
     rows, width = x_ref.shape
-    sub = split_rows(rows, 256)
-    gain, bias = gain_ref[...], bias_ref[...]
+    sub = rows
+    gain, bias = one_row(gain_ref), one_row(bias_ref)
     for b in range(0, rows, sub):
         prod_s[b : b + sub] = dot(x_ref[b : b + sub], wo_ref[...], 1, 0)
         for c in range(b, b + sub, 16):
@@ -135,13 +139,13 @@
             q_s[p * tokens : (p + 1) * tokens, v * 128 : (v + 1) * 128] = g_s[
                 v, pl.ds(p, tokens, stride=count), :
             ].astype(BF16)
-    mixed = q_s[...]
+    mixed = q_s[...].T
     scale = 1.0 / (math.sqrt(depth) * softcap)
     side = 128 // tokens
     pair = lax.broadcasted_iota(jnp.int32, (rows, 128), 0) % count
     for b in range(blocks):
         keys[b].wait()
-        raw = dot(key_s[b * rows : (b + 1) * rows], mixed, 1, 1)
+        raw = dot(key_s[b * rows : (b + 1) * rows], mixed, 1, 0)
         mine = raw[:, :128]
         for v in range(1, count // side):
             mine = jnp.where(pair >= v * side, raw[:, v * 128 : (v + 1) * 128], mine)
@@ -262,7 +266,7 @@
     emb = emb_s.shape[1]
     seq = total // count
     rows = total // blocks
-    sub = split_rows(rows, 256)
+    sub = rows
     thin = split_rows(total, 128)
     step = split_rows(sub, 48)
     first = [
@@ -274,6 +278,7 @@
             )
         )
     ]
+    first, second = first[:5], first[5:]
     loads = [
         [
             pltpu.make_async_copy(
@@ -286,12 +291,14 @@
     last = pltpu.make_async_copy(payload_in, payload_s, last_sem)
     for copy in first:
         copy.start()
-    gain, bias = gain_ref[...], bias_ref[...]
+    gain, bias = one_row(gain_ref), one_row(bias_ref)
     gain_w = two_parts(gain, wp_ref[...])
     bias_w = two_parts(bias, wp_ref[...])
     qg_s[...] = jnp.zeros_like(qg_s)
     for copy in first:
         copy.wait()
+    for copy in second:
+        copy.start()
     for pair in loads:
         for copy in pair:
             copy.start()
@@ -313,6 +320,8 @@
     for r in range(count):
         qg_s[qidx_ref[r]] += un_s[r]
     total_eg = jnp.zeros((1, emb), F32)
+    for copy in second:
+        copy.wait()
     for b in range(0, total, thin):
         e = emb_s[b : b + thin]
         upstream = up_s[b : b + thin]
@@ -345,7 +354,7 @@
         else:
             wo_s[part * span : (part + 1) * span] += value
 
-    parts = rows // sub if width % (rows // sub * 128) == 0 else 1
+    parts = 1
     stores = []
     for b in range(blocks):
         for copy in loads[b]:
@@ -410,7 +419,7 @@
     total, width = normed.shape
     emb = wp.shape[1]
     blocks = x.shape[0]
-    sub = split_rows(total // blocks, 256)
+    sub = total // blocks
     chunks = width // CORES // chunk
     prob, log, units, qunit, qdir, qlen = scores
     manual = [maps, prob, log, units, qunit, embeds, x, normed, inverse, payload]
@@ -446,23 +455,23 @@
 
 def context_kernel(sg_ref, wo_ref, after_ref, out_ref, token_ref):
     token_ref[...] = jnp.zeros_like(token_ref)
-    out_ref[...] = dot(sg_ref[...], wo_ref[...], 1, 1).astype(BF16)
-
-
-def context_grad(sg, out_weight, after):
+    out_ref[...] = dot(sg_ref[...], wo_ref[...], 1, 0).astype(BF16)
+
+
+def context_grad(sg, weight_turned, after):
     total, width = sg.shape
     rows = split_rows(total, 720)
     block = pl.BlockSpec((rows, width), lambda s: (s, 0))
     return pl.pallas_call(
         context_kernel,
         grid=(total // rows,),
-        in_specs=[block, pl.BlockSpec(out_weight.shape, lambda s: (0, 0)), ANY],
+        in_specs=[block, pl.BlockSpec(weight_turned.shape, lambda s: (0, 0)), ANY],
         out_specs=[block, pl.BlockSpec(TOKEN.shape, lambda s: (0, 0))],
         out_shape=[jax.ShapeDtypeStruct(sg.shape, BF16), TOKEN],
         compiler_params=params(),
         cost_estimate=cost(2 * total * width * width, 4 * total * width),
         name="context_grad",
-    )(sg, out_weight, after)
+    )(sg, weight_turned, after)
 
 
 def split_sum_kernel(inputs, outputs, after, index_ref, *rest):
@@ -588,39 +597,38 @@
     def shift_t(x, k):
         return lax.ppermute(x, "tensor", [(t, (t + k) % nt) for t in range(nt)])
 
+    dest_group = passage_dest // (count * nt)
+    rows = jnp.arange(count, dtype=jnp.int32)
+    rank = jnp.sum(
+        (dest_group[:, None] == dest_group[None, :]) & (rows[None, :] < rows[:, None]), axis=1, dtype=jnp.int32
+    )
+    place = dest_group * per + rank
+    positions = jnp.sum(
+        jnp.where(place[:, None] == rows[None, :], (passage_dest % count)[:, None], 0), axis=0
+    )
+    queries = query_states.reshape(group_queries * tokens, width)
+    extra = jnp.pad(positions.astype(BF16)[None, :], ((0, 15), (0, width - count)))
+    payload = jnp.concatenate([queries, extra], axis=0)
     part = depth // dp
     mine = jnp.stack(
         [lax.dynamic_slice_in_dim(w, me * part, part, 0) for w in (teacher_query, teacher_key)]
     )
+    payload, mine = lax.optimization_barrier((jnp.broadcast_to(payload[None], (dp,) + payload.shape), mine))
+    payload = lax.all_to_all(payload, "dp", split_axis=0, concat_axis=0, tiled=True)
     along = jnp.concatenate([shift_t(mine, k) for k in range(1, nt)], axis=0)
+    along, payload = lax.optimization_barrier((along, payload))
     pieces = [along] + [shift_chip(along, k) for k in range(1, chips)]
     shifts = jnp.arange(chips, dtype=jnp.int32)
     behind = (chip - shifts) % chips
     piece_rows = jnp.concatenate([behind * CORES + core, behind * CORES + 1 - core]).astype(jnp.int32)
-
-    dest_group = passage_dest // (count * nt)
-    rows = jnp.arange(count, dtype=jnp.int32)
-    rank = jnp.sum(
-        (dest_group[:, None] == dest_group[None, :]) & (rows[None, :] < rows[:, None]), axis=1, dtype=jnp.int32
-    )
-    place = dest_group * per + rank
-    positions = jnp.sum(
-        jnp.where(place[:, None] == rows[None, :], (passage_dest % count)[:, None], 0), axis=0
-    )
-    queries = query_states.reshape(group_queries * tokens, width)
-    extra = jnp.pad(positions.astype(BF16)[None, :], ((0, 15), (0, width - count)))
-    payload = jnp.concatenate([queries, extra], axis=0)
-    payload = lax.all_to_all(
-        jnp.broadcast_to(payload[None], (dp,) + payload.shape), "dp", split_axis=0, concat_axis=0, tiled=True
-    )
     midx = place.astype(jnp.int32)
     qidx = (passage_dest // per_query).astype(jnp.int32)
 
-    gain2, bias2 = gain.reshape(1, width), bias.reshape(1, width)
+    gain2, bias2 = gain.reshape(-1, 128), bias.reshape(-1, 128)
     x = flat(context)
     normed, embeds, inverse, turned = student_forward(x, flat(stream), out_weight, gain2, bias2, proj_weight)
-    pieces[1:], payload, normed, embeds, inverse, turned = lax.optimization_barrier(
-        (pieces[1:], payload, normed, embeds, inverse, turned)
+    pieces[1:], payload, normed, embeds, inverse, turned, weight_turned, proj_turned = lax.optimization_barrier(
+        (pieces[1:], payload, normed, embeds, inverse, turned, out_weight.T, proj_weight.T)
     )
     pieces = pieces + [swap_core(a) for a in pieces]
     told = payload[:, group_queries * tokens, :count].astype(jnp.int32)
@@ -633,7 +641,7 @@
     chunk = width // (CORES * chips * nt)
     sg, send, keep = student_backward(
         qidx, midx, passage_len, core.astype(jnp.int32).reshape(1), maps, scores, payload,
-        embeds, turned, normed, inverse, gain2, bias2, proj_weight, proj_weight.T,
+        embeds, turned, normed, inverse, gain2, bias2, proj_weight, proj_turned,
         count, tokens, group_queries, chunk,
     )
 
@@ -641,7 +649,7 @@
     t_shifts = jnp.arange(nt, dtype=jnp.int32)
     t_ahead = ((mt + t_shifts) % nt).astype(jnp.int32)
     parts, token = split_sum([keep, swap_core(send)], ahead, "sum_cores")
-    grad_context, token = context_grad(sg, out_weight, token)
+    grad_context, token = context_grad(sg, weight_turned, token)
     parts = [parts[0]] + [shift_chip(parts[k], k) for k in range(1, chips)]
     parts, _ = split_sum(parts, t_ahead, "sum_plane", (token,))
     parts = [parts[0]] + [shift_t(parts[k], k) for k in range(1, nt)]

time: 138 us -> 143 us (1.036)
  waiting for transfers between devices: 23.9 us -> 26.9 us
  starting transfers between devices: 35.6 us -> 38 us
    ppermute x9, waiting for transfers between devices: 7.88 us -> 14.6 us  [shift_t(): return lax.ppermute(x, 'tensor', [(t, (t + k) % nt) for t in range(nt)])]
    ppermute x9, waiting for transfers between devices: 9.97 us -> 5.31 us  [shift_chip(): lax.ppermute(x, 'dp', [(c * CORES + o, (c + k) % chips * CORES + o) for c...]
    reshape x2 -> x0, local copies, waits for them, and re-layouts: 2.55 us -> none  [local(): gain2, bias2 = (gain.reshape(1, width), bias.reshape(1, width))]
    unnamed x33 -> x32, local copies, waits for them, and re-layouts: 4.65 us -> 7 us
    all_to_all x1, starting transfers between devices: 3.72 us -> 5.17 us  [local(): lax.all_to_all(payload, 'dp', split_axis=0, concat_axis=0, tiled=True)]
  transfers between devices with their start and end apart: 29 -> 29, of which waited for: 16 -> 17; matrix products, arithmetic and copies ran while one was open for 6% -> 3% of each run, Pallas kernels for 18% -> 17%
where the time goes in v3:
time: 143 us; the launch traced here: 142 us
  Pallas kernels  63.8 us (45%)
  starting transfers between devices  38 us (27%)
  waiting for transfers between devices  26.9 us (19%)
  local copies, waits for them, and re-layouts  9.41 us (7%)
  other arithmetic  2.85 us (2%)
    pallas_call x1, Pallas kernels, student_backward(): pl.pallas_call(functools.partial(backward_kernel, tokens, count, blocks,...  22.4 us
    ppermute x9, starting transfers between devices, shift_t(): return lax.ppermute(x, 'tensor', [(t, (t + k) % nt) for t in range(nt)])  15.2 us
    ppermute x9, waiting for transfers between devices, shift_t(): return lax.ppermute(x, 'tensor', [(t, (t + k) % nt) for t in range(nt)])  14.6 us
    pallas_call x1, Pallas kernels, student_forward(): pl.pallas_call(forward_kernel, grid=(total // rows,), in_specs=[block(wid...  12.5 us
    pallas_call x1, Pallas kernels, teacher_maps(): pl.pallas_call(functools.partial(teacher_kernel, parts, count, tokens), i...  12.4 us
    ppermute x9, starting transfers between devices, shift_chip(): lax.ppermute(x, 'dp', [(c * CORES + o, (c + k) % chips * CORES + o) for c...  12.3 us
    pallas_call x1, Pallas kernels, context_grad(): pl.pallas_call(context_kernel, grid=(total // rows,), in_specs=[block, pl...  7.44 us
    unnamed x32, local copies, waits for them, and re-layouts  7 us
  transfers between devices with their start and end apart: 29, of which 17 were waited for; matrix products, arithmetic and copies ran while one was open for 3% of the time, Pallas kernels for 17%

profile of v3, /device:TPU:0, one launch (start us, length us, event | category | flops | bytes accessed | tf_op | source)
XLA Modules:
  0.0 142.0 jit_solution(11780921013321132458)
XLA Ops:
  4.2 5.2 %all-to-all-start = ((bf16[8,48,768]{2,1,0:T(8,128)(2,1)}), bf16[8,48,768]{2,1,0:T(8,128)(2,1)S(1)}, u32[]{:S(2)}, u32[]{:S(2)}) async-start(bf16[8,48,768]{2,1,0:T(8,128)(2,1)} %broadcast_in_dim.16), calls=%async_computation | async-start | bytes 1179648 | tf_op jit(solution)/shard_map/all_to_all | solution.py:617
  11.0 2.6 %collective-permute-start.1 = (bf16[2,128,256]{2,1,0:T(8,128)(2,1)S(1)}, bf16[2,128,256]{2,1,0:T(8,128)(2,1)S(1)}, u32[]{:S(2)}, u32[]{:S(2)}) collective-permute-start(bf16[2,128,256]{2,1,0:T(8,128)(2,1)S(1)} %pad_maximum_fusion.2), channel_id=1, source_target_pairs={{0,2},{1,3},{2,0},{3,1},{4,6},{5,7},{6,4},{7,5},{8,10},{9,11},{10,... | collective-permute-start | bytes 393224 | tf_op jit(solution)/shard_map/ppermute | solution.py:598
  14.9 2.7 %collective-permute-done = bf16[2,128,256]{2,1,0:T(8,128)(2,1)S(1)} collective-permute-done((bf16[2,128,256]{2,1,0:T(8,128)(2,1)S(1)}, bf16[2,128,256]{2,1,0:T(8,128)(2,1)S(1)}, u32[]{:S(2)}, u32[]{:S(2)}) %collective-permute-start) | collective-permute-done | bytes 131104 | tf_op jit(solution)/shard_map/ppermute | solution.py:598
  17.6 5.3 %collective-permute-done.1 = bf16[2,128,256]{2,1,0:T(8,128)(2,1)S(1)} collective-permute-done((bf16[2,128,256]{2,1,0:T(8,128)(2,1)S(1)}, bf16[2,128,256]{2,1,0:T(8,128)(2,1)S(1)}, u32[]{:S(2)}, u32[]{:S(2)}) %collective-permute-start.1) | collective-permute-done | bytes 131104 | tf_op jit(solution)/shard_map/ppermute | solution.py:598
  22.9 1.7 %collective-permute-start.3 = (bf16[6,128,256]{2,1,0:T(8,128)(2,1)S(1)}, bf16[6,128,256]{2,1,0:T(8,128)(2,1)S(1)}, u32[]{:S(2)}, u32[]{:S(2)}) collective-permute-start(bf16[6,128,256]{2,1,0:T(8,128)(2,1)S(1)} %pad_maximum_fusion.rest_0_), channel_id=1, source_target_pairs={{0,8},{4,12},{8,16},{12,20},{16,24},{20,28},{24,0},{28,4},{1,9},{5... | collective-permute-start | bytes 1179656 | tf_op jit(solution)/shard_map/ppermute | solution.py:590
  27.6 2.4 %copy.22 = bf16[768,768]{0,1:T(8,128)(2,1)} copy(bf16[768,768]{1,0:T(8,128)(2,1)} %wo_ref.1) | data formatting | bytes 2359296 | tf_op args[2]
  30.8 12.5 %student_forward.1 = (bf16[2880,768]{1,0:T(8,128)(2,1)}, f32[2880,128]{1,0:T(8,128)}, f32[2880,128]{1,0:T(8,128)}, bf16[4,768,720]{2,1,0:T(8,128)(2,1)}) custom-call(bf16[2880,768]{1,0:T(8,128)(2,1)} %bitcast.41, bf16[2880,768]{1,0:T(8,128)(2,1)} %bitcast.42, bf16[768,768]{1,0:T(8,128)(2,1)} %wo_ref.1, f32[6,128]{1,0:T(8,128)} %bitcast.45, ...), custom_call_target="tpu_custom_call" | custom-call | flops 3963617280 | bytes 17694720 | tf_op jit(solution)/shard_map/student_forward/pallas_call | solution.py:74
  47.6 12.4 %teacher_maps.1 = (bf16[16,32,180]{2,1,0:T(8,128)(2,1)}, f32[8,128]{1,0:T(8,128)}) custom-call(s32[16]{0:T(128)} %reshape.108.order_ref, s32[8]{0:T(128)} %pad_add_fusion.rows_ref, bf16[3392,1024]{1,0:T(8,128)(2,1)} %bitcast.40, bf16[1024,256]{1,0:T(8,128)(2,1)} %wq_ref.1, bf16[1024,256]{1,0:T(8,128)(2,1)} %wk_ref.1, bf16[6,128,256]{2,1,0:T(8,128)(2,1)} %copy-done.4, ...), custom_call_target="tpu_custom_call" | custom-call | flops 4294967296 | bytes 11141120 | tf_op jit(solution)/shard_map/teacher_maps/pallas_call | solution.py:174
  60.1 3.6 %all-to-all-start.1 = ((bf16[16,32,180]{2,1,0:T(8,128)(2,1)}), bf16[16,32,180]{2,1,0:T(8,128)(2,1)S(1)}, u32[]{:S(2)}, u32[]{:S(2)}) async-start(bf16[16,32,180]{2,1,0:T(8,128)(2,1)} %get-tuple-element.63), calls=%async_computation.1 | async-start | bytes 524288 | tf_op jit(solution)/shard_map/all_to_all | solution.py:639
  63.7 4.2 %student_scores.1 = (f32[16,32,180]{2,1,0:T(8,128)}, f32[16,32,180]{2,1,0:T(8,128)}, bf16[16,180,128]{2,1,0:T(8,128)(2,1)}, bf16[8,32,128]{2,1,0:T(8,128)(2,1)}, f32[256,128]{1,0:T(8,128)}, /*index=5*/f32[256,128]{1,0:T(8,128)}) custom-call(s32[16]{0:T(128)} %copy-done.13, s32[16]{0:T(128)} %len_ref.3, bf16[8,48,768]{2,1,0:T(8,128)(2,1)} %copy-done.3, ...), custom_call_target="tpu_custom_call" | custom-call | flops 1000000000 | bytes 1474560 | tf_op jit(solution)/shard_map/student_scores/pallas_call | solution.py:230
  67.9 2.5 %all-to-all-done.1.maps_in = bf16[16,32,180]{2,1,0:T(8,128)(2,1)S(1)} async-done(((bf16[16,32,180]{2,1,0:T(8,128)(2,1)}), bf16[16,32,180]{2,1,0:T(8,128)(2,1)S(1)}, u32[]{:S(2)}, u32[]{:S(2)}) %all-to-all-start.1) | async-done | bytes 184352 | tf_op jit(solution)/shard_map/all_to_all | solution.py:639
  71.1 22.4 %student_backward.1 = (bf16[2880,768]{1,0:T(8,128)(2,1)}, bf16[16,24,1024]{2,1,0:T(8,128)(2,1)}, bf16[16,24,1024]{2,1,0:T(8,128)(2,1)}) custom-call(s32[16]{0:T(128)} %copy-done.13, s32[16]{0:T(128)} %copy-done.14, s32[16]{0:T(128)} %len_ref.3, s32[1]{0:T(128)} %bitcast.core_ref, bf16[16,32,180]{2,1,0:T(8,128)(2,1)} %copy-done.5, ...), custom_call_target="tpu_custom_call" | custom-call | flops 4529848320 | bytes 17694720 | tf_op jit(solution)/shard_map/student_backward/pallas_call | solution.py:427
  93.5 2.4 %collective-permute-done.10.rest_1_ = bf16[16,24,1024]{2,1,0:T(8,128)(2,1)S(1)} collective-permute-done((bf16[16,24,1024]{2,1,0:T(8,128)(2,1)}, bf16[16,24,1024]{2,1,0:T(8,128)(2,1)S(1)}, u32[]{:S(2)}, u32[]{:S(2)}) %collective-permute-start.10) | collective-permute-done | bytes 786464 | tf_op jit(solution)/shard_map/ppermute | solution.py:595
  100.1 2.3 %collective-permute-start.13 = (bf16[4,24,1024]{2,1,0:T(8,128)(2,1)S(1)}, bf16[4,24,1024]{2,1,0:T(8,128)(2,1)S(1)}, u32[]{:S(2)}, u32[]{:S(2)}) collective-permute-start(bf16[4,24,1024]{2,1,0:T(8,128)(2,1)S(1)} %get-tuple-element.81), channel_id=1, source_target_pairs={{0,24},{4,28},{8,0},{12,4},{16,8},{20,12},{24,16},{28,20},{1,25},{... | collective-permute-start | bytes 589832 | tf_op jit(solution)/shard_map/ppermute | solution.py:590
  102.4 7.4 %context_grad.1 = (bf16[2880,768]{1,0:T(8,128)(2,1)}, f32[8,128]{1,0:T(8,128)}) custom-call(bf16[2880,768]{1,0:T(8,128)(2,1)} %get-tuple-element.82.sg_ref, bf16[768,768]{1,0:T(8,128)(2,1)} %bitcast.34, f32[8,128]{1,0:T(8,128)} %copy-done.2), custom_call_target="tpu_custom_call" | custom-call | flops 3397386240 | bytes 8847360 | tf_op jit(solution)/shard_map/context_grad/pallas_call | solution.py:465
  112.4 3.3 %collective-permute-start.14 = (bf16[24,1024]{1,0:T(8,128)(2,1)S(1)}, bf16[24,1024]{1,0:T(8,128)(2,1)S(1)}, u32[]{:S(2)}, u32[]{:S(2)}) collective-permute-start(bf16[24,1024]{1,0:T(8,128)(2,1)S(1)} %get-tuple-element.87), channel_id=1, source_target_pairs={{0,1},{1,2},{2,3},{3,0},{4,5},{5,6},{6,7},{7,4},{8,9},{9,10},{10,1... | collective-permute-start | bytes 147464 | tf_op jit(solution)/shard_map/ppermute | solution.py:598
  115.6 1.6 %collective-permute-start.15 = (bf16[24,1024]{1,0:T(8,128)(2,1)S(1)}, bf16[24,1024]{1,0:T(8,128)(2,1)S(1)}, u32[]{:S(2)}, u32[]{:S(2)}) collective-permute-start(bf16[24,1024]{1,0:T(8,128)(2,1)S(1)} %get-tuple-element.88), channel_id=1, source_target_pairs={{0,2},{1,3},{2,0},{3,1},{4,6},{5,7},{6,4},{7,5},{8,10},{9,11},{10,... | collective-permute-start | bytes 147464 | tf_op jit(solution)/shard_map/ppermute | solution.py:598
  119.2 1.9 %collective-permute-done.15.refs_2_ = bf16[24,1024]{1,0:T(8,128)(2,1)S(1)} collective-permute-done((bf16[24,1024]{1,0:T(8,128)(2,1)S(1)}, bf16[24,1024]{1,0:T(8,128)(2,1)S(1)}, u32[]{:S(2)}, u32[]{:S(2)}) %collective-permute-start.15) | collective-permute-done | bytes 49184 | tf_op jit(solution)/shard_map/ppermute | solution.py:598
  122.3 2.3 %collective-permute-start.18 = (bf16[24,1024]{1,0:T(8,128)(2,1)S(1)}, bf16[24,1024]{1,0:T(8,128)(2,1)S(1)}, u32[]{:S(2)}, u32[]{:S(2)}) collective-permute-start(bf16[24,1024]{1,0:T(8,128)(2,1)S(1)} %sum_tensor.1), channel_id=1, source_target_pairs={{0,2},{1,3},{2,0},{3,1},{4,6},{5,7},{6,4},{7,5},{8,10},{9,11},{10,... | collective-permute-start | bytes 147464 | tf_op jit(solution)/shard_map/ppermute | solution.py:598
  125.7 2.0 %collective-permute-done.17 = bf16[24,1024]{1,0:T(8,128)(2,1)S(1)} collective-permute-done((bf16[24,1024]{1,0:T(8,128)(2,1)S(1)}, bf16[24,1024]{1,0:T(8,128)(2,1)S(1)}, u32[]{:S(2)}, u32[]{:S(2)}) %collective-permute-start.17) | collective-permute-done | bytes 49184 | tf_op jit(solution)/shard_map/ppermute | solution.py:598
  128.7 2.0 %collective-permute-start.20 = (bf16[4,24,1024]{2,1,0:T(8,128)(2,1)S(1)}, bf16[4,24,1024]{2,1,0:T(8,128)(2,1)S(1)}, u32[]{:S(2)}, u32[]{:S(2)}) collective-permute-start(bf16[4,24,1024]{2,1,0:T(8,128)(2,1)S(1)} %pad_maximum_fusion.1.rest_0_), channel_id=1, source_target_pairs={{0,8},{4,12},{8,16},{12,20},{16,24},{20,28},{24,0},{28,4},{1,9},{5... | collective-permute-start | bytes 589832 | tf_op jit(solution)/shard_map/ppermute | solution.py:590
  133.1 2.7 %collective-permute-done.20.rest_1_ = bf16[4,24,1024]{2,1,0:T(8,128)(2,1)S(1)} collective-permute-done((bf16[4,24,1024]{2,1,0:T(8,128)(2,1)S(1)}, bf16[4,24,1024]{2,1,0:T(8,128)(2,1)S(1)}, u32[]{:S(2)}, u32[]{:S(2)}) %collective-permute-start.20) | collective-permute-done | bytes 196640 | tf_op jit(solution)/shard_map/ppermute | solution.py:590
  135.8 2.0 %collective-permute-done.21.rest_2_ = bf16[4,24,1024]{2,1,0:T(8,128)(2,1)S(1)} collective-permute-done((bf16[4,24,1024]{2,1,0:T(8,128)(2,1)S(1)}, bf16[4,24,1024]{2,1,0:T(8,128)(2,1)S(1)}, u32[]{:S(2)}, u32[]{:S(2)}) %collective-permute-start.21) | collective-permute-done | bytes 196640 | tf_op jit(solution)/shard_map/ppermute | solution.py:590
  139.5 2.3 %unpack.1 = (f32[32,24,768]{2,1,0:T(8,128)}, f32[32,24,128]{2,1,0:T(8,128)}, f32[6,128]{1,0:T(8,128)}, f32[6,128]{1,0:T(8,128)}, f32[1]{0:T(128)}) custom-call(s32[32]{0:T(128)S(1)} %add.110.index_ref, bf16[4,24,1024]{2,1,0:T(8,128)(2,1)S(1)} %pad_maximum_fusion.1.rest_0_, bf16[4,24,1024]{2,1,0:T(8,128)(2,1)S(1)} %collective-permute-done.20.rest_1_, ...), custom_call_target="tpu_custom_call" | custom-call | tf_op jit(solution)/shard_map/unpack/pallas_call | solution.py:546
  (98 shorter events, 31.1 us)
Async XLA Ops:
  4.2 18.7 %all-to-all-start = ((bf16[8,48,768]{2,1,0:T(8,128)(2,1)}), bf16[8,48,768]{2,1,0:T(8,128)(2,1)S(1)}, u32[]{:S(2)}, u32[]{:S(2)}) async-start(bf16[8,48,768]{2,1,0:T(8,128)(2,1)} %broadcast_in_dim.16), calls=%async_computation | async-start | bytes 1179648 | tf_op jit(solution)/shard_map/all_to_all | solution.py:617
  9.4 8.2 %collective-permute-start = (bf16[2,128,256]{2,1,0:T(8,128)(2,1)S(1)}, bf16[2,128,256]{2,1,0:T(8,128)(2,1)S(1)}, u32[]{:S(2)}, u32[]{:S(2)}) collective-permute-start(bf16[2,128,256]{2,1,0:T(8,128)(2,1)S(1)} %pad_maximum_fusion.2), channel_id=1, source_target_pairs={{0,1},{1,2},{2,3},{3,0},{4,5},{5,6},{6,7},{7,4},{8,9},{9,10},{10,1... | collective-permute-start | bytes 393224 | tf_op jit(solution)/shard_map/ppermute | solution.py:598
  11.0 11.9 %collective-permute-start.1 = (bf16[2,128,256]{2,1,0:T(8,128)(2,1)S(1)}, bf16[2,128,256]{2,1,0:T(8,128)(2,1)S(1)}, u32[]{:S(2)}, u32[]{:S(2)}) collective-permute-start(bf16[2,128,256]{2,1,0:T(8,128)(2,1)S(1)} %pad_maximum_fusion.2), channel_id=1, source_target_pairs={{0,2},{1,3},{2,0},{3,1},{4,6},{5,7},{6,4},{7,5},{8,10},{9,11},{10,... | collective-permute-start | bytes 393224 | tf_op jit(solution)/shard_map/ppermute | solution.py:598
  13.6 9.3 %collective-permute-start.2 = (bf16[2,128,256]{2,1,0:T(8,128)(2,1)S(1)}, bf16[2,128,256]{2,1,0:T(8,128)(2,1)S(1)}, u32[]{:S(2)}, u32[]{:S(2)}) collective-permute-start(bf16[2,128,256]{2,1,0:T(8,128)(2,1)S(1)} %pad_maximum_fusion.2), channel_id=1, source_target_pairs={{0,3},{1,0},{2,1},{3,2},{4,7},{5,4},{6,5},{7,6},{8,11},{9,8},{10,9... | collective-permute-start | bytes 393224 | tf_op jit(solution)/shard_map/ppermute | solution.py:598
  22.9 20.5 %collective-permute-start.3 = (bf16[6,128,256]{2,1,0:T(8,128)(2,1)S(1)}, bf16[6,128,256]{2,1,0:T(8,128)(2,1)S(1)}, u32[]{:S(2)}, u32[]{:S(2)}) collective-permute-start(bf16[6,128,256]{2,1,0:T(8,128)(2,1)S(1)} %pad_maximum_fusion.rest_0_), channel_id=1, source_target_pairs={{0,8},{4,12},{8,16},{12,20},{16,24},{20,28},{24,0},{28,4},{1,9},{5... | collective-permute-start | bytes 1179656 | tf_op jit(solution)/shard_map/ppermute | solution.py:590
  24.7 18.8 %collective-permute-start.4 = (bf16[6,128,256]{2,1,0:T(8,128)(2,1)S(1)}, bf16[6,128,256]{2,1,0:T(8,128)(2,1)S(1)}, u32[]{:S(2)}, u32[]{:S(2)}) collective-permute-start(bf16[6,128,256]{2,1,0:T(8,128)(2,1)S(1)} %pad_maximum_fusion.rest_0_), channel_id=1, source_target_pairs={{0,16},{4,20},{8,24},{12,28},{16,0},{20,4},{24,8},{28,12},{1,17},{... | collective-permute-start | bytes 1179656 | tf_op jit(solution)/shard_map/ppermute | solution.py:590
  26.1 17.4 %collective-permute-start.5 = (bf16[6,128,256]{2,1,0:T(8,128)(2,1)S(1)}, bf16[6,128,256]{2,1,0:T(8,128)(2,1)S(1)}, u32[]{:S(2)}, u32[]{:S(2)}) collective-permute-start(bf16[6,128,256]{2,1,0:T(8,128)(2,1)S(1)} %pad_maximum_fusion.rest_0_), channel_id=1, source_target_pairs={{0,24},{4,28},{8,0},{12,4},{16,8},{20,12},{24,16},{28,20},{1,25},{... | collective-permute-start | bytes 1179656 | tf_op jit(solution)/shard_map/ppermute | solution.py:590
  44.1 2.8 %collective-permute-start.8 = (bf16[6,128,256]{2,1,0:T(8,128)(2,1)S(1)}, bf16[6,128,256]{2,1,0:T(8,128)(2,1)S(1)}, u32[]{:S(2)}, u32[]{:S(2)}) collective-permute-start(bf16[6,128,256]{2,1,0:T(8,128)(2,1)S(1)} %collective-permute-done.4.rest_2_), channel_id=1, source_target_pairs={{0,4},{4,0},{8,12},{12,8},{16,20},{20,16},{24,28},{28,24},{1,5},{5... | collective-permute-start | bytes 1179656 | tf_op jit(solution)/shard_map/ppermute | solution.py:595
  44.1 2.8 %collective-permute-start.9 = (bf16[6,128,256]{2,1,0:T(8,128)(2,1)S(1)}, bf16[6,128,256]{2,1,0:T(8,128)(2,1)}, u32[]{:S(2)}, u32[]{:S(2)}) collective-permute-start(bf16[6,128,256]{2,1,0:T(8,128)(2,1)S(1)} %collective-permute-done.5.rest_3_), channel_id=1, source_target_pairs={{0,4},{4,0},{8,12},{12,8},{16,20},{20,16},{24,28},{28,24},{1,5},{5... | collective-permute-start | bytes 1179656 | tf_op jit(solution)/shard_map/ppermute | solution.py:595
  60.1 10.3 %all-to-all-start.1 = ((bf16[16,32,180]{2,1,0:T(8,128)(2,1)}), bf16[16,32,180]{2,1,0:T(8,128)(2,1)S(1)}, u32[]{:S(2)}, u32[]{:S(2)}) async-start(bf16[16,32,180]{2,1,0:T(8,128)(2,1)} %get-tuple-element.63), calls=%async_computation.1 | async-start | bytes 524288 | tf_op jit(solution)/shard_map/all_to_all | solution.py:639
  98.9 10.9 %collective-permute-start.11 = (bf16[4,24,1024]{2,1,0:T(8,128)(2,1)S(1)}, bf16[4,24,1024]{2,1,0:T(8,128)(2,1)S(1)}, u32[]{:S(2)}, u32[]{:S(2)}) collective-permute-start(bf16[4,24,1024]{2,1,0:T(8,128)(2,1)S(1)} %get-tuple-element.79), channel_id=1, source_target_pairs={{0,8},{4,12},{8,16},{12,20},{16,24},{20,28},{24,0},{28,4},{1,9},{5... | collective-permute-start | bytes 589832 | tf_op jit(solution)/shard_map/ppermute | solution.py:590
  99.5 10.9 %collective-permute-start.12 = (bf16[4,24,1024]{2,1,0:T(8,128)(2,1)S(1)}, bf16[4,24,1024]{2,1,0:T(8,128)(2,1)S(1)}, u32[]{:S(2)}, u32[]{:S(2)}) collective-permute-start(bf16[4,24,1024]{2,1,0:T(8,128)(2,1)S(1)} %get-tuple-element.80), channel_id=1, source_target_pairs={{0,16},{4,20},{8,24},{12,28},{16,0},{20,4},{24,8},{28,12},{1,17},{... | collective-permute-start | bytes 589832 | tf_op jit(solution)/shard_map/ppermute | solution.py:590
  100.1 10.3 %collective-permute-start.13 = (bf16[4,24,1024]{2,1,0:T(8,128)(2,1)S(1)}, bf16[4,24,1024]{2,1,0:T(8,128)(2,1)S(1)}, u32[]{:S(2)}, u32[]{:S(2)}) collective-permute-start(bf16[4,24,1024]{2,1,0:T(8,128)(2,1)S(1)} %get-tuple-element.81), channel_id=1, source_target_pairs={{0,24},{4,28},{8,0},{12,4},{16,8},{20,12},{24,16},{28,20},{1,25},{... | collective-permute-start | bytes 589832 | tf_op jit(solution)/shard_map/ppermute | solution.py:590
  112.4 6.8 %collective-permute-start.14 = (bf16[24,1024]{1,0:T(8,128)(2,1)S(1)}, bf16[24,1024]{1,0:T(8,128)(2,1)S(1)}, u32[]{:S(2)}, u32[]{:S(2)}) collective-permute-start(bf16[24,1024]{1,0:T(8,128)(2,1)S(1)} %get-tuple-element.87), channel_id=1, source_target_pairs={{0,1},{1,2},{2,3},{3,0},{4,5},{5,6},{6,7},{7,4},{8,9},{9,10},{10,1... | collective-permute-start | bytes 147464 | tf_op jit(solution)/shard_map/ppermute | solution.py:598
  115.6 5.5 %collective-permute-start.15 = (bf16[24,1024]{1,0:T(8,128)(2,1)S(1)}, bf16[24,1024]{1,0:T(8,128)(2,1)S(1)}, u32[]{:S(2)}, u32[]{:S(2)}) collective-permute-start(bf16[24,1024]{1,0:T(8,128)(2,1)S(1)} %get-tuple-element.88), channel_id=1, source_target_pairs={{0,2},{1,3},{2,0},{3,1},{4,6},{5,7},{6,4},{7,5},{8,10},{9,11},{10,... | collective-permute-start | bytes 147464 | tf_op jit(solution)/shard_map/ppermute | solution.py:598
  117.3 4.3 %collective-permute-start.16 = (bf16[24,1024]{1,0:T(8,128)(2,1)S(1)}, bf16[24,1024]{1,0:T(8,128)(2,1)S(1)}, u32[]{:S(2)}, u32[]{:S(2)}) collective-permute-start(bf16[24,1024]{1,0:T(8,128)(2,1)S(1)} %get-tuple-element.89), channel_id=1, source_target_pairs={{0,3},{1,0},{2,1},{3,2},{4,7},{5,4},{6,5},{7,6},{8,11},{9,8},{10,9... | collective-permute-start | bytes 147464 | tf_op jit(solution)/shard_map/ppermute | solution.py:598
  121.6 6.0 %collective-permute-start.17 = (bf16[24,1024]{1,0:T(8,128)(2,1)S(1)}, bf16[24,1024]{1,0:T(8,128)(2,1)S(1)}, u32[]{:S(2)}, u32[]{:S(2)}) collective-permute-start(bf16[24,1024]{1,0:T(8,128)(2,1)S(1)} %sum_tensor.1), channel_id=1, source_target_pairs={{0,1},{1,2},{2,3},{3,0},{4,5},{5,6},{6,7},{7,4},{8,9},{9,10},{10,1... | collective-permute-start | bytes 147464 | tf_op jit(solution)/shard_map/ppermute | solution.py:598
  122.3 6.1 %collective-permute-start.18 = (bf16[24,1024]{1,0:T(8,128)(2,1)S(1)}, bf16[24,1024]{1,0:T(8,128)(2,1)S(1)}, u32[]{:S(2)}, u32[]{:S(2)}) collective-permute-start(bf16[24,1024]{1,0:T(8,128)(2,1)S(1)} %sum_tensor.1), channel_id=1, source_target_pairs={{0,2},{1,3},{2,0},{3,1},{4,6},{5,7},{6,4},{7,5},{8,10},{9,11},{10,... | collective-permute-start | bytes 147464 | tf_op jit(solution)/shard_map/ppermute | solution.py:598
  124.5 4.2 %collective-permute-start.19 = (bf16[24,1024]{1,0:T(8,128)(2,1)S(1)}, bf16[24,1024]{1,0:T(8,128)(2,1)S(1)}, u32[]{:S(2)}, u32[]{:S(2)}) collective-permute-start(bf16[24,1024]{1,0:T(8,128)(2,1)S(1)} %sum_tensor.1), channel_id=1, source_target_pairs={{0,3},{1,0},{2,1},{3,2},{4,7},{5,4},{6,5},{7,6},{8,11},{9,8},{10,9... | collective-permute-start | bytes 147464 | tf_op jit(solution)/shard_map/ppermute | solution.py:598
  128.7 7.1 %collective-permute-start.20 = (bf16[4,24,1024]{2,1,0:T(8,128)(2,1)S(1)}, bf16[4,24,1024]{2,1,0:T(8,128)(2,1)S(1)}, u32[]{:S(2)}, u32[]{:S(2)}) collective-permute-start(bf16[4,24,1024]{2,1,0:T(8,128)(2,1)S(1)} %pad_maximum_fusion.1.rest_0_), channel_id=1, source_target_pairs={{0,8},{4,12},{8,16},{12,20},{16,24},{20,28},{24,0},{28,4},{1,9},{5... | collective-permute-start | bytes 589832 | tf_op jit(solution)/shard_map/ppermute | solution.py:590
  130.7 7.1 %collective-permute-start.21 = (bf16[4,24,1024]{2,1,0:T(8,128)(2,1)S(1)}, bf16[4,24,1024]{2,1,0:T(8,128)(2,1)S(1)}, u32[]{:S(2)}, u32[]{:S(2)}) collective-permute-start(bf16[4,24,1024]{2,1,0:T(8,128)(2,1)S(1)} %pad_maximum_fusion.1.rest_0_), channel_id=1, source_target_pairs={{0,16},{4,20},{8,24},{12,28},{16,0},{20,4},{24,8},{28,12},{1,17},{... | collective-permute-start | bytes 589832 | tf_op jit(solution)/shard_map/ppermute | solution.py:590
  132.1 5.7 %collective-permute-start.22 = (bf16[4,24,1024]{2,1,0:T(8,128)(2,1)S(1)}, bf16[4,24,1024]{2,1,0:T(8,128)(2,1)S(1)}, u32[]{:S(2)}, u32[]{:S(2)}) collective-permute-start(bf16[4,24,1024]{2,1,0:T(8,128)(2,1)S(1)} %pad_maximum_fusion.1.rest_0_), channel_id=1, source_target_pairs={{0,24},{4,28},{8,0},{12,4},{16,8},{20,12},{24,16},{28,20},{1,25},{... | collective-permute-start | bytes 589832 | tf_op jit(solution)/shard_map/ppermute | solution.py:590
  133.0 5.4 %collective-permute-start.23 = (bf16[4,24,1024]{2,1,0:T(8,128)(2,1)S(1)}, bf16[4,24,1024]{2,1,0:T(8,128)(2,1)S(1)}, u32[]{:S(2)}, u32[]{:S(2)}) collective-permute-start(bf16[4,24,1024]{2,1,0:T(8,128)(2,1)S(1)} %pad_maximum_fusion.1.rest_0_), channel_id=1, source_target_pairs={{0,4},{4,0},{8,12},{12,8},{16,20},{20,16},{24,28},{28,24},{1,5},{5... | collective-permute-start | bytes 589832 | tf_op jit(solution)/shard_map/ppermute | solution.py:595
  135.8 2.7 %collective-permute-start.24 = (bf16[4,24,1024]{2,1,0:T(8,128)(2,1)S(1)}, bf16[4,24,1024]{2,1,0:T(8,128)(2,1)S(1)}, u32[]{:S(2)}, u32[]{:S(2)}) collective-permute-start(bf16[4,24,1024]{2,1,0:T(8,128)(2,1)S(1)} %collective-permute-done.20.rest_1_), channel_id=1, source_target_pairs={{0,4},{4,0},{8,12},{12,8},{16,20},{20,16},{24,28},{28,24},{1,5},{5... | collective-permute-start | bytes 589832 | tf_op jit(solution)/shard_map/ppermute | solution.py:595
  (20 other events, 183.2 us)

commit v4 on v3

--- a/solution.py
+++ b/solution.py
@@ -35,6 +35,10 @@
     return max(n for n in range(16, most + 1, 16) if rows % n == 0)
 
 
+def loop(count, body):
+    lax.fori_loop(0, count, lambda n, _: (body(n), 0)[1], 0)
+
+
 def one_row(ref):
     return jnp.concatenate([ref[v : v + 1] for v in range(ref.shape[0])], axis=1)
 
@@ -49,19 +53,30 @@
 
 def forward_kernel(x_ref, str_ref, wo_ref, gain_ref, bias_ref, wp_ref, normed_ref, emb_ref, inv_ref, turned_ref, prod_s, hid_s):
     rows, width = x_ref.shape
-    sub = rows
+    sub = split_rows(rows, 256)
+    thin = split_rows(sub, 48)
     gain, bias = one_row(gain_ref), one_row(bias_ref)
-    for b in range(0, rows, sub):
-        prod_s[b : b + sub] = dot(x_ref[b : b + sub], wo_ref[...], 1, 0)
-        for c in range(b, b + sub, 16):
-            summed = prod_s[c : c + 16] + str_ref[c : c + 16].astype(F32)
+
+    def block(n):
+        first = pl.multiple_of(n * sub, sub)
+        part = pl.ds(first, sub)
+        prod_s[...] = dot(x_ref[part], wo_ref[...], 1, 0)
+
+        def chunk(c):
+            inner = pl.ds(pl.multiple_of(c * thin, thin), thin)
+            outer = pl.ds(pl.multiple_of(first + c * thin, thin), thin)
+            summed = prod_s[inner] + str_ref[outer].astype(F32)
             centred = summed - jnp.mean(summed, axis=-1, keepdims=True)
             inverse = lax.rsqrt(jnp.mean(centred * centred, axis=-1, keepdims=True) + epsilon)
             normed = centred * inverse
-            normed_ref[c : c + 16] = normed.astype(BF16)
-            inv_ref[c : c + 16] = jnp.broadcast_to(inverse, (16, inv_ref.shape[1]))
-            hid_s[c : c + 16] = (normed * gain + bias).astype(BF16)
-        emb_ref[b : b + sub] = dot(hid_s[b : b + sub], wp_ref[...], 1, 0)
+            normed_ref[outer] = normed.astype(BF16)
+            inv_ref[outer] = jnp.broadcast_to(inverse, (thin, inv_ref.shape[1]))
+            hid_s[inner] = (normed * gain + bias).astype(BF16)
+
+        loop(sub // thin, chunk)
+        emb_ref[part] = dot(hid_s[...], wp_ref[...], 1, 0)
+
+    loop(rows // sub, block)
     turned_ref[0] = x_ref[...].T
 
 
@@ -69,6 +84,7 @@
     total, width = x.shape
     emb = proj_weight.shape[1]
     rows = split_rows(total, 720)
+    sub = split_rows(rows, 256)
     block = lambda last: pl.BlockSpec((rows, last), lambda s: (s, 0))
     whole = lambda a: pl.BlockSpec(a.shape, lambda s: (0,) * a.ndim)
     return pl.pallas_call(
@@ -82,7 +98,7 @@
             jax.ShapeDtypeStruct((total, 128), F32),
             jax.ShapeDtypeStruct((total // rows, width, rows), BF16),
         ],
-        scratch_shapes=[pltpu.VMEM((rows, width), F32), pltpu.VMEM((rows, width), BF16)],
+        scratch_shapes=[pltpu.VMEM((sub, width), F32), pltpu.VMEM((sub, width), BF16)],
         compiler_params=params(),
         cost_estimate=cost(2 * total * width * (width + emb), 8 * total * width),
         name="student_forward",
@@ -91,9 +107,10 @@
 
 def teacher_kernel(parts, count, tokens, order_ref, rows_ref, states_ref, wq_ref, wk_ref, *rest):
     pieces, out_ref, token_ref = rest[:parts], rest[parts], rest[parts + 1]
-    w_s, own_s, q_s, g_s, key_s, e_s, map_s, q_sem, key_sem, w_sem, own_sem = rest[parts + 2 :]
+    w_s, q_s, g_s, m_s, key_s, e_s, map_s, turned_s, q_sem, key_sem, w_sem, own_sem = rest[parts + 2 :]
     depth = q_s.shape[1]
     slices = w_s.shape[0] // 2
+    others = pieces[0].shape[0]
     part_rows = pieces[0].shape[1]
     total = key_s.shape[0]
     seq = total // count
@@ -101,14 +118,14 @@
     rows = total // blocks
     first = count * tokens
     own = [
-        pltpu.make_async_copy(wq_ref, own_s.at[0], own_sem.at[0]),
-        pltpu.make_async_copy(wk_ref, own_s.at[1], own_sem.at[1]),
+        pltpu.make_async_copy(wq_ref, w_s.at[others], own_sem.at[0]),
+        pltpu.make_async_copy(wk_ref, w_s.at[others + 1], own_sem.at[1]),
     ]
     queries = pltpu.make_async_copy(states_ref.at[pl.ds(0, first)], q_s, q_sem)
     gathered = [
         pltpu.make_async_copy(
             pieces[a],
-            w_s.at[:, pl.ds(pl.multiple_of(rows_ref[a] * part_rows, part_rows), part_rows), :],
+            w_s.at[pl.ds(0, others), pl.ds(pl.multiple_of(rows_ref[a] * part_rows, part_rows), part_rows), :],
             w_sem.at[a],
         )
         for a in range(parts)
@@ -123,44 +140,61 @@
     for copy in own + gathered:
         copy.start()
     queries.wait()
-    for copy in own:
+    for copy in own + gathered:
         copy.wait()
     for copy in keys:
         copy.start()
     q = q_s[...]
-    mixed = dot(dot(q, own_s[0], 1, 0).astype(BF16), own_s[1], 1, 1)
-    for copy in gathered:
-        copy.wait()
-    for k in range(slices):
-        mixed = mixed + dot(dot(q, w_s[2 * k], 1, 0).astype(BF16), w_s[2 * k + 1], 1, 1)
+    m_s[...] = jnp.zeros_like(m_s)
+
+    def mix(k):
+        m_s[...] += dot(dot(q, w_s[2 * k], 1, 0).astype(BF16), w_s[2 * k + 1], 1, 1)
+
+    loop(slices, mix)
     for v in range(depth // 128):
-        g_s[v] = mixed[:, v * 128 : (v + 1) * 128]
-        for p in range(count):
-            q_s[p * tokens : (p + 1) * tokens, v * 128 : (v + 1) * 128] = g_s[
+        g_s[v] = m_s[:, v * 128 : (v + 1) * 128]
+
+    def reorder(p):
+        for v in range(depth // 128):
+            q_s[pl.ds(pl.multiple_of(p * tokens, tokens), tokens), v * 128 : (v + 1) * 128] = g_s[
                 v, pl.ds(p, tokens, stride=count), :
             ].astype(BF16)
-    mixed = q_s[...].T
+
+    loop(count, reorder)
+    turned_s[...] = q_s[...].T
     scale = 1.0 / (math.sqrt(depth) * softcap)
     side = 128 // tokens
-    pair = lax.broadcasted_iota(jnp.int32, (rows, 128), 0) % count
-    for b in range(blocks):
-        keys[b].wait()
-        raw = dot(key_s[b * rows : (b + 1) * rows], mixed, 1, 0)
+    sub = split_rows(rows, 256)
+    pair = lax.broadcasted_iota(jnp.int32, (sub, 128), 0) % count
+    for copy in keys:
+        copy.wait()
+
+    def score(n):
+        part = pl.ds(pl.multiple_of(n * sub, sub), sub)
+        raw = dot(key_s[part], turned_s[...], 1, 0)
         mine = raw[:, :128]
         for v in range(1, count // side):
             mine = jnp.where(pair >= v * side, raw[:, v * 128 : (v + 1) * 128], mine)
-        e_s[b * rows : (b + 1) * rows] = jnp.exp(softcap * jnp.tanh(mine * scale))
+        e_s[part] = jnp.exp(softcap * jnp.tanh(mine * scale))
+
+    loop(total // sub, score)
     lane = lax.broadcasted_iota(jnp.int32, (seq, 128), 1) // tokens
     filler = jnp.zeros((up(seq, 128) - seq, 128), F32)
-    for g in range(count // side):
+
+    def split(g):
         both = e_s[pl.ds(g * side, seq, stride=count), :]
         for v in range(1, side):
             both = jnp.where(lane == v, e_s[pl.ds(g * side + v, seq, stride=count), :], both)
         turned = jnp.concatenate([both, filler], axis=0).T
         for v in range(side):
             map_s[g * side + v] = turned[v * tokens : (v + 1) * tokens, :seq].astype(BF16)
-    for n in range(count):
+
+    loop(count // side, split)
+
+    def place(n):
         out_ref[n] = map_s[order_ref[n]]
+
+    loop(count, place)
     token_ref[...] = jnp.zeros_like(token_ref)
 
 
@@ -177,13 +211,14 @@
         out_specs=[VMEM, VMEM],
         out_shape=[jax.ShapeDtypeStruct((count, tokens, keys // count), BF16), TOKEN],
         scratch_shapes=[
-            pltpu.VMEM((slices, depth, heads), BF16),
-            pltpu.VMEM((2, depth, heads), BF16),
+            pltpu.VMEM((slices + 2, depth, heads), BF16),
             pltpu.VMEM((count * tokens, depth), BF16),
             pltpu.VMEM((depth // 128, count * tokens, 128), F32),
+            pltpu.VMEM((count * tokens, depth), F32),
             pltpu.VMEM((keys, depth), BF16),
             pltpu.VMEM((keys, 128), F32),
             pltpu.VMEM((count, tokens, keys // count), BF16),
+            pltpu.VMEM((depth, count * tokens), BF16),
             pltpu.SemaphoreType.DMA,
             pltpu.SemaphoreType.DMA((blocks,)),
             pltpu.SemaphoreType.DMA((parts,)),
@@ -196,31 +231,38 @@
 
 
 def scores_kernel(tokens, count, group_queries, qidx_ref, len_ref, payload_ref, emb_ref, wp_ref, after_ref,
-                  prob_ref, log_ref, units_ref, qunit_ref, qdir_ref, qlen_ref, qs_s, dir_s):
+                  prob_ref, log_ref, units_ref, qunit_ref, qdir_ref, qlen_ref, dir_s):
     total, emb = emb_ref.shape
     seq = total // count
     sub = split_rows(total, 128)
-    each = group_queries * tokens
-    for k in range(payload_ref.shape[0]):
-        qs_s[k * each : (k + 1) * each] = payload_ref[k, :each]
-    qe = dot(qs_s[...], wp_ref[...], 1, 0)
+    qe = dot(payload_ref[...].reshape(-1, payload_ref.shape[2]), wp_ref[...], 1, 0)
     length = jnp.sqrt(jnp.sum(qe * qe, axis=-1, keepdims=True) + epsilon)
     qdir = qe / length
     qdir_ref[...] = qdir
     qlen_ref[...] = jnp.broadcast_to(length, qlen_ref.shape)
     qunit_ref[...] = qdir.astype(BF16).reshape(qunit_ref.shape)
-    for b in range(0, total, sub):
-        e = emb_ref[b : b + sub]
-        dir_s[b : b + sub] = e / jnp.sqrt(jnp.sum(e * e, axis=-1, keepdims=True) + epsilon)
-    for r in range(count):
-        units = dir_s[pl.ds(r, seq, stride=count), :].astype(BF16)
-        units_ref[r] = units
-        logits = dot(qunit_ref[qidx_ref[r]], units, 1, 1) / sharpness
-        valid = lax.broadcasted_iota(jnp.int32, logits.shape, 1) < len_ref[r]
-        student = jnp.where(valid, jnp.exp(logits), 0.0)
-        student_total = jnp.sum(student, axis=-1, keepdims=True)
-        prob_ref[r] = student / student_total
-        log_ref[r] = logits - jnp.log(student_total)
+
+    def direct(n):
+        part = pl.ds(pl.multiple_of(n * sub, sub), sub)
+        e = emb_ref[part]
+        dir_s[part] = e / jnp.sqrt(jnp.sum(e * e, axis=-1, keepdims=True) + epsilon)
+
+    loop(total // sub, direct)
+    side = 4 if count % 4 == 0 else 1
+
+    def score(n):
+        for v in range(side):
+            r = n * side + v
+            units = dir_s[pl.ds(r, seq, stride=count), :].astype(BF16)
+            units_ref[r] = units
+            logits = dot(qunit_ref[qidx_ref[r]], units, 1, 1) / sharpness
+            valid = lax.broadcasted_iota(jnp.int32, logits.shape, 1) < len_ref[r]
+            student = jnp.where(valid, jnp.exp(logits), 0.0)
+            student_total = jnp.sum(student, axis=-1, keepdims=True)
+            prob_ref[r] = student / student_total
+            log_ref[r] = logits - jnp.log(student_total)
+
+    loop(count // side, score)
 
 
 def student_scores(qidx, lens, payload, embeds, wp, after, count, tokens, group_queries):
@@ -239,7 +281,7 @@
             jax.ShapeDtypeStruct((queries * tokens, emb), F32),
             jax.ShapeDtypeStruct((queries * tokens, 128), F32),
         ],
-        scratch_shapes=[pltpu.VMEM((queries * tokens, payload.shape[2]), BF16), pltpu.VMEM((total, emb), F32)],
+        scratch_shapes=[pltpu.VMEM((total, emb), F32)],
         compiler_params=params(),
         cost_estimate=cost(1e9, 4 * total * emb),
         name="student_scores",
@@ -259,14 +301,14 @@
     qdir_ref, qlen_ref, gain_ref, bias_ref, wp_ref, wpt_ref,
     sg_out, send_ref, keep_ref,
     maps_s, prob_s, log_s, units_s, qunit_s, emb_s, x_s, normed_s, inv_s, payload_s,
-    up_s, eg_s, mean_s, along_s, un_s, qg_s, hg_both, sg_s, wo_s, nt_s, right_s,
+    up_s, eg_s, mean_s, along_s, un_s, qg_s, hg_s, sg_s, wo_s, nt_s, right_s,
     first_sem, block_sem, out_sem, last_sem,
 ):
     total, width = normed_s.shape
     emb = emb_s.shape[1]
     seq = total // count
     rows = total // blocks
-    sub = rows
+    sub = split_rows(rows, 256)
     thin = split_rows(total, 128)
     step = split_rows(sub, 48)
     first = [
@@ -304,78 +346,79 @@
             copy.start()
     last.start()
 
-    spread = jnp.zeros((tokens, 1), F32)
-    for r in range(count):
-        teacher = maps_s[midx_ref[r]].astype(F32)
-        valid = lax.broadcasted_iota(jnp.int32, teacher.shape, 1) < len_ref[r]
-        teacher_log = jnp.log(teacher)
-        teacher = jnp.where(valid, teacher, 0.0)
-        teacher_total = jnp.sum(teacher, axis=-1, keepdims=True)
-        teacher_prob = teacher / teacher_total
-        gap = (teacher_log - jnp.log(teacher_total)) - log_s[r]
-        spread += jnp.sum(jnp.where(valid, teacher_prob * gap, 0.0), axis=-1, keepdims=True)
-        slope = ((prob_s[r] - teacher_prob) / (tokens * sharpness)).astype(BF16)
-        up_s[pl.ds(r, seq, stride=count), :] = dot(slope, qunit_s[qidx_ref[r]], 0, 0).astype(BF16).astype(F32)
-        un_s[r] = dot(slope, units_s[r], 1, 0)
-    for r in range(count):
+    side = 4 if count % 4 == 0 else 1
+
+    def score(n, spread):
+        for v in range(side):
+            r = n * side + v
+            teacher = maps_s[midx_ref[r]].astype(F32)
+            valid = lax.broadcasted_iota(jnp.int32, teacher.shape, 1) < len_ref[r]
+            teacher_log = jnp.log(teacher)
+            teacher = jnp.where(valid, teacher, 0.0)
+            teacher_total = jnp.sum(teacher, axis=-1, keepdims=True)
+            teacher_prob = teacher / teacher_total
+            gap = (teacher_log - jnp.log(teacher_total)) - log_s[r]
+            spread += jnp.sum(jnp.where(valid, teacher_prob * gap, 0.0), axis=-1, keepdims=True)
+            slope = ((prob_s[r] - teacher_prob) / (tokens * sharpness)).astype(BF16)
+            up_s[pl.ds(r, seq, stride=count), :] = dot(slope, qunit_s[qidx_ref[r]], 0, 0).astype(BF16).astype(F32)
+            un_s[r] = dot(slope, units_s[r], 1, 0)
+        return spread
+
+    spread = lax.fori_loop(0, count // side, score, jnp.zeros((tokens, 1), F32))
+
+    def gather(r):
         qg_s[qidx_ref[r]] += un_s[r]
-    total_eg = jnp.zeros((1, emb), F32)
+
+    loop(count, gather)
     for copy in second:
         copy.wait()
-    for b in range(0, total, thin):
-        e = emb_s[b : b + thin]
-        upstream = up_s[b : b + thin]
+
+    def narrow(n, total_eg):
+        part = pl.ds(pl.multiple_of(n * thin, thin), thin)
+        e = emb_s[part]
+        upstream = up_s[part]
         length = jnp.sqrt(jnp.sum(e * e, axis=-1, keepdims=True) + epsilon)
         direction = e / length
         eg = (upstream - direction * jnp.sum(direction * upstream, axis=-1, keepdims=True)) / length
         eg = eg.astype(BF16)
-        eg_s[b : b + thin] = eg
+        eg_s[part] = eg
         eg = eg.astype(F32)
-        total_eg += jnp.sum(eg, axis=0, keepdims=True)
-        inverse = inv_s[b : b + thin]
-        mean_s[b : b + thin] = inverse * (jnp.sum(eg * gain_w, axis=-1, keepdims=True) / width)
-        along_s[b : b + thin] = inverse * (jnp.sum(eg * (e - bias_w), axis=-1, keepdims=True) / width)
+        inverse = inv_s[part]
+        mean_s[part] = inverse * (jnp.sum(eg * gain_w, axis=-1, keepdims=True) / width)
+        along_s[part] = inverse * (jnp.sum(eg * (e - bias_w), axis=-1, keepdims=True) / width)
+        return total_eg + jnp.sum(eg, axis=0, keepdims=True)
+
+    total_eg = lax.fori_loop(0, total // thin, narrow, jnp.zeros((1, emb), F32))
+    wo_s[...] = jnp.zeros_like(wo_s)
+    nt_s[...] = jnp.zeros_like(nt_s)
 
     def wide(b):
-        hg_s = hg_both.at[b // sub % 2]
-        hg_s[...] = dot(eg_s[b : b + sub], wpt_ref[...], 1, 0)
-        for c in range(b, b + sub, step):
-            inverse, mean, along = inv_s[c : c + step], mean_s[c : c + step], along_s[c : c + step]
-            for v in range(0, width, 128):
-                scaled = hg_s[c - b : c - b + step, v : v + 128] * gain[:, v : v + 128]
-                normed = normed_s[c : c + step, v : v + 128].astype(F32)
-                sg_s[c : c + step, v : v + 128] = (inverse * scaled - mean - normed * along).astype(BF16)
-
-    def products(b, part, parts):
-        span = width // parts
-        value = dot(x_s[b, part * span : (part + 1) * span], sg_s[b * rows : (b + 1) * rows], 1, 0)
-        if b == 0:
-            wo_s[part * span : (part + 1) * span] = value
-        else:
-            wo_s[part * span : (part + 1) * span] += value
-
-    parts = 1
-    stores = []
-    for b in range(blocks):
-        for copy in loads[b]:
-            copy.wait()
-        for n in range(rows // sub):
-            wide(b * rows + n * sub)
-            if b > 0 and n < parts:
-                products(b - 1, n, parts)
-        stores.append(
-            pltpu.make_async_copy(
-                sg_s.at[pl.ds(b * rows, rows)], sg_out.at[pl.ds(b * rows, rows)], out_sem.at[b]
-            )
-        )
-        stores[-1].start()
-        value = dot(eg_s[b * rows : (b + 1) * rows], normed_s[b * rows : (b + 1) * rows], 0, 0)
-        if b == 0:
-            nt_s[...] = value
-        else:
-            nt_s[...] += value
-    for n in range(parts):
-        products(blocks - 1, n, parts)
+        base = pl.multiple_of(b * rows, rows)
+        pltpu.make_async_copy(normed_in.at[pl.ds(base, rows)], normed_s.at[pl.ds(base, rows)], block_sem.at[2 * b]).wait()
+
+        def piece(n):
+            first = pl.multiple_of(base + n * sub, sub)
+            hg_s[...] = dot(eg_s[pl.ds(first, sub)], wpt_ref[...], 1, 0)
+
+            def chunk(c):
+                inner = pl.ds(pl.multiple_of(c * step, step), step)
+                outer = pl.ds(pl.multiple_of(first + c * step, step), step)
+                inverse, mean, along = inv_s[outer], mean_s[outer], along_s[outer]
+                for v in range(0, width, 128):
+                    scaled = hg_s[inner, v : v + 128] * gain[:, v : v + 128]
+                    normed = normed_s[outer, v : v + 128].astype(F32)
+                    sg_s[outer, v : v + 128] = (inverse * scaled - mean - normed * along).astype(BF16)
+
+            loop(sub // step, chunk)
+
+        loop(rows // sub, piece)
+        part = pl.ds(base, rows)
+        pltpu.make_async_copy(sg_s.at[part], sg_out.at[part], out_sem.at[b]).start()
+        pltpu.make_async_copy(x_in.at[b], x_s.at[b], block_sem.at[2 * b + 1]).wait()
+        wo_s[...] += dot(x_s[b], sg_s[part], 1, 0)
+        nt_s[...] += dot(eg_s[part], normed_s[part], 0, 0)
+
+    loop(blocks, wide)
 
     last.wait()
     qg = qg_s[...].reshape(qdir_ref.shape)
@@ -383,12 +426,8 @@
     qeg = (qg - qdir * jnp.sum(qdir * qg, axis=-1, keepdims=True)) / qlen_ref[:, :1]
     high = qeg.astype(BF16)
     low = (qeg - high.astype(F32)).astype(BF16)
-    each = group_queries * tokens
-    proj_query = jnp.zeros((emb, width), F32)
-    for k in range(payload_s.shape[0]):
-        qs = payload_s[k, :each]
-        part = slice(k * each, (k + 1) * each)
-        proj_query = proj_query + (dot(high[part], qs, 0, 0) + dot(low[part], qs, 0, 0))
+    qs = payload_s[...].reshape(-1, width)
+    proj_query = dot(high, qs, 0, 0) + dot(low, qs, 0, 0)
     nt = nt_s[...]
     s = jnp.broadcast_to(total_eg, (emb, emb)).T[:, :1]
     wpt = wpt_ref[...].astype(F32)
@@ -408,8 +447,9 @@
         for c in range(half // chunk):
             ref[c, :, :width] = left[c * chunk : (c + 1) * chunk]
             ref[c, :, width:] = right[c * chunk : (c + 1) * chunk]
-    for copy in stores:
-        copy.wait()
+    for b in range(blocks):
+        part = pl.ds(b * rows, rows)
+        pltpu.make_async_copy(sg_s.at[part], sg_out.at[part], out_sem.at[b]).wait()
 
 
 def student_backward(
@@ -419,7 +459,7 @@
     total, width = normed.shape
     emb = wp.shape[1]
     blocks = x.shape[0]
-    sub = total // blocks
+    sub = split_rows(total // blocks, 256)
     chunks = width // CORES // chunk
     prob, log, units, qunit, qdir, qlen = scores
     manual = [maps, prob, log, units, qunit, embeds, x, normed, inverse, payload]
@@ -436,7 +476,7 @@
             pltpu.VMEM((total, 128), F32),
             pltpu.VMEM((count, tokens, emb), F32),
             pltpu.VMEM(qunit.shape, F32),
-            pltpu.VMEM((2, sub, width), F32),
+            pltpu.VMEM((sub, width), F32),
             pltpu.VMEM((total, width), BF16),
             pltpu.VMEM((width, width), F32),
             pltpu.VMEM((emb, width), F32),
@@ -455,7 +495,13 @@
 
 def context_kernel(sg_ref, wo_ref, after_ref, out_ref, token_ref):
     token_ref[...] = jnp.zeros_like(token_ref)
-    out_ref[...] = dot(sg_ref[...], wo_ref[...], 1, 0).astype(BF16)
+    sub = split_rows(sg_ref.shape[0], 256)
+
+    def block(n):
+        part = pl.ds(pl.multiple_of(n * sub, sub), sub)
+        out_ref[part] = dot(sg_ref[part], wo_ref[...], 1, 0).astype(BF16)
+
+    loop(sg_ref.shape[0] // sub, block)
 
 
 def context_grad(sg, weight_turned, after):
@@ -606,17 +652,14 @@
     positions = jnp.sum(
         jnp.where(place[:, None] == rows[None, :], (passage_dest % count)[:, None], 0), axis=0
     )
-    queries = query_states.reshape(group_queries * tokens, width)
-    extra = jnp.pad(positions.astype(BF16)[None, :], ((0, 15), (0, width - count)))
-    payload = jnp.concatenate([queries, extra], axis=0)
+    positions = positions.astype(jnp.int32).reshape(dp, per)
     part = depth // dp
     mine = jnp.stack(
         [lax.dynamic_slice_in_dim(w, me * part, part, 0) for w in (teacher_query, teacher_key)]
     )
-    payload, mine = lax.optimization_barrier((jnp.broadcast_to(payload[None], (dp,) + payload.shape), mine))
-    payload = lax.all_to_all(payload, "dp", split_axis=0, concat_axis=0, tiled=True)
     along = jnp.concatenate([shift_t(mine, k) for k in range(1, nt)], axis=0)
-    along, payload = lax.optimization_barrier((along, payload))
+    order = lax.all_to_all(positions, "dp", split_axis=0, concat_axis=0, tiled=True).reshape(-1)
+    along, order = lax.optimization_barrier((along, order))
     pieces = [along] + [shift_chip(along, k) for k in range(1, chips)]
     shifts = jnp.arange(chips, dtype=jnp.int32)
     behind = (chip - shifts) % chips
@@ -627,12 +670,12 @@
     gain2, bias2 = gain.reshape(-1, 128), bias.reshape(-1, 128)
     x = flat(context)
     normed, embeds, inverse, turned = student_forward(x, flat(stream), out_weight, gain2, bias2, proj_weight)
+    payload = jnp.broadcast_to(query_states.reshape(1, -1, width), (dp, group_queries * tokens, width))
     pieces[1:], payload, normed, embeds, inverse, turned, weight_turned, proj_turned = lax.optimization_barrier(
         (pieces[1:], payload, normed, embeds, inverse, turned, out_weight.T, proj_weight.T)
     )
     pieces = pieces + [swap_core(a) for a in pieces]
-    told = payload[:, group_queries * tokens, :count].astype(jnp.int32)
-    order = lax.dynamic_slice_in_dim(told, me * per, per, 1).reshape(-1)
+    payload = lax.all_to_all(payload, "dp", split_axis=0, concat_axis=0, tiled=True)
     maps, token = teacher_maps(
         order, piece_rows, flat(teacher_states), teacher_query, teacher_key, pieces, count, tokens
     )

time: 143 us -> 169 us (1.18)
  Pallas kernels: 63.8 us -> 93.3 us
  waiting for transfers between devices: 26.9 us -> 15.4 us
  blocking collectives: 0 us -> 8.17 us
  local copies, waits for them, and re-layouts: 9.41 us -> 11.4 us
  starting transfers between devices: 38 us -> 36.1 us
    pallas_call x1, Pallas kernels: 12.5 us -> 27.5 us  [student_forward(): pl.pallas_call(forward_kernel, grid=(total // rows,), in_specs=[block(wid...]
    all_to_all x0 -> x1, blocking collectives: none -> 8.17 us  [local(): lax.all_to_all(positions, 'dp', split_axis=0, concat_axis=0, tiled=True)]
    ppermute x9, waiting for transfers between devices: 14.6 us -> 7.02 us  [shift_t(): return lax.ppermute(x, 'tensor', [(t, (t + k) % nt) for t in range(nt)])]
    pallas_call x1, Pallas kernels: 22.4 us -> 28.3 us  [student_backward(): pl.pallas_call(functools.partial(backward_kernel, tokens, count, blocks,...]
    pallas_call x1, Pallas kernels: 12.4 us -> 16.7 us  [teacher_maps(): pl.pallas_call(functools.partial(teacher_kernel, parts, count, tokens), i...]
    pallas_call x1, Pallas kernels: 4.19 us -> 7.66 us  [student_scores(): pl.pallas_call(functools.partial(scores_kernel, tokens, count, group_quer...]
    all_to_all x1, waiting for transfers between devices: 2.49 us -> 0.01 us  [local(): maps = lax.all_to_all(maps, 'dp', split_axis=0, concat_axis=0, tiled=True)]
    all_to_all x1, starting transfers between devices: 5.17 us -> 3.45 us  [local(): lax.all_to_all(payload, 'dp', split_axis=0, concat_axis=0, tiled=True)]
  transfers between devices with their start and end apart: 29 -> 29, of which waited for: 17 -> 11; matrix products, arithmetic and copies ran while one was open for 3% -> 5% of each run, Pallas kernels for 17% -> 36%
where the time goes in v4:
time: 169 us; the launch traced here: 168 us
  Pallas kernels  93.3 us (55%)
  starting transfers between devices  36.1 us (21%)
  waiting for transfers between devices  15.4 us (9%)
  local copies, waits for them, and re-layouts  11.4 us (7%)
  blocking collectives  8.17 us (5%)
  other arithmetic  2.54 us (2%)
    pallas_call x1, Pallas kernels, student_backward(): pl.pallas_call(functools.partial(backward_kernel, tokens, count, blocks,...  28.3 us
    pallas_call x1, Pallas kernels, student_forward(): pl.pallas_call(forward_kernel, grid=(total // rows,), in_specs=[block(wid...  27.5 us
    pallas_call x1, Pallas kernels, teacher_maps(): pl.pallas_call(functools.partial(teacher_kernel, parts, count, tokens), i...  16.7 us
    ppermute x9, starting transfers between devices, shift_t(): return lax.ppermute(x, 'tensor', [(t, (t + k) % nt) for t in range(nt)])  14.7 us
    ppermute x9, starting transfers between devices, shift_chip(): lax.ppermute(x, 'dp', [(c * CORES + o, (c + k) % chips * CORES + o) for c...  11.8 us
    pallas_call x1, Pallas kernels, context_grad(): pl.pallas_call(context_kernel, grid=(total // rows,), in_specs=[block, pl...  8.5 us
    unnamed x34, local copies, waits for them, and re-layouts  8.4 us
    all_to_all x1, blocking collectives, local(): lax.all_to_all(positions, 'dp', split_axis=0, concat_axis=0, tiled=True)  8.17 us
  transfers between devices with their start and end apart: 29, of which 11 were waited for; matrix products, arithmetic and copies ran while one was open for 5% of the time, Pallas kernels for 36%

profile of v4, /device:TPU:0, one launch (start us, length us, event | category | flops | bytes accessed | tf_op | source)
XLA Modules:
  0.0 167.9 jit_solution(12366764585572403358)
XLA Ops:
  1.5 3.1 %collective-permute-start = (bf16[2,128,256]{2,1,0:T(8,128)(2,1)S(1)}, bf16[2,128,256]{2,1,0:T(8,128)(2,1)S(1)}, u32[]{:S(2)}, u32[]{:S(2)}) collective-permute-start(bf16[2,128,256]{2,1,0:T(8,128)(2,1)S(1)} %pad_maximum_fusion.2), channel_id=1, source_target_pairs={{0,1},{1,2},{2,3},{3,0},{4,5},{5,6},{6,7},{7,4},{8,9},{9,10},{10,1... | collective-permute-start | bytes 393224 | tf_op jit(solution)/shard_map/ppermute | solution.py:644
  4.6 2.6 %collective-permute-start.1 = (bf16[2,128,256]{2,1,0:T(8,128)(2,1)S(1)}, bf16[2,128,256]{2,1,0:T(8,128)(2,1)S(1)}, u32[]{:S(2)}, u32[]{:S(2)}) collective-permute-start(bf16[2,128,256]{2,1,0:T(8,128)(2,1)S(1)} %pad_maximum_fusion.2), channel_id=1, source_target_pairs={{0,2},{1,3},{2,0},{3,1},{4,6},{5,7},{6,4},{7,5},{8,10},{9,11},{10,... | collective-permute-start | bytes 393224 | tf_op jit(solution)/shard_map/ppermute | solution.py:644
  9.6 8.2 %all_to_all.19 = s32[8,1,2]{2,1,0:T(1,128)S(1)} all-to-all(s32[8,1,2]{2,1,0:T(1,128)S(1)} %bitcast.39), channel_id=1, replica_groups=mesh['dp'=8,'tensor'=4] {'dp'}, dimensions={0} | all-to-all | bytes 128 | tf_op jit(solution)/shard_map/all_to_all | solution.py:661
  20.8 2.4 %collective-permute-start.5 = (bf16[6,128,256]{2,1,0:T(8,128)(2,1)S(1)}, bf16[6,128,256]{2,1,0:T(8,128)(2,1)S(1)}, u32[]{:S(2)}, u32[]{:S(2)}) collective-permute-start(bf16[6,128,256]{2,1,0:T(8,128)(2,1)S(1)} %pad_maximum_fusion.rest_0_), channel_id=1, source_target_pairs={{0,24},{4,28},{8,0},{12,4},{16,8},{20,12},{24,16},{28,20},{1,25},{... | collective-permute-start | bytes 1179656 | tf_op jit(solution)/shard_map/ppermute | solution.py:636
  23.1 2.4 %copy.26 = bf16[768,768]{0,1:T(8,128)(2,1)} copy(bf16[768,768]{1,0:T(8,128)(2,1)} %wo_ref.1) | data formatting | bytes 2359296 | tf_op args[2]
  25.5 1.8 %copy.27 = bf16[768,128]{0,1:T(8,128)(2,1)} copy(bf16[768,128]{1,0:T(8,128)(2,1)} %wp_ref.5) | data formatting | bytes 393216 | tf_op args[5]
  27.3 27.5 %student_forward.1 = (bf16[2880,768]{1,0:T(8,128)(2,1)}, f32[2880,128]{1,0:T(8,128)}, f32[2880,128]{1,0:T(8,128)}, bf16[4,768,720]{2,1,0:T(8,128)(2,1)}) custom-call(bf16[2880,768]{1,0:T(8,128)(2,1)} %bitcast.41, bf16[2880,768]{1,0:T(8,128)(2,1)} %bitcast.42, bf16[768,768]{1,0:T(8,128)(2,1)} %wo_ref.1, f32[6,128]{1,0:T(8,128)} %bitcast.45, ...), custom_call_target="tpu_custom_call" | custom-call | flops 3963617280 | bytes 17694720 | tf_op jit(solution)/shard_map/student_forward/pallas_call | solution.py:90
  57.6 3.5 %all-to-all-start.2 = ((bf16[8,32,768]{2,1,0:T(8,128)(2,1)}), bf16[8,32,768]{2,1,0:T(8,128)(2,1)S(1)}, u32[]{:S(2)}, u32[]{:S(2)}) async-start(bf16[8,32,768]{2,1,0:T(8,128)(2,1)} %broadcast_in_dim.19), calls=%async_computation.2 | async-start | bytes 786432 | tf_op jit(solution)/shard_map/all_to_all | solution.py:678
  62.2 16.7 %teacher_maps.1 = (bf16[16,32,180]{2,1,0:T(8,128)(2,1)}, f32[8,128]{1,0:T(8,128)}) custom-call(s32[16]{0:T(128)} %reshape.93.order_ref, s32[8]{0:T(128)} %pad_add_fusion.rows_ref, bf16[3392,1024]{1,0:T(8,128)(2,1)} %bitcast.40, bf16[1024,256]{1,0:T(8,128)(2,1)} %wq_ref.1, bf16[1024,256]{1,0:T(8,128)(2,1)} %wk_ref.1, bf16[6,128,256]{2,1,0:T(8,128)(2,1)} %copy-done.3, ...), custom_call_target="tpu_custom_call" | custom-call | flops 4294967296 | bytes 11141120 | tf_op jit(solution)/shard_map/teacher_maps/pallas_call | solution.py:208
  78.9 4.1 %all-to-all-start.1 = ((bf16[16,32,180]{2,1,0:T(8,128)(2,1)}), bf16[16,32,180]{2,1,0:T(8,128)(2,1)S(1)}, u32[]{:S(2)}, u32[]{:S(2)}) async-start(bf16[16,32,180]{2,1,0:T(8,128)(2,1)} %get-tuple-element.58), calls=%async_computation.1 | async-start | bytes 524288 | tf_op jit(solution)/shard_map/all_to_all | solution.py:682
  83.1 7.7 %student_scores.1 = (f32[16,32,180]{2,1,0:T(8,128)}, f32[16,32,180]{2,1,0:T(8,128)}, bf16[16,180,128]{2,1,0:T(8,128)(2,1)}, bf16[8,32,128]{2,1,0:T(8,128)(2,1)}, f32[256,128]{1,0:T(8,128)}, /*index=5*/f32[256,128]{1,0:T(8,128)}) custom-call(s32[16]{0:T(128)} %copy-done.14, s32[16]{0:T(128)} %len_ref.3, bf16[8,32,768]{2,1,0:T(8,128)(2,1)} %copy-done.4, ...), custom_call_target="tpu_custom_call" | custom-call | flops 1000000000 | bytes 1474560 | tf_op jit(solution)/shard_map/student_scores/pallas_call | solution.py:272
  91.4 28.3 %student_backward.1 = (bf16[2880,768]{1,0:T(8,128)(2,1)}, bf16[16,24,1024]{2,1,0:T(8,128)(2,1)}, bf16[16,24,1024]{2,1,0:T(8,128)(2,1)}) custom-call(s32[16]{0:T(128)} %copy-done.14, s32[16]{0:T(128)} %copy-done.15, s32[16]{0:T(128)} %len_ref.3, s32[1]{0:T(128)} %bitcast.core_ref, bf16[16,32,180]{2,1,0:T(8,128)(2,1)} %copy-done.5, ...), custom_call_target="tpu_custom_call" | custom-call | flops 4529848320 | bytes 17694720 | tf_op jit(solution)/shard_map/student_backward/pallas_call | solution.py:467
  120.3 2.1 %collective-permute-done.10.rest_1_ = bf16[16,24,1024]{2,1,0:T(8,128)(2,1)S(1)} collective-permute-done((bf16[16,24,1024]{2,1,0:T(8,128)(2,1)}, bf16[16,24,1024]{2,1,0:T(8,128)(2,1)S(1)}, u32[]{:S(2)}, u32[]{:S(2)}) %collective-permute-start.10) | collective-permute-done | bytes 786464 | tf_op jit(solution)/shard_map/ppermute | solution.py:641
  125.1 1.9 %collective-permute-start.11 = (bf16[4,24,1024]{2,1,0:T(8,128)(2,1)S(1)}, bf16[4,24,1024]{2,1,0:T(8,128)(2,1)S(1)}, u32[]{:S(2)}, u32[]{:S(2)}) collective-permute-start(bf16[4,24,1024]{2,1,0:T(8,128)(2,1)S(1)} %get-tuple-element.75), channel_id=1, source_target_pairs={{0,8},{4,12},{8,16},{12,20},{16,24},{20,28},{24,0},{28,4},{1,9},{5... | collective-permute-start | bytes 589832 | tf_op jit(solution)/shard_map/ppermute | solution.py:636
  130.0 8.5 %context_grad.1 = (bf16[2880,768]{1,0:T(8,128)(2,1)}, f32[8,128]{1,0:T(8,128)}) custom-call(bf16[2880,768]{1,0:T(8,128)(2,1)} %get-tuple-element.78.sg_ref, bf16[768,768]{1,0:T(8,128)(2,1)} %bitcast.33, f32[8,128]{1,0:T(8,128)} %copy-done.2), custom_call_target="tpu_custom_call" | custom-call | flops 3397386240 | bytes 8847360 | tf_op jit(solution)/shard_map/context_grad/pallas_call | solution.py:511
  141.1 1.5 collective-permute-start.15
  142.7 1.6 collective-permute-start.16
  144.3 2.2 %collective-permute-done.14.refs_1_ = bf16[24,1024]{1,0:T(8,128)(2,1)S(1)} collective-permute-done((bf16[24,1024]{1,0:T(8,128)(2,1)S(1)}, bf16[24,1024]{1,0:T(8,128)(2,1)S(1)}, u32[]{:S(2)}, u32[]{:S(2)}) %collective-permute-start.14) | collective-permute-done | bytes 49184 | tf_op jit(solution)/shard_map/ppermute | solution.py:644
  149.0 1.8 %collective-permute-start.18 = (bf16[24,1024]{1,0:T(8,128)(2,1)S(1)}, bf16[24,1024]{1,0:T(8,128)(2,1)S(1)}, u32[]{:S(2)}, u32[]{:S(2)}) collective-permute-start(bf16[24,1024]{1,0:T(8,128)(2,1)S(1)} %sum_tensor.1), channel_id=1, source_target_pairs={{0,2},{1,3},{2,0},{3,1},{4,6},{5,7},{6,4},{7,5},{8,10},{9,11},{10,... | collective-permute-start | bytes 147464 | tf_op jit(solution)/shard_map/ppermute | solution.py:644
  151.6 2.1 %collective-permute-done.17 = bf16[24,1024]{1,0:T(8,128)(2,1)S(1)} collective-permute-done((bf16[24,1024]{1,0:T(8,128)(2,1)S(1)}, bf16[24,1024]{1,0:T(8,128)(2,1)S(1)}, u32[]{:S(2)}, u32[]{:S(2)}) %collective-permute-start.17) | collective-permute-done | bytes 49184 | tf_op jit(solution)/shard_map/ppermute | solution.py:644
  156.6 2.2 %collective-permute-start.22 = (bf16[4,24,1024]{2,1,0:T(8,128)(2,1)S(1)}, bf16[4,24,1024]{2,1,0:T(8,128)(2,1)S(1)}, u32[]{:S(2)}, u32[]{:S(2)}) collective-permute-start(bf16[4,24,1024]{2,1,0:T(8,128)(2,1)S(1)} %pad_maximum_fusion.1.rest_0_), channel_id=1, source_target_pairs={{0,24},{4,28},{8,0},{12,4},{16,8},{20,12},{24,16},{28,20},{1,25},{... | collective-permute-start | bytes 589832 | tf_op jit(solution)/shard_map/ppermute | solution.py:636
  158.9 3.3 %collective-permute-done.20.rest_1_ = bf16[4,24,1024]{2,1,0:T(8,128)(2,1)S(1)} collective-permute-done((bf16[4,24,1024]{2,1,0:T(8,128)(2,1)S(1)}, bf16[4,24,1024]{2,1,0:T(8,128)(2,1)S(1)}, u32[]{:S(2)}, u32[]{:S(2)}) %collective-permute-start.20) | collective-permute-done | bytes 196640 | tf_op jit(solution)/shard_map/ppermute | solution.py:636
  162.1 1.7 %collective-permute-done.21.rest_2_ = bf16[4,24,1024]{2,1,0:T(8,128)(2,1)S(1)} collective-permute-done((bf16[4,24,1024]{2,1,0:T(8,128)(2,1)S(1)}, bf16[4,24,1024]{2,1,0:T(8,128)(2,1)S(1)}, u32[]{:S(2)}, u32[]{:S(2)}) %collective-permute-start.21) | collective-permute-done | bytes 196640 | tf_op jit(solution)/shard_map/ppermute | solution.py:636
  165.6 2.3 %unpack.1 = (f32[32,24,768]{2,1,0:T(8,128)}, f32[32,24,128]{2,1,0:T(8,128)}, f32[6,128]{1,0:T(8,128)}, f32[6,128]{1,0:T(8,128)}, f32[1]{0:T(128)}) custom-call(s32[32]{0:T(128)S(1)} %add.105.index_ref, bf16[4,24,1024]{2,1,0:T(8,128)(2,1)S(1)} %pad_maximum_fusion.1.rest_0_, bf16[4,24,1024]{2,1,0:T(8,128)(2,1)S(1)} %collective-permute-done.20.rest_1_, ...), custom_call_target="tpu_custom_call" | custom-call | tf_op jit(solution)/shard_map/unpack/pallas_call | solution.py:592
  (100 shorter events, 27.7 us)
Async XLA Ops:
  1.5 18.0 %collective-permute-start = (bf16[2,128,256]{2,1,0:T(8,128)(2,1)S(1)}, bf16[2,128,256]{2,1,0:T(8,128)(2,1)S(1)}, u32[]{:S(2)}, u32[]{:S(2)}) collective-permute-start(bf16[2,128,256]{2,1,0:T(8,128)(2,1)S(1)} %pad_maximum_fusion.2), channel_id=1, source_target_pairs={{0,1},{1,2},{2,3},{3,0},{4,5},{5,6},{6,7},{7,4},{8,9},{9,10},{10,1... | collective-permute-start | bytes 393224 | tf_op jit(solution)/shard_map/ppermute | solution.py:644
  4.6 14.9 %collective-permute-start.1 = (bf16[2,128,256]{2,1,0:T(8,128)(2,1)S(1)}, bf16[2,128,256]{2,1,0:T(8,128)(2,1)S(1)}, u32[]{:S(2)}, u32[]{:S(2)}) collective-permute-start(bf16[2,128,256]{2,1,0:T(8,128)(2,1)S(1)} %pad_maximum_fusion.2), channel_id=1, source_target_pairs={{0,2},{1,3},{2,0},{3,1},{4,6},{5,7},{6,4},{7,5},{8,10},{9,11},{10,... | collective-permute-start | bytes 393224 | tf_op jit(solution)/shard_map/ppermute | solution.py:644
  7.2 12.3 %collective-permute-start.2 = (bf16[2,128,256]{2,1,0:T(8,128)(2,1)S(1)}, bf16[2,128,256]{2,1,0:T(8,128)(2,1)S(1)}, u32[]{:S(2)}, u32[]{:S(2)}) collective-permute-start(bf16[2,128,256]{2,1,0:T(8,128)(2,1)S(1)} %pad_maximum_fusion.2), channel_id=1, source_target_pairs={{0,3},{1,0},{2,1},{3,2},{4,7},{5,4},{6,5},{7,6},{8,11},{9,8},{10,9... | collective-permute-start | bytes 393224 | tf_op jit(solution)/shard_map/ppermute | solution.py:644
  19.6 35.3 %collective-permute-start.3 = (bf16[6,128,256]{2,1,0:T(8,128)(2,1)S(1)}, bf16[6,128,256]{2,1,0:T(8,128)(2,1)S(1)}, u32[]{:S(2)}, u32[]{:S(2)}) collective-permute-start(bf16[6,128,256]{2,1,0:T(8,128)(2,1)S(1)} %pad_maximum_fusion.rest_0_), channel_id=1, source_target_pairs={{0,8},{4,12},{8,16},{12,20},{16,24},{20,28},{24,0},{28,4},{1,9},{5... | collective-permute-start | bytes 1179656 | tf_op jit(solution)/shard_map/ppermute | solution.py:636
  20.2 34.7 %collective-permute-start.4 = (bf16[6,128,256]{2,1,0:T(8,128)(2,1)S(1)}, bf16[6,128,256]{2,1,0:T(8,128)(2,1)S(1)}, u32[]{:S(2)}, u32[]{:S(2)}) collective-permute-start(bf16[6,128,256]{2,1,0:T(8,128)(2,1)S(1)} %pad_maximum_fusion.rest_0_), channel_id=1, source_target_pairs={{0,16},{4,20},{8,24},{12,28},{16,0},{20,4},{24,8},{28,12},{1,17},{... | collective-permute-start | bytes 1179656 | tf_op jit(solution)/shard_map/ppermute | solution.py:636
  20.8 34.2 %collective-permute-start.5 = (bf16[6,128,256]{2,1,0:T(8,128)(2,1)S(1)}, bf16[6,128,256]{2,1,0:T(8,128)(2,1)S(1)}, u32[]{:S(2)}, u32[]{:S(2)}) collective-permute-start(bf16[6,128,256]{2,1,0:T(8,128)(2,1)S(1)} %pad_maximum_fusion.rest_0_), channel_id=1, source_target_pairs={{0,24},{4,28},{8,0},{12,4},{16,8},{20,12},{24,16},{28,20},{1,25},{... | collective-permute-start | bytes 1179656 | tf_op jit(solution)/shard_map/ppermute | solution.py:636
  54.8 6.2 %collective-permute-start.6 = (bf16[6,128,256]{2,1,0:T(8,128)(2,1)S(1)}, bf16[6,128,256]{2,1,0:T(8,128)(2,1)S(1)}, u32[]{:S(2)}, u32[]{:S(2)}) collective-permute-start(bf16[6,128,256]{2,1,0:T(8,128)(2,1)S(1)} %pad_maximum_fusion.rest_0_), channel_id=1, source_target_pairs={{0,4},{4,0},{8,12},{12,8},{16,20},{20,16},{24,28},{28,24},{1,5},{5... | collective-permute-start | bytes 1179656 | tf_op jit(solution)/shard_map/ppermute | solution.py:641
  55.9 5.1 %collective-permute-start.7 = (bf16[6,128,256]{2,1,0:T(8,128)(2,1)S(1)}, bf16[6,128,256]{2,1,0:T(8,128)(2,1)S(1)}, u32[]{:S(2)}, u32[]{:S(2)}) collective-permute-start(bf16[6,128,256]{2,1,0:T(8,128)(2,1)S(1)} %collective-permute-done.3.rest_1_), channel_id=1, source_target_pairs={{0,4},{4,0},{8,12},{12,8},{16,20},{20,16},{24,28},{28,24},{1,5},{5... | collective-permute-start | bytes 1179656 | tf_op jit(solution)/shard_map/ppermute | solution.py:641
  56.4 4.7 %collective-permute-start.8 = (bf16[6,128,256]{2,1,0:T(8,128)(2,1)S(1)}, bf16[6,128,256]{2,1,0:T(8,128)(2,1)S(1)}, u32[]{:S(2)}, u32[]{:S(2)}) collective-permute-start(bf16[6,128,256]{2,1,0:T(8,128)(2,1)S(1)} %collective-permute-done.4.rest_2_), channel_id=1, source_target_pairs={{0,4},{4,0},{8,12},{12,8},{16,20},{20,16},{24,28},{28,24},{1,5},{5... | collective-permute-start | bytes 1179656 | tf_op jit(solution)/shard_map/ppermute | solution.py:641
  56.4 4.7 %collective-permute-start.9 = (bf16[6,128,256]{2,1,0:T(8,128)(2,1)S(1)}, bf16[6,128,256]{2,1,0:T(8,128)(2,1)S(1)}, u32[]{:S(2)}, u32[]{:S(2)}) collective-permute-start(bf16[6,128,256]{2,1,0:T(8,128)(2,1)S(1)} %collective-permute-done.5.rest_3_), channel_id=1, source_target_pairs={{0,4},{4,0},{8,12},{12,8},{16,20},{20,16},{24,28},{28,24},{1,5},{5... | collective-permute-start | bytes 1179656 | tf_op jit(solution)/shard_map/ppermute | solution.py:641
  57.6 21.3 %all-to-all-start.2 = ((bf16[8,32,768]{2,1,0:T(8,128)(2,1)}), bf16[8,32,768]{2,1,0:T(8,128)(2,1)S(1)}, u32[]{:S(2)}, u32[]{:S(2)}) async-start(bf16[8,32,768]{2,1,0:T(8,128)(2,1)} %broadcast_in_dim.19), calls=%async_computation.2 | async-start | bytes 786432 | tf_op jit(solution)/shard_map/all_to_all | solution.py:678
  78.9 11.8 %all-to-all-start.1 = ((bf16[16,32,180]{2,1,0:T(8,128)(2,1)}), bf16[16,32,180]{2,1,0:T(8,128)(2,1)S(1)}, u32[]{:S(2)}, u32[]{:S(2)}) async-start(bf16[16,32,180]{2,1,0:T(8,128)(2,1)} %get-tuple-element.58), calls=%async_computation.1 | async-start | bytes 524288 | tf_op jit(solution)/shard_map/all_to_all | solution.py:682
  125.1 13.3 %collective-permute-start.11 = (bf16[4,24,1024]{2,1,0:T(8,128)(2,1)S(1)}, bf16[4,24,1024]{2,1,0:T(8,128)(2,1)S(1)}, u32[]{:S(2)}, u32[]{:S(2)}) collective-permute-start(bf16[4,24,1024]{2,1,0:T(8,128)(2,1)S(1)} %get-tuple-element.75), channel_id=1, source_target_pairs={{0,8},{4,12},{8,16},{12,20},{16,24},{20,28},{24,0},{28,4},{1,9},{5... | collective-permute-start | bytes 589832 | tf_op jit(solution)/shard_map/ppermute | solution.py:636
  127.0 11.4 %collective-permute-start.12 = (bf16[4,24,1024]{2,1,0:T(8,128)(2,1)S(1)}, bf16[4,24,1024]{2,1,0:T(8,128)(2,1)S(1)}, u32[]{:S(2)}, u32[]{:S(2)}) collective-permute-start(bf16[4,24,1024]{2,1,0:T(8,128)(2,1)S(1)} %get-tuple-element.76), channel_id=1, source_target_pairs={{0,16},{4,20},{8,24},{12,28},{16,0},{20,4},{24,8},{28,12},{1,17},{... | collective-permute-start | bytes 589832 | tf_op jit(solution)/shard_map/ppermute | solution.py:636
  128.5 10.0 %collective-permute-start.13 = (bf16[4,24,1024]{2,1,0:T(8,128)(2,1)S(1)}, bf16[4,24,1024]{2,1,0:T(8,128)(2,1)S(1)}, u32[]{:S(2)}, u32[]{:S(2)}) collective-permute-start(bf16[4,24,1024]{2,1,0:T(8,128)(2,1)S(1)} %get-tuple-element.77), channel_id=1, source_target_pairs={{0,24},{4,28},{8,0},{12,4},{16,8},{20,12},{24,16},{28,20},{1,25},{... | collective-permute-start | bytes 589832 | tf_op jit(solution)/shard_map/ppermute | solution.py:636
  140.5 6.0 %collective-permute-start.14 = (bf16[24,1024]{1,0:T(8,128)(2,1)S(1)}, bf16[24,1024]{1,0:T(8,128)(2,1)S(1)}, u32[]{:S(2)}, u32[]{:S(2)}) collective-permute-start(bf16[24,1024]{1,0:T(8,128)(2,1)S(1)} %get-tuple-element.83), channel_id=1, source_target_pairs={{0,1},{1,2},{2,3},{3,0},{4,5},{5,6},{6,7},{7,4},{8,9},{9,10},{10,1... | collective-permute-start | bytes 147464 | tf_op jit(solution)/shard_map/ppermute | solution.py:644
  141.1 6.5 %collective-permute-start.15 = (bf16[24,1024]{1,0:T(8,128)(2,1)S(1)}, bf16[24,1024]{1,0:T(8,128)(2,1)S(1)}, u32[]{:S(2)}, u32[]{:S(2)}) collective-permute-start(bf16[24,1024]{1,0:T(8,128)(2,1)S(1)} %get-tuple-element.84), channel_id=1, source_target_pairs={{0,2},{1,3},{2,0},{3,1},{4,6},{5,7},{6,4},{7,5},{8,10},{9,11},{10,... | collective-permute-start | bytes 147464 | tf_op jit(solution)/shard_map/ppermute | solution.py:644
  142.7 5.0 %collective-permute-start.16 = (bf16[24,1024]{1,0:T(8,128)(2,1)S(1)}, bf16[24,1024]{1,0:T(8,128)(2,1)S(1)}, u32[]{:S(2)}, u32[]{:S(2)}) collective-permute-start(bf16[24,1024]{1,0:T(8,128)(2,1)S(1)} %get-tuple-element.85), channel_id=1, source_target_pairs={{0,3},{1,0},{2,1},{3,2},{4,7},{5,4},{6,5},{7,6},{8,11},{9,8},{10,9... | collective-permute-start | bytes 147464 | tf_op jit(solution)/shard_map/ppermute | solution.py:644
  147.7 6.0 %collective-permute-start.17 = (bf16[24,1024]{1,0:T(8,128)(2,1)S(1)}, bf16[24,1024]{1,0:T(8,128)(2,1)S(1)}, u32[]{:S(2)}, u32[]{:S(2)}) collective-permute-start(bf16[24,1024]{1,0:T(8,128)(2,1)S(1)} %sum_tensor.1), channel_id=1, source_target_pairs={{0,1},{1,2},{2,3},{3,0},{4,5},{5,6},{6,7},{7,4},{8,9},{9,10},{10,1... | collective-permute-start | bytes 147464 | tf_op jit(solution)/shard_map/ppermute | solution.py:644
  149.0 5.7 %collective-permute-start.18 = (bf16[24,1024]{1,0:T(8,128)(2,1)S(1)}, bf16[24,1024]{1,0:T(8,128)(2,1)S(1)}, u32[]{:S(2)}, u32[]{:S(2)}) collective-permute-start(bf16[24,1024]{1,0:T(8,128)(2,1)S(1)} %sum_tensor.1), channel_id=1, source_target_pairs={{0,2},{1,3},{2,0},{3,1},{4,6},{5,7},{6,4},{7,5},{8,10},{9,11},{10,... | collective-permute-start | bytes 147464 | tf_op jit(solution)/shard_map/ppermute | solution.py:644
  155.3 6.9 %collective-permute-start.20 = (bf16[4,24,1024]{2,1,0:T(8,128)(2,1)S(1)}, bf16[4,24,1024]{2,1,0:T(8,128)(2,1)S(1)}, u32[]{:S(2)}, u32[]{:S(2)}) collective-permute-start(bf16[4,24,1024]{2,1,0:T(8,128)(2,1)S(1)} %pad_maximum_fusion.1.rest_0_), channel_id=1, source_target_pairs={{0,8},{4,12},{8,16},{12,20},{16,24},{20,28},{24,0},{28,4},{1,9},{5... | collective-permute-start | bytes 589832 | tf_op jit(solution)/shard_map/ppermute | solution.py:636
  156.1 7.8 %collective-permute-start.21 = (bf16[4,24,1024]{2,1,0:T(8,128)(2,1)S(1)}, bf16[4,24,1024]{2,1,0:T(8,128)(2,1)S(1)}, u32[]{:S(2)}, u32[]{:S(2)}) collective-permute-start(bf16[4,24,1024]{2,1,0:T(8,128)(2,1)S(1)} %pad_maximum_fusion.1.rest_0_), channel_id=1, source_target_pairs={{0,16},{4,20},{8,24},{12,28},{16,0},{20,4},{24,8},{28,12},{1,17},{... | collective-permute-start | bytes 589832 | tf_op jit(solution)/shard_map/ppermute | solution.py:636
  156.6 7.5 %collective-permute-start.22 = (bf16[4,24,1024]{2,1,0:T(8,128)(2,1)S(1)}, bf16[4,24,1024]{2,1,0:T(8,128)(2,1)S(1)}, u32[]{:S(2)}, u32[]{:S(2)}) collective-permute-start(bf16[4,24,1024]{2,1,0:T(8,128)(2,1)S(1)} %pad_maximum_fusion.1.rest_0_), channel_id=1, source_target_pairs={{0,24},{4,28},{8,0},{12,4},{16,8},{20,12},{24,16},{28,20},{1,25},{... | collective-permute-start | bytes 589832 | tf_op jit(solution)/shard_map/ppermute | solution.py:636
  158.8 5.7 %collective-permute-start.23 = (bf16[4,24,1024]{2,1,0:T(8,128)(2,1)S(1)}, bf16[4,24,1024]{2,1,0:T(8,128)(2,1)S(1)}, u32[]{:S(2)}, u32[]{:S(2)}) collective-permute-start(bf16[4,24,1024]{2,1,0:T(8,128)(2,1)S(1)} %pad_maximum_fusion.1.rest_0_), channel_id=1, source_target_pairs={{0,4},{4,0},{8,12},{12,8},{16,20},{20,16},{24,28},{28,24},{1,5},{5... | collective-permute-start | bytes 589832 | tf_op jit(solution)/shard_map/ppermute | solution.py:641
  (21 other events, 195.9 us)

commit v5 on v3

--- a/solution.py
+++ b/solution.py
@@ -14,6 +14,7 @@
 CORES = 2
 VMEM_LIMIT = 56 * 1024 * 1024
 SMALL_LIMIT = 14 * 1024 * 1024
+BACKWARD_LIMIT = 46 * 1024 * 1024
 
 F32 = jnp.float32
 BF16 = jnp.bfloat16
@@ -89,7 +90,7 @@
     )(x, stream, out_weight, gain, bias, proj_weight)
 
 
-def teacher_kernel(parts, count, tokens, order_ref, rows_ref, states_ref, wq_ref, wk_ref, *rest):
+def teacher_kernel(parts, count, tokens, order_ref, from_ref, rows_ref, states_ref, wq_ref, wk_ref, *rest):
     pieces, out_ref, token_ref = rest[:parts], rest[parts], rest[parts + 1]
     w_s, own_s, q_s, g_s, key_s, e_s, map_s, q_sem, key_sem, w_sem, own_sem = rest[parts + 2 :]
     depth = q_s.shape[1]
@@ -107,7 +108,7 @@
     queries = pltpu.make_async_copy(states_ref.at[pl.ds(0, first)], q_s, q_sem)
     gathered = [
         pltpu.make_async_copy(
-            pieces[a],
+            pieces[a].at[pl.ds(0, w_s.shape[0])],
             w_s.at[:, pl.ds(pl.multiple_of(rows_ref[a] * part_rows, part_rows), part_rows), :],
             w_sem.at[a],
         )
@@ -159,21 +160,21 @@
         turned = jnp.concatenate([both, filler], axis=0).T
         for v in range(side):
             map_s[g * side + v] = turned[v * tokens : (v + 1) * tokens, :seq].astype(BF16)
+    per = count // parts
     for n in range(count):
-        out_ref[n] = map_s[order_ref[n]]
+        out_ref[n] = map_s[order_ref[from_ref[n // per], n % per]]
     token_ref[...] = jnp.zeros_like(token_ref)
 
 
-def teacher_maps(order, rows, states, wq, wk, pieces, count, tokens):
+def teacher_maps(order, source, rows, slices, states, wq, wk, pieces, count, tokens):
     total, depth = states.shape
     keys = total - count * tokens
     heads = wq.shape[1]
     parts = len(pieces)
-    slices = pieces[0].shape[0]
     blocks = keys // split_rows(keys, 720)
     return pl.pallas_call(
         functools.partial(teacher_kernel, parts, count, tokens),
-        in_specs=[SMEM, SMEM] + [ANY] * (3 + parts),
+        in_specs=[SMEM] * 3 + [ANY] * (3 + parts),
         out_specs=[VMEM, VMEM],
         out_shape=[jax.ShapeDtypeStruct((count, tokens, keys // count), BF16), TOKEN],
         scratch_shapes=[
@@ -192,17 +193,39 @@
         compiler_params=params(),
         cost_estimate=cost(8 * count * tokens * depth * depth, 2 * states.size + 4 * depth * depth),
         name="teacher_maps",
-    )(order, rows, states, wq, wk, *pieces)
-
-
-def scores_kernel(tokens, count, group_queries, qidx_ref, len_ref, payload_ref, emb_ref, wp_ref, after_ref,
-                  prob_ref, log_ref, units_ref, qunit_ref, qdir_ref, qlen_ref, qs_s, dir_s):
+    )(order, source, rows, states, wq, wk, *pieces)
+
+
+def rider_copies(pieces, slices, held, sem):
+    part = pieces[0].shape[1]
+    return [
+        pltpu.make_async_copy(
+            pieces[a].at[slices + x], held.at[a, pl.ds(x * part, part)], sem.at[a * (pieces[0].shape[0] - slices) + x]
+        )
+        for a in range(len(pieces))
+        for x in range(pieces[0].shape[0] - slices)
+    ]
+
+
+def rider_states(held, a, each, width):
+    heads = held.shape[2]
+    return jnp.concatenate([held[a, n * each : (n + 1) * each] for n in range(width // heads)], axis=1)
+
+
+def scores_kernel(tokens, count, group_queries, slices, parts, qidx_ref, len_ref, emb_ref, wp_ref, after_ref, *rest):
+    pieces = rest[:parts]
+    (prob_ref, log_ref, units_ref, qunit_ref, qdir_ref, qlen_ref, qs_s, dir_s, held_s, sem) = rest[parts:]
+    copies = rider_copies(pieces, slices, held_s, sem)
+    for copy in copies:
+        copy.start()
     total, emb = emb_ref.shape
     seq = total // count
     sub = split_rows(total, 128)
     each = group_queries * tokens
-    for k in range(payload_ref.shape[0]):
-        qs_s[k * each : (k + 1) * each] = payload_ref[k, :each]
+    for copy in copies:
+        copy.wait()
+    for a in range(parts):
+        qs_s[a * each : (a + 1) * each] = rider_states(held_s, a, each, qs_s.shape[1])
     qe = dot(qs_s[...], wp_ref[...], 1, 0)
     length = jnp.sqrt(jnp.sum(qe * qe, axis=-1, keepdims=True) + epsilon)
     qdir = qe / length
@@ -223,13 +246,16 @@
         log_ref[r] = logits - jnp.log(student_total)
 
 
-def student_scores(qidx, lens, payload, embeds, wp, after, count, tokens, group_queries):
+def student_scores(qidx, lens, embeds, wp, after, pieces, slices, count, tokens, group_queries):
     total, emb = embeds.shape
     seq = total // count
-    queries = payload.shape[0] * group_queries
+    parts = len(pieces)
+    queries = parts * group_queries
+    riders, part, heads = pieces[0].shape
+    riders -= slices
     return pl.pallas_call(
-        functools.partial(scores_kernel, tokens, count, group_queries),
-        in_specs=[SMEM, SMEM, VMEM, VMEM, VMEM, ANY],
+        functools.partial(scores_kernel, tokens, count, group_queries, slices, parts),
+        in_specs=[SMEM, SMEM, VMEM, VMEM] + [ANY] * (1 + parts),
         out_specs=[VMEM] * 6,
         out_shape=[
             jax.ShapeDtypeStruct((count, tokens, seq), F32),
@@ -239,11 +265,16 @@
             jax.ShapeDtypeStruct((queries * tokens, emb), F32),
             jax.ShapeDtypeStruct((queries * tokens, 128), F32),
         ],
-        scratch_shapes=[pltpu.VMEM((queries * tokens, payload.shape[2]), BF16), pltpu.VMEM((total, emb), F32)],
+        scratch_shapes=[
+            pltpu.VMEM((queries * tokens, wp.shape[0]), BF16),
+            pltpu.VMEM((total, emb), F32),
+            pltpu.VMEM((parts, riders * part, heads), BF16),
+            pltpu.SemaphoreType.DMA((parts * riders,)),
+        ],
         compiler_params=params(),
         cost_estimate=cost(1e9, 4 * total * emb),
         name="student_scores",
-    )(qidx, lens, payload, embeds, wp, after)
+    )(qidx, lens, embeds, wp, after, *pieces)
 
 
 def two_parts(a, b):
@@ -253,22 +284,22 @@
 
 
 def backward_kernel(
-    tokens, count, blocks, group_queries,
-    qidx_ref, midx_ref, len_ref, core_ref,
-    maps_in, prob_in, log_in, units_in, qunit_in, emb_in, x_in, normed_in, inv_in, payload_in,
+    tokens, count, blocks, group_queries, slices, parts,
+    qidx_ref, midx_ref, len_ref, core_ref, *rest,
+):
+    pieces = rest[:parts]
+    (maps_in, prob_in, log_in, units_in, qunit_in, emb_in, x_in, normed_in, inv_in,
     qdir_ref, qlen_ref, gain_ref, bias_ref, wp_ref, wpt_ref,
     sg_out, send_ref, keep_ref,
-    maps_s, prob_s, log_s, units_s, qunit_s, emb_s, x_s, normed_s, inv_s, payload_s,
-    up_s, eg_s, mean_s, along_s, un_s, qg_s, hg_both, sg_s, wo_s, nt_s, right_s,
-    first_sem, block_sem, out_sem, last_sem,
-):
+    maps_s, prob_s, log_s, units_s, qunit_s, emb_s, x_s, normed_s, inv_s, held_s,
+    up_s, eg_s, mean_s, along_s, un_s, qg_s, hg_s, sg_s, wo_s, nt_s, right_s,
+    first_sem, block_sem, out_sem, last_sem) = rest[parts:]
     total, width = normed_s.shape
     emb = emb_s.shape[1]
     seq = total // count
     rows = total // blocks
-    sub = rows
+    sub = split_rows(rows, 256)
     thin = split_rows(total, 128)
-    step = split_rows(sub, 48)
     first = [
         pltpu.make_async_copy(src, dst, first_sem.at[n])
         for n, (src, dst) in enumerate(
@@ -288,7 +319,7 @@
         ]
         for b in range(blocks)
     ]
-    last = pltpu.make_async_copy(payload_in, payload_s, last_sem)
+    last = rider_copies(pieces, slices, held_s, last_sem)
     for copy in first:
         copy.start()
     gain, bias = one_row(gain_ref), one_row(bias_ref)
@@ -302,7 +333,8 @@
     for pair in loads:
         for copy in pair:
             copy.start()
-    last.start()
+    for copy in last:
+        copy.start()
 
     spread = jnp.zeros((tokens, 1), F32)
     for r in range(count):
@@ -336,48 +368,32 @@
         mean_s[b : b + thin] = inverse * (jnp.sum(eg * gain_w, axis=-1, keepdims=True) / width)
         along_s[b : b + thin] = inverse * (jnp.sum(eg * (e - bias_w), axis=-1, keepdims=True) / width)
 
-    def wide(b):
-        hg_s = hg_both.at[b // sub % 2]
-        hg_s[...] = dot(eg_s[b : b + sub], wpt_ref[...], 1, 0)
-        for c in range(b, b + sub, step):
-            inverse, mean, along = inv_s[c : c + step], mean_s[c : c + step], along_s[c : c + step]
-            for v in range(0, width, 128):
-                scaled = hg_s[c - b : c - b + step, v : v + 128] * gain[:, v : v + 128]
-                normed = normed_s[c : c + step, v : v + 128].astype(F32)
-                sg_s[c : c + step, v : v + 128] = (inverse * scaled - mean - normed * along).astype(BF16)
-
-    def products(b, part, parts):
-        span = width // parts
-        value = dot(x_s[b, part * span : (part + 1) * span], sg_s[b * rows : (b + 1) * rows], 1, 0)
-        if b == 0:
-            wo_s[part * span : (part + 1) * span] = value
-        else:
-            wo_s[part * span : (part + 1) * span] += value
-
-    parts = 1
-    stores = []
-    for b in range(blocks):
-        for copy in loads[b]:
-            copy.wait()
-        for n in range(rows // sub):
-            wide(b * rows + n * sub)
-            if b > 0 and n < parts:
-                products(b - 1, n, parts)
-        stores.append(
-            pltpu.make_async_copy(
-                sg_s.at[pl.ds(b * rows, rows)], sg_out.at[pl.ds(b * rows, rows)], out_sem.at[b]
-            )
-        )
-        stores[-1].start()
-        value = dot(eg_s[b * rows : (b + 1) * rows], normed_s[b * rows : (b + 1) * rows], 0, 0)
-        if b == 0:
-            nt_s[...] = value
-        else:
-            nt_s[...] += value
-    for n in range(parts):
-        products(blocks - 1, n, parts)
-
-    last.wait()
+    wo_s[...] = jnp.zeros_like(wo_s)
+    nt_s[...] = jnp.zeros_like(nt_s)
+
+    def wide(b, _):
+        base = pl.multiple_of(b * rows, rows)
+        part = pl.ds(base, rows)
+        pltpu.make_async_copy(normed_in.at[part], normed_s.at[part], block_sem.at[2 * b]).wait()
+        for n in range(0, rows, sub):
+            hg_s[n : n + sub] = dot(eg_s[pl.ds(base + n, sub)], wpt_ref[...], 1, 0)
+            for c in range(n, n + sub, 16):
+                here = pl.ds(base + c, 16)
+                inverse, mean, along = inv_s[here], mean_s[here], along_s[here]
+                for v in range(0, width, 128):
+                    scaled = hg_s[c : c + 16, v : v + 128] * gain[:, v : v + 128]
+                    normed = normed_s[here, v : v + 128].astype(F32)
+                    sg_s[here, v : v + 128] = (inverse * scaled - mean - normed * along).astype(BF16)
+        pltpu.make_async_copy(sg_s.at[part], sg_out.at[part], out_sem.at[b]).start()
+        pltpu.make_async_copy(x_in.at[b], x_s.at[b], block_sem.at[2 * b + 1]).wait()
+        wo_s[...] += dot(x_s[b], sg_s[part], 1, 0)
+        nt_s[...] += dot(eg_s[part], normed_s[part], 0, 0)
+        return 0
+
+    lax.fori_loop(0, blocks, wide, 0)
+
+    for copy in last:
+        copy.wait()
     qg = qg_s[...].reshape(qdir_ref.shape)
     qdir = qdir_ref[...]
     qeg = (qg - qdir * jnp.sum(qdir * qg, axis=-1, keepdims=True)) / qlen_ref[:, :1]
@@ -385,8 +401,8 @@
     low = (qeg - high.astype(F32)).astype(BF16)
     each = group_queries * tokens
     proj_query = jnp.zeros((emb, width), F32)
-    for k in range(payload_s.shape[0]):
-        qs = payload_s[k, :each]
+    for k in range(parts):
+        qs = rider_states(held_s, k, each, width)
         part = slice(k * each, (k + 1) * each)
         proj_query = proj_query + (dot(high[part], qs, 0, 0) + dot(low[part], qs, 0, 0))
     nt = nt_s[...]
@@ -408,35 +424,39 @@
         for c in range(half // chunk):
             ref[c, :, :width] = left[c * chunk : (c + 1) * chunk]
             ref[c, :, width:] = right[c * chunk : (c + 1) * chunk]
-    for copy in stores:
-        copy.wait()
+    for b in range(blocks):
+        part = pl.ds(b * rows, rows)
+        pltpu.make_async_copy(sg_s.at[part], sg_out.at[part], out_sem.at[b]).wait()
 
 
 def student_backward(
-    qidx, midx, lens, core, maps, scores, payload, embeds, x, normed, inverse, gain, bias, wp, wpt,
+    qidx, midx, lens, core, maps, scores, pieces, slices, embeds, x, normed, inverse, gain, bias, wp, wpt,
     count, tokens, group_queries, chunk,
 ):
     total, width = normed.shape
     emb = wp.shape[1]
     blocks = x.shape[0]
-    sub = total // blocks
     chunks = width // CORES // chunk
     prob, log, units, qunit, qdir, qlen = scores
-    manual = [maps, prob, log, units, qunit, embeds, x, normed, inverse, payload]
+    manual = [maps, prob, log, units, qunit, embeds, x, normed, inverse]
+    parts = len(pieces)
+    riders, part, heads = pieces[0].shape
+    riders -= slices
     packed = jax.ShapeDtypeStruct((chunks, chunk, width + emb + 128), BF16)
     return pl.pallas_call(
-        functools.partial(backward_kernel, tokens, count, blocks, group_queries),
-        in_specs=[SMEM] * 4 + [ANY] * len(manual) + [VMEM] * 6,
+        functools.partial(backward_kernel, tokens, count, blocks, group_queries, slices, parts),
+        in_specs=[SMEM] * 4 + [ANY] * (parts + len(manual)) + [VMEM] * 6,
         out_specs=[ANY, VMEM, VMEM],
         scratch_shapes=[pltpu.VMEM(a.shape, a.dtype) for a in manual]
         + [
+            pltpu.VMEM((parts, riders * part, heads), BF16),
             pltpu.VMEM((total, emb), F32),
             pltpu.VMEM((total, emb), BF16),
             pltpu.VMEM((total, 128), F32),
             pltpu.VMEM((total, 128), F32),
             pltpu.VMEM((count, tokens, emb), F32),
             pltpu.VMEM(qunit.shape, F32),
-            pltpu.VMEM((2, sub, width), F32),
+            pltpu.VMEM((total // blocks, width), F32),
             pltpu.VMEM((total, width), BF16),
             pltpu.VMEM((width, width), F32),
             pltpu.VMEM((emb, width), F32),
@@ -444,34 +464,34 @@
             pltpu.SemaphoreType.DMA((7,)),
             pltpu.SemaphoreType.DMA((2 * blocks,)),
             pltpu.SemaphoreType.DMA((blocks,)),
-            pltpu.SemaphoreType.DMA,
+            pltpu.SemaphoreType.DMA((parts * riders,)),
         ],
         out_shape=[jax.ShapeDtypeStruct((total, width), BF16), packed, packed],
-        compiler_params=params(),
+        compiler_params=pltpu.CompilerParams(vmem_limit_bytes=BACKWARD_LIMIT),
         cost_estimate=cost(2 * total * width * (width + 2 * emb), 8 * total * width),
         name="student_backward",
-    )(qidx, midx, lens, core, *manual, qdir, qlen, gain, bias, wp, wpt)
+    )(qidx, midx, lens, core, *pieces, *manual, qdir, qlen, gain, bias, wp, wpt)
 
 
 def context_kernel(sg_ref, wo_ref, after_ref, out_ref, token_ref):
     token_ref[...] = jnp.zeros_like(token_ref)
-    out_ref[...] = dot(sg_ref[...], wo_ref[...], 1, 0).astype(BF16)
-
-
-def context_grad(sg, weight_turned, after):
+    out_ref[...] = dot(sg_ref[...], wo_ref[...], 1, 1).astype(BF16)
+
+
+def context_grad(sg, out_weight, after):
     total, width = sg.shape
     rows = split_rows(total, 720)
     block = pl.BlockSpec((rows, width), lambda s: (s, 0))
     return pl.pallas_call(
         context_kernel,
         grid=(total // rows,),
-        in_specs=[block, pl.BlockSpec(weight_turned.shape, lambda s: (0, 0)), ANY],
+        in_specs=[block, pl.BlockSpec(out_weight.shape, lambda s: (0, 0)), ANY],
         out_specs=[block, pl.BlockSpec(TOKEN.shape, lambda s: (0, 0))],
         out_shape=[jax.ShapeDtypeStruct(sg.shape, BF16), TOKEN],
         compiler_params=params(),
         cost_estimate=cost(2 * total * width * width, 4 * total * width),
         name="context_grad",
-    )(sg, weight_turned, after)
+    )(sg, out_weight, after)
 
 
 def split_sum_kernel(inputs, outputs, after, index_ref, *rest):
@@ -606,41 +626,50 @@
     positions = jnp.sum(
         jnp.where(place[:, None] == rows[None, :], (passage_dest % count)[:, None], 0), axis=0
     )
-    queries = query_states.reshape(group_queries * tokens, width)
-    extra = jnp.pad(positions.astype(BF16)[None, :], ((0, 15), (0, width - count)))
-    payload = jnp.concatenate([queries, extra], axis=0)
+    each = group_queries * tokens
+    states = query_states.reshape(each, width)
+    column_blocks = [states[:, n * heads : (n + 1) * heads] for n in range(width // heads)]
+    extra = jnp.pad(positions.astype(BF16)[None, :], ((0, 15), (0, heads - count)))
+    rider = jnp.concatenate(column_blocks + [extra], axis=0)
+
     part = depth // dp
     mine = jnp.stack(
         [lax.dynamic_slice_in_dim(w, me * part, part, 0) for w in (teacher_query, teacher_key)]
     )
-    payload, mine = lax.optimization_barrier((jnp.broadcast_to(payload[None], (dp,) + payload.shape), mine))
-    payload = lax.all_to_all(payload, "dp", split_axis=0, concat_axis=0, tiled=True)
-    along = jnp.concatenate([shift_t(mine, k) for k in range(1, nt)], axis=0)
-    along, payload = lax.optimization_barrier((along, payload))
+    rider = jnp.pad(rider, ((0, -rider.shape[0] % part), (0, 0))).reshape(-1, part, heads)
+    slices = 2 * (nt - 1)
+    along = jnp.concatenate([shift_t(mine, k) for k in range(1, nt)] + [rider], axis=0)
     pieces = [along] + [shift_chip(along, k) for k in range(1, chips)]
     shifts = jnp.arange(chips, dtype=jnp.int32)
     behind = (chip - shifts) % chips
     piece_rows = jnp.concatenate([behind * CORES + core, behind * CORES + 1 - core]).astype(jnp.int32)
     midx = place.astype(jnp.int32)
-    qidx = (passage_dest // per_query).astype(jnp.int32)
+    def piece_of(group):
+        return (chip - group // CORES) % chips + jnp.where(group % CORES == core, 0, chips)
+
+    qidx = passage_dest // per_query - dest_group * group_queries + piece_of(dest_group) * group_queries
+    qidx = qidx.astype(jnp.int32)
+    source = piece_of(jnp.arange(dp, dtype=jnp.int32)).astype(jnp.int32)
 
     gain2, bias2 = gain.reshape(-1, 128), bias.reshape(-1, 128)
     x = flat(context)
     normed, embeds, inverse, turned = student_forward(x, flat(stream), out_weight, gain2, bias2, proj_weight)
-    pieces[1:], payload, normed, embeds, inverse, turned, weight_turned, proj_turned = lax.optimization_barrier(
-        (pieces[1:], payload, normed, embeds, inverse, turned, out_weight.T, proj_weight.T)
+    pieces[1:], normed, embeds, inverse, turned, proj_turned = lax.optimization_barrier(
+        (pieces[1:], normed, embeds, inverse, turned, proj_weight.T)
     )
     pieces = pieces + [swap_core(a) for a in pieces]
-    told = payload[:, group_queries * tokens, :count].astype(jnp.int32)
-    order = lax.dynamic_slice_in_dim(told, me * per, per, 1).reshape(-1)
+    told = [a[slices:].reshape(-1, heads)[width // heads * each, :count] for a in pieces]
+    order = lax.dynamic_slice_in_dim(jnp.stack(told), me * per, per, 1).astype(jnp.int32)
     maps, token = teacher_maps(
-        order, piece_rows, flat(teacher_states), teacher_query, teacher_key, pieces, count, tokens
+        order, source, piece_rows, slices, flat(teacher_states), teacher_query, teacher_key, pieces, count, tokens
     )
     maps = lax.all_to_all(maps, "dp", split_axis=0, concat_axis=0, tiled=True)
-    scores = student_scores(qidx, passage_len, payload, embeds, proj_weight, token, count, tokens, group_queries)
+    scores = student_scores(
+        qidx, passage_len, embeds, proj_weight, token, pieces, slices, count, tokens, group_queries
+    )
     chunk = width // (CORES * chips * nt)
     sg, send, keep = student_backward(
-        qidx, midx, passage_len, core.astype(jnp.int32).reshape(1), maps, scores, payload,
+        qidx, midx, passage_len, core.astype(jnp.int32).reshape(1), maps, scores, pieces, slices,
         embeds, turned, normed, inverse, gain2, bias2, proj_weight, proj_turned,
         count, tokens, group_queries, chunk,
     )
@@ -649,7 +678,7 @@
     t_shifts = jnp.arange(nt, dtype=jnp.int32)
     t_ahead = ((mt + t_shifts) % nt).astype(jnp.int32)
     parts, token = split_sum([keep, swap_core(send)], ahead, "sum_cores")
-    grad_context, token = context_grad(sg, weight_turned, token)
+    grad_context, token = context_grad(sg, out_weight, token)
     parts = [parts[0]] + [shift_chip(parts[k], k) for k in range(1, chips)]
     parts, _ = split_sum(parts, t_ahead, "sum_plane", (token,))
     parts = [parts[0]] + [shift_t(parts[k], k) for k in range(1, nt)]

time: 143 us -> 148 us (1.035)
  local copies, waits for them, and re-layouts: 9.41 us -> 15.6 us
  starting transfers between devices: 38 us -> 35.1 us
    unnamed x32 -> x65, local copies, waits for them, and re-layouts: 7 us -> 13.7 us
    ppermute x9, waiting for transfers between devices: 14.6 us -> 9.06 us  [shift_t(): return lax.ppermute(x, 'tensor', [(t, (t + k) % nt) for t in range(nt)])]
    ppermute x9, waiting for transfers between devices: 5.31 us -> 10.7 us  [shift_chip(): lax.ppermute(x, 'dp', [(c * CORES + o, (c + k) % chips * CORES + o) for c...]
    all_to_all x1 -> x0, starting transfers between devices: 5.17 us -> none  [local(): lax.all_to_all(payload, 'dp', split_axis=0, concat_axis=0, tiled=True)]
    ppermute x9, starting transfers between devices: 15.2 us -> 17.5 us  [shift_t(): return lax.ppermute(x, 'tensor', [(t, (t + k) % nt) for t in range(nt)])]
    add x0 -> x3, other arithmetic: none -> 1.84 us  [the longest x2 1.83 us: piece_of(): (chip - group // CORES) % chips + jnp.where(group % CORES == core, 0, chips)]
    ppermute x9, waiting for transfers between devices: 4.51 us -> 6 us  [swap_core(): return lax.ppermute(x, 'dp', [(d, d ^ 1) for d in range(dp)])]
  transfers between devices with their start and end apart: 29 -> 28, of which waited for: 17 -> 19; matrix products, arithmetic and copies ran while one was open for 3% -> 3% of each run, Pallas kernels for 17% -> 17%
where the time goes in v5:
time: 148 us; the launch traced here: 147 us
  Pallas kernels  64.4 us (44%)
  starting transfers between devices  35.1 us (24%)
  waiting for transfers between devices  27.2 us (18%)
  local copies, waits for them, and re-layouts  15.6 us (11%)
  other arithmetic  3.12 us (2%)
    pallas_call x1, Pallas kernels, student_backward(): pl.pallas_call(functools.partial(backward_kernel, tokens, count, blocks,...  21.9 us
    ppermute x9, starting transfers between devices, shift_t(): return lax.ppermute(x, 'tensor', [(t, (t + k) % nt) for t in range(nt)])  17.5 us
    unnamed x65, local copies, waits for them, and re-layouts  13.7 us
    pallas_call x1, Pallas kernels, student_forward(): pl.pallas_call(forward_kernel, grid=(total // rows,), in_specs=[block(wid...  12.5 us
    pallas_call x1, Pallas kernels, teacher_maps(): pl.pallas_call(functools.partial(teacher_kernel, parts, count, tokens), i...  12.5 us
    ppermute x9, starting transfers between devices, shift_chip(): lax.ppermute(x, 'dp', [(c * CORES + o, (c + k) % chips * CORES + o) for c...  12.2 us
    ppermute x9, waiting for transfers between devices, shift_chip(): lax.ppermute(x, 'dp', [(c * CORES + o, (c + k) % chips * CORES + o) for c...  10.7 us
    ppermute x9, waiting for transfers between devices, shift_t(): return lax.ppermute(x, 'tensor', [(t, (t + k) % nt) for t in range(nt)])  9.06 us
  transfers between devices with their start and end apart: 28, of which 19 were waited for; matrix products, arithmetic and copies ran while one was open for 3% of the time, Pallas kernels for 17%

profile of v5, /device:TPU:0, one launch (start us, length us, event | category | flops | bytes accessed | tf_op | source)
XLA Modules:
  0.0 146.6 jit_solution(3682534441843535003)
XLA Ops:
  1.5 3.1 %collective-permute-start = (bf16[2,128,256]{2,1,0:T(8,128)(2,1)S(1)}, bf16[2,128,256]{2,1,0:T(8,128)(2,1)S(1)}, u32[]{:S(2)}, u32[]{:S(2)}) collective-permute-start(bf16[2,128,256]{2,1,0:T(8,128)(2,1)S(1)} %pad_maximum_fusion.2), channel_id=1, source_target_pairs={{0,1},{1,2},{2,3},{3,0},{4,5},{5,6},{6,7},{7,4},{8,9},{9,10},{10,1... | collective-permute-start | bytes 393224 | tf_op jit(solution)/shard_map/ppermute | solution.py:618
  4.6 2.6 %collective-permute-start.1 = (bf16[2,128,256]{2,1,0:T(8,128)(2,1)S(1)}, bf16[2,128,256]{2,1,0:T(8,128)(2,1)S(1)}, u32[]{:S(2)}, u32[]{:S(2)}) collective-permute-start(bf16[2,128,256]{2,1,0:T(8,128)(2,1)S(1)} %pad_maximum_fusion.2), channel_id=1, source_target_pairs={{0,2},{1,3},{2,0},{3,1},{4,6},{5,7},{6,4},{7,5},{8,10},{9,11},{10,... | collective-permute-start | bytes 393224 | tf_op jit(solution)/shard_map/ppermute | solution.py:618
  10.9 1.7 %copy.20 = bf16[768,128]{0,1:T(8,128)(2,1)} copy(bf16[768,128]{1,0:T(8,128)(2,1)} %rest_21_.1) | data formatting | bytes 393216 | tf_op args[5]
  12.6 3.2 %collective-permute-done.1 = bf16[2,128,256]{2,1,0:T(8,128)(2,1)S(1)} collective-permute-done((bf16[2,128,256]{2,1,0:T(8,128)(2,1)S(1)}, bf16[2,128,256]{2,1,0:T(8,128)(2,1)S(1)}, u32[]{:S(2)}, u32[]{:S(2)}) %collective-permute-start.1) | collective-permute-done | bytes 131104 | tf_op jit(solution)/shard_map/ppermute | solution.py:618
  15.9 1.5 %collective-permute-start.3 = (bf16[7,128,256]{2,1,0:T(8,128)(2,1)S(1)}, bf16[7,128,256]{2,1,0:T(8,128)(2,1)S(1)}, u32[]{:S(2)}, u32[]{:S(2)}) collective-permute-start(bf16[7,128,256]{2,1,0:T(8,128)(2,1)S(1)} %pad_maximum_fusion.rest_0_), channel_id=1, source_target_pairs={{0,8},{4,12},{8,16},{12,20},{16,24},{20,28},{24,0},{28,4},{1,9},{5... | collective-permute-start | bytes 1376264 | tf_op jit(solution)/shard_map/ppermute | solution.py:610
  17.5 1.5 %collective-permute-start.4 = (bf16[7,128,256]{2,1,0:T(8,128)(2,1)S(1)}, bf16[7,128,256]{2,1,0:T(8,128)(2,1)S(1)}, u32[]{:S(2)}, u32[]{:S(2)}) collective-permute-start(bf16[7,128,256]{2,1,0:T(8,128)(2,1)S(1)} %pad_maximum_fusion.rest_0_), channel_id=1, source_target_pairs={{0,16},{4,20},{8,24},{12,28},{16,0},{20,4},{24,8},{28,12},{1,17},{... | collective-permute-start | bytes 1376264 | tf_op jit(solution)/shard_map/ppermute | solution.py:610
  21.1 12.5 %student_forward.1 = (bf16[2880,768]{1,0:T(8,128)(2,1)}, f32[2880,128]{1,0:T(8,128)}, f32[2880,128]{1,0:T(8,128)}, bf16[4,768,720]{2,1,0:T(8,128)(2,1)}) custom-call(bf16[2880,768]{1,0:T(8,128)(2,1)} %bitcast.59, bf16[2880,768]{1,0:T(8,128)(2,1)} %bitcast.60, bf16[768,768]{1,0:T(8,128)(2,1)} %wo_ref.3, f32[6,128]{1,0:T(8,128)} %bitcast.50, ...), custom_call_target="tpu_custom_call" | custom-call | flops 3963617280 | bytes 17694720 | tf_op jit(solution)/shard_map/student_forward/pallas_call | solution.py:75
  33.7 5.4 %collective-permute-done.4.rest_2_ = bf16[7,128,256]{2,1,0:T(8,128)(2,1)S(1)} collective-permute-done((bf16[7,128,256]{2,1,0:T(8,128)(2,1)S(1)}, bf16[7,128,256]{2,1,0:T(8,128)(2,1)S(1)}, u32[]{:S(2)}, u32[]{:S(2)}) %collective-permute-start.4) | collective-permute-done | bytes 458784 | tf_op jit(solution)/shard_map/ppermute | solution.py:610
  43.9 12.5 %teacher_maps.1 = (bf16[16,32,180]{2,1,0:T(8,128)(2,1)}, f32[8,128]{1,0:T(8,128)}) custom-call(s32[8,2]{1,0:T(8,128)} %dynamic-slice_convert_fusion.order_ref, s32[8]{0:T(128)} %get-tuple-element.92.from_ref, s32[8]{0:T(128)} %get-tuple-element.93.rows_ref, bf16[3392,1024]{1,0:T(8,128)(2,1)} %bitcast.58, bf16[1024,256]{1,0:T(8,128)(2,1)} %wq_ref.1, ...), custom_call_target="tpu_custom_call" | custom-call | flops 4294967296 | bytes 11141120 | tf_op jit(solution)/shard_map/teacher_maps/pallas_call | solution.py:175
  56.5 4.5 %all-to-all-start = ((bf16[16,32,180]{2,1,0:T(8,128)(2,1)}), bf16[16,32,180]{2,1,0:T(8,128)(2,1)}, u32[]{:S(2)}, u32[]{:S(2)}) async-start(bf16[16,32,180]{2,1,0:T(8,128)(2,1)} %get-tuple-element.52), calls=%async_computation | async-start | bytes 524288 | tf_op jit(solution)/shard_map/all_to_all | solution.py:666
  61.0 5.3 %student_scores.1 = (f32[16,32,180]{2,1,0:T(8,128)}, f32[16,32,180]{2,1,0:T(8,128)}, bf16[16,180,128]{2,1,0:T(8,128)(2,1)}, bf16[8,32,128]{2,1,0:T(8,128)(2,1)}, f32[256,128]{1,0:T(8,128)}, /*index=5*/f32[256,128]{1,0:T(8,128)}) custom-call(s32[16]{0:T(128)} %get-tuple-element.84.qidx_ref, s32[16]{0:T(128)} %len_ref.3, ...), custom_call_target="tpu_custom_call" | custom-call | flops 1000000000 | bytes 1474560 | tf_op jit(solution)/shard_map/student_scores/pallas_call | solution.py:256
  75.7 21.9 %student_backward.1 = (bf16[2880,768]{1,0:T(8,128)(2,1)}, bf16[16,24,1024]{2,1,0:T(8,128)(2,1)}, bf16[16,24,1024]{2,1,0:T(8,128)(2,1)S(1)}) custom-call(s32[16]{0:T(128)S(1)} %copy-done.26, s32[16]{0:T(128)S(1)} %multiply_add_fusion.midx_ref, s32[16]{0:T(128)S(1)} %copy-done.30, s32[1]{0:T(128)} %bitcast.core_ref, bf16[7,128,256]{2,1,0:T(8,128)(2,1)S(1)} %copy-done.1, ...), custom_call_target="tpu_custom_call" | custom-call | flops 4529848320 | bytes 17694720 | tf_op jit(solution)/shard_map/student_backward/pallas_call | solution.py:446
  98.5 2.5 %collective-permute-done.10.rest_1_ = bf16[16,24,1024]{2,1,0:T(8,128)(2,1)S(1)} collective-permute-done((bf16[16,24,1024]{2,1,0:T(8,128)(2,1)}, bf16[16,24,1024]{2,1,0:T(8,128)(2,1)S(1)}, u32[]{:S(2)}, u32[]{:S(2)}) %collective-permute-start.10) | collective-permute-done | bytes 786464 | tf_op jit(solution)/shard_map/ppermute | solution.py:615
  105.5 1.7 %collective-permute-start.13 = (bf16[4,24,1024]{2,1,0:T(8,128)(2,1)S(1)}, bf16[4,24,1024]{2,1,0:T(8,128)(2,1)S(1)}, u32[]{:S(2)}, u32[]{:S(2)}) collective-permute-start(bf16[4,24,1024]{2,1,0:T(8,128)(2,1)S(1)} %get-tuple-element.70), channel_id=1, source_target_pairs={{0,24},{4,28},{8,0},{12,4},{16,8},{20,12},{24,16},{28,20},{1,25},{... | collective-permute-start | bytes 589832 | tf_op jit(solution)/shard_map/ppermute | solution.py:610
  107.1 7.5 %context_grad.1 = (bf16[2880,768]{1,0:T(8,128)(2,1)}, f32[8,128]{1,0:T(8,128)}) custom-call(bf16[2880,768]{1,0:T(8,128)(2,1)} %get-tuple-element.71.sg_ref, bf16[768,768]{1,0:T(8,128)(2,1)} %wo_ref.3, f32[8,128]{1,0:T(8,128)} %copy-done.31), custom_call_target="tpu_custom_call" | custom-call | flops 3397386240 | bytes 8847360 | tf_op jit(solution)/shard_map/context_grad/pallas_call | solution.py:485
  117.1 3.4 %collective-permute-start.14 = (bf16[24,1024]{1,0:T(8,128)(2,1)S(1)}, bf16[24,1024]{1,0:T(8,128)(2,1)S(1)}, u32[]{:S(2)}, u32[]{:S(2)}) collective-permute-start(bf16[24,1024]{1,0:T(8,128)(2,1)S(1)} %get-tuple-element.75), channel_id=1, source_target_pairs={{0,1},{1,2},{2,3},{3,0},{4,5},{5,6},{6,7},{7,4},{8,9},{9,10},{10,1... | collective-permute-start | bytes 147464 | tf_op jit(solution)/shard_map/ppermute | solution.py:618
  121.0 1.8 %collective-permute-start.16 = (bf16[24,1024]{1,0:T(8,128)(2,1)S(1)}, bf16[24,1024]{1,0:T(8,128)(2,1)S(1)}, u32[]{:S(2)}, u32[]{:S(2)}) collective-permute-start(bf16[24,1024]{1,0:T(8,128)(2,1)S(1)} %get-tuple-element.77), channel_id=1, source_target_pairs={{0,3},{1,0},{2,1},{3,2},{4,7},{5,4},{6,5},{7,6},{8,11},{9,8},{10,9... | collective-permute-start | bytes 147464 | tf_op jit(solution)/shard_map/ppermute | solution.py:618
  123.2 2.5 %collective-permute-done.15.refs_2_ = bf16[24,1024]{1,0:T(8,128)(2,1)S(1)} collective-permute-done((bf16[24,1024]{1,0:T(8,128)(2,1)S(1)}, bf16[24,1024]{1,0:T(8,128)(2,1)S(1)}, u32[]{:S(2)}, u32[]{:S(2)}) %collective-permute-start.15) | collective-permute-done | bytes 49184 | tf_op jit(solution)/shard_map/ppermute | solution.py:618
  126.9 2.5 %collective-permute-start.18 = (bf16[24,1024]{1,0:T(8,128)(2,1)S(1)}, bf16[24,1024]{1,0:T(8,128)(2,1)S(1)}, u32[]{:S(2)}, u32[]{:S(2)}) collective-permute-start(bf16[24,1024]{1,0:T(8,128)(2,1)S(1)} %sum_tensor.1), channel_id=1, source_target_pairs={{0,2},{1,3},{2,0},{3,1},{4,6},{5,7},{6,4},{7,5},{8,10},{9,11},{10,... | collective-permute-start | bytes 147464 | tf_op jit(solution)/shard_map/ppermute | solution.py:618
  133.5 1.5 %collective-permute-start.20 = (bf16[4,24,1024]{2,1,0:T(8,128)(2,1)S(1)}, bf16[4,24,1024]{2,1,0:T(8,128)(2,1)S(1)}, u32[]{:S(2)}, u32[]{:S(2)}) collective-permute-start(bf16[4,24,1024]{2,1,0:T(8,128)(2,1)S(1)} %pad_maximum_fusion.1.rest_0_), channel_id=1, source_target_pairs={{0,8},{4,12},{8,16},{12,20},{16,24},{20,28},{24,0},{28,4},{1,9},{5... | collective-permute-start | bytes 589832 | tf_op jit(solution)/shard_map/ppermute | solution.py:610
  135.0 1.6 %collective-permute-start.21 = (bf16[4,24,1024]{2,1,0:T(8,128)(2,1)S(1)}, bf16[4,24,1024]{2,1,0:T(8,128)(2,1)S(1)}, u32[]{:S(2)}, u32[]{:S(2)}) collective-permute-start(bf16[4,24,1024]{2,1,0:T(8,128)(2,1)S(1)} %pad_maximum_fusion.1.rest_0_), channel_id=1, source_target_pairs={{0,16},{4,20},{8,24},{12,28},{16,0},{20,4},{24,8},{28,12},{1,17},{... | collective-permute-start | bytes 589832 | tf_op jit(solution)/shard_map/ppermute | solution.py:610
  137.9 2.4 %collective-permute-done.20.rest_1_ = bf16[4,24,1024]{2,1,0:T(8,128)(2,1)S(1)} collective-permute-done((bf16[4,24,1024]{2,1,0:T(8,128)(2,1)S(1)}, bf16[4,24,1024]{2,1,0:T(8,128)(2,1)S(1)}, u32[]{:S(2)}, u32[]{:S(2)}) %collective-permute-start.20) | collective-permute-done | bytes 196640 | tf_op jit(solution)/shard_map/ppermute | solution.py:610
  140.3 2.0 %collective-permute-done.21.rest_2_ = bf16[4,24,1024]{2,1,0:T(8,128)(2,1)S(1)} collective-permute-done((bf16[4,24,1024]{2,1,0:T(8,128)(2,1)S(1)}, bf16[4,24,1024]{2,1,0:T(8,128)(2,1)S(1)}, u32[]{:S(2)}, u32[]{:S(2)}) %collective-permute-start.21) | collective-permute-done | bytes 196640 | tf_op jit(solution)/shard_map/ppermute | solution.py:610
  144.1 2.3 %unpack.1 = (f32[32,24,768]{2,1,0:T(8,128)}, f32[32,24,128]{2,1,0:T(8,128)}, f32[6,128]{1,0:T(8,128)}, f32[6,128]{1,0:T(8,128)}, f32[1]{0:T(128)}) custom-call(s32[32]{0:T(128)S(1)} %add.139.index_ref, bf16[4,24,1024]{2,1,0:T(8,128)(2,1)S(1)} %pad_maximum_fusion.1.rest_0_, bf16[4,24,1024]{2,1,0:T(8,128)(2,1)S(1)} %collective-permute-done.20.rest_1_, ...), custom_call_target="tpu_custom_call" | custom-call | tf_op jit(solution)/shard_map/unpack/pallas_call | solution.py:566
  (144 shorter events, 37.9 us)
Async XLA Ops:
  1.5 11.1 %collective-permute-start = (bf16[2,128,256]{2,1,0:T(8,128)(2,1)S(1)}, bf16[2,128,256]{2,1,0:T(8,128)(2,1)S(1)}, u32[]{:S(2)}, u32[]{:S(2)}) collective-permute-start(bf16[2,128,256]{2,1,0:T(8,128)(2,1)S(1)} %pad_maximum_fusion.2), channel_id=1, source_target_pairs={{0,1},{1,2},{2,3},{3,0},{4,5},{5,6},{6,7},{7,4},{8,9},{9,10},{10,1... | collective-permute-start | bytes 393224 | tf_op jit(solution)/shard_map/ppermute | solution.py:618
  4.6 11.2 %collective-permute-start.1 = (bf16[2,128,256]{2,1,0:T(8,128)(2,1)S(1)}, bf16[2,128,256]{2,1,0:T(8,128)(2,1)S(1)}, u32[]{:S(2)}, u32[]{:S(2)}) collective-permute-start(bf16[2,128,256]{2,1,0:T(8,128)(2,1)S(1)} %pad_maximum_fusion.2), channel_id=1, source_target_pairs={{0,2},{1,3},{2,0},{3,1},{4,6},{5,7},{6,4},{7,5},{8,10},{9,11},{10,... | collective-permute-start | bytes 393224 | tf_op jit(solution)/shard_map/ppermute | solution.py:618
  7.2 8.6 %collective-permute-start.2 = (bf16[2,128,256]{2,1,0:T(8,128)(2,1)S(1)}, bf16[2,128,256]{2,1,0:T(8,128)(2,1)S(1)}, u32[]{:S(2)}, u32[]{:S(2)}) collective-permute-start(bf16[2,128,256]{2,1,0:T(8,128)(2,1)S(1)} %pad_maximum_fusion.2), channel_id=1, source_target_pairs={{0,3},{1,0},{2,1},{3,2},{4,7},{5,4},{6,5},{7,6},{8,11},{9,8},{10,9... | collective-permute-start | bytes 393224 | tf_op jit(solution)/shard_map/ppermute | solution.py:618
  15.9 17.7 %collective-permute-start.3 = (bf16[7,128,256]{2,1,0:T(8,128)(2,1)S(1)}, bf16[7,128,256]{2,1,0:T(8,128)(2,1)S(1)}, u32[]{:S(2)}, u32[]{:S(2)}) collective-permute-start(bf16[7,128,256]{2,1,0:T(8,128)(2,1)S(1)} %pad_maximum_fusion.rest_0_), channel_id=1, source_target_pairs={{0,8},{4,12},{8,16},{12,20},{16,24},{20,28},{24,0},{28,4},{1,9},{5... | collective-permute-start | bytes 1376264 | tf_op jit(solution)/shard_map/ppermute | solution.py:610
  17.5 21.6 %collective-permute-start.4 = (bf16[7,128,256]{2,1,0:T(8,128)(2,1)S(1)}, bf16[7,128,256]{2,1,0:T(8,128)(2,1)S(1)}, u32[]{:S(2)}, u32[]{:S(2)}) collective-permute-start(bf16[7,128,256]{2,1,0:T(8,128)(2,1)S(1)} %pad_maximum_fusion.rest_0_), channel_id=1, source_target_pairs={{0,16},{4,20},{8,24},{12,28},{16,0},{20,4},{24,8},{28,12},{1,17},{... | collective-permute-start | bytes 1376264 | tf_op jit(solution)/shard_map/ppermute | solution.py:610
  19.0 20.2 %collective-permute-start.5 = (bf16[7,128,256]{2,1,0:T(8,128)(2,1)S(1)}, bf16[7,128,256]{2,1,0:T(8,128)(2,1)S(1)}, u32[]{:S(2)}, u32[]{:S(2)}) collective-permute-start(bf16[7,128,256]{2,1,0:T(8,128)(2,1)S(1)} %pad_maximum_fusion.rest_0_), channel_id=1, source_target_pairs={{0,24},{4,28},{8,0},{12,4},{16,8},{20,12},{24,16},{28,20},{1,25},{... | collective-permute-start | bytes 1376264 | tf_op jit(solution)/shard_map/ppermute | solution.py:610
  33.6 6.2 %collective-permute-start.6 = (bf16[7,128,256]{2,1,0:T(8,128)(2,1)S(1)}, bf16[7,128,256]{2,1,0:T(8,128)(2,1)S(1)}, u32[]{:S(2)}, u32[]{:S(2)}) collective-permute-start(bf16[7,128,256]{2,1,0:T(8,128)(2,1)S(1)} %pad_maximum_fusion.rest_0_), channel_id=1, source_target_pairs={{0,4},{4,0},{8,12},{12,8},{16,20},{20,16},{24,28},{28,24},{1,5},{5... | collective-permute-start | bytes 1376264 | tf_op jit(solution)/shard_map/ppermute | solution.py:615
  39.7 2.6 %collective-permute-start.9 = (bf16[7,128,256]{2,1,0:T(8,128)(2,1)S(1)}, bf16[7,128,256]{2,1,0:T(8,128)(2,1)S(1)}, u32[]{:S(2)}, u32[]{:S(2)}) collective-permute-start(bf16[7,128,256]{2,1,0:T(8,128)(2,1)S(1)} %collective-permute-done.5.rest_3_), channel_id=1, source_target_pairs={{0,4},{4,0},{8,12},{12,8},{16,20},{20,16},{24,28},{28,24},{1,5},{5... | collective-permute-start | bytes 1376264 | tf_op jit(solution)/shard_map/ppermute | solution.py:615
  56.5 11.3 %all-to-all-start = ((bf16[16,32,180]{2,1,0:T(8,128)(2,1)}), bf16[16,32,180]{2,1,0:T(8,128)(2,1)}, u32[]{:S(2)}, u32[]{:S(2)}) async-start(bf16[16,32,180]{2,1,0:T(8,128)(2,1)} %get-tuple-element.52), calls=%async_computation | async-start | bytes 524288 | tf_op jit(solution)/shard_map/all_to_all | solution.py:666
  98.5 2.5 %collective-permute-start.10 = (bf16[16,24,1024]{2,1,0:T(8,128)(2,1)}, bf16[16,24,1024]{2,1,0:T(8,128)(2,1)S(1)}, u32[]{:S(2)}, u32[]{:S(2)}) collective-permute-start(bf16[16,24,1024]{2,1,0:T(8,128)(2,1)} %get-tuple-element.66), channel_id=1, source_target_pairs={{0,4},{4,0},{8,12},{12,8},{16,20},{20,16},{24,28},{28,24},{1,5},{5... | collective-permute-start | bytes 2359304 | tf_op jit(solution)/shard_map/ppermute | solution.py:615
  103.7 11.0 %collective-permute-start.11 = (bf16[4,24,1024]{2,1,0:T(8,128)(2,1)S(1)}, bf16[4,24,1024]{2,1,0:T(8,128)(2,1)S(1)}, u32[]{:S(2)}, u32[]{:S(2)}) collective-permute-start(bf16[4,24,1024]{2,1,0:T(8,128)(2,1)S(1)} %get-tuple-element.68), channel_id=1, source_target_pairs={{0,8},{4,12},{8,16},{12,20},{16,24},{20,28},{24,0},{28,4},{1,9},{5... | collective-permute-start | bytes 589832 | tf_op jit(solution)/shard_map/ppermute | solution.py:610
  104.2 10.9 %collective-permute-start.12 = (bf16[4,24,1024]{2,1,0:T(8,128)(2,1)S(1)}, bf16[4,24,1024]{2,1,0:T(8,128)(2,1)S(1)}, u32[]{:S(2)}, u32[]{:S(2)}) collective-permute-start(bf16[4,24,1024]{2,1,0:T(8,128)(2,1)S(1)} %get-tuple-element.69), channel_id=1, source_target_pairs={{0,16},{4,20},{8,24},{12,28},{16,0},{20,4},{24,8},{28,12},{1,17},{... | collective-permute-start | bytes 589832 | tf_op jit(solution)/shard_map/ppermute | solution.py:610
  105.5 9.6 %collective-permute-start.13 = (bf16[4,24,1024]{2,1,0:T(8,128)(2,1)S(1)}, bf16[4,24,1024]{2,1,0:T(8,128)(2,1)S(1)}, u32[]{:S(2)}, u32[]{:S(2)}) collective-permute-start(bf16[4,24,1024]{2,1,0:T(8,128)(2,1)S(1)} %get-tuple-element.70), channel_id=1, source_target_pairs={{0,24},{4,28},{8,0},{12,4},{16,8},{20,12},{24,16},{28,20},{1,25},{... | collective-permute-start | bytes 589832 | tf_op jit(solution)/shard_map/ppermute | solution.py:610
  117.1 6.1 %collective-permute-start.14 = (bf16[24,1024]{1,0:T(8,128)(2,1)S(1)}, bf16[24,1024]{1,0:T(8,128)(2,1)S(1)}, u32[]{:S(2)}, u32[]{:S(2)}) collective-permute-start(bf16[24,1024]{1,0:T(8,128)(2,1)S(1)} %get-tuple-element.75), channel_id=1, source_target_pairs={{0,1},{1,2},{2,3},{3,0},{4,5},{5,6},{6,7},{7,4},{8,9},{9,10},{10,1... | collective-permute-start | bytes 147464 | tf_op jit(solution)/shard_map/ppermute | solution.py:618
  120.5 5.2 %collective-permute-start.15 = (bf16[24,1024]{1,0:T(8,128)(2,1)S(1)}, bf16[24,1024]{1,0:T(8,128)(2,1)S(1)}, u32[]{:S(2)}, u32[]{:S(2)}) collective-permute-start(bf16[24,1024]{1,0:T(8,128)(2,1)S(1)} %get-tuple-element.76), channel_id=1, source_target_pairs={{0,2},{1,3},{2,0},{3,1},{4,6},{5,7},{6,4},{7,5},{8,10},{9,11},{10,... | collective-permute-start | bytes 147464 | tf_op jit(solution)/shard_map/ppermute | solution.py:618
  121.0 4.7 %collective-permute-start.16 = (bf16[24,1024]{1,0:T(8,128)(2,1)S(1)}, bf16[24,1024]{1,0:T(8,128)(2,1)S(1)}, u32[]{:S(2)}, u32[]{:S(2)}) collective-permute-start(bf16[24,1024]{1,0:T(8,128)(2,1)S(1)} %get-tuple-element.77), channel_id=1, source_target_pairs={{0,3},{1,0},{2,1},{3,2},{4,7},{5,4},{6,5},{7,6},{8,11},{9,8},{10,9... | collective-permute-start | bytes 147464 | tf_op jit(solution)/shard_map/ppermute | solution.py:618
  125.7 6.0 %collective-permute-start.17 = (bf16[24,1024]{1,0:T(8,128)(2,1)S(1)}, bf16[24,1024]{1,0:T(8,128)(2,1)S(1)}, u32[]{:S(2)}, u32[]{:S(2)}) collective-permute-start(bf16[24,1024]{1,0:T(8,128)(2,1)S(1)} %sum_tensor.1), channel_id=1, source_target_pairs={{0,1},{1,2},{2,3},{3,0},{4,5},{5,6},{6,7},{7,4},{8,9},{9,10},{10,1... | collective-permute-start | bytes 147464 | tf_op jit(solution)/shard_map/ppermute | solution.py:618
  126.9 5.9 %collective-permute-start.18 = (bf16[24,1024]{1,0:T(8,128)(2,1)S(1)}, bf16[24,1024]{1,0:T(8,128)(2,1)S(1)}, u32[]{:S(2)}, u32[]{:S(2)}) collective-permute-start(bf16[24,1024]{1,0:T(8,128)(2,1)S(1)} %sum_tensor.1), channel_id=1, source_target_pairs={{0,2},{1,3},{2,0},{3,1},{4,6},{5,7},{6,4},{7,5},{8,10},{9,11},{10,... | collective-permute-start | bytes 147464 | tf_op jit(solution)/shard_map/ppermute | solution.py:618
  129.4 4.1 %collective-permute-start.19 = (bf16[24,1024]{1,0:T(8,128)(2,1)S(1)}, bf16[24,1024]{1,0:T(8,128)(2,1)S(1)}, u32[]{:S(2)}, u32[]{:S(2)}) collective-permute-start(bf16[24,1024]{1,0:T(8,128)(2,1)S(1)} %sum_tensor.1), channel_id=1, source_target_pairs={{0,3},{1,0},{2,1},{3,2},{4,7},{5,4},{6,5},{7,6},{8,11},{9,8},{10,9... | collective-permute-start | bytes 147464 | tf_op jit(solution)/shard_map/ppermute | solution.py:618
  133.5 6.8 %collective-permute-start.20 = (bf16[4,24,1024]{2,1,0:T(8,128)(2,1)S(1)}, bf16[4,24,1024]{2,1,0:T(8,128)(2,1)S(1)}, u32[]{:S(2)}, u32[]{:S(2)}) collective-permute-start(bf16[4,24,1024]{2,1,0:T(8,128)(2,1)S(1)} %pad_maximum_fusion.1.rest_0_), channel_id=1, source_target_pairs={{0,8},{4,12},{8,16},{12,20},{16,24},{20,28},{24,0},{28,4},{1,9},{5... | collective-permute-start | bytes 589832 | tf_op jit(solution)/shard_map/ppermute | solution.py:610
  135.0 7.3 %collective-permute-start.21 = (bf16[4,24,1024]{2,1,0:T(8,128)(2,1)S(1)}, bf16[4,24,1024]{2,1,0:T(8,128)(2,1)S(1)}, u32[]{:S(2)}, u32[]{:S(2)}) collective-permute-start(bf16[4,24,1024]{2,1,0:T(8,128)(2,1)S(1)} %pad_maximum_fusion.1.rest_0_), channel_id=1, source_target_pairs={{0,16},{4,20},{8,24},{12,28},{16,0},{20,4},{24,8},{28,12},{1,17},{... | collective-permute-start | bytes 589832 | tf_op jit(solution)/shard_map/ppermute | solution.py:610
  136.6 6.1 %collective-permute-start.22 = (bf16[4,24,1024]{2,1,0:T(8,128)(2,1)S(1)}, bf16[4,24,1024]{2,1,0:T(8,128)(2,1)S(1)}, u32[]{:S(2)}, u32[]{:S(2)}) collective-permute-start(bf16[4,24,1024]{2,1,0:T(8,128)(2,1)S(1)} %pad_maximum_fusion.1.rest_0_), channel_id=1, source_target_pairs={{0,24},{4,28},{8,0},{12,4},{16,8},{20,12},{24,16},{28,20},{1,25},{... | collective-permute-start | bytes 589832 | tf_op jit(solution)/shard_map/ppermute | solution.py:610
  137.9 5.1 %collective-permute-start.23 = (bf16[4,24,1024]{2,1,0:T(8,128)(2,1)S(1)}, bf16[4,24,1024]{2,1,0:T(8,128)(2,1)S(1)}, u32[]{:S(2)}, u32[]{:S(2)}) collective-permute-start(bf16[4,24,1024]{2,1,0:T(8,128)(2,1)S(1)} %pad_maximum_fusion.1.rest_0_), channel_id=1, source_target_pairs={{0,4},{4,0},{8,12},{12,8},{16,20},{20,16},{24,28},{28,24},{1,5},{5... | collective-permute-start | bytes 589832 | tf_op jit(solution)/shard_map/ppermute | solution.py:615
  140.3 2.7 %collective-permute-start.24 = (bf16[4,24,1024]{2,1,0:T(8,128)(2,1)S(1)}, bf16[4,24,1024]{2,1,0:T(8,128)(2,1)S(1)}, u32[]{:S(2)}, u32[]{:S(2)}) collective-permute-start(bf16[4,24,1024]{2,1,0:T(8,128)(2,1)S(1)} %collective-permute-done.20.rest_1_), channel_id=1, source_target_pairs={{0,4},{4,0},{8,12},{12,8},{16,20},{20,16},{24,28},{28,24},{1,5},{5... | collective-permute-start | bytes 589832 | tf_op jit(solution)/shard_map/ppermute | solution.py:615
  (36 other events, 202.1 us)

commit v6 on v5

--- a/solution.py
+++ b/solution.py
@@ -14,14 +14,12 @@
 CORES = 2
 VMEM_LIMIT = 56 * 1024 * 1024
 SMALL_LIMIT = 14 * 1024 * 1024
-BACKWARD_LIMIT = 46 * 1024 * 1024
 
 F32 = jnp.float32
 BF16 = jnp.bfloat16
 VMEM = pl.BlockSpec(memory_space=pltpu.VMEM)
 SMEM = pl.BlockSpec(memory_space=pltpu.SMEM)
 ANY = pl.BlockSpec(memory_space=pl.ANY)
-TOKEN = jax.ShapeDtypeStruct((8, 128), F32)
 
 
 def up(n, m):
@@ -90,16 +88,39 @@
     )(x, stream, out_weight, gain, bias, proj_weight)
 
 
-def teacher_kernel(parts, count, tokens, order_ref, from_ref, rows_ref, states_ref, wq_ref, wk_ref, *rest):
-    pieces, out_ref, token_ref = rest[:parts], rest[parts], rest[parts + 1]
-    w_s, own_s, q_s, g_s, key_s, e_s, map_s, q_sem, key_sem, w_sem, own_sem = rest[parts + 2 :]
+def pair_keys_kernel(count, tokens, states_ref, out_ref, wide_s):
+    total = wide_s.shape[0]
+    first = count * tokens
+    sub = split_rows(total, 256)
+    for b in range(0, total, sub):
+        wide_s[b : b + sub] = states_ref[first + b : first + b + sub].astype(F32)
+    for p in range(count):
+        out_ref[p] = wide_s[pl.ds(p, total // count, stride=count), :].astype(BF16)
+
+
+def pair_keys(states, count, tokens):
+    total, depth = states.shape
+    keys = total - count * tokens
+    return pl.pallas_call(
+        functools.partial(pair_keys_kernel, count, tokens),
+        grid=(depth // 128,),
+        in_specs=[pl.BlockSpec((total, 128), lambda s: (0, s))],
+        out_specs=pl.BlockSpec((count, keys // count, 128), lambda s: (0, 0, s)),
+        out_shape=jax.ShapeDtypeStruct((count, keys // count, depth), BF16),
+        scratch_shapes=[pltpu.VMEM((keys, 128), F32)],
+        compiler_params=params(),
+        cost_estimate=cost(1e9, 4 * states.size),
+        name="pair_keys",
+    )(states)
+
+
+def teacher_kernel(parts, count, tokens, order_ref, from_ref, rows_ref, states_ref, keys_ref, wq_ref, wk_ref, *rest):
+    pieces, out_ref = rest[:parts], rest[parts]
+    w_s, own_s, q_s, g_s, key_s, map_s, q_sem, key_sem, w_sem, own_sem = rest[parts + 1 :]
     depth = q_s.shape[1]
     slices = w_s.shape[0] // 2
     part_rows = pieces[0].shape[1]
-    total = key_s.shape[0]
-    seq = total // count
-    blocks = key_sem.shape[0]
-    rows = total // blocks
+    seq = key_s.shape[1]
     first = count * tokens
     own = [
         pltpu.make_async_copy(wq_ref, own_s.at[0], own_sem.at[0]),
@@ -114,12 +135,7 @@
         )
         for a in range(parts)
     ]
-    keys = [
-        pltpu.make_async_copy(
-            states_ref.at[pl.ds(first + b * rows, rows)], key_s.at[pl.ds(b * rows, rows)], key_sem.at[b]
-        )
-        for b in range(blocks)
-    ]
+    keys = [pltpu.make_async_copy(keys_ref.at[p], key_s.at[p], key_sem.at[p]) for p in range(count)]
     queries.start()
     for copy in own + gathered:
         copy.start()
@@ -143,57 +159,49 @@
     mixed = q_s[...].T
     scale = 1.0 / (math.sqrt(depth) * softcap)
     side = 128 // tokens
-    pair = lax.broadcasted_iota(jnp.int32, (rows, 128), 0) % count
-    for b in range(blocks):
-        keys[b].wait()
-        raw = dot(key_s[b * rows : (b + 1) * rows], mixed, 1, 0)
-        mine = raw[:, :128]
-        for v in range(1, count // side):
-            mine = jnp.where(pair >= v * side, raw[:, v * 128 : (v + 1) * 128], mine)
-        e_s[b * rows : (b + 1) * rows] = jnp.exp(softcap * jnp.tanh(mine * scale))
     lane = lax.broadcasted_iota(jnp.int32, (seq, 128), 1) // tokens
     filler = jnp.zeros((up(seq, 128) - seq, 128), F32)
     for g in range(count // side):
-        both = e_s[pl.ds(g * side, seq, stride=count), :]
-        for v in range(1, side):
-            both = jnp.where(lane == v, e_s[pl.ds(g * side + v, seq, stride=count), :], both)
+        both = None
+        for v in range(side):
+            keys[g * side + v].wait()
+            raw = dot(key_s[g * side + v], mixed[:, g * 128 : (g + 1) * 128], 1, 0)
+            both = raw if both is None else jnp.where(lane == v, raw, both)
+        both = jnp.exp(softcap * jnp.tanh(both * scale))
         turned = jnp.concatenate([both, filler], axis=0).T
         for v in range(side):
             map_s[g * side + v] = turned[v * tokens : (v + 1) * tokens, :seq].astype(BF16)
     per = count // parts
     for n in range(count):
         out_ref[n] = map_s[order_ref[from_ref[n // per], n % per]]
-    token_ref[...] = jnp.zeros_like(token_ref)
-
-
-def teacher_maps(order, source, rows, slices, states, wq, wk, pieces, count, tokens):
-    total, depth = states.shape
-    keys = total - count * tokens
+
+
+def teacher_maps(order, source, rows, slices, states, keys, wq, wk, pieces, count, tokens):
+    depth = states.shape[1]
+    seq = keys.shape[1]
     heads = wq.shape[1]
     parts = len(pieces)
-    blocks = keys // split_rows(keys, 720)
     return pl.pallas_call(
         functools.partial(teacher_kernel, parts, count, tokens),
-        in_specs=[SMEM] * 3 + [ANY] * (3 + parts),
-        out_specs=[VMEM, VMEM],
-        out_shape=[jax.ShapeDtypeStruct((count, tokens, keys // count), BF16), TOKEN],
+        in_specs=[SMEM] * 3 + [ANY] * (4 + parts),
+        out_specs=VMEM,
+        out_shape=jax.ShapeDtypeStruct((count, tokens, seq), BF16),
         scratch_shapes=[
             pltpu.VMEM((slices, depth, heads), BF16),
             pltpu.VMEM((2, depth, heads), BF16),
             pltpu.VMEM((count * tokens, depth), BF16),
             pltpu.VMEM((depth // 128, count * tokens, 128), F32),
-            pltpu.VMEM((keys, depth), BF16),
-            pltpu.VMEM((keys, 128), F32),
-            pltpu.VMEM((count, tokens, keys // count), BF16),
+            pltpu.VMEM((count, seq, depth), BF16),
+            pltpu.VMEM((count, tokens, seq), BF16),
             pltpu.SemaphoreType.DMA,
-            pltpu.SemaphoreType.DMA((blocks,)),
+            pltpu.SemaphoreType.DMA((count,)),
             pltpu.SemaphoreType.DMA((parts,)),
             pltpu.SemaphoreType.DMA((2,)),
         ],
         compiler_params=params(),
         cost_estimate=cost(8 * count * tokens * depth * depth, 2 * states.size + 4 * depth * depth),
         name="teacher_maps",
-    )(order, source, rows, states, wq, wk, *pieces)
+    )(order, source, rows, states, keys, wq, wk, *pieces)
 
 
 def rider_copies(pieces, slices, held, sem):
@@ -212,7 +220,7 @@
     return jnp.concatenate([held[a, n * each : (n + 1) * each] for n in range(width // heads)], axis=1)
 
 
-def scores_kernel(tokens, count, group_queries, slices, parts, qidx_ref, len_ref, emb_ref, wp_ref, after_ref, *rest):
+def scores_kernel(tokens, count, group_queries, slices, parts, qidx_ref, len_ref, emb_ref, wp_ref, *rest):
     pieces = rest[:parts]
     (prob_ref, log_ref, units_ref, qunit_ref, qdir_ref, qlen_ref, qs_s, dir_s, held_s, sem) = rest[parts:]
     copies = rider_copies(pieces, slices, held_s, sem)
@@ -222,6 +230,9 @@
     seq = total // count
     sub = split_rows(total, 128)
     each = group_queries * tokens
+    for b in range(0, total, sub):
+        e = emb_ref[b : b + sub]
+        dir_s[b : b + sub] = e / jnp.sqrt(jnp.sum(e * e, axis=-1, keepdims=True) + epsilon)
     for copy in copies:
         copy.wait()
     for a in range(parts):
@@ -232,9 +243,6 @@
     qdir_ref[...] = qdir
     qlen_ref[...] = jnp.broadcast_to(length, qlen_ref.shape)
     qunit_ref[...] = qdir.astype(BF16).reshape(qunit_ref.shape)
-    for b in range(0, total, sub):
-        e = emb_ref[b : b + sub]
-        dir_s[b : b + sub] = e / jnp.sqrt(jnp.sum(e * e, axis=-1, keepdims=True) + epsilon)
     for r in range(count):
         units = dir_s[pl.ds(r, seq, stride=count), :].astype(BF16)
         units_ref[r] = units
@@ -246,7 +254,7 @@
         log_ref[r] = logits - jnp.log(student_total)
 
 
-def student_scores(qidx, lens, embeds, wp, after, pieces, slices, count, tokens, group_queries):
+def student_scores(qidx, lens, embeds, wp, pieces, slices, count, tokens, group_queries):
     total, emb = embeds.shape
     seq = total // count
     parts = len(pieces)
@@ -255,7 +263,7 @@
     riders -= slices
     return pl.pallas_call(
         functools.partial(scores_kernel, tokens, count, group_queries, slices, parts),
-        in_specs=[SMEM, SMEM, VMEM, VMEM] + [ANY] * (1 + parts),
+        in_specs=[SMEM, SMEM, VMEM, VMEM] + [ANY] * parts,
         out_specs=[VMEM] * 6,
         out_shape=[
             jax.ShapeDtypeStruct((count, tokens, seq), F32),
@@ -274,7 +282,7 @@
         compiler_params=params(),
         cost_estimate=cost(1e9, 4 * total * emb),
         name="student_scores",
-    )(qidx, lens, embeds, wp, after, *pieces)
+    )(qidx, lens, embeds, wp, *pieces)
 
 
 def two_parts(a, b):
@@ -467,60 +475,56 @@
             pltpu.SemaphoreType.DMA((parts * riders,)),
         ],
         out_shape=[jax.ShapeDtypeStruct((total, width), BF16), packed, packed],
-        compiler_params=pltpu.CompilerParams(vmem_limit_bytes=BACKWARD_LIMIT),
+        compiler_params=params(),
         cost_estimate=cost(2 * total * width * (width + 2 * emb), 8 * total * width),
         name="student_backward",
     )(qidx, midx, lens, core, *pieces, *manual, qdir, qlen, gain, bias, wp, wpt)
 
 
-def context_kernel(sg_ref, wo_ref, after_ref, out_ref, token_ref):
-    token_ref[...] = jnp.zeros_like(token_ref)
+def context_kernel(sg_ref, wo_ref, out_ref):
     out_ref[...] = dot(sg_ref[...], wo_ref[...], 1, 1).astype(BF16)
 
 
-def context_grad(sg, out_weight, after):
+def context_grad(sg, out_weight):
     total, width = sg.shape
     rows = split_rows(total, 720)
     block = pl.BlockSpec((rows, width), lambda s: (s, 0))
     return pl.pallas_call(
         context_kernel,
         grid=(total // rows,),
-        in_specs=[block, pl.BlockSpec(out_weight.shape, lambda s: (0, 0)), ANY],
-        out_specs=[block, pl.BlockSpec(TOKEN.shape, lambda s: (0, 0))],
-        out_shape=[jax.ShapeDtypeStruct(sg.shape, BF16), TOKEN],
+        in_specs=[block, pl.BlockSpec(out_weight.shape, lambda s: (0, 0))],
+        out_specs=block,
+        out_shape=jax.ShapeDtypeStruct(sg.shape, BF16),
         compiler_params=params(),
         cost_estimate=cost(2 * total * width * width, 4 * total * width),
         name="context_grad",
-    )(sg, out_weight, after)
-
-
-def split_sum_kernel(inputs, outputs, after, index_ref, *rest):
-    ins, outs = rest[:inputs], rest[inputs + after : inputs + after + outputs]
-    token_ref, total_s = rest[-2:]
+    )(sg, out_weight)
+
+
+def split_sum_kernel(inputs, outputs, index_ref, *rest):
+    ins, outs, total_s = rest[:inputs], rest[inputs : inputs + outputs], rest[-1]
     total = ins[0][...].astype(F32)
     for ref in ins[1:]:
         total = total + ref[...].astype(F32)
     total_s[...] = total.astype(BF16).reshape(total_s.shape)
     for k in range(outputs):
         outs[k][...] = total_s[index_ref[k]].reshape(outs[k].shape)
-    token_ref[...] = jnp.zeros_like(token_ref)
-
-
-def split_sum(arrays, index, name, after=()):
+
+
+def split_sum(arrays, index, name):
     outputs = index.shape[0]
     shape = arrays[0].shape
     lead = shape[0] // outputs
     out = shape[1:] if lead == 1 else (lead,) + shape[1:]
-    *parts, token = pl.pallas_call(
-        functools.partial(split_sum_kernel, len(arrays), outputs, len(after)),
-        in_specs=[SMEM] + [VMEM] * len(arrays) + [ANY] * len(after),
-        out_specs=[VMEM] * (outputs + 1),
-        out_shape=[jax.ShapeDtypeStruct(out, BF16)] * outputs + [TOKEN],
+    return pl.pallas_call(
+        functools.partial(split_sum_kernel, len(arrays), outputs),
+        in_specs=[SMEM] + [VMEM] * len(arrays),
+        out_specs=[VMEM] * outputs,
+        out_shape=[jax.ShapeDtypeStruct(out, BF16)] * outputs,
         scratch_shapes=[pltpu.VMEM((outputs, lead) + shape[1:], BF16)],
         compiler_params=pltpu.CompilerParams(vmem_limit_bytes=SMALL_LIMIT),
         name=name,
-    )(index, *arrays, *after)
-    return parts, token
+    )(index, *arrays)
 
 
 def sum_kernel(*refs):
@@ -543,20 +547,28 @@
 
 def unpack_kernel(parts, width, emb, tokens, scale, index_ref, *rest):
     ins = rest[:parts]
-    wo_ref, proj_ref, gain_ref, bias_ref, loss_ref, small_s = rest[parts:]
+    wo_out, proj_out, gain_ref, bias_ref, loss_ref, wo_s, proj_s, small_s, wo_sem, proj_sem = rest[parts:]
     per = ins[0].shape[0]
+    copies = []
     for a in range(parts):
         for k in range(per):
-            c = index_ref[a * per + k]
+            n = a * per + k
+            c = index_ref[n]
             value = ins[a][k].astype(F32)
-            wo_ref[c] = value[:, :width]
-            proj_ref[c] = value[:, width : width + emb]
+            wo_s[n] = value[:, :width]
+            proj_s[n] = value[:, width : width + emb]
             small_s[c] = value[:, width + emb :]
+            copies.append(pltpu.make_async_copy(wo_s.at[n], wo_out.at[c], wo_sem.at[n]))
+            copies.append(pltpu.make_async_copy(proj_s.at[n], proj_out.at[c], proj_sem.at[n]))
+            copies[-2].start()
+            copies[-1].start()
     turned = small_s[...].reshape(width, 128).T
     for v in range(width // 128):
         gain_ref[v : v + 1] = turned[0:1, v * 128 : (v + 1) * 128]
         bias_ref[v : v + 1] = turned[1:2, v * 128 : (v + 1) * 128]
     loss_ref[0] = jnp.sum(turned[tokens : 2 * tokens, 0:1]) * scale
+    for copy in copies:
+        copy.wait()
 
 
 def unpack(arrays, index, width, emb, tokens, scale):
@@ -566,11 +578,12 @@
     return pl.pallas_call(
         functools.partial(unpack_kernel, parts, width, emb, tokens, scale),
         in_specs=[SMEM] + [VMEM] * parts,
-        out_specs=[VMEM] * 4 + [SMEM],
+        out_specs=[ANY] * 2 + [VMEM] * 2 + [SMEM],
         out_shape=[jax.ShapeDtypeStruct((chunks, chunk, n), F32) for n in (width, emb)]
         + [jax.ShapeDtypeStruct((width // 128, 128), F32)] * 2
         + [jax.ShapeDtypeStruct((1,), F32)],
-        scratch_shapes=[pltpu.VMEM((chunks, chunk, 128), F32)],
+        scratch_shapes=[pltpu.VMEM((chunks, chunk, n), F32) for n in (width, emb, 128)]
+        + [pltpu.SemaphoreType.DMA((chunks,))] * 2,
         compiler_params=pltpu.CompilerParams(vmem_limit_bytes=SMALL_LIMIT),
         name="unpack",
     )(index, *arrays)
@@ -654,18 +667,20 @@
     gain2, bias2 = gain.reshape(-1, 128), bias.reshape(-1, 128)
     x = flat(context)
     normed, embeds, inverse, turned = student_forward(x, flat(stream), out_weight, gain2, bias2, proj_weight)
-    pieces[1:], normed, embeds, inverse, turned, proj_turned = lax.optimization_barrier(
-        (pieces[1:], normed, embeds, inverse, turned, proj_weight.T)
+    keys = pair_keys(flat(teacher_states), count, tokens)
+    pieces[1:], normed, embeds, inverse, turned, keys, proj_turned = lax.optimization_barrier(
+        (pieces[1:], normed, embeds, inverse, turned, keys, proj_weight.T)
     )
     pieces = pieces + [swap_core(a) for a in pieces]
     told = [a[slices:].reshape(-1, heads)[width // heads * each, :count] for a in pieces]
     order = lax.dynamic_slice_in_dim(jnp.stack(told), me * per, per, 1).astype(jnp.int32)
-    maps, token = teacher_maps(
-        order, source, piece_rows, slices, flat(teacher_states), teacher_query, teacher_key, pieces, count, tokens
-    )
+    maps = teacher_maps(
+        order, source, piece_rows, slices, flat(teacher_states), keys, teacher_query, teacher_key, pieces, count, tokens
+    )
+    maps, embeds = lax.optimization_barrier((maps, embeds))
     maps = lax.all_to_all(maps, "dp", split_axis=0, concat_axis=0, tiled=True)
     scores = student_scores(
-        qidx, passage_len, embeds, proj_weight, token, pieces, slices, count, tokens, group_queries
+        qidx, passage_len, embeds, proj_weight, pieces, slices, count, tokens, group_queries
     )
     chunk = width // (CORES * chips * nt)
     sg, send, keep = student_backward(
@@ -677,10 +692,12 @@
     ahead = ((chip + shifts) % chips).astype(jnp.int32)
     t_shifts = jnp.arange(nt, dtype=jnp.int32)
     t_ahead = ((mt + t_shifts) % nt).astype(jnp.int32)
-    parts, token = split_sum([keep, swap_core(send)], ahead, "sum_cores")
-    grad_context, token = context_grad(sg, out_weight, token)
+    parts = split_sum([keep, swap_core(send)], ahead, "sum_cores")
+    parts, sg = lax.optimization_barrier((parts, sg))
+    grad_context = context_grad(sg, out_weight)
     parts = [parts[0]] + [shift_chip(parts[k], k) for k in range(1, chips)]
-    parts, _ = split_sum(parts, t_ahead, "sum_plane", (token,))
+    parts, grad_context = lax.optimization_barrier((parts, grad_context))
+    parts = split_sum(parts, t_ahead, "sum_plane")
     parts = [parts[0]] + [shift_t(parts[k], k) for k in range(1, nt)]
     total = plain_sum(parts, "sum_tensor")
     line = jnp.stack([total] + [shift_t(total, k) for k in range(1, nt)])

time: 148 us -> 146 us (0.986)
  Pallas kernels: 64.4 us -> 77.6 us
  local copies, waits for them, and re-layouts: 15.6 us -> 6.24 us
  waiting for transfers between devices: 27.2 us -> 22.2 us
    pallas_call x2 -> x3, Pallas kernels: 2.29 us -> 11.6 us  [the longest x1 9.89 us: pair_keys(): pl.pallas_call(functools.partial(pair_keys_kernel, count, tokens), grid=(...]
    unnamed x65 -> x23, local copies, waits for them, and re-layouts: 13.7 us -> 4.42 us
    ppermute x9, waiting for transfers between devices: 10.7 us -> 5.1 us  [shift_chip(): lax.ppermute(x, 'dp', [(c * CORES + o, (c + k) % chips * CORES + o) for c...]
    pallas_call x1, Pallas kernels: 21.9 us -> 24.8 us  [student_backward(): pl.pallas_call(functools.partial(backward_kernel, tokens, count, blocks,...]
  transfers between devices with their start and end apart: 28 -> 28, of which waited for: 19 -> 19; matrix products, arithmetic and copies ran while one was open for 3% -> 3% of each run, Pallas kernels for 17% -> 24%
where the time goes in v6:
time: 146 us; the launch traced here: 145 us
  Pallas kernels  77.6 us (53%)
  starting transfers between devices  34.3 us (23%)
  waiting for transfers between devices  22.2 us (15%)
  local copies, waits for them, and re-layouts  6.24 us (4%)
  other arithmetic  3.15 us (2%)
    pallas_call x1, Pallas kernels, student_backward(): pl.pallas_call(functools.partial(backward_kernel, tokens, count, blocks,...  24.8 us
    ppermute x9, starting transfers between devices, shift_t(): return lax.ppermute(x, 'tensor', [(t, (t + k) % nt) for t in range(nt)])  16.7 us
    pallas_call x1, Pallas kernels, teacher_maps(): pl.pallas_call(functools.partial(teacher_kernel, parts, count, tokens), i...  12.8 us
    pallas_call x1, Pallas kernels, student_forward(): pl.pallas_call(forward_kernel, grid=(total // rows,), in_specs=[block(wid...  12.5 us
    ppermute x9, starting transfers between devices, shift_chip(): lax.ppermute(x, 'dp', [(c * CORES + o, (c + k) % chips * CORES + o) for c...  12.3 us
    pallas_call x1, Pallas kernels, pair_keys(): pl.pallas_call(functools.partial(pair_keys_kernel, count, tokens), grid=(...  9.89 us
    ppermute x9, waiting for transfers between devices, shift_t(): return lax.ppermute(x, 'tensor', [(t, (t + k) % nt) for t in range(nt)])  9.34 us
    pallas_call x1, Pallas kernels, context_grad(): pl.pallas_call(context_kernel, grid=(total // rows,), in_specs=[block, pl...  7.52 us
  transfers between devices with their start and end apart: 28, of which 19 were waited for; matrix products, arithmetic and copies ran while one was open for 3% of the time, Pallas kernels for 24%

profile of v6, /device:TPU:0, one launch (start us, length us, event | category | flops | bytes accessed | tf_op | source)
XLA Modules:
  0.0 144.6 jit_solution(5539966240632417750)
XLA Ops:
  1.5 3.1 %collective-permute-start = (bf16[2,128,256]{2,1,0:T(8,128)(2,1)S(1)}, bf16[2,128,256]{2,1,0:T(8,128)(2,1)S(1)}, u32[]{:S(2)}, u32[]{:S(2)}) collective-permute-start(bf16[2,128,256]{2,1,0:T(8,128)(2,1)S(1)} %pad_maximum_fusion.2), channel_id=1, source_target_pairs={{0,1},{1,2},{2,3},{3,0},{4,5},{5,6},{6,7},{7,4},{8,9},{9,10},{10,1... | collective-permute-start | bytes 393224 | tf_op jit(solution)/shard_map/ppermute | solution.py:631
  4.6 2.6 %collective-permute-start.1 = (bf16[2,128,256]{2,1,0:T(8,128)(2,1)S(1)}, bf16[2,128,256]{2,1,0:T(8,128)(2,1)S(1)}, u32[]{:S(2)}, u32[]{:S(2)}) collective-permute-start(bf16[2,128,256]{2,1,0:T(8,128)(2,1)S(1)} %pad_maximum_fusion.2), channel_id=1, source_target_pairs={{0,2},{1,3},{2,0},{3,1},{4,6},{5,7},{6,4},{7,5},{8,10},{9,11},{10,... | collective-permute-start | bytes 393224 | tf_op jit(solution)/shard_map/ppermute | solution.py:631
  11.5 1.8 %copy.20 = bf16[768,128]{0,1:T(8,128)(2,1)} copy(bf16[768,128]{1,0:T(8,128)(2,1)} %rest_21_.1) | data formatting | bytes 393216 | tf_op args[5]
  13.3 2.6 %collective-permute-done.1 = bf16[2,128,256]{2,1,0:T(8,128)(2,1)S(1)} collective-permute-done((bf16[2,128,256]{2,1,0:T(8,128)(2,1)S(1)}, bf16[2,128,256]{2,1,0:T(8,128)(2,1)S(1)}, u32[]{:S(2)}, u32[]{:S(2)}) %collective-permute-start.1) | collective-permute-done | bytes 131104 | tf_op jit(solution)/shard_map/ppermute | solution.py:631
  15.9 1.5 %collective-permute-start.3 = (bf16[7,128,256]{2,1,0:T(8,128)(2,1)S(1)}, bf16[7,128,256]{2,1,0:T(8,128)(2,1)S(1)}, u32[]{:S(2)}, u32[]{:S(2)}) collective-permute-start(bf16[7,128,256]{2,1,0:T(8,128)(2,1)S(1)} %pad_maximum_fusion.rest_0_), channel_id=1, source_target_pairs={{0,8},{4,12},{8,16},{12,20},{16,24},{20,28},{24,0},{28,4},{1,9},{5... | collective-permute-start | bytes 1376264 | tf_op jit(solution)/shard_map/ppermute | solution.py:623
  20.4 9.9 %pair_keys.1.keys_ref = bf16[16,180,1024]{2,1,0:T(8,128)(2,1)} custom-call(bf16[3392,1024]{1,0:T(8,128)(2,1)} %bitcast.49), custom_call_target="tpu_custom_call" | custom-call | flops 1000000000 | bytes 13893632 | tf_op jit(solution)/shard_map/pair_keys/pallas_call | solution.py:104
  30.3 12.5 %student_forward.1 = (bf16[2880,768]{1,0:T(8,128)(2,1)}, f32[2880,128]{1,0:T(8,128)}, f32[2880,128]{1,0:T(8,128)}, bf16[4,768,720]{2,1,0:T(8,128)(2,1)}) custom-call(bf16[2880,768]{1,0:T(8,128)(2,1)} %bitcast.60, bf16[2880,768]{1,0:T(8,128)(2,1)} %bitcast.61, bf16[768,768]{1,0:T(8,128)(2,1)} %wo_ref.3, f32[6,128]{1,0:T(8,128)} %bitcast.56, ...), custom_call_target="tpu_custom_call" | custom-call | flops 3963617280 | bytes 17694720 | tf_op jit(solution)/shard_map/student_forward/pallas_call | solution.py:73
  48.3 12.8 %teacher_maps.1 = bf16[16,32,180]{2,1,0:T(8,128)(2,1)} custom-call(s32[8,2]{1,0:T(8,128)} %dynamic-slice_convert_fusion.order_ref, s32[8]{0:T(128)} %get-tuple-element.108.from_ref, s32[8]{0:T(128)} %get-tuple-element.109.rows_ref, bf16[3392,1024]{1,0:T(8,128)(2,1)} %bitcast.50, bf16[16,180,1024]{2,1,0:T(8,128)(2,1)} %pair_keys.1.keys_ref, ...), custom_call_target="tpu_custom_call" | custom-call | flops 4294967296 | bytes 11141120 | tf_op jit(solution)/shard_map/teacher_maps/pallas_call | solution.py:184
  61.1 3.6 %all-to-all-start = ((bf16[16,32,180]{2,1,0:T(8,128)(2,1)}), bf16[16,32,180]{2,1,0:T(8,128)(2,1)S(1)}, u32[]{:S(2)}, u32[]{:S(2)}) async-start(bf16[16,32,180]{2,1,0:T(8,128)(2,1)} %teacher_maps.1), calls=%async_computation | async-start | bytes 524288 | tf_op jit(solution)/shard_map/all_to_all | solution.py:681
  64.7 4.9 %student_scores.1 = (f32[16,32,180]{2,1,0:T(8,128)}, f32[16,32,180]{2,1,0:T(8,128)}, bf16[16,180,128]{2,1,0:T(8,128)(2,1)}, bf16[8,32,128]{2,1,0:T(8,128)(2,1)}, f32[256,128]{1,0:T(8,128)}, /*index=5*/f32[256,128]{1,0:T(8,128)}) custom-call(s32[16]{0:T(128)} %get-tuple-element.100.qidx_ref, s32[16]{0:T(128)} %len_ref.3, ...), custom_call_target="tpu_custom_call" | custom-call | flops 1000000000 | bytes 1474560 | tf_op jit(solution)/shard_map/student_scores/pallas_call | solution.py:264
  69.7 1.8 %all-to-all-done.rest_8_ = bf16[16,32,180]{2,1,0:T(8,128)(2,1)S(1)} async-done(((bf16[16,32,180]{2,1,0:T(8,128)(2,1)}), bf16[16,32,180]{2,1,0:T(8,128)(2,1)S(1)}, u32[]{:S(2)}, u32[]{:S(2)}) %all-to-all-start) | async-done | bytes 184352 | tf_op jit(solution)/shard_map/all_to_all | solution.py:681
  72.1 24.8 %student_backward.1 = (bf16[2880,768]{1,0:T(8,128)(2,1)}, bf16[16,24,1024]{2,1,0:T(8,128)(2,1)}, bf16[16,24,1024]{2,1,0:T(8,128)(2,1)}) custom-call(s32[16]{0:T(128)} %get-tuple-element.100.qidx_ref, s32[16]{0:T(128)} %copy-done.10, s32[16]{0:T(128)} %len_ref.3, s32[1]{0:T(128)} %bitcast.core_ref, bf16[7,128,256]{2,1,0:T(8,128)(2,1)} %copy-done.1, ...), custom_call_target="tpu_custom_call" | custom-call | flops 4529848320 | bytes 17694720 | tf_op jit(solution)/shard_map/student_backward/pallas_call | solution.py:454
  97.0 2.4 %collective-permute-done.10.rest_1_ = bf16[16,24,1024]{2,1,0:T(8,128)(2,1)S(1)} collective-permute-done((bf16[16,24,1024]{2,1,0:T(8,128)(2,1)}, bf16[16,24,1024]{2,1,0:T(8,128)(2,1)S(1)}, u32[]{:S(2)}, u32[]{:S(2)}) %collective-permute-start.10) | collective-permute-done | bytes 786464 | tf_op jit(solution)/shard_map/ppermute | solution.py:628
  103.1 2.0 %collective-permute-start.13 = (bf16[4,24,1024]{2,1,0:T(8,128)(2,1)S(1)}, bf16[4,24,1024]{2,1,0:T(8,128)(2,1)S(1)}, u32[]{:S(2)}, u32[]{:S(2)}) collective-permute-start(bf16[4,24,1024]{2,1,0:T(8,128)(2,1)S(1)} %get-tuple-element.84), channel_id=1, source_target_pairs={{0,24},{4,28},{8,0},{12,4},{16,8},{20,12},{24,16},{28,20},{1,25},{... | collective-permute-start | bytes 589832 | tf_op jit(solution)/shard_map/ppermute | solution.py:623
  105.1 7.5 %context_grad.1 = bf16[2880,768]{1,0:T(8,128)(2,1)} custom-call(bf16[2880,768]{1,0:T(8,128)(2,1)} %get-tuple-element.85.sg_ref, bf16[768,768]{1,0:T(8,128)(2,1)} %wo_ref.3), custom_call_target="tpu_custom_call" | custom-call | flops 3397386240 | bytes 8847360 | tf_op jit(solution)/shard_map/context_grad/pallas_call | solution.py:492
  113.8 3.3 %collective-permute-start.14 = (bf16[24,1024]{1,0:T(8,128)(2,1)S(1)}, bf16[24,1024]{1,0:T(8,128)(2,1)S(1)}, u32[]{:S(2)}, u32[]{:S(2)}) collective-permute-start(bf16[24,1024]{1,0:T(8,128)(2,1)S(1)} %get-tuple-element.91), channel_id=1, source_target_pairs={{0,1},{1,2},{2,3},{3,0},{4,5},{5,6},{6,7},{7,4},{8,9},{9,10},{10,1... | collective-permute-start | bytes 147464 | tf_op jit(solution)/shard_map/ppermute | solution.py:631
  117.1 1.6 %collective-permute-start.15 = (bf16[24,1024]{1,0:T(8,128)(2,1)S(1)}, bf16[24,1024]{1,0:T(8,128)(2,1)S(1)}, u32[]{:S(2)}, u32[]{:S(2)}) collective-permute-start(bf16[24,1024]{1,0:T(8,128)(2,1)S(1)} %get-tuple-element.92), channel_id=1, source_target_pairs={{0,2},{1,3},{2,0},{3,1},{4,6},{5,7},{6,4},{7,5},{8,10},{9,11},{10,... | collective-permute-start | bytes 147464 | tf_op jit(solution)/shard_map/ppermute | solution.py:631
  120.7 2.1 %collective-permute-done.15.refs_2_ = bf16[24,1024]{1,0:T(8,128)(2,1)S(1)} collective-permute-done((bf16[24,1024]{1,0:T(8,128)(2,1)S(1)}, bf16[24,1024]{1,0:T(8,128)(2,1)S(1)}, u32[]{:S(2)}, u32[]{:S(2)}) %collective-permute-start.15) | collective-permute-done | bytes 49184 | tf_op jit(solution)/shard_map/ppermute | solution.py:631
  123.8 2.3 %collective-permute-start.18 = (bf16[24,1024]{1,0:T(8,128)(2,1)S(1)}, bf16[24,1024]{1,0:T(8,128)(2,1)S(1)}, u32[]{:S(2)}, u32[]{:S(2)}) collective-permute-start(bf16[24,1024]{1,0:T(8,128)(2,1)S(1)} %sum_tensor.1), channel_id=1, source_target_pairs={{0,2},{1,3},{2,0},{3,1},{4,6},{5,7},{6,4},{7,5},{8,10},{9,11},{10,... | collective-permute-start | bytes 147464 | tf_op jit(solution)/shard_map/ppermute | solution.py:631
  127.2 2.1 %collective-permute-done.17 = bf16[24,1024]{1,0:T(8,128)(2,1)S(1)} collective-permute-done((bf16[24,1024]{1,0:T(8,128)(2,1)S(1)}, bf16[24,1024]{1,0:T(8,128)(2,1)S(1)}, u32[]{:S(2)}, u32[]{:S(2)}) %collective-permute-start.17) | collective-permute-done | bytes 49184 | tf_op jit(solution)/shard_map/ppermute | solution.py:631
  131.8 1.9 %collective-permute-start.21 = (bf16[4,24,1024]{2,1,0:T(8,128)(2,1)S(1)}, bf16[4,24,1024]{2,1,0:T(8,128)(2,1)S(1)}, u32[]{:S(2)}, u32[]{:S(2)}) collective-permute-start(bf16[4,24,1024]{2,1,0:T(8,128)(2,1)S(1)} %pad_maximum_fusion.1.rest_0_), channel_id=1, source_target_pairs={{0,16},{4,20},{8,24},{12,28},{16,0},{20,4},{24,8},{28,12},{1,17},{... | collective-permute-start | bytes 589832 | tf_op jit(solution)/shard_map/ppermute | solution.py:623
  134.8 2.5 %collective-permute-done.20.rest_1_ = bf16[4,24,1024]{2,1,0:T(8,128)(2,1)S(1)} collective-permute-done((bf16[4,24,1024]{2,1,0:T(8,128)(2,1)S(1)}, bf16[4,24,1024]{2,1,0:T(8,128)(2,1)S(1)}, u32[]{:S(2)}, u32[]{:S(2)}) %collective-permute-start.20) | collective-permute-done | bytes 196640 | tf_op jit(solution)/shard_map/ppermute | solution.py:623
  137.3 2.0 %collective-permute-done.21.rest_2_ = bf16[4,24,1024]{2,1,0:T(8,128)(2,1)S(1)} collective-permute-done((bf16[4,24,1024]{2,1,0:T(8,128)(2,1)S(1)}, bf16[4,24,1024]{2,1,0:T(8,128)(2,1)S(1)}, u32[]{:S(2)}, u32[]{:S(2)}) %collective-permute-start.21) | collective-permute-done | bytes 196640 | tf_op jit(solution)/shard_map/ppermute | solution.py:623
  141.0 3.4 %unpack.1 = (f32[32,24,768]{2,1,0:T(8,128)}, f32[32,24,128]{2,1,0:T(8,128)}, f32[6,128]{1,0:T(8,128)}, f32[6,128]{1,0:T(8,128)}, f32[1]{0:T(128)}) custom-call(s32[32]{0:T(128)S(1)} %add.139.index_ref, bf16[4,24,1024]{2,1,0:T(8,128)(2,1)S(1)} %pad_maximum_fusion.1.rest_0_, bf16[4,24,1024]{2,1,0:T(8,128)(2,1)S(1)} %collective-permute-done.20.rest_1_, ...), custom_call_target="tpu_custom_call" | custom-call | tf_op jit(solution)/shard_map/unpack/pallas_call | solution.py:578
  (103 shorter events, 28.5 us)
Async XLA Ops:
  1.5 11.7 %collective-permute-start = (bf16[2,128,256]{2,1,0:T(8,128)(2,1)S(1)}, bf16[2,128,256]{2,1,0:T(8,128)(2,1)S(1)}, u32[]{:S(2)}, u32[]{:S(2)}) collective-permute-start(bf16[2,128,256]{2,1,0:T(8,128)(2,1)S(1)} %pad_maximum_fusion.2), channel_id=1, source_target_pairs={{0,1},{1,2},{2,3},{3,0},{4,5},{5,6},{6,7},{7,4},{8,9},{9,10},{10,1... | collective-permute-start | bytes 393224 | tf_op jit(solution)/shard_map/ppermute | solution.py:631
  4.6 11.2 %collective-permute-start.1 = (bf16[2,128,256]{2,1,0:T(8,128)(2,1)S(1)}, bf16[2,128,256]{2,1,0:T(8,128)(2,1)S(1)}, u32[]{:S(2)}, u32[]{:S(2)}) collective-permute-start(bf16[2,128,256]{2,1,0:T(8,128)(2,1)S(1)} %pad_maximum_fusion.2), channel_id=1, source_target_pairs={{0,2},{1,3},{2,0},{3,1},{4,6},{5,7},{6,4},{7,5},{8,10},{9,11},{10,... | collective-permute-start | bytes 393224 | tf_op jit(solution)/shard_map/ppermute | solution.py:631
  7.2 8.6 %collective-permute-start.2 = (bf16[2,128,256]{2,1,0:T(8,128)(2,1)S(1)}, bf16[2,128,256]{2,1,0:T(8,128)(2,1)S(1)}, u32[]{:S(2)}, u32[]{:S(2)}) collective-permute-start(bf16[2,128,256]{2,1,0:T(8,128)(2,1)S(1)} %pad_maximum_fusion.2), channel_id=1, source_target_pairs={{0,3},{1,0},{2,1},{3,2},{4,7},{5,4},{6,5},{7,6},{8,11},{9,8},{10,9... | collective-permute-start | bytes 393224 | tf_op jit(solution)/shard_map/ppermute | solution.py:631
  15.9 27.0 %collective-permute-start.3 = (bf16[7,128,256]{2,1,0:T(8,128)(2,1)S(1)}, bf16[7,128,256]{2,1,0:T(8,128)(2,1)S(1)}, u32[]{:S(2)}, u32[]{:S(2)}) collective-permute-start(bf16[7,128,256]{2,1,0:T(8,128)(2,1)S(1)} %pad_maximum_fusion.rest_0_), channel_id=1, source_target_pairs={{0,8},{4,12},{8,16},{12,20},{16,24},{20,28},{24,0},{28,4},{1,9},{5... | collective-permute-start | bytes 1376264 | tf_op jit(solution)/shard_map/ppermute | solution.py:623
  17.5 25.5 %collective-permute-start.4 = (bf16[7,128,256]{2,1,0:T(8,128)(2,1)S(1)}, bf16[7,128,256]{2,1,0:T(8,128)(2,1)S(1)}, u32[]{:S(2)}, u32[]{:S(2)}) collective-permute-start(bf16[7,128,256]{2,1,0:T(8,128)(2,1)S(1)} %pad_maximum_fusion.rest_0_), channel_id=1, source_target_pairs={{0,16},{4,20},{8,24},{12,28},{16,0},{20,4},{24,8},{28,12},{1,17},{... | collective-permute-start | bytes 1376264 | tf_op jit(solution)/shard_map/ppermute | solution.py:623
  19.0 24.0 %collective-permute-start.5 = (bf16[7,128,256]{2,1,0:T(8,128)(2,1)S(1)}, bf16[7,128,256]{2,1,0:T(8,128)(2,1)S(1)}, u32[]{:S(2)}, u32[]{:S(2)}) collective-permute-start(bf16[7,128,256]{2,1,0:T(8,128)(2,1)S(1)} %pad_maximum_fusion.rest_0_), channel_id=1, source_target_pairs={{0,24},{4,28},{8,0},{12,4},{16,8},{20,12},{24,16},{28,20},{1,25},{... | collective-permute-start | bytes 1376264 | tf_op jit(solution)/shard_map/ppermute | solution.py:623
  43.6 2.5 %collective-permute-start.8 = (bf16[7,128,256]{2,1,0:T(8,128)(2,1)S(1)}, bf16[7,128,256]{2,1,0:T(8,128)(2,1)S(1)}, u32[]{:S(2)}, u32[]{:S(2)}) collective-permute-start(bf16[7,128,256]{2,1,0:T(8,128)(2,1)S(1)} %collective-permute-done.4.rest_2_), channel_id=1, source_target_pairs={{0,4},{4,0},{8,12},{12,8},{16,20},{20,16},{24,28},{28,24},{1,5},{5... | collective-permute-start | bytes 1376264 | tf_op jit(solution)/shard_map/ppermute | solution.py:628
  43.7 3.1 %collective-permute-start.9 = (bf16[7,128,256]{2,1,0:T(8,128)(2,1)S(1)}, bf16[7,128,256]{2,1,0:T(8,128)(2,1)S(1)}, u32[]{:S(2)}, u32[]{:S(2)}) collective-permute-start(bf16[7,128,256]{2,1,0:T(8,128)(2,1)S(1)} %collective-permute-done.5.rest_3_), channel_id=1, source_target_pairs={{0,4},{4,0},{8,12},{12,8},{16,20},{20,16},{24,28},{28,24},{1,5},{5... | collective-permute-start | bytes 1376264 | tf_op jit(solution)/shard_map/ppermute | solution.py:628
  61.1 10.3 %all-to-all-start = ((bf16[16,32,180]{2,1,0:T(8,128)(2,1)}), bf16[16,32,180]{2,1,0:T(8,128)(2,1)S(1)}, u32[]{:S(2)}, u32[]{:S(2)}) async-start(bf16[16,32,180]{2,1,0:T(8,128)(2,1)} %teacher_maps.1), calls=%async_computation | async-start | bytes 524288 | tf_op jit(solution)/shard_map/all_to_all | solution.py:681
  96.9 2.6 %collective-permute-start.10 = (bf16[16,24,1024]{2,1,0:T(8,128)(2,1)}, bf16[16,24,1024]{2,1,0:T(8,128)(2,1)S(1)}, u32[]{:S(2)}, u32[]{:S(2)}) collective-permute-start(bf16[16,24,1024]{2,1,0:T(8,128)(2,1)} %get-tuple-element.75), channel_id=1, source_target_pairs={{0,4},{4,0},{8,12},{12,8},{16,20},{20,16},{24,28},{28,24},{1,5},{5... | collective-permute-start | bytes 2359304 | tf_op jit(solution)/shard_map/ppermute | solution.py:628
  101.6 11.0 %collective-permute-start.11 = (bf16[4,24,1024]{2,1,0:T(8,128)(2,1)S(1)}, bf16[4,24,1024]{2,1,0:T(8,128)(2,1)S(1)}, u32[]{:S(2)}, u32[]{:S(2)}) collective-permute-start(bf16[4,24,1024]{2,1,0:T(8,128)(2,1)S(1)} %get-tuple-element.82), channel_id=1, source_target_pairs={{0,8},{4,12},{8,16},{12,20},{16,24},{20,28},{24,0},{28,4},{1,9},{5... | collective-permute-start | bytes 589832 | tf_op jit(solution)/shard_map/ppermute | solution.py:623
  102.2 10.9 %collective-permute-start.12 = (bf16[4,24,1024]{2,1,0:T(8,128)(2,1)S(1)}, bf16[4,24,1024]{2,1,0:T(8,128)(2,1)S(1)}, u32[]{:S(2)}, u32[]{:S(2)}) collective-permute-start(bf16[4,24,1024]{2,1,0:T(8,128)(2,1)S(1)} %get-tuple-element.83), channel_id=1, source_target_pairs={{0,16},{4,20},{8,24},{12,28},{16,0},{20,4},{24,8},{28,12},{1,17},{... | collective-permute-start | bytes 589832 | tf_op jit(solution)/shard_map/ppermute | solution.py:623
  103.1 9.9 %collective-permute-start.13 = (bf16[4,24,1024]{2,1,0:T(8,128)(2,1)S(1)}, bf16[4,24,1024]{2,1,0:T(8,128)(2,1)S(1)}, u32[]{:S(2)}, u32[]{:S(2)}) collective-permute-start(bf16[4,24,1024]{2,1,0:T(8,128)(2,1)S(1)} %get-tuple-element.84), channel_id=1, source_target_pairs={{0,24},{4,28},{8,0},{12,4},{16,8},{20,12},{24,16},{28,20},{1,25},{... | collective-permute-start | bytes 589832 | tf_op jit(solution)/shard_map/ppermute | solution.py:623
  113.8 6.9 %collective-permute-start.14 = (bf16[24,1024]{1,0:T(8,128)(2,1)S(1)}, bf16[24,1024]{1,0:T(8,128)(2,1)S(1)}, u32[]{:S(2)}, u32[]{:S(2)}) collective-permute-start(bf16[24,1024]{1,0:T(8,128)(2,1)S(1)} %get-tuple-element.91), channel_id=1, source_target_pairs={{0,1},{1,2},{2,3},{3,0},{4,5},{5,6},{6,7},{7,4},{8,9},{9,10},{10,1... | collective-permute-start | bytes 147464 | tf_op jit(solution)/shard_map/ppermute | solution.py:631
  117.1 5.7 %collective-permute-start.15 = (bf16[24,1024]{1,0:T(8,128)(2,1)S(1)}, bf16[24,1024]{1,0:T(8,128)(2,1)S(1)}, u32[]{:S(2)}, u32[]{:S(2)}) collective-permute-start(bf16[24,1024]{1,0:T(8,128)(2,1)S(1)} %get-tuple-element.92), channel_id=1, source_target_pairs={{0,2},{1,3},{2,0},{3,1},{4,6},{5,7},{6,4},{7,5},{8,10},{9,11},{10,... | collective-permute-start | bytes 147464 | tf_op jit(solution)/shard_map/ppermute | solution.py:631
  118.8 4.4 %collective-permute-start.16 = (bf16[24,1024]{1,0:T(8,128)(2,1)S(1)}, bf16[24,1024]{1,0:T(8,128)(2,1)S(1)}, u32[]{:S(2)}, u32[]{:S(2)}) collective-permute-start(bf16[24,1024]{1,0:T(8,128)(2,1)S(1)} %get-tuple-element.93), channel_id=1, source_target_pairs={{0,3},{1,0},{2,1},{3,2},{4,7},{5,4},{6,5},{7,6},{8,11},{9,8},{10,9... | collective-permute-start | bytes 147464 | tf_op jit(solution)/shard_map/ppermute | solution.py:631
  123.2 6.0 %collective-permute-start.17 = (bf16[24,1024]{1,0:T(8,128)(2,1)S(1)}, bf16[24,1024]{1,0:T(8,128)(2,1)S(1)}, u32[]{:S(2)}, u32[]{:S(2)}) collective-permute-start(bf16[24,1024]{1,0:T(8,128)(2,1)S(1)} %sum_tensor.1), channel_id=1, source_target_pairs={{0,1},{1,2},{2,3},{3,0},{4,5},{5,6},{6,7},{7,4},{8,9},{9,10},{10,1... | collective-permute-start | bytes 147464 | tf_op jit(solution)/shard_map/ppermute | solution.py:631
  123.8 6.1 %collective-permute-start.18 = (bf16[24,1024]{1,0:T(8,128)(2,1)S(1)}, bf16[24,1024]{1,0:T(8,128)(2,1)S(1)}, u32[]{:S(2)}, u32[]{:S(2)}) collective-permute-start(bf16[24,1024]{1,0:T(8,128)(2,1)S(1)} %sum_tensor.1), channel_id=1, source_target_pairs={{0,2},{1,3},{2,0},{3,1},{4,6},{5,7},{6,4},{7,5},{8,10},{9,11},{10,... | collective-permute-start | bytes 147464 | tf_op jit(solution)/shard_map/ppermute | solution.py:631
  126.1 4.2 %collective-permute-start.19 = (bf16[24,1024]{1,0:T(8,128)(2,1)S(1)}, bf16[24,1024]{1,0:T(8,128)(2,1)S(1)}, u32[]{:S(2)}, u32[]{:S(2)}) collective-permute-start(bf16[24,1024]{1,0:T(8,128)(2,1)S(1)} %sum_tensor.1), channel_id=1, source_target_pairs={{0,3},{1,0},{2,1},{3,2},{4,7},{5,4},{6,5},{7,6},{8,11},{9,8},{10,9... | collective-permute-start | bytes 147464 | tf_op jit(solution)/shard_map/ppermute | solution.py:631
  130.3 7.0 %collective-permute-start.20 = (bf16[4,24,1024]{2,1,0:T(8,128)(2,1)S(1)}, bf16[4,24,1024]{2,1,0:T(8,128)(2,1)S(1)}, u32[]{:S(2)}, u32[]{:S(2)}) collective-permute-start(bf16[4,24,1024]{2,1,0:T(8,128)(2,1)S(1)} %pad_maximum_fusion.1.rest_0_), channel_id=1, source_target_pairs={{0,8},{4,12},{8,16},{12,20},{16,24},{20,28},{24,0},{28,4},{1,9},{5... | collective-permute-start | bytes 589832 | tf_op jit(solution)/shard_map/ppermute | solution.py:623
  131.8 7.5 %collective-permute-start.21 = (bf16[4,24,1024]{2,1,0:T(8,128)(2,1)S(1)}, bf16[4,24,1024]{2,1,0:T(8,128)(2,1)S(1)}, u32[]{:S(2)}, u32[]{:S(2)}) collective-permute-start(bf16[4,24,1024]{2,1,0:T(8,128)(2,1)S(1)} %pad_maximum_fusion.1.rest_0_), channel_id=1, source_target_pairs={{0,16},{4,20},{8,24},{12,28},{16,0},{20,4},{24,8},{28,12},{1,17},{... | collective-permute-start | bytes 589832 | tf_op jit(solution)/shard_map/ppermute | solution.py:623
  133.8 5.7 %collective-permute-start.22 = (bf16[4,24,1024]{2,1,0:T(8,128)(2,1)S(1)}, bf16[4,24,1024]{2,1,0:T(8,128)(2,1)S(1)}, u32[]{:S(2)}, u32[]{:S(2)}) collective-permute-start(bf16[4,24,1024]{2,1,0:T(8,128)(2,1)S(1)} %pad_maximum_fusion.1.rest_0_), channel_id=1, source_target_pairs={{0,24},{4,28},{8,0},{12,4},{16,8},{20,12},{24,16},{28,20},{1,25},{... | collective-permute-start | bytes 589832 | tf_op jit(solution)/shard_map/ppermute | solution.py:623
  134.8 5.2 %collective-permute-start.23 = (bf16[4,24,1024]{2,1,0:T(8,128)(2,1)S(1)}, bf16[4,24,1024]{2,1,0:T(8,128)(2,1)S(1)}, u32[]{:S(2)}, u32[]{:S(2)}) collective-permute-start(bf16[4,24,1024]{2,1,0:T(8,128)(2,1)S(1)} %pad_maximum_fusion.1.rest_0_), channel_id=1, source_target_pairs={{0,4},{4,0},{8,12},{12,8},{16,20},{20,16},{24,28},{28,24},{1,5},{5... | collective-permute-start | bytes 589832 | tf_op jit(solution)/shard_map/ppermute | solution.py:628
  137.3 2.7 %collective-permute-start.24 = (bf16[4,24,1024]{2,1,0:T(8,128)(2,1)S(1)}, bf16[4,24,1024]{2,1,0:T(8,128)(2,1)S(1)}, u32[]{:S(2)}, u32[]{:S(2)}) collective-permute-start(bf16[4,24,1024]{2,1,0:T(8,128)(2,1)S(1)} %collective-permute-done.20.rest_1_), channel_id=1, source_target_pairs={{0,4},{4,0},{8,12},{12,8},{16,20},{20,16},{24,28},{28,24},{1,5},{5... | collective-permute-start | bytes 589832 | tf_op jit(solution)/shard_map/ppermute | solution.py:628
  (15 other events, 81.6 us)

commit v7 on v5

--- a/solution.py
+++ b/solution.py
@@ -14,14 +14,12 @@
 CORES = 2
 VMEM_LIMIT = 56 * 1024 * 1024
 SMALL_LIMIT = 14 * 1024 * 1024
-BACKWARD_LIMIT = 46 * 1024 * 1024
 
 F32 = jnp.float32
 BF16 = jnp.bfloat16
 VMEM = pl.BlockSpec(memory_space=pltpu.VMEM)
 SMEM = pl.BlockSpec(memory_space=pltpu.SMEM)
 ANY = pl.BlockSpec(memory_space=pl.ANY)
-TOKEN = jax.ShapeDtypeStruct((8, 128), F32)
 
 
 def up(n, m):
@@ -91,8 +89,8 @@
 
 
 def teacher_kernel(parts, count, tokens, order_ref, from_ref, rows_ref, states_ref, wq_ref, wk_ref, *rest):
-    pieces, out_ref, token_ref = rest[:parts], rest[parts], rest[parts + 1]
-    w_s, own_s, q_s, g_s, key_s, e_s, map_s, q_sem, key_sem, w_sem, own_sem = rest[parts + 2 :]
+    pieces, out_ref = rest[:parts], rest[parts]
+    w_s, own_s, q_s, a_s, g_s, key_s, e_s, map_s, q_sem, key_sem, w_sem, own_sem = rest[parts + 1 :]
     depth = q_s.shape[1]
     slices = w_s.shape[0] // 2
     part_rows = pieces[0].shape[1]
@@ -129,11 +127,14 @@
     for copy in keys:
         copy.start()
     q = q_s[...]
-    mixed = dot(dot(q, own_s[0], 1, 0).astype(BF16), own_s[1], 1, 1)
+    heads = own_s.shape[2]
+    a_s[:, slices * heads :] = dot(q, own_s[0], 1, 0).astype(BF16)
     for copy in gathered:
         copy.wait()
     for k in range(slices):
-        mixed = mixed + dot(dot(q, w_s[2 * k], 1, 0).astype(BF16), w_s[2 * k + 1], 1, 1)
+        a_s[:, k * heads : (k + 1) * heads] = dot(q, w_s[2 * k], 1, 0).astype(BF16)
+    keys_weight = jnp.concatenate([w_s[2 * k + 1] for k in range(slices)] + [own_s[1]], axis=1)
+    mixed = dot(a_s[...], keys_weight, 1, 1)
     for v in range(depth // 128):
         g_s[v] = mixed[:, v * 128 : (v + 1) * 128]
         for p in range(count):
@@ -163,7 +164,6 @@
     per = count // parts
     for n in range(count):
         out_ref[n] = map_s[order_ref[from_ref[n // per], n % per]]
-    token_ref[...] = jnp.zeros_like(token_ref)
 
 
 def teacher_maps(order, source, rows, slices, states, wq, wk, pieces, count, tokens):
@@ -175,12 +175,13 @@
     return pl.pallas_call(
         functools.partial(teacher_kernel, parts, count, tokens),
         in_specs=[SMEM] * 3 + [ANY] * (3 + parts),
-        out_specs=[VMEM, VMEM],
-        out_shape=[jax.ShapeDtypeStruct((count, tokens, keys // count), BF16), TOKEN],
+        out_specs=VMEM,
+        out_shape=jax.ShapeDtypeStruct((count, tokens, keys // count), BF16),
         scratch_shapes=[
             pltpu.VMEM((slices, depth, heads), BF16),
             pltpu.VMEM((2, depth, heads), BF16),
             pltpu.VMEM((count * tokens, depth), BF16),
+            pltpu.VMEM((count * tokens, (slices // 2 + 1) * heads), BF16),
             pltpu.VMEM((depth // 128, count * tokens, 128), F32),
             pltpu.VMEM((keys, depth), BF16),
             pltpu.VMEM((keys, 128), F32),
@@ -212,9 +213,9 @@
     return jnp.concatenate([held[a, n * each : (n + 1) * each] for n in range(width // heads)], axis=1)
 
 
-def scores_kernel(tokens, count, group_queries, slices, parts, qidx_ref, len_ref, emb_ref, wp_ref, after_ref, *rest):
+def scores_kernel(tokens, count, group_queries, slices, parts, qidx_ref, len_ref, emb_ref, wp_ref, *rest):
     pieces = rest[:parts]
-    (prob_ref, log_ref, units_ref, qunit_ref, qdir_ref, qlen_ref, qs_s, dir_s, held_s, sem) = rest[parts:]
+    (prob_ref, log_ref, units_ref, qunit_ref, qdir_ref, qlen_ref, qs_ref, dir_s, held_s, sem) = rest[parts:]
     copies = rider_copies(pieces, slices, held_s, sem)
     for copy in copies:
         copy.start()
@@ -222,19 +223,19 @@
     seq = total // count
     sub = split_rows(total, 128)
     each = group_queries * tokens
+    for b in range(0, total, sub):
+        e = emb_ref[b : b + sub]
+        dir_s[b : b + sub] = e / jnp.sqrt(jnp.sum(e * e, axis=-1, keepdims=True) + epsilon)
     for copy in copies:
         copy.wait()
     for a in range(parts):
-        qs_s[a * each : (a + 1) * each] = rider_states(held_s, a, each, qs_s.shape[1])
-    qe = dot(qs_s[...], wp_ref[...], 1, 0)
+        qs_ref[a * each : (a + 1) * each] = rider_states(held_s, a, each, qs_ref.shape[1])
+    qe = dot(qs_ref[...], wp_ref[...], 1, 0)
     length = jnp.sqrt(jnp.sum(qe * qe, axis=-1, keepdims=True) + epsilon)
     qdir = qe / length
     qdir_ref[...] = qdir
     qlen_ref[...] = jnp.broadcast_to(length, qlen_ref.shape)
     qunit_ref[...] = qdir.astype(BF16).reshape(qunit_ref.shape)
-    for b in range(0, total, sub):
-        e = emb_ref[b : b + sub]
-        dir_s[b : b + sub] = e / jnp.sqrt(jnp.sum(e * e, axis=-1, keepdims=True) + epsilon)
     for r in range(count):
         units = dir_s[pl.ds(r, seq, stride=count), :].astype(BF16)
         units_ref[r] = units
@@ -246,7 +247,7 @@
         log_ref[r] = logits - jnp.log(student_total)
 
 
-def student_scores(qidx, lens, embeds, wp, after, pieces, slices, count, tokens, group_queries):
+def student_scores(qidx, lens, embeds, wp, pieces, slices, count, tokens, group_queries):
     total, emb = embeds.shape
     seq = total // count
     parts = len(pieces)
@@ -255,8 +256,8 @@
     riders -= slices
     return pl.pallas_call(
         functools.partial(scores_kernel, tokens, count, group_queries, slices, parts),
-        in_specs=[SMEM, SMEM, VMEM, VMEM] + [ANY] * (1 + parts),
-        out_specs=[VMEM] * 6,
+        in_specs=[SMEM, SMEM, VMEM, VMEM] + [ANY] * parts,
+        out_specs=[VMEM] * 7,
         out_shape=[
             jax.ShapeDtypeStruct((count, tokens, seq), F32),
             jax.ShapeDtypeStruct((count, tokens, seq), F32),
@@ -264,9 +265,9 @@
             jax.ShapeDtypeStruct((queries, tokens, emb), BF16),
             jax.ShapeDtypeStruct((queries * tokens, emb), F32),
             jax.ShapeDtypeStruct((queries * tokens, 128), F32),
+            jax.ShapeDtypeStruct((queries * tokens, wp.shape[0]), BF16),
         ],
         scratch_shapes=[
-            pltpu.VMEM((queries * tokens, wp.shape[0]), BF16),
             pltpu.VMEM((total, emb), F32),
             pltpu.VMEM((parts, riders * part, heads), BF16),
             pltpu.SemaphoreType.DMA((parts * riders,)),
@@ -274,7 +275,7 @@
         compiler_params=params(),
         cost_estimate=cost(1e9, 4 * total * emb),
         name="student_scores",
-    )(qidx, lens, embeds, wp, after, *pieces)
+    )(qidx, lens, embeds, wp, *pieces)
 
 
 def two_parts(a, b):
@@ -284,16 +285,15 @@
 
 
 def backward_kernel(
-    tokens, count, blocks, group_queries, slices, parts,
-    qidx_ref, midx_ref, len_ref, core_ref, *rest,
-):
-    pieces = rest[:parts]
-    (maps_in, prob_in, log_in, units_in, qunit_in, emb_in, x_in, normed_in, inv_in,
+    tokens, count, blocks,
+    qidx_ref, midx_ref, len_ref, core_ref,
+    maps_in, prob_in, log_in, units_in, qunit_in, emb_in, x_in, normed_in, inv_in, qs_in,
     qdir_ref, qlen_ref, gain_ref, bias_ref, wp_ref, wpt_ref,
     sg_out, send_ref, keep_ref,
-    maps_s, prob_s, log_s, units_s, qunit_s, emb_s, x_s, normed_s, inv_s, held_s,
+    maps_s, prob_s, log_s, units_s, qunit_s, emb_s, x_s, normed_s, inv_s, qs_s,
     up_s, eg_s, mean_s, along_s, un_s, qg_s, hg_s, sg_s, wo_s, nt_s, right_s,
-    first_sem, block_sem, out_sem, last_sem) = rest[parts:]
+    first_sem, block_sem, out_sem, last_sem,
+):
     total, width = normed_s.shape
     emb = emb_s.shape[1]
     seq = total // count
@@ -319,7 +319,7 @@
         ]
         for b in range(blocks)
     ]
-    last = rider_copies(pieces, slices, held_s, last_sem)
+    last = pltpu.make_async_copy(qs_in, qs_s, last_sem)
     for copy in first:
         copy.start()
     gain, bias = one_row(gain_ref), one_row(bias_ref)
@@ -333,8 +333,7 @@
     for pair in loads:
         for copy in pair:
             copy.start()
-    for copy in last:
-        copy.start()
+    last.start()
 
     spread = jnp.zeros((tokens, 1), F32)
     for r in range(count):
@@ -392,19 +391,14 @@
 
     lax.fori_loop(0, blocks, wide, 0)
 
-    for copy in last:
-        copy.wait()
+    last.wait()
     qg = qg_s[...].reshape(qdir_ref.shape)
     qdir = qdir_ref[...]
     qeg = (qg - qdir * jnp.sum(qdir * qg, axis=-1, keepdims=True)) / qlen_ref[:, :1]
     high = qeg.astype(BF16)
     low = (qeg - high.astype(F32)).astype(BF16)
-    each = group_queries * tokens
-    proj_query = jnp.zeros((emb, width), F32)
-    for k in range(parts):
-        qs = rider_states(held_s, k, each, width)
-        part = slice(k * each, (k + 1) * each)
-        proj_query = proj_query + (dot(high[part], qs, 0, 0) + dot(low[part], qs, 0, 0))
+    qs = qs_s[...]
+    proj_query = dot(high, qs, 0, 0) + dot(low, qs, 0, 0)
     nt = nt_s[...]
     s = jnp.broadcast_to(total_eg, (emb, emb)).T[:, :1]
     wpt = wpt_ref[...].astype(F32)
@@ -430,26 +424,22 @@
 
 
 def student_backward(
-    qidx, midx, lens, core, maps, scores, pieces, slices, embeds, x, normed, inverse, gain, bias, wp, wpt,
+    qidx, midx, lens, core, maps, scores, embeds, x, normed, inverse, gain, bias, wp, wpt,
     count, tokens, group_queries, chunk,
 ):
     total, width = normed.shape
     emb = wp.shape[1]
     blocks = x.shape[0]
     chunks = width // CORES // chunk
-    prob, log, units, qunit, qdir, qlen = scores
-    manual = [maps, prob, log, units, qunit, embeds, x, normed, inverse]
-    parts = len(pieces)
-    riders, part, heads = pieces[0].shape
-    riders -= slices
+    prob, log, units, qunit, qdir, qlen, qs = scores
+    manual = [maps, prob, log, units, qunit, embeds, x, normed, inverse, qs]
     packed = jax.ShapeDtypeStruct((chunks, chunk, width + emb + 128), BF16)
     return pl.pallas_call(
-        functools.partial(backward_kernel, tokens, count, blocks, group_queries, slices, parts),
-        in_specs=[SMEM] * 4 + [ANY] * (parts + len(manual)) + [VMEM] * 6,
+        functools.partial(backward_kernel, tokens, count, blocks),
+        in_specs=[SMEM] * 4 + [ANY] * len(manual) + [VMEM] * 6,
         out_specs=[ANY, VMEM, VMEM],
         scratch_shapes=[pltpu.VMEM(a.shape, a.dtype) for a in manual]
         + [
-            pltpu.VMEM((parts, riders * part, heads), BF16),
             pltpu.VMEM((total, emb), F32),
             pltpu.VMEM((total, emb), BF16),
             pltpu.VMEM((total, 128), F32),
@@ -464,63 +454,59 @@
             pltpu.SemaphoreType.DMA((7,)),
             pltpu.SemaphoreType.DMA((2 * blocks,)),
             pltpu.SemaphoreType.DMA((blocks,)),
-            pltpu.SemaphoreType.DMA((parts * riders,)),
+            pltpu.SemaphoreType.DMA,
         ],
         out_shape=[jax.ShapeDtypeStruct((total, width), BF16), packed, packed],
-        compiler_params=pltpu.CompilerParams(vmem_limit_bytes=BACKWARD_LIMIT),
+        compiler_params=params(),
         cost_estimate=cost(2 * total * width * (width + 2 * emb), 8 * total * width),
         name="student_backward",
-    )(qidx, midx, lens, core, *pieces, *manual, qdir, qlen, gain, bias, wp, wpt)
-
-
-def context_kernel(sg_ref, wo_ref, after_ref, out_ref, token_ref):
-    token_ref[...] = jnp.zeros_like(token_ref)
+    )(qidx, midx, lens, core, *manual, qdir, qlen, gain, bias, wp, wpt)
+
+
+def context_kernel(sg_ref, wo_ref, out_ref):
     out_ref[...] = dot(sg_ref[...], wo_ref[...], 1, 1).astype(BF16)
 
 
-def context_grad(sg, out_weight, after):
+def context_grad(sg, out_weight):
     total, width = sg.shape
     rows = split_rows(total, 720)
     block = pl.BlockSpec((rows, width), lambda s: (s, 0))
     return pl.pallas_call(
         context_kernel,
         grid=(total // rows,),
-        in_specs=[block, pl.BlockSpec(out_weight.shape, lambda s: (0, 0)), ANY],
-        out_specs=[block, pl.BlockSpec(TOKEN.shape, lambda s: (0, 0))],
-        out_shape=[jax.ShapeDtypeStruct(sg.shape, BF16), TOKEN],
+        in_specs=[block, pl.BlockSpec(out_weight.shape, lambda s: (0, 0))],
+        out_specs=block,
+        out_shape=jax.ShapeDtypeStruct(sg.shape, BF16),
         compiler_params=params(),
         cost_estimate=cost(2 * total * width * width, 4 * total * width),
         name="context_grad",
-    )(sg, out_weight, after)
-
-
-def split_sum_kernel(inputs, outputs, after, index_ref, *rest):
-    ins, outs = rest[:inputs], rest[inputs + after : inputs + after + outputs]
-    token_ref, total_s = rest[-2:]
+    )(sg, out_weight)
+
+
+def split_sum_kernel(inputs, outputs, index_ref, *rest):
+    ins, outs, total_s = rest[:inputs], rest[inputs : inputs + outputs], rest[-1]
     total = ins[0][...].astype(F32)
     for ref in ins[1:]:
         total = total + ref[...].astype(F32)
     total_s[...] = total.astype(BF16).reshape(total_s.shape)
     for k in range(outputs):
         outs[k][...] = total_s[index_ref[k]].reshape(outs[k].shape)
-    token_ref[...] = jnp.zeros_like(token_ref)
-
-
-def split_sum(arrays, index, name, after=()):
+
+
+def split_sum(arrays, index, name):
     outputs = index.shape[0]
     shape = arrays[0].shape
     lead = shape[0] // outputs
     out = shape[1:] if lead == 1 else (lead,) + shape[1:]
-    *parts, token = pl.pallas_call(
-        functools.partial(split_sum_kernel, len(arrays), outputs, len(after)),
-        in_specs=[SMEM] + [VMEM] * len(arrays) + [ANY] * len(after),
-        out_specs=[VMEM] * (outputs + 1),
-        out_shape=[jax.ShapeDtypeStruct(out, BF16)] * outputs + [TOKEN],
+    return pl.pallas_call(
+        functools.partial(split_sum_kernel, len(arrays), outputs),
+        in_specs=[SMEM] + [VMEM] * len(arrays),
+        out_specs=[VMEM] * outputs,
+        out_shape=[jax.ShapeDtypeStruct(out, BF16)] * outputs,
         scratch_shapes=[pltpu.VMEM((outputs, lead) + shape[1:], BF16)],
         compiler_params=pltpu.CompilerParams(vmem_limit_bytes=SMALL_LIMIT),
         name=name,
-    )(index, *arrays, *after)
-    return parts, token
+    )(index, *arrays)
 
 
 def sum_kernel(*refs):
@@ -660,16 +646,17 @@
     pieces = pieces + [swap_core(a) for a in pieces]
     told = [a[slices:].reshape(-1, heads)[width // heads * each, :count] for a in pieces]
     order = lax.dynamic_slice_in_dim(jnp.stack(told), me * per, per, 1).astype(jnp.int32)
-    maps, token = teacher_maps(
+    maps = teacher_maps(
         order, source, piece_rows, slices, flat(teacher_states), teacher_query, teacher_key, pieces, count, tokens
     )
+    maps, embeds = lax.optimization_barrier((maps, embeds))
     maps = lax.all_to_all(maps, "dp", split_axis=0, concat_axis=0, tiled=True)
     scores = student_scores(
-        qidx, passage_len, embeds, proj_weight, token, pieces, slices, count, tokens, group_queries
+        qidx, passage_len, embeds, proj_weight, pieces, slices, count, tokens, group_queries
     )
     chunk = width // (CORES * chips * nt)
     sg, send, keep = student_backward(
-        qidx, midx, passage_len, core.astype(jnp.int32).reshape(1), maps, scores, pieces, slices,
+        qidx, midx, passage_len, core.astype(jnp.int32).reshape(1), maps, scores,
         embeds, turned, normed, inverse, gain2, bias2, proj_weight, proj_turned,
         count, tokens, group_queries, chunk,
     )
@@ -677,10 +664,12 @@
     ahead = ((chip + shifts) % chips).astype(jnp.int32)
     t_shifts = jnp.arange(nt, dtype=jnp.int32)
     t_ahead = ((mt + t_shifts) % nt).astype(jnp.int32)
-    parts, token = split_sum([keep, swap_core(send)], ahead, "sum_cores")
-    grad_context, token = context_grad(sg, out_weight, token)
+    parts = split_sum([keep, swap_core(send)], ahead, "sum_cores")
+    parts, sg = lax.optimization_barrier((parts, sg))
+    grad_context = context_grad(sg, out_weight)
     parts = [parts[0]] + [shift_chip(parts[k], k) for k in range(1, chips)]
-    parts, _ = split_sum(parts, t_ahead, "sum_plane", (token,))
+    parts, grad_context = lax.optimization_barrier((parts, grad_context))
+    parts = split_sum(parts, t_ahead, "sum_plane")
     parts = [parts[0]] + [shift_t(parts[k], k) for k in range(1, nt)]
     total = plain_sum(parts, "sum_tensor")
     line = jnp.stack([total] + [shift_t(total, k) for k in range(1, nt)])

time: 148 us -> 136 us (0.919)
  local copies, waits for them, and re-layouts: 15.6 us -> 6.23 us
    unnamed x65 -> x23, local copies, waits for them, and re-layouts: 13.7 us -> 4.4 us
  transfers between devices with their start and end apart: 28 -> 28, of which waited for: 19 -> 18; matrix products, arithmetic and copies ran while one was open for 3% -> 4% of each run, Pallas kernels for 17% -> 19%
where the time goes in v7:
time: 136 us; the launch traced here: 135 us
  Pallas kernels  63 us (46%)
  starting transfers between devices  34.6 us (25%)
  waiting for transfers between devices  27 us (20%)
  local copies, waits for them, and re-layouts  6.23 us (5%)
  other arithmetic  3.13 us (2%)
    pallas_call x1, Pallas kernels, student_backward(): pl.pallas_call(functools.partial(backward_kernel, tokens, count, blocks),...  22.2 us
    ppermute x9, starting transfers between devices, shift_t(): return lax.ppermute(x, 'tensor', [(t, (t + k) % nt) for t in range(nt)])  17.6 us
    pallas_call x1, Pallas kernels, student_forward(): pl.pallas_call(forward_kernel, grid=(total // rows,), in_specs=[block(wid...  12.5 us
    ppermute x9, starting transfers between devices, shift_chip(): lax.ppermute(x, 'dp', [(c * CORES + o, (c + k) % chips * CORES + o) for c...  12.2 us
    pallas_call x1, Pallas kernels, teacher_maps(): pl.pallas_call(functools.partial(teacher_kernel, parts, count, tokens), i...  11.6 us
    ppermute x9, waiting for transfers between devices, shift_chip(): lax.ppermute(x, 'dp', [(c * CORES + o, (c + k) % chips * CORES + o) for c...  10.4 us
    ppermute x9, waiting for transfers between devices, shift_t(): return lax.ppermute(x, 'tensor', [(t, (t + k) % nt) for t in range(nt)])  9.11 us
    pallas_call x1, Pallas kernels, context_grad(): pl.pallas_call(context_kernel, grid=(total // rows,), in_specs=[block, pl...  7.52 us
  transfers between devices with their start and end apart: 28, of which 18 were waited for; matrix products, arithmetic and copies ran while one was open for 4% of the time, Pallas kernels for 19%

profile of v7, /device:TPU:0, one launch (start us, length us, event | category | flops | bytes accessed | tf_op | source)
XLA Modules:
  0.0 135.0 jit_solution(16880560336510121463)
XLA Ops:
  1.5 3.1 %collective-permute-start = (bf16[2,128,256]{2,1,0:T(8,128)(2,1)S(1)}, bf16[2,128,256]{2,1,0:T(8,128)(2,1)S(1)}, u32[]{:S(2)}, u32[]{:S(2)}) collective-permute-start(bf16[2,128,256]{2,1,0:T(8,128)(2,1)S(1)} %pad_maximum_fusion.2), channel_id=1, source_target_pairs={{0,1},{1,2},{2,3},{3,0},{4,5},{5,6},{6,7},{7,4},{8,9},{9,10},{10,1... | collective-permute-start | bytes 393224 | tf_op jit(solution)/shard_map/ppermute | solution.py:604
  4.6 2.6 %collective-permute-start.1 = (bf16[2,128,256]{2,1,0:T(8,128)(2,1)S(1)}, bf16[2,128,256]{2,1,0:T(8,128)(2,1)S(1)}, u32[]{:S(2)}, u32[]{:S(2)}) collective-permute-start(bf16[2,128,256]{2,1,0:T(8,128)(2,1)S(1)} %pad_maximum_fusion.2), channel_id=1, source_target_pairs={{0,2},{1,3},{2,0},{3,1},{4,6},{5,7},{6,4},{7,5},{8,10},{9,11},{10,... | collective-permute-start | bytes 393224 | tf_op jit(solution)/shard_map/ppermute | solution.py:604
  10.8 1.8 %copy.20 = bf16[768,128]{0,1:T(8,128)(2,1)} copy(bf16[768,128]{1,0:T(8,128)(2,1)} %wp_ref.5) | data formatting | bytes 393216 | tf_op args[5]
  12.6 3.2 %collective-permute-done.1 = bf16[2,128,256]{2,1,0:T(8,128)(2,1)S(1)} collective-permute-done((bf16[2,128,256]{2,1,0:T(8,128)(2,1)S(1)}, bf16[2,128,256]{2,1,0:T(8,128)(2,1)S(1)}, u32[]{:S(2)}, u32[]{:S(2)}) %collective-permute-start.1) | collective-permute-done | bytes 131104 | tf_op jit(solution)/shard_map/ppermute | solution.py:604
  15.9 1.5 %collective-permute-start.3 = (bf16[7,128,256]{2,1,0:T(8,128)(2,1)S(1)}, bf16[7,128,256]{2,1,0:T(8,128)(2,1)S(1)}, u32[]{:S(2)}, u32[]{:S(2)}) collective-permute-start(bf16[7,128,256]{2,1,0:T(8,128)(2,1)S(1)} %pad_maximum_fusion.rest_0_), channel_id=1, source_target_pairs={{0,8},{4,12},{8,16},{12,20},{16,24},{20,28},{24,0},{28,4},{1,9},{5... | collective-permute-start | bytes 1376264 | tf_op jit(solution)/shard_map/ppermute | solution.py:596
  21.1 12.5 %student_forward.1 = (bf16[2880,768]{1,0:T(8,128)(2,1)}, f32[2880,128]{1,0:T(8,128)}, f32[2880,128]{1,0:T(8,128)}, bf16[4,768,720]{2,1,0:T(8,128)(2,1)}) custom-call(bf16[2880,768]{1,0:T(8,128)(2,1)} %bitcast.55, bf16[2880,768]{1,0:T(8,128)(2,1)} %bitcast.56, bf16[768,768]{1,0:T(8,128)(2,1)} %wo_ref.3, f32[6,128]{1,0:T(8,128)} %bitcast.59, ...), custom_call_target="tpu_custom_call" | custom-call | flops 3963617280 | bytes 17694720 | tf_op jit(solution)/shard_map/student_forward/pallas_call | solution.py:73
  33.7 5.3 %collective-permute-done.4.rest_2_ = bf16[7,128,256]{2,1,0:T(8,128)(2,1)S(1)} collective-permute-done((bf16[7,128,256]{2,1,0:T(8,128)(2,1)S(1)}, bf16[7,128,256]{2,1,0:T(8,128)(2,1)S(1)}, u32[]{:S(2)}, u32[]{:S(2)}) %collective-permute-start.4) | collective-permute-done | bytes 458784 | tf_op jit(solution)/shard_map/ppermute | solution.py:596
  43.8 11.6 %teacher_maps.1 = bf16[16,32,180]{2,1,0:T(8,128)(2,1)} custom-call(s32[8,2]{1,0:T(8,128)} %dynamic-slice_convert_fusion.order_ref, s32[8]{0:T(128)} %get-tuple-element.108.from_ref, s32[8]{0:T(128)} %get-tuple-element.109.rows_ref, bf16[3392,1024]{1,0:T(8,128)(2,1)} %bitcast.54, bf16[1024,256]{1,0:T(8,128)(2,1)} %wq_ref.1, bf16[1024,256]{1,0:T(8,128)(2,1)} %wk_ref.1, ...), custom_call_target="tpu_custom_call" | custom-call | flops 4294967296 | bytes 11141120 | tf_op jit(solution)/shard_map/teacher_maps/pallas_call | solution.py:175
  55.4 3.6 %all-to-all-start = ((bf16[16,32,180]{2,1,0:T(8,128)(2,1)}), bf16[16,32,180]{2,1,0:T(8,128)(2,1)S(1)}, u32[]{:S(2)}, u32[]{:S(2)}) async-start(bf16[16,32,180]{2,1,0:T(8,128)(2,1)} %teacher_maps.1), calls=%async_computation | async-start | bytes 524288 | tf_op jit(solution)/shard_map/all_to_all | solution.py:653
  59.0 5.1 %student_scores.1 = (f32[16,32,180]{2,1,0:T(8,128)}, f32[16,32,180]{2,1,0:T(8,128)}, bf16[16,180,128]{2,1,0:T(8,128)(2,1)}, bf16[8,32,128]{2,1,0:T(8,128)(2,1)},...) custom-call(s32[16]{0:T(128)} %get-tuple-element.100.qidx_ref, s32[16]{0:T(128)} %len_ref.3, ...), custom_call_target="tpu_custom_call" | custom-call | flops 1000000000 | bytes 1474560 | tf_op jit(solution)/shard_map/student_scores/pallas_call | solution.py:257
  64.1 1.6 %all-to-all-done.maps_in = bf16[16,32,180]{2,1,0:T(8,128)(2,1)S(1)} async-done(((bf16[16,32,180]{2,1,0:T(8,128)(2,1)}), bf16[16,32,180]{2,1,0:T(8,128)(2,1)S(1)}, u32[]{:S(2)}, u32[]{:S(2)}) %all-to-all-start) | async-done | bytes 184352 | tf_op jit(solution)/shard_map/all_to_all | solution.py:653
  66.4 22.2 %student_backward.1 = (bf16[2880,768]{1,0:T(8,128)(2,1)}, bf16[16,24,1024]{2,1,0:T(8,128)(2,1)}, bf16[16,24,1024]{2,1,0:T(8,128)(2,1)}) custom-call(s32[16]{0:T(128)} %get-tuple-element.100.qidx_ref, s32[16]{0:T(128)} %copy-done.10, s32[16]{0:T(128)} %len_ref.3, s32[1]{0:T(128)} %bitcast.core_ref, bf16[16,32,180]{2,1,0:T(8,128)(2,1)} %copy-done.9, ...), custom_call_target="tpu_custom_call" | custom-call | flops 4529848320 | bytes 17694720 | tf_op jit(solution)/shard_map/student_backward/pallas_call | solution.py:437
  88.7 2.4 %collective-permute-done.10.rest_1_ = bf16[16,24,1024]{2,1,0:T(8,128)(2,1)S(1)} collective-permute-done((bf16[16,24,1024]{2,1,0:T(8,128)(2,1)}, bf16[16,24,1024]{2,1,0:T(8,128)(2,1)S(1)}, u32[]{:S(2)}, u32[]{:S(2)}) %collective-permute-start.10) | collective-permute-done | bytes 786464 | tf_op jit(solution)/shard_map/ppermute | solution.py:601
  95.0 1.8 %collective-permute-start.13 = (bf16[4,24,1024]{2,1,0:T(8,128)(2,1)S(1)}, bf16[4,24,1024]{2,1,0:T(8,128)(2,1)S(1)}, u32[]{:S(2)}, u32[]{:S(2)}) collective-permute-start(bf16[4,24,1024]{2,1,0:T(8,128)(2,1)S(1)} %get-tuple-element.84), channel_id=1, source_target_pairs={{0,24},{4,28},{8,0},{12,4},{16,8},{20,12},{24,16},{28,20},{1,25},{... | collective-permute-start | bytes 589832 | tf_op jit(solution)/shard_map/ppermute | solution.py:596
  96.9 7.5 %context_grad.1 = bf16[2880,768]{1,0:T(8,128)(2,1)} custom-call(bf16[2880,768]{1,0:T(8,128)(2,1)} %get-tuple-element.85.sg_ref, bf16[768,768]{1,0:T(8,128)(2,1)} %wo_ref.3), custom_call_target="tpu_custom_call" | custom-call | flops 3397386240 | bytes 8847360 | tf_op jit(solution)/shard_map/context_grad/pallas_call | solution.py:474
  105.5 3.4 %collective-permute-start.14 = (bf16[24,1024]{1,0:T(8,128)(2,1)S(1)}, bf16[24,1024]{1,0:T(8,128)(2,1)S(1)}, u32[]{:S(2)}, u32[]{:S(2)}) collective-permute-start(bf16[24,1024]{1,0:T(8,128)(2,1)S(1)} %get-tuple-element.91), channel_id=1, source_target_pairs={{0,1},{1,2},{2,3},{3,0},{4,5},{5,6},{6,7},{7,4},{8,9},{9,10},{10,1... | collective-permute-start | bytes 147464 | tf_op jit(solution)/shard_map/ppermute | solution.py:604
  109.5 1.8 %collective-permute-start.16 = (bf16[24,1024]{1,0:T(8,128)(2,1)S(1)}, bf16[24,1024]{1,0:T(8,128)(2,1)S(1)}, u32[]{:S(2)}, u32[]{:S(2)}) collective-permute-start(bf16[24,1024]{1,0:T(8,128)(2,1)S(1)} %get-tuple-element.93), channel_id=1, source_target_pairs={{0,3},{1,0},{2,1},{3,2},{4,7},{5,4},{6,5},{7,6},{8,11},{9,8},{10,9... | collective-permute-start | bytes 147464 | tf_op jit(solution)/shard_map/ppermute | solution.py:604
  111.7 2.5 %collective-permute-done.15.refs_2_ = bf16[24,1024]{1,0:T(8,128)(2,1)S(1)} collective-permute-done((bf16[24,1024]{1,0:T(8,128)(2,1)S(1)}, bf16[24,1024]{1,0:T(8,128)(2,1)S(1)}, u32[]{:S(2)}, u32[]{:S(2)}) %collective-permute-start.15) | collective-permute-done | bytes 49184 | tf_op jit(solution)/shard_map/ppermute | solution.py:604
  115.4 2.5 %collective-permute-start.18 = (bf16[24,1024]{1,0:T(8,128)(2,1)S(1)}, bf16[24,1024]{1,0:T(8,128)(2,1)S(1)}, u32[]{:S(2)}, u32[]{:S(2)}) collective-permute-start(bf16[24,1024]{1,0:T(8,128)(2,1)S(1)} %sum_tensor.1), channel_id=1, source_target_pairs={{0,2},{1,3},{2,0},{3,1},{4,6},{5,7},{6,4},{7,5},{8,10},{9,11},{10,... | collective-permute-start | bytes 147464 | tf_op jit(solution)/shard_map/ppermute | solution.py:604
  122.1 1.6 %collective-permute-start.20 = (bf16[4,24,1024]{2,1,0:T(8,128)(2,1)S(1)}, bf16[4,24,1024]{2,1,0:T(8,128)(2,1)S(1)}, u32[]{:S(2)}, u32[]{:S(2)}) collective-permute-start(bf16[4,24,1024]{2,1,0:T(8,128)(2,1)S(1)} %pad_maximum_fusion.1.rest_0_), channel_id=1, source_target_pairs={{0,8},{4,12},{8,16},{12,20},{16,24},{20,28},{24,0},{28,4},{1,9},{5... | collective-permute-start | bytes 589832 | tf_op jit(solution)/shard_map/ppermute | solution.py:596
  123.6 1.5 %collective-permute-start.21 = (bf16[4,24,1024]{2,1,0:T(8,128)(2,1)S(1)}, bf16[4,24,1024]{2,1,0:T(8,128)(2,1)S(1)}, u32[]{:S(2)}, u32[]{:S(2)}) collective-permute-start(bf16[4,24,1024]{2,1,0:T(8,128)(2,1)S(1)} %pad_maximum_fusion.1.rest_0_), channel_id=1, source_target_pairs={{0,16},{4,20},{8,24},{12,28},{16,0},{20,4},{24,8},{28,12},{1,17},{... | collective-permute-start | bytes 589832 | tf_op jit(solution)/shard_map/ppermute | solution.py:596
  126.4 2.4 %collective-permute-done.20.rest_1_ = bf16[4,24,1024]{2,1,0:T(8,128)(2,1)S(1)} collective-permute-done((bf16[4,24,1024]{2,1,0:T(8,128)(2,1)S(1)}, bf16[4,24,1024]{2,1,0:T(8,128)(2,1)S(1)}, u32[]{:S(2)}, u32[]{:S(2)}) %collective-permute-start.20) | collective-permute-done | bytes 196640 | tf_op jit(solution)/shard_map/ppermute | solution.py:596
  128.8 2.0 %collective-permute-done.21.rest_2_ = bf16[4,24,1024]{2,1,0:T(8,128)(2,1)S(1)} collective-permute-done((bf16[4,24,1024]{2,1,0:T(8,128)(2,1)S(1)}, bf16[4,24,1024]{2,1,0:T(8,128)(2,1)S(1)}, u32[]{:S(2)}, u32[]{:S(2)}) %collective-permute-start.21) | collective-permute-done | bytes 196640 | tf_op jit(solution)/shard_map/ppermute | solution.py:596
  132.5 2.3 %unpack.1 = (f32[32,24,768]{2,1,0:T(8,128)}, f32[32,24,128]{2,1,0:T(8,128)}, f32[6,128]{1,0:T(8,128)}, f32[6,128]{1,0:T(8,128)}, f32[1]{0:T(128)}) custom-call(s32[32]{0:T(128)S(1)} %add.139.index_ref, bf16[4,24,1024]{2,1,0:T(8,128)(2,1)S(1)} %pad_maximum_fusion.1.rest_0_, bf16[4,24,1024]{2,1,0:T(8,128)(2,1)S(1)} %collective-permute-done.20.rest_1_, ...), custom_call_target="tpu_custom_call" | custom-call | tf_op jit(solution)/shard_map/unpack/pallas_call | solution.py:552
  (102 shorter events, 27.8 us)
Async XLA Ops:
  1.5 11.1 %collective-permute-start = (bf16[2,128,256]{2,1,0:T(8,128)(2,1)S(1)}, bf16[2,128,256]{2,1,0:T(8,128)(2,1)S(1)}, u32[]{:S(2)}, u32[]{:S(2)}) collective-permute-start(bf16[2,128,256]{2,1,0:T(8,128)(2,1)S(1)} %pad_maximum_fusion.2), channel_id=1, source_target_pairs={{0,1},{1,2},{2,3},{3,0},{4,5},{5,6},{6,7},{7,4},{8,9},{9,10},{10,1... | collective-permute-start | bytes 393224 | tf_op jit(solution)/shard_map/ppermute | solution.py:604
  4.6 11.2 %collective-permute-start.1 = (bf16[2,128,256]{2,1,0:T(8,128)(2,1)S(1)}, bf16[2,128,256]{2,1,0:T(8,128)(2,1)S(1)}, u32[]{:S(2)}, u32[]{:S(2)}) collective-permute-start(bf16[2,128,256]{2,1,0:T(8,128)(2,1)S(1)} %pad_maximum_fusion.2), channel_id=1, source_target_pairs={{0,2},{1,3},{2,0},{3,1},{4,6},{5,7},{6,4},{7,5},{8,10},{9,11},{10,... | collective-permute-start | bytes 393224 | tf_op jit(solution)/shard_map/ppermute | solution.py:604
  7.2 8.6 %collective-permute-start.2 = (bf16[2,128,256]{2,1,0:T(8,128)(2,1)S(1)}, bf16[2,128,256]{2,1,0:T(8,128)(2,1)S(1)}, u32[]{:S(2)}, u32[]{:S(2)}) collective-permute-start(bf16[2,128,256]{2,1,0:T(8,128)(2,1)S(1)} %pad_maximum_fusion.2), channel_id=1, source_target_pairs={{0,3},{1,0},{2,1},{3,2},{4,7},{5,4},{6,5},{7,6},{8,11},{9,8},{10,9... | collective-permute-start | bytes 393224 | tf_op jit(solution)/shard_map/ppermute | solution.py:604
  15.9 17.8 %collective-permute-start.3 = (bf16[7,128,256]{2,1,0:T(8,128)(2,1)S(1)}, bf16[7,128,256]{2,1,0:T(8,128)(2,1)S(1)}, u32[]{:S(2)}, u32[]{:S(2)}) collective-permute-start(bf16[7,128,256]{2,1,0:T(8,128)(2,1)S(1)} %pad_maximum_fusion.rest_0_), channel_id=1, source_target_pairs={{0,8},{4,12},{8,16},{12,20},{16,24},{20,28},{24,0},{28,4},{1,9},{5... | collective-permute-start | bytes 1376264 | tf_op jit(solution)/shard_map/ppermute | solution.py:596
  17.5 21.6 %collective-permute-start.4 = (bf16[7,128,256]{2,1,0:T(8,128)(2,1)S(1)}, bf16[7,128,256]{2,1,0:T(8,128)(2,1)S(1)}, u32[]{:S(2)}, u32[]{:S(2)}) collective-permute-start(bf16[7,128,256]{2,1,0:T(8,128)(2,1)S(1)} %pad_maximum_fusion.rest_0_), channel_id=1, source_target_pairs={{0,16},{4,20},{8,24},{12,28},{16,0},{20,4},{24,8},{28,12},{1,17},{... | collective-permute-start | bytes 1376264 | tf_op jit(solution)/shard_map/ppermute | solution.py:596
  19.0 20.2 %collective-permute-start.5 = (bf16[7,128,256]{2,1,0:T(8,128)(2,1)S(1)}, bf16[7,128,256]{2,1,0:T(8,128)(2,1)S(1)}, u32[]{:S(2)}, u32[]{:S(2)}) collective-permute-start(bf16[7,128,256]{2,1,0:T(8,128)(2,1)S(1)} %pad_maximum_fusion.rest_0_), channel_id=1, source_target_pairs={{0,24},{4,28},{8,0},{12,4},{16,8},{20,12},{24,16},{28,20},{1,25},{... | collective-permute-start | bytes 1376264 | tf_op jit(solution)/shard_map/ppermute | solution.py:596
  33.6 6.1 %collective-permute-start.6 = (bf16[7,128,256]{2,1,0:T(8,128)(2,1)S(1)}, bf16[7,128,256]{2,1,0:T(8,128)(2,1)S(1)}, u32[]{:S(2)}, u32[]{:S(2)}) collective-permute-start(bf16[7,128,256]{2,1,0:T(8,128)(2,1)S(1)} %pad_maximum_fusion.rest_0_), channel_id=1, source_target_pairs={{0,4},{4,0},{8,12},{12,8},{16,20},{20,16},{24,28},{28,24},{1,5},{5... | collective-permute-start | bytes 1376264 | tf_op jit(solution)/shard_map/ppermute | solution.py:601
  39.7 2.6 %collective-permute-start.9 = (bf16[7,128,256]{2,1,0:T(8,128)(2,1)S(1)}, bf16[7,128,256]{2,1,0:T(8,128)(2,1)S(1)}, u32[]{:S(2)}, u32[]{:S(2)}) collective-permute-start(bf16[7,128,256]{2,1,0:T(8,128)(2,1)S(1)} %collective-permute-done.5.rest_3_), channel_id=1, source_target_pairs={{0,4},{4,0},{8,12},{12,8},{16,20},{20,16},{24,28},{28,24},{1,5},{5... | collective-permute-start | bytes 1376264 | tf_op jit(solution)/shard_map/ppermute | solution.py:601
  55.4 10.3 %all-to-all-start = ((bf16[16,32,180]{2,1,0:T(8,128)(2,1)}), bf16[16,32,180]{2,1,0:T(8,128)(2,1)S(1)}, u32[]{:S(2)}, u32[]{:S(2)}) async-start(bf16[16,32,180]{2,1,0:T(8,128)(2,1)} %teacher_maps.1), calls=%async_computation | async-start | bytes 524288 | tf_op jit(solution)/shard_map/all_to_all | solution.py:653
  88.6 2.6 %collective-permute-start.10 = (bf16[16,24,1024]{2,1,0:T(8,128)(2,1)}, bf16[16,24,1024]{2,1,0:T(8,128)(2,1)S(1)}, u32[]{:S(2)}, u32[]{:S(2)}) collective-permute-start(bf16[16,24,1024]{2,1,0:T(8,128)(2,1)} %get-tuple-element.75), channel_id=1, source_target_pairs={{0,4},{4,0},{8,12},{12,8},{16,20},{20,16},{24,28},{28,24},{1,5},{5... | collective-permute-start | bytes 2359304 | tf_op jit(solution)/shard_map/ppermute | solution.py:601
  93.3 11.0 %collective-permute-start.11 = (bf16[4,24,1024]{2,1,0:T(8,128)(2,1)S(1)}, bf16[4,24,1024]{2,1,0:T(8,128)(2,1)S(1)}, u32[]{:S(2)}, u32[]{:S(2)}) collective-permute-start(bf16[4,24,1024]{2,1,0:T(8,128)(2,1)S(1)} %get-tuple-element.82), channel_id=1, source_target_pairs={{0,8},{4,12},{8,16},{12,20},{16,24},{20,28},{24,0},{28,4},{1,9},{5... | collective-permute-start | bytes 589832 | tf_op jit(solution)/shard_map/ppermute | solution.py:596
  93.9 10.9 %collective-permute-start.12 = (bf16[4,24,1024]{2,1,0:T(8,128)(2,1)S(1)}, bf16[4,24,1024]{2,1,0:T(8,128)(2,1)S(1)}, u32[]{:S(2)}, u32[]{:S(2)}) collective-permute-start(bf16[4,24,1024]{2,1,0:T(8,128)(2,1)S(1)} %get-tuple-element.83), channel_id=1, source_target_pairs={{0,16},{4,20},{8,24},{12,28},{16,0},{20,4},{24,8},{28,12},{1,17},{... | collective-permute-start | bytes 589832 | tf_op jit(solution)/shard_map/ppermute | solution.py:596
  95.0 9.8 %collective-permute-start.13 = (bf16[4,24,1024]{2,1,0:T(8,128)(2,1)S(1)}, bf16[4,24,1024]{2,1,0:T(8,128)(2,1)S(1)}, u32[]{:S(2)}, u32[]{:S(2)}) collective-permute-start(bf16[4,24,1024]{2,1,0:T(8,128)(2,1)S(1)} %get-tuple-element.84), channel_id=1, source_target_pairs={{0,24},{4,28},{8,0},{12,4},{16,8},{20,12},{24,16},{28,20},{1,25},{... | collective-permute-start | bytes 589832 | tf_op jit(solution)/shard_map/ppermute | solution.py:596
  105.5 6.2 %collective-permute-start.14 = (bf16[24,1024]{1,0:T(8,128)(2,1)S(1)}, bf16[24,1024]{1,0:T(8,128)(2,1)S(1)}, u32[]{:S(2)}, u32[]{:S(2)}) collective-permute-start(bf16[24,1024]{1,0:T(8,128)(2,1)S(1)} %get-tuple-element.91), channel_id=1, source_target_pairs={{0,1},{1,2},{2,3},{3,0},{4,5},{5,6},{6,7},{7,4},{8,9},{9,10},{10,1... | collective-permute-start | bytes 147464 | tf_op jit(solution)/shard_map/ppermute | solution.py:604
  109.0 5.3 %collective-permute-start.15 = (bf16[24,1024]{1,0:T(8,128)(2,1)S(1)}, bf16[24,1024]{1,0:T(8,128)(2,1)S(1)}, u32[]{:S(2)}, u32[]{:S(2)}) collective-permute-start(bf16[24,1024]{1,0:T(8,128)(2,1)S(1)} %get-tuple-element.92), channel_id=1, source_target_pairs={{0,2},{1,3},{2,0},{3,1},{4,6},{5,7},{6,4},{7,5},{8,10},{9,11},{10,... | collective-permute-start | bytes 147464 | tf_op jit(solution)/shard_map/ppermute | solution.py:604
  109.5 4.7 %collective-permute-start.16 = (bf16[24,1024]{1,0:T(8,128)(2,1)S(1)}, bf16[24,1024]{1,0:T(8,128)(2,1)S(1)}, u32[]{:S(2)}, u32[]{:S(2)}) collective-permute-start(bf16[24,1024]{1,0:T(8,128)(2,1)S(1)} %get-tuple-element.93), channel_id=1, source_target_pairs={{0,3},{1,0},{2,1},{3,2},{4,7},{5,4},{6,5},{7,6},{8,11},{9,8},{10,9... | collective-permute-start | bytes 147464 | tf_op jit(solution)/shard_map/ppermute | solution.py:604
  114.3 6.0 %collective-permute-start.17 = (bf16[24,1024]{1,0:T(8,128)(2,1)S(1)}, bf16[24,1024]{1,0:T(8,128)(2,1)S(1)}, u32[]{:S(2)}, u32[]{:S(2)}) collective-permute-start(bf16[24,1024]{1,0:T(8,128)(2,1)S(1)} %sum_tensor.1), channel_id=1, source_target_pairs={{0,1},{1,2},{2,3},{3,0},{4,5},{5,6},{6,7},{7,4},{8,9},{9,10},{10,1... | collective-permute-start | bytes 147464 | tf_op jit(solution)/shard_map/ppermute | solution.py:604
  115.4 5.9 %collective-permute-start.18 = (bf16[24,1024]{1,0:T(8,128)(2,1)S(1)}, bf16[24,1024]{1,0:T(8,128)(2,1)S(1)}, u32[]{:S(2)}, u32[]{:S(2)}) collective-permute-start(bf16[24,1024]{1,0:T(8,128)(2,1)S(1)} %sum_tensor.1), channel_id=1, source_target_pairs={{0,2},{1,3},{2,0},{3,1},{4,6},{5,7},{6,4},{7,5},{8,10},{9,11},{10,... | collective-permute-start | bytes 147464 | tf_op jit(solution)/shard_map/ppermute | solution.py:604
  117.9 4.1 %collective-permute-start.19 = (bf16[24,1024]{1,0:T(8,128)(2,1)S(1)}, bf16[24,1024]{1,0:T(8,128)(2,1)S(1)}, u32[]{:S(2)}, u32[]{:S(2)}) collective-permute-start(bf16[24,1024]{1,0:T(8,128)(2,1)S(1)} %sum_tensor.1), channel_id=1, source_target_pairs={{0,3},{1,0},{2,1},{3,2},{4,7},{5,4},{6,5},{7,6},{8,11},{9,8},{10,9... | collective-permute-start | bytes 147464 | tf_op jit(solution)/shard_map/ppermute | solution.py:604
  122.1 6.8 %collective-permute-start.20 = (bf16[4,24,1024]{2,1,0:T(8,128)(2,1)S(1)}, bf16[4,24,1024]{2,1,0:T(8,128)(2,1)S(1)}, u32[]{:S(2)}, u32[]{:S(2)}) collective-permute-start(bf16[4,24,1024]{2,1,0:T(8,128)(2,1)S(1)} %pad_maximum_fusion.1.rest_0_), channel_id=1, source_target_pairs={{0,8},{4,12},{8,16},{12,20},{16,24},{20,28},{24,0},{28,4},{1,9},{5... | collective-permute-start | bytes 589832 | tf_op jit(solution)/shard_map/ppermute | solution.py:596
  123.6 7.2 %collective-permute-start.21 = (bf16[4,24,1024]{2,1,0:T(8,128)(2,1)S(1)}, bf16[4,24,1024]{2,1,0:T(8,128)(2,1)S(1)}, u32[]{:S(2)}, u32[]{:S(2)}) collective-permute-start(bf16[4,24,1024]{2,1,0:T(8,128)(2,1)S(1)} %pad_maximum_fusion.1.rest_0_), channel_id=1, source_target_pairs={{0,16},{4,20},{8,24},{12,28},{16,0},{20,4},{24,8},{28,12},{1,17},{... | collective-permute-start | bytes 589832 | tf_op jit(solution)/shard_map/ppermute | solution.py:596
  125.2 5.7 %collective-permute-start.22 = (bf16[4,24,1024]{2,1,0:T(8,128)(2,1)S(1)}, bf16[4,24,1024]{2,1,0:T(8,128)(2,1)S(1)}, u32[]{:S(2)}, u32[]{:S(2)}) collective-permute-start(bf16[4,24,1024]{2,1,0:T(8,128)(2,1)S(1)} %pad_maximum_fusion.1.rest_0_), channel_id=1, source_target_pairs={{0,24},{4,28},{8,0},{12,4},{16,8},{20,12},{24,16},{28,20},{1,25},{... | collective-permute-start | bytes 589832 | tf_op jit(solution)/shard_map/ppermute | solution.py:596
  126.4 5.1 %collective-permute-start.23 = (bf16[4,24,1024]{2,1,0:T(8,128)(2,1)S(1)}, bf16[4,24,1024]{2,1,0:T(8,128)(2,1)S(1)}, u32[]{:S(2)}, u32[]{:S(2)}) collective-permute-start(bf16[4,24,1024]{2,1,0:T(8,128)(2,1)S(1)} %pad_maximum_fusion.1.rest_0_), channel_id=1, source_target_pairs={{0,4},{4,0},{8,12},{12,8},{16,20},{20,16},{24,28},{28,24},{1,5},{5... | collective-permute-start | bytes 589832 | tf_op jit(solution)/shard_map/ppermute | solution.py:601
  128.8 2.7 %collective-permute-start.24 = (bf16[4,24,1024]{2,1,0:T(8,128)(2,1)S(1)}, bf16[4,24,1024]{2,1,0:T(8,128)(2,1)S(1)}, u32[]{:S(2)}, u32[]{:S(2)}) collective-permute-start(bf16[4,24,1024]{2,1,0:T(8,128)(2,1)S(1)} %collective-permute-done.20.rest_1_), channel_id=1, source_target_pairs={{0,4},{4,0},{8,12},{12,8},{16,20},{20,16},{24,28},{28,24},{1,5},{5... | collective-permute-start | bytes 589832 | tf_op jit(solution)/shard_map/ppermute | solution.py:601
  (15 other events, 79.8 us)

commit v8 on v7

--- a/solution.py
+++ b/solution.py
@@ -46,7 +46,8 @@
     return pl.CostEstimate(flops=int(flops), bytes_accessed=int(nbytes), transcendentals=0)
 
 
-def forward_kernel(x_ref, str_ref, wo_ref, gain_ref, bias_ref, wp_ref, normed_ref, emb_ref, inv_ref, turned_ref, prod_s, hid_s):
+def forward_kernel(x_ref, str_ref, wo_ref, gain_ref, bias_ref, wp_ref, *rest):
+    normed_ref, emb_ref, inv_ref, turned_ref, prod_s, hid_s = rest[-6:]
     rows, width = x_ref.shape
     sub = rows
     gain, bias = one_row(gain_ref), one_row(bias_ref)
@@ -64,17 +65,18 @@
     turned_ref[0] = x_ref[...].T
 
 
-def student_forward(x, stream, out_weight, gain, bias, proj_weight):
+def student_forward(x, stream, out_weight, gain, bias, proj_weight, first, last, before=()):
     total, width = x.shape
     emb = proj_weight.shape[1]
     rows = split_rows(total, 720)
-    block = lambda last: pl.BlockSpec((rows, last), lambda s: (s, 0))
+    block = lambda n: pl.BlockSpec((rows, n), lambda s: (s + first, 0))
     whole = lambda a: pl.BlockSpec(a.shape, lambda s: (0,) * a.ndim)
+    inputs = (x, stream, out_weight, gain, bias, proj_weight)
     return pl.pallas_call(
         forward_kernel,
-        grid=(total // rows,),
-        in_specs=[block(width), block(width)] + [whole(a) for a in (out_weight, gain, bias, proj_weight)],
-        out_specs=[block(width), block(emb), block(128), pl.BlockSpec((1, width, rows), lambda s: (s, 0, 0))],
+        grid=(last - first,),
+        in_specs=[block(width), block(width)] + [whole(a) for a in inputs[2:]] + [ANY] * len(before),
+        out_specs=[block(width), block(emb), block(128), pl.BlockSpec((1, width, rows), lambda s: (s + first, 0, 0))],
         out_shape=[
             jax.ShapeDtypeStruct((total, width), BF16),
             jax.ShapeDtypeStruct((total, emb), F32),
@@ -82,10 +84,11 @@
             jax.ShapeDtypeStruct((total // rows, width, rows), BF16),
         ],
         scratch_shapes=[pltpu.VMEM((rows, width), F32), pltpu.VMEM((rows, width), BF16)],
+        input_output_aliases={len(inputs) + n: n for n in range(len(before))},
         compiler_params=params(),
-        cost_estimate=cost(2 * total * width * (width + emb), 8 * total * width),
+        cost_estimate=cost(2 * (last - first) * rows * width * (width + emb), 8 * (last - first) * rows * width),
         name="student_forward",
-    )(x, stream, out_weight, gain, bias, proj_weight)
+    )(*inputs, *before)
 
 
 def teacher_kernel(parts, count, tokens, order_ref, from_ref, rows_ref, states_ref, wq_ref, wk_ref, *rest):
@@ -413,11 +416,10 @@
     chunk = send_ref.shape[1]
     for ref, which in ((send_ref, 1 - core_ref[0]), (keep_ref, core_ref[0])):
         start = pl.multiple_of(which * half, half)
-        left = wo_s[pl.ds(start, half)].astype(BF16)
-        right = right_s[pl.ds(start, half)].astype(BF16)
+        left, right = wo_s[pl.ds(start, half)], right_s[pl.ds(start, half)]
         for c in range(half // chunk):
-            ref[c, :, :width] = left[c * chunk : (c + 1) * chunk]
-            ref[c, :, width:] = right[c * chunk : (c + 1) * chunk]
+            ref[c, :, :width] = left[c * chunk : (c + 1) * chunk].astype(BF16)
+            ref[c, :, width:] = right[c * chunk : (c + 1) * chunk].astype(BF16)
     for b in range(blocks):
         part = pl.ds(b * rows, rows)
         pltpu.make_async_copy(sg_s.at[part], sg_out.at[part], out_sem.at[b]).wait()
@@ -463,24 +465,26 @@
     )(qidx, midx, lens, core, *manual, qdir, qlen, gain, bias, wp, wpt)
 
 
-def context_kernel(sg_ref, wo_ref, out_ref):
+def context_kernel(sg_ref, wo_ref, *rest):
+    out_ref = rest[-1]
     out_ref[...] = dot(sg_ref[...], wo_ref[...], 1, 1).astype(BF16)
 
 
-def context_grad(sg, out_weight):
+def context_grad(sg, out_weight, first, last, before=()):
     total, width = sg.shape
     rows = split_rows(total, 720)
-    block = pl.BlockSpec((rows, width), lambda s: (s, 0))
+    block = pl.BlockSpec((rows, width), lambda s: (s + first, 0))
     return pl.pallas_call(
         context_kernel,
-        grid=(total // rows,),
-        in_specs=[block, pl.BlockSpec(out_weight.shape, lambda s: (0, 0))],
+        grid=(last - first,),
+        in_specs=[block, pl.BlockSpec(out_weight.shape, lambda s: (0, 0))] + [ANY] * len(before),
         out_specs=block,
         out_shape=jax.ShapeDtypeStruct(sg.shape, BF16),
+        input_output_aliases={2: 0} if before else {},
         compiler_params=params(),
-        cost_estimate=cost(2 * total * width * width, 4 * total * width),
+        cost_estimate=cost(2 * (last - first) * rows * width * width, 4 * (last - first) * rows * width),
         name="context_grad",
-    )(sg, out_weight)
+    )(sg, out_weight, *before)
 
 
 def split_sum_kernel(inputs, outputs, index_ref, *rest):
@@ -592,9 +596,14 @@
     def flat(a):
         return a.transpose(1, 0, 2).reshape(-1, a.shape[2])
 
+    paired = chips & (chips - 1) == 0
+
+    def partner(c, k):
+        return c ^ k if paired else (c + k) % chips
+
     def shift_chip(x, k):
         return lax.ppermute(
-            x, "dp", [(c * CORES + o, (c + k) % chips * CORES + o) for c in range(chips) for o in range(CORES)]
+            x, "dp", [(c * CORES + o, partner(c, k) * CORES + o) for c in range(chips) for o in range(CORES)]
         )
 
     def swap_core(x):
@@ -619,27 +628,43 @@
     rider = jnp.concatenate(column_blocks + [extra], axis=0)
 
     part = depth // dp
-    mine = jnp.stack(
-        [lax.dynamic_slice_in_dim(w, me * part, part, 0) for w in (teacher_query, teacher_key)]
-    )
+    slices = 2 * (nt - 1)
+    by_hops = sorted(range(1, chips), key=lambda k: (bin(k).count("1"), k))
+    far = by_hops[len(by_hops) - chips // 4 :] if paired else []
+
+    def slice_of(c):
+        start = (c * CORES + core) * part
+        return jnp.stack([lax.dynamic_slice_in_dim(w, start, part, 0) for w in (teacher_query, teacher_key)])
+
+    mine, far_mine = slice_of(chip), [slice_of(partner(chip, k)) for k in far]
     rider = jnp.pad(rider, ((0, -rider.shape[0] % part), (0, 0))).reshape(-1, part, heads)
-    slices = 2 * (nt - 1)
     along = jnp.concatenate([shift_t(mine, k) for k in range(1, nt)] + [rider], axis=0)
-    pieces = [along] + [shift_chip(along, k) for k in range(1, chips)]
+    gain2, bias2 = gain.reshape(-1, 128), bias.reshape(-1, 128)
+    x = flat(context)
+    blocks = x.shape[0] // split_rows(x.shape[0], 720)
+    forward = functools.partial(student_forward, x, flat(stream), out_weight, gain2, bias2, proj_weight)
+    begun = forward(0, 1)
+    along, far_mine, begun = lax.optimization_barrier((along, far_mine, begun))
+    pieces = [along] + [None] * (chips - 1)
+    for k in range(1, chips):
+        if k not in far:
+            pieces[k] = shift_chip(along, k)
+    for k, other in zip(far, far_mine):
+        received = [shift_t(other, n) for n in range(1, nt)]
+        pieces[k] = jnp.concatenate(received + [shift_chip(rider, k)], axis=0)
     shifts = jnp.arange(chips, dtype=jnp.int32)
-    behind = (chip - shifts) % chips
+    behind = chip ^ shifts if paired else (chip - shifts) % chips
     piece_rows = jnp.concatenate([behind * CORES + core, behind * CORES + 1 - core]).astype(jnp.int32)
     midx = place.astype(jnp.int32)
     def piece_of(group):
-        return (chip - group // CORES) % chips + jnp.where(group % CORES == core, 0, chips)
+        apart = chip ^ (group // CORES) if paired else (chip - group // CORES) % chips
+        return apart + jnp.where(group % CORES == core, 0, chips)
 
     qidx = passage_dest // per_query - dest_group * group_queries + piece_of(dest_group) * group_queries
     qidx = qidx.astype(jnp.int32)
     source = piece_of(jnp.arange(dp, dtype=jnp.int32)).astype(jnp.int32)
 
-    gain2, bias2 = gain.reshape(-1, 128), bias.reshape(-1, 128)
-    x = flat(context)
-    normed, embeds, inverse, turned = student_forward(x, flat(stream), out_weight, gain2, bias2, proj_weight)
+    normed, embeds, inverse, turned = forward(1, blocks, begun) if blocks > 1 else begun
     pieces[1:], normed, embeds, inverse, turned, proj_turned = lax.optimization_barrier(
         (pieces[1:], normed, embeds, inverse, turned, proj_weight.T)
     )
@@ -661,18 +686,22 @@
         count, tokens, group_queries, chunk,
     )
 
-    ahead = ((chip + shifts) % chips).astype(jnp.int32)
+    ahead = partner(chip, shifts).astype(jnp.int32)
     t_shifts = jnp.arange(nt, dtype=jnp.int32)
     t_ahead = ((mt + t_shifts) % nt).astype(jnp.int32)
     parts = split_sum([keep, swap_core(send)], ahead, "sum_cores")
     parts, sg = lax.optimization_barrier((parts, sg))
-    grad_context = context_grad(sg, out_weight)
+    most = max(blocks - 1, 1)
+    grad_context = context_grad(sg, out_weight, 0, most)
     parts = [parts[0]] + [shift_chip(parts[k], k) for k in range(1, chips)]
     parts, grad_context = lax.optimization_barrier((parts, grad_context))
     parts = split_sum(parts, t_ahead, "sum_plane")
     parts = [parts[0]] + [shift_t(parts[k], k) for k in range(1, nt)]
     total = plain_sum(parts, "sum_tensor")
     line = jnp.stack([total] + [shift_t(total, k) for k in range(1, nt)])
+    if most < blocks:
+        line, sg, grad_context = lax.optimization_barrier((line, sg, grad_context))
+        grad_context = context_grad(sg, out_weight, most, blocks, (grad_context,))
     plane = [line] + [shift_chip(line, k) for k in range(1, chips)]
     arrays = plane + [swap_core(a) for a in plane]
     base = jnp.concatenate([core * chips + behind, (1 - core) * chips + behind]) * nt

time: 136 us -> 138 us (1.015)
  Pallas kernels: 63 us -> 68.8 us
  waiting for transfers between devices: 27 us -> 24 us
    pallas_call x2 -> x4, Pallas kernels: 20.1 us -> 25.9 us  [the longest x2 15.9 us: student_forward(): pl.pallas_call(forward_kernel, grid=(last - first,), in_specs=[block(widt...]
    ppermute x9, waiting for transfers between devices: 10.4 us -> 7.21 us  [shift_chip(): lax.ppermute(x, 'dp', [(c * CORES + o, partner(c, k) * CORES + o) for c i...]
    ppermute x9 -> x12, waiting for transfers between devices: 9.11 us -> 10 us  [shift_t(): return lax.ppermute(x, 'tensor', [(t, (t + k) % nt) for t in range(nt)])]
    unnamed x23 -> x25, local copies, waits for them, and re-layouts: 4.4 us -> 3.49 us
    ppermute x9 -> x12, starting transfers between devices: 17.6 us -> 18.3 us  [shift_t(): return lax.ppermute(x, 'tensor', [(t, (t + k) % nt) for t in range(nt)])]
  transfers between devices with their start and end apart: 28 -> 31, of which waited for: 18 -> 15; matrix products, arithmetic and copies ran while one was open for 4% -> 3% of each run, Pallas kernels for 19% -> 22%
where the time goes in v8:
time: 138 us
  Pallas kernels  68.8 us (50%)
  starting transfers between devices  35.2 us (26%)
  waiting for transfers between devices  24 us (17%)
  local copies, waits for them, and re-layouts  5.4 us (4%)
  other arithmetic  3.16 us (2%)
    pallas_call x1, Pallas kernels, student_backward(): pl.pallas_call(functools.partial(backward_kernel, tokens, count, blocks),...  22.2 us
    ppermute x12, starting transfers between devices, shift_t(): return lax.ppermute(x, 'tensor', [(t, (t + k) % nt) for t in range(nt)])  18.3 us
    pallas_call x2, Pallas kernels, student_forward(): pl.pallas_call(forward_kernel, grid=(last - first,), in_specs=[block(widt...  15.9 us
    ppermute x9, starting transfers between devices, shift_chip(): lax.ppermute(x, 'dp', [(c * CORES + o, partner(c, k) * CORES + o) for c i...  11.9 us
    pallas_call x1, Pallas kernels, teacher_maps(): pl.pallas_call(functools.partial(teacher_kernel, parts, count, tokens), i...  11.6 us
    ppermute x12, waiting for transfers between devices, shift_t(): return lax.ppermute(x, 'tensor', [(t, (t + k) % nt) for t in range(nt)])  10 us
    pallas_call x2, Pallas kernels, context_grad(): pl.pallas_call(context_kernel, grid=(last - first,), in_specs=[block, pl....  10 us
    ppermute x9, waiting for transfers between devices, shift_chip(): lax.ppermute(x, 'dp', [(c * CORES + o, partner(c, k) * CORES + o) for c i...  7.21 us
  transfers between devices with their start and end apart: 31, of which 15 were waited for; matrix products, arithmetic and copies ran while one was open for 3% of the time, Pallas kernels for 22%

profile of v8, /device:TPU:0, one launch (start us, length us, event | category | flops | bytes accessed | tf_op | source)
XLA Modules:
  0.0 137.8 jit_solution(10501408334365056115)
XLA Ops:
  1.7 3.1 %collective-permute-start = (bf16[2,128,256]{2,1,0:T(8,128)(2,1)S(1)}, bf16[2,128,256]{2,1,0:T(8,128)(2,1)S(1)}, u32[]{:S(2)}, u32[]{:S(2)}) collective-permute-start(bf16[2,128,256]{2,1,0:T(8,128)(2,1)S(1)} %pad_maximum_fusion.3), channel_id=1, source_target_pairs={{0,1},{1,2},{2,3},{3,0},{4,5},{5,6},{6,7},{7,4},{8,9},{9,10},{10,1... | collective-permute-start | bytes 393224 | tf_op jit(solution)/shard_map/ppermute | solution.py:613
  4.7 2.6 %collective-permute-start.1 = (bf16[2,128,256]{2,1,0:T(8,128)(2,1)S(1)}, bf16[2,128,256]{2,1,0:T(8,128)(2,1)S(1)}, u32[]{:S(2)}, u32[]{:S(2)}) collective-permute-start(bf16[2,128,256]{2,1,0:T(8,128)(2,1)S(1)} %pad_maximum_fusion.3), channel_id=1, source_target_pairs={{0,2},{1,3},{2,0},{3,1},{4,6},{5,7},{6,4},{7,5},{8,10},{9,11},{10,... | collective-permute-start | bytes 393224 | tf_op jit(solution)/shard_map/ppermute | solution.py:613
  10.9 2.5 %collective-permute-start.8 = (bf16[1,128,256]{2,1,0:T(8,128)(2,1)S(1)}, bf16[1,128,256]{2,1,0:T(8,128)(2,1)S(1)}, u32[]{:S(2)}, u32[]{:S(2)}) collective-permute-start(bf16[1,128,256]{2,1,0:T(8,128)(2,1)S(1)} %pad_bitcast_fusion), channel_id=1, source_target_pairs={{0,24},{4,28},{8,16},{12,20},{16,8},{20,12},{24,0},{28,4},{1,25},{... | collective-permute-start | bytes 196616 | tf_op jit(solution)/shard_map/ppermute | solution.py:605
  14.1 5.6 %student_forward.2 = (bf16[2880,768]{1,0:T(8,128)(2,1)}, f32[2880,128]{1,0:T(8,128)}, f32[2880,128]{1,0:T(8,128)}, bf16[4,768,720]{2,1,0:T(8,128)(2,1)}) custom-call(bf16[2880,768]{1,0:T(8,128)(2,1)} %bitcast.55, bf16[2880,768]{1,0:T(8,128)(2,1)} %bitcast.57, bf16[768,768]{1,0:T(8,128)(2,1)} %wo_ref.7, f32[6,128]{1,0:T(8,128)} %bitcast.65, ...), custom_call_target="tpu_custom_call" | custom-call | flops 990904320 | bytes 4423680 | tf_op jit(solution)/shard_map/student_forward/pallas_call | solution.py:75
  24.0 10.2 %student_forward.3 = (bf16[2880,768]{1,0:T(8,128)(2,1)}, f32[2880,128]{1,0:T(8,128)}, f32[2880,128]{1,0:T(8,128)}, bf16[4,768,720]{2,1,0:T(8,128)(2,1)}) custom-call(bf16[2880,768]{1,0:T(8,128)(2,1)} %bitcast.56, bf16[2880,768]{1,0:T(8,128)(2,1)} %bitcast.58, ...), custom_call_target="tpu_custom_call", output_to_operand_aliasing={{0}: (6, {}), {1}: (7, {}), {2}: (8, {}), {3}: (9, {})} | custom-call | flops 2972712960 | bytes 13271040 | tf_op jit(solution)/shard_map/student_forward/pallas_call | solution.py:75
  34.3 1.6 %collective-permute-start.7 = (bf16[2,128,256]{2,1,0:T(8,128)(2,1)S(1)}, bf16[2,128,256]{2,1,0:T(8,128)(2,1)S(1)}, u32[]{:S(2)}, u32[]{:S(2)}) collective-permute-start(bf16[2,128,256]{2,1,0:T(8,128)(2,1)S(1)} %pad_maximum_fusion.4), channel_id=1, source_target_pairs={{0,3},{1,0},{2,1},{3,2},{4,7},{5,4},{6,5},{7,6},{8,11},{9,8},{10,9... | collective-permute-start | bytes 393224 | tf_op jit(solution)/shard_map/ppermute | solution.py:613
  36.0 3.4 %collective-permute-done.7 = bf16[2,128,256]{2,1,0:T(8,128)(2,1)S(1)} collective-permute-done((bf16[2,128,256]{2,1,0:T(8,128)(2,1)S(1)}, bf16[2,128,256]{2,1,0:T(8,128)(2,1)S(1)}, u32[]{:S(2)}, u32[]{:S(2)}) %collective-permute-start.7) | collective-permute-done | bytes 131104 | tf_op jit(solution)/shard_map/ppermute | solution.py:613
  44.3 11.6 %teacher_maps.1 = bf16[16,32,180]{2,1,0:T(8,128)(2,1)} custom-call(s32[8,2]{1,0:T(8,128)} %dynamic-slice_convert_fusion.order_ref, s32[8]{0:T(128)} %get-tuple-element.138.from_ref, s32[8]{0:T(128)} %get-tuple-element.139.rows_ref, bf16[3392,1024]{1,0:T(8,128)(2,1)} %bitcast.71, bf16[1024,256]{1,0:T(8,128)(2,1)} %wq_ref.1, bf16[1024,256]{1,0:T(8,128)(2,1)} %wk_ref.1, ...), custom_call_target="tpu_custom_call" | custom-call | flops 4294967296 | bytes 11141120 | tf_op jit(solution)/shard_map/teacher_maps/pallas_call | solution.py:178
  55.9 3.7 %all-to-all-start = ((bf16[16,32,180]{2,1,0:T(8,128)(2,1)}), bf16[16,32,180]{2,1,0:T(8,128)(2,1)S(1)}, u32[]{:S(2)}, u32[]{:S(2)}) async-start(bf16[16,32,180]{2,1,0:T(8,128)(2,1)} %teacher_maps.1), calls=%async_computation | async-start | bytes 524288 | tf_op jit(solution)/shard_map/all_to_all | solution.py:678
  59.6 5.1 %student_scores.1 = (f32[16,32,180]{2,1,0:T(8,128)}, f32[16,32,180]{2,1,0:T(8,128)}, bf16[16,180,128]{2,1,0:T(8,128)(2,1)}, bf16[8,32,128]{2,1,0:T(8,128)(2,1)},...) custom-call(s32[16]{0:T(128)} %get-tuple-element.126.qidx_ref, s32[16]{0:T(128)} %len_ref.3, ...), custom_call_target="tpu_custom_call" | custom-call | flops 1000000000 | bytes 1474560 | tf_op jit(solution)/shard_map/student_scores/pallas_call | solution.py:260
  64.7 1.9 %all-to-all-done.maps_in = bf16[16,32,180]{2,1,0:T(8,128)(2,1)S(1)} async-done(((bf16[16,32,180]{2,1,0:T(8,128)(2,1)}), bf16[16,32,180]{2,1,0:T(8,128)(2,1)S(1)}, u32[]{:S(2)}, u32[]{:S(2)}) %all-to-all-start) | async-done | bytes 184352 | tf_op jit(solution)/shard_map/all_to_all | solution.py:678
  67.3 22.2 %student_backward.1 = (bf16[2880,768]{1,0:T(8,128)(2,1)}, bf16[16,24,1024]{2,1,0:T(8,128)(2,1)}, bf16[16,24,1024]{2,1,0:T(8,128)(2,1)}) custom-call(s32[16]{0:T(128)} %get-tuple-element.126.qidx_ref, s32[16]{0:T(128)} %copy-done.11, s32[16]{0:T(128)} %len_ref.3, s32[1]{0:T(128)} %bitcast.core_ref, bf16[16,32,180]{2,1,0:T(8,128)(2,1)} %copy-done.10, ...), custom_call_target="tpu_custom_call" | custom-call | flops 4529848320 | bytes 17694720 | tf_op jit(solution)/shard_map/student_backward/pallas_call | solution.py:439
  89.6 2.5 %collective-permute-done.13.rest_1_ = bf16[16,24,1024]{2,1,0:T(8,128)(2,1)S(1)} collective-permute-done((bf16[16,24,1024]{2,1,0:T(8,128)(2,1)}, bf16[16,24,1024]{2,1,0:T(8,128)(2,1)S(1)}, u32[]{:S(2)}, u32[]{:S(2)}) %collective-permute-start.13) | collective-permute-done | bytes 786464 | tf_op jit(solution)/shard_map/ppermute | solution.py:610
  95.8 1.9 %collective-permute-start.16 = (bf16[4,24,1024]{2,1,0:T(8,128)(2,1)S(1)}, bf16[4,24,1024]{2,1,0:T(8,128)(2,1)S(1)}, u32[]{:S(2)}, u32[]{:S(2)}) collective-permute-start(bf16[4,24,1024]{2,1,0:T(8,128)(2,1)S(1)} %get-tuple-element.107), channel_id=1, source_target_pairs={{0,24},{4,28},{8,16},{12,20},{16,8},{20,12},{24,0},{28,4},{1,25},{... | collective-permute-start | bytes 589832 | tf_op jit(solution)/shard_map/ppermute | solution.py:605
  97.7 6.4 %context_grad.2.rest_0_ = bf16[2880,768]{1,0:T(8,128)(2,1)} custom-call(bf16[2880,768]{1,0:T(8,128)(2,1)} %get-tuple-element.124.sg_ref, bf16[768,768]{1,0:T(8,128)(2,1)} %wo_ref.7), custom_call_target="tpu_custom_call" | custom-call | flops 2548039680 | bytes 6635520 | tf_op jit(solution)/shard_map/context_grad/pallas_call | solution.py:477
  106.4 2.1 %collective-permute-start.17 = (bf16[24,1024]{1,0:T(8,128)(2,1)S(1)}, bf16[24,1024]{1,0:T(8,128)(2,1)S(1)}, u32[]{:S(2)}, u32[]{:S(2)}) collective-permute-start(bf16[24,1024]{1,0:T(8,128)(2,1)S(1)} %get-tuple-element.114), channel_id=1, source_target_pairs={{0,1},{1,2},{2,3},{3,0},{4,5},{5,6},{6,7},{7,4},{8,9},{9,10},{10,1... | collective-permute-start | bytes 147464 | tf_op jit(solution)/shard_map/ppermute | solution.py:613
  108.5 1.8 %collective-permute-start.18 = (bf16[24,1024]{1,0:T(8,128)(2,1)S(1)}, bf16[24,1024]{1,0:T(8,128)(2,1)S(1)}, u32[]{:S(2)}, u32[]{:S(2)}) collective-permute-start(bf16[24,1024]{1,0:T(8,128)(2,1)S(1)} %get-tuple-element.115), channel_id=1, source_target_pairs={{0,2},{1,3},{2,0},{3,1},{4,6},{5,7},{6,4},{7,5},{8,10},{9,11},{10,... | collective-permute-start | bytes 147464 | tf_op jit(solution)/shard_map/ppermute | solution.py:613
  110.9 1.8 %collective-permute-done.17.refs_1_ = bf16[24,1024]{1,0:T(8,128)(2,1)S(1)} collective-permute-done((bf16[24,1024]{1,0:T(8,128)(2,1)S(1)}, bf16[24,1024]{1,0:T(8,128)(2,1)S(1)}, u32[]{:S(2)}, u32[]{:S(2)}) %collective-permute-start.17) | collective-permute-done | bytes 49184 | tf_op jit(solution)/shard_map/ppermute | solution.py:613
  115.1 2.4 %collective-permute-start.21 = (bf16[24,1024]{1,0:T(8,128)(2,1)S(1)}, bf16[24,1024]{1,0:T(8,128)(2,1)S(1)}, u32[]{:S(2)}, u32[]{:S(2)}) collective-permute-start(bf16[24,1024]{1,0:T(8,128)(2,1)S(1)} %sum_tensor.1), channel_id=1, source_target_pairs={{0,2},{1,3},{2,0},{3,1},{4,6},{5,7},{6,4},{7,5},{8,10},{9,11},{10,... | collective-permute-start | bytes 147464 | tf_op jit(solution)/shard_map/ppermute | solution.py:613
  118.5 2.0 %collective-permute-done.20 = bf16[24,1024]{1,0:T(8,128)(2,1)S(1)} collective-permute-done((bf16[24,1024]{1,0:T(8,128)(2,1)S(1)}, bf16[24,1024]{1,0:T(8,128)(2,1)S(1)}, u32[]{:S(2)}, u32[]{:S(2)}) %collective-permute-start.20) | collective-permute-done | bytes 49184 | tf_op jit(solution)/shard_map/ppermute | solution.py:613
  125.3 2.1 %collective-permute-done.23.rest_1_ = bf16[4,24,1024]{2,1,0:T(8,128)(2,1)S(1)} collective-permute-done((bf16[4,24,1024]{2,1,0:T(8,128)(2,1)S(1)}, bf16[4,24,1024]{2,1,0:T(8,128)(2,1)S(1)}, u32[]{:S(2)}, u32[]{:S(2)}) %collective-permute-start.23) | collective-permute-done | bytes 196640 | tf_op jit(solution)/shard_map/ppermute | solution.py:605
  127.4 3.5 %collective-permute-done.24.rest_2_ = bf16[4,24,1024]{2,1,0:T(8,128)(2,1)S(1)} collective-permute-done((bf16[4,24,1024]{2,1,0:T(8,128)(2,1)S(1)}, bf16[4,24,1024]{2,1,0:T(8,128)(2,1)S(1)}, u32[]{:S(2)}, u32[]{:S(2)}) %collective-permute-start.24) | collective-permute-done | bytes 196640 | tf_op jit(solution)/shard_map/ppermute | solution.py:605
  131.6 3.7 %context_grad.3 = bf16[2880,768]{1,0:T(8,128)(2,1)} custom-call(bf16[2880,768]{1,0:T(8,128)(2,1)} %get-tuple-element.124.sg_ref, bf16[768,768]{1,0:T(8,128)(2,1)} %wo_ref.7, bf16[2880,768]{1,0:T(8,128)(2,1)} %context_grad.2.rest_0_), custom_call_target="tpu_custom_call", output_to_operand_aliasing={{}: (2, {})} | custom-call | flops 849346560 | bytes 2211840 | tf_op jit(solution)/shard_map/context_grad/pallas_call | solution.py:477
  135.3 2.3 %unpack.1 = (f32[32,24,768]{2,1,0:T(8,128)}, f32[32,24,128]{2,1,0:T(8,128)}, f32[6,128]{1,0:T(8,128)}, f32[6,128]{1,0:T(8,128)}, f32[1]{0:T(128)}) custom-call(s32[32]{0:T(128)S(1)} %add.124.index_ref, bf16[4,24,1024]{2,1,0:T(8,128)(2,1)S(1)} %pad_maximum_fusion.2.rest_0_, bf16[4,24,1024]{2,1,0:T(8,128)(2,1)S(1)} %collective-permute-done.23.rest_1_, ...), custom_call_target="tpu_custom_call" | custom-call | tf_op jit(solution)/shard_map/unpack/pallas_call | solution.py:556
  (116 shorter events, 30.7 us)
Async XLA Ops:
  1.7 18.9 %collective-permute-start = (bf16[2,128,256]{2,1,0:T(8,128)(2,1)S(1)}, bf16[2,128,256]{2,1,0:T(8,128)(2,1)S(1)}, u32[]{:S(2)}, u32[]{:S(2)}) collective-permute-start(bf16[2,128,256]{2,1,0:T(8,128)(2,1)S(1)} %pad_maximum_fusion.3), channel_id=1, source_target_pairs={{0,1},{1,2},{2,3},{3,0},{4,5},{5,6},{6,7},{7,4},{8,9},{9,10},{10,1... | collective-permute-start | bytes 393224 | tf_op jit(solution)/shard_map/ppermute | solution.py:613
  4.7 15.9 %collective-permute-start.1 = (bf16[2,128,256]{2,1,0:T(8,128)(2,1)S(1)}, bf16[2,128,256]{2,1,0:T(8,128)(2,1)S(1)}, u32[]{:S(2)}, u32[]{:S(2)}) collective-permute-start(bf16[2,128,256]{2,1,0:T(8,128)(2,1)S(1)} %pad_maximum_fusion.3), channel_id=1, source_target_pairs={{0,2},{1,3},{2,0},{3,1},{4,6},{5,7},{6,4},{7,5},{8,10},{9,11},{10,... | collective-permute-start | bytes 393224 | tf_op jit(solution)/shard_map/ppermute | solution.py:613
  7.3 13.3 %collective-permute-start.2 = (bf16[2,128,256]{2,1,0:T(8,128)(2,1)S(1)}, bf16[2,128,256]{2,1,0:T(8,128)(2,1)S(1)}, u32[]{:S(2)}, u32[]{:S(2)}) collective-permute-start(bf16[2,128,256]{2,1,0:T(8,128)(2,1)S(1)} %pad_maximum_fusion.3), channel_id=1, source_target_pairs={{0,3},{1,0},{2,1},{3,2},{4,7},{5,4},{6,5},{7,6},{8,11},{9,8},{10,9... | collective-permute-start | bytes 393224 | tf_op jit(solution)/shard_map/ppermute | solution.py:613
  10.9 23.3 %collective-permute-start.8 = (bf16[1,128,256]{2,1,0:T(8,128)(2,1)S(1)}, bf16[1,128,256]{2,1,0:T(8,128)(2,1)S(1)}, u32[]{:S(2)}, u32[]{:S(2)}) collective-permute-start(bf16[1,128,256]{2,1,0:T(8,128)(2,1)S(1)} %pad_bitcast_fusion), channel_id=1, source_target_pairs={{0,24},{4,28},{8,16},{12,20},{16,8},{20,12},{24,0},{28,4},{1,25},{... | collective-permute-start | bytes 196616 | tf_op jit(solution)/shard_map/ppermute | solution.py:605
  20.7 15.2 %collective-permute-start.5 = (bf16[2,128,256]{2,1,0:T(8,128)(2,1)S(1)}, bf16[2,128,256]{2,1,0:T(8,128)(2,1)S(1)}, u32[]{:S(2)}, u32[]{:S(2)}) collective-permute-start(bf16[2,128,256]{2,1,0:T(8,128)(2,1)S(1)} %pad_maximum_fusion.4), channel_id=1, source_target_pairs={{0,1},{1,2},{2,3},{3,0},{4,5},{5,6},{6,7},{7,4},{8,9},{9,10},{10,1... | collective-permute-start | bytes 393224 | tf_op jit(solution)/shard_map/ppermute | solution.py:613
  21.4 14.6 %collective-permute-start.6 = (bf16[2,128,256]{2,1,0:T(8,128)(2,1)S(1)}, bf16[2,128,256]{2,1,0:T(8,128)(2,1)S(1)}, u32[]{:S(2)}, u32[]{:S(2)}) collective-permute-start(bf16[2,128,256]{2,1,0:T(8,128)(2,1)S(1)} %pad_maximum_fusion.4), channel_id=1, source_target_pairs={{0,2},{1,3},{2,0},{3,1},{4,6},{5,7},{6,4},{7,5},{8,10},{9,11},{10,... | collective-permute-start | bytes 393224 | tf_op jit(solution)/shard_map/ppermute | solution.py:613
  21.8 17.8 %collective-permute-start.3 = (bf16[7,128,256]{2,1,0:T(8,128)(2,1)S(1)}, bf16[7,128,256]{2,1,0:T(8,128)(2,1)S(1)}, u32[]{:S(2)}, u32[]{:S(2)}) collective-permute-start(bf16[7,128,256]{2,1,0:T(8,128)(2,1)S(1)} %pad_maximum_fusion.rest_0_), channel_id=1, source_target_pairs={{0,8},{4,12},{8,0},{12,4},{16,24},{20,28},{24,16},{28,20},{1,9},{5... | collective-permute-start | bytes 1376264 | tf_op jit(solution)/shard_map/ppermute | solution.py:605
  22.5 17.0 %collective-permute-start.4 = (bf16[7,128,256]{2,1,0:T(8,128)(2,1)S(1)}, bf16[7,128,256]{2,1,0:T(8,128)(2,1)S(1)}, u32[]{:S(2)}, u32[]{:S(2)}) collective-permute-start(bf16[7,128,256]{2,1,0:T(8,128)(2,1)S(1)} %pad_maximum_fusion.rest_0_), channel_id=1, source_target_pairs={{0,16},{4,20},{8,24},{12,28},{16,0},{20,4},{24,8},{28,12},{1,17},{... | collective-permute-start | bytes 1376264 | tf_op jit(solution)/shard_map/ppermute | solution.py:605
  34.3 5.2 %collective-permute-start.7 = (bf16[2,128,256]{2,1,0:T(8,128)(2,1)S(1)}, bf16[2,128,256]{2,1,0:T(8,128)(2,1)S(1)}, u32[]{:S(2)}, u32[]{:S(2)}) collective-permute-start(bf16[2,128,256]{2,1,0:T(8,128)(2,1)S(1)} %pad_maximum_fusion.4), channel_id=1, source_target_pairs={{0,3},{1,0},{2,1},{3,2},{4,7},{5,4},{6,5},{7,6},{8,11},{9,8},{10,9... | collective-permute-start | bytes 393224 | tf_op jit(solution)/shard_map/ppermute | solution.py:613
  55.9 10.7 %all-to-all-start = ((bf16[16,32,180]{2,1,0:T(8,128)(2,1)}), bf16[16,32,180]{2,1,0:T(8,128)(2,1)S(1)}, u32[]{:S(2)}, u32[]{:S(2)}) async-start(bf16[16,32,180]{2,1,0:T(8,128)(2,1)} %teacher_maps.1), calls=%async_computation | async-start | bytes 524288 | tf_op jit(solution)/shard_map/all_to_all | solution.py:678
  94.2 9.9 %collective-permute-start.14 = (bf16[4,24,1024]{2,1,0:T(8,128)(2,1)S(1)}, bf16[4,24,1024]{2,1,0:T(8,128)(2,1)S(1)}, u32[]{:S(2)}, u32[]{:S(2)}) collective-permute-start(bf16[4,24,1024]{2,1,0:T(8,128)(2,1)S(1)} %get-tuple-element.105), channel_id=1, source_target_pairs={{0,8},{4,12},{8,0},{12,4},{16,24},{20,28},{24,16},{28,20},{1,9},{5... | collective-permute-start | bytes 589832 | tf_op jit(solution)/shard_map/ppermute | solution.py:605
  94.8 10.9 %collective-permute-start.15 = (bf16[4,24,1024]{2,1,0:T(8,128)(2,1)S(1)}, bf16[4,24,1024]{2,1,0:T(8,128)(2,1)S(1)}, u32[]{:S(2)}, u32[]{:S(2)}) collective-permute-start(bf16[4,24,1024]{2,1,0:T(8,128)(2,1)S(1)} %get-tuple-element.106), channel_id=1, source_target_pairs={{0,16},{4,20},{8,24},{12,28},{16,0},{20,4},{24,8},{28,12},{1,17},{... | collective-permute-start | bytes 589832 | tf_op jit(solution)/shard_map/ppermute | solution.py:605
  95.8 9.8 %collective-permute-start.16 = (bf16[4,24,1024]{2,1,0:T(8,128)(2,1)S(1)}, bf16[4,24,1024]{2,1,0:T(8,128)(2,1)S(1)}, u32[]{:S(2)}, u32[]{:S(2)}) collective-permute-start(bf16[4,24,1024]{2,1,0:T(8,128)(2,1)S(1)} %get-tuple-element.107), channel_id=1, source_target_pairs={{0,24},{4,28},{8,16},{12,20},{16,8},{20,12},{24,0},{28,4},{1,25},{... | collective-permute-start | bytes 589832 | tf_op jit(solution)/shard_map/ppermute | solution.py:605
  106.4 6.3 %collective-permute-start.17 = (bf16[24,1024]{1,0:T(8,128)(2,1)S(1)}, bf16[24,1024]{1,0:T(8,128)(2,1)S(1)}, u32[]{:S(2)}, u32[]{:S(2)}) collective-permute-start(bf16[24,1024]{1,0:T(8,128)(2,1)S(1)} %get-tuple-element.114), channel_id=1, source_target_pairs={{0,1},{1,2},{2,3},{3,0},{4,5},{5,6},{6,7},{7,4},{8,9},{9,10},{10,1... | collective-permute-start | bytes 147464 | tf_op jit(solution)/shard_map/ppermute | solution.py:613
  108.5 5.4 %collective-permute-start.18 = (bf16[24,1024]{1,0:T(8,128)(2,1)S(1)}, bf16[24,1024]{1,0:T(8,128)(2,1)S(1)}, u32[]{:S(2)}, u32[]{:S(2)}) collective-permute-start(bf16[24,1024]{1,0:T(8,128)(2,1)S(1)} %get-tuple-element.115), channel_id=1, source_target_pairs={{0,2},{1,3},{2,0},{3,1},{4,6},{5,7},{6,4},{7,5},{8,10},{9,11},{10,... | collective-permute-start | bytes 147464 | tf_op jit(solution)/shard_map/ppermute | solution.py:613
  114.4 6.0 %collective-permute-start.20 = (bf16[24,1024]{1,0:T(8,128)(2,1)S(1)}, bf16[24,1024]{1,0:T(8,128)(2,1)S(1)}, u32[]{:S(2)}, u32[]{:S(2)}) collective-permute-start(bf16[24,1024]{1,0:T(8,128)(2,1)S(1)} %sum_tensor.1), channel_id=1, source_target_pairs={{0,1},{1,2},{2,3},{3,0},{4,5},{5,6},{6,7},{7,4},{8,9},{9,10},{10,1... | collective-permute-start | bytes 147464 | tf_op jit(solution)/shard_map/ppermute | solution.py:613
  115.1 6.2 %collective-permute-start.21 = (bf16[24,1024]{1,0:T(8,128)(2,1)S(1)}, bf16[24,1024]{1,0:T(8,128)(2,1)S(1)}, u32[]{:S(2)}, u32[]{:S(2)}) collective-permute-start(bf16[24,1024]{1,0:T(8,128)(2,1)S(1)} %sum_tensor.1), channel_id=1, source_target_pairs={{0,2},{1,3},{2,0},{3,1},{4,6},{5,7},{6,4},{7,5},{8,10},{9,11},{10,... | collective-permute-start | bytes 147464 | tf_op jit(solution)/shard_map/ppermute | solution.py:613
  121.6 5.7 %collective-permute-start.23 = (bf16[4,24,1024]{2,1,0:T(8,128)(2,1)S(1)}, bf16[4,24,1024]{2,1,0:T(8,128)(2,1)S(1)}, u32[]{:S(2)}, u32[]{:S(2)}) collective-permute-start(bf16[4,24,1024]{2,1,0:T(8,128)(2,1)S(1)} %pad_maximum_fusion.2.rest_0_), channel_id=1, source_target_pairs={{0,8},{4,12},{8,0},{12,4},{16,24},{20,28},{24,16},{28,20},{1,9},{5... | collective-permute-start | bytes 589832 | tf_op jit(solution)/shard_map/ppermute | solution.py:605
  123.1 7.8 %collective-permute-start.24 = (bf16[4,24,1024]{2,1,0:T(8,128)(2,1)S(1)}, bf16[4,24,1024]{2,1,0:T(8,128)(2,1)S(1)}, u32[]{:S(2)}, u32[]{:S(2)}) collective-permute-start(bf16[4,24,1024]{2,1,0:T(8,128)(2,1)S(1)} %pad_maximum_fusion.2.rest_0_), channel_id=1, source_target_pairs={{0,16},{4,20},{8,24},{12,28},{16,0},{20,4},{24,8},{28,12},{1,17},{... | collective-permute-start | bytes 589832 | tf_op jit(solution)/shard_map/ppermute | solution.py:605
  123.7 7.2 %collective-permute-start.25 = (bf16[4,24,1024]{2,1,0:T(8,128)(2,1)S(1)}, bf16[4,24,1024]{2,1,0:T(8,128)(2,1)S(1)}, u32[]{:S(2)}, u32[]{:S(2)}) collective-permute-start(bf16[4,24,1024]{2,1,0:T(8,128)(2,1)S(1)} %pad_maximum_fusion.2.rest_0_), channel_id=1, source_target_pairs={{0,24},{4,28},{8,16},{12,20},{16,8},{20,12},{24,0},{28,4},{1,25},{... | collective-permute-start | bytes 589832 | tf_op jit(solution)/shard_map/ppermute | solution.py:605
  125.3 9.9 %collective-permute-start.26 = (bf16[4,24,1024]{2,1,0:T(8,128)(2,1)S(1)}, bf16[4,24,1024]{2,1,0:T(8,128)(2,1)S(1)}, u32[]{:S(2)}, u32[]{:S(2)}) collective-permute-start(bf16[4,24,1024]{2,1,0:T(8,128)(2,1)S(1)} %pad_maximum_fusion.2.rest_0_), channel_id=1, source_target_pairs={{0,4},{4,0},{8,12},{12,8},{16,20},{20,16},{24,28},{28,24},{1,5},{5... | collective-permute-start | bytes 589832 | tf_op jit(solution)/shard_map/ppermute | solution.py:610
  127.4 7.9 %collective-permute-start.27 = (bf16[4,24,1024]{2,1,0:T(8,128)(2,1)S(1)}, bf16[4,24,1024]{2,1,0:T(8,128)(2,1)S(1)}, u32[]{:S(2)}, u32[]{:S(2)}) collective-permute-start(bf16[4,24,1024]{2,1,0:T(8,128)(2,1)S(1)} %collective-permute-done.23.rest_1_), channel_id=1, source_target_pairs={{0,4},{4,0},{8,12},{12,8},{16,20},{20,16},{24,28},{28,24},{1,5},{5... | collective-permute-start | bytes 589832 | tf_op jit(solution)/shard_map/ppermute | solution.py:610
  130.9 4.3 %collective-permute-start.28 = (bf16[4,24,1024]{2,1,0:T(8,128)(2,1)S(1)}, bf16[4,24,1024]{2,1,0:T(8,128)(2,1)S(1)}, u32[]{:S(2)}, u32[]{:S(2)}) collective-permute-start(bf16[4,24,1024]{2,1,0:T(8,128)(2,1)S(1)} %collective-permute-done.24.rest_2_), channel_id=1, source_target_pairs={{0,4},{4,0},{8,12},{12,8},{16,20},{20,16},{24,28},{28,24},{1,5},{5... | collective-permute-start | bytes 589832 | tf_op jit(solution)/shard_map/ppermute | solution.py:610
  130.9 4.3 %collective-permute-start.29 = (bf16[4,24,1024]{2,1,0:T(8,128)(2,1)S(1)}, bf16[4,24,1024]{2,1,0:T(8,128)(2,1)S(1)}, u32[]{:S(2)}, u32[]{:S(2)}) collective-permute-start(bf16[4,24,1024]{2,1,0:T(8,128)(2,1)S(1)} %collective-permute-done.25.rest_3_), channel_id=1, source_target_pairs={{0,4},{4,0},{8,12},{12,8},{16,20},{20,16},{24,28},{28,24},{1,5},{5... | collective-permute-start | bytes 589832 | tf_op jit(solution)/shard_map/ppermute | solution.py:610
  (19 other events, 78.4 us)

commit v9 on v8

--- a/solution.py
+++ b/solution.py
@@ -46,8 +46,8 @@
     return pl.CostEstimate(flops=int(flops), bytes_accessed=int(nbytes), transcendentals=0)
 
 
-def forward_kernel(x_ref, str_ref, wo_ref, gain_ref, bias_ref, wp_ref, *rest):
-    normed_ref, emb_ref, inv_ref, turned_ref, prod_s, hid_s = rest[-6:]
+def forward_kernel(x_ref, str_ref, wo_ref, gain_ref, bias_ref, wp_ref,
+                   normed_ref, emb_ref, inv_ref, turned_ref, prod_s, hid_s):
     rows, width = x_ref.shape
     sub = rows
     gain, bias = one_row(gain_ref), one_row(bias_ref)
@@ -65,18 +65,18 @@
     turned_ref[0] = x_ref[...].T
 
 
-def student_forward(x, stream, out_weight, gain, bias, proj_weight, first, last, before=()):
+def student_forward(x, stream, out_weight, gain, bias, proj_weight):
     total, width = x.shape
     emb = proj_weight.shape[1]
     rows = split_rows(total, 720)
-    block = lambda n: pl.BlockSpec((rows, n), lambda s: (s + first, 0))
+    block = lambda n: pl.BlockSpec((rows, n), lambda s: (s, 0))
     whole = lambda a: pl.BlockSpec(a.shape, lambda s: (0,) * a.ndim)
     inputs = (x, stream, out_weight, gain, bias, proj_weight)
     return pl.pallas_call(
         forward_kernel,
-        grid=(last - first,),
-        in_specs=[block(width), block(width)] + [whole(a) for a in inputs[2:]] + [ANY] * len(before),
-        out_specs=[block(width), block(emb), block(128), pl.BlockSpec((1, width, rows), lambda s: (s + first, 0, 0))],
+        grid=(total // rows,),
+        in_specs=[block(width), block(width)] + [whole(a) for a in inputs[2:]],
+        out_specs=[block(width), block(emb), block(128), pl.BlockSpec((1, width, rows), lambda s: (s, 0, 0))],
         out_shape=[
             jax.ShapeDtypeStruct((total, width), BF16),
             jax.ShapeDtypeStruct((total, emb), F32),
@@ -84,11 +84,10 @@
             jax.ShapeDtypeStruct((total // rows, width, rows), BF16),
         ],
         scratch_shapes=[pltpu.VMEM((rows, width), F32), pltpu.VMEM((rows, width), BF16)],
-        input_output_aliases={len(inputs) + n: n for n in range(len(before))},
         compiler_params=params(),
-        cost_estimate=cost(2 * (last - first) * rows * width * (width + emb), 8 * (last - first) * rows * width),
+        cost_estimate=cost(2 * total * width * (width + emb), 8 * total * width),
         name="student_forward",
-    )(*inputs, *before)
+    )(*inputs)
 
 
 def teacher_kernel(parts, count, tokens, order_ref, from_ref, rows_ref, states_ref, wq_ref, wk_ref, *rest):
@@ -465,26 +464,24 @@
     )(qidx, midx, lens, core, *manual, qdir, qlen, gain, bias, wp, wpt)
 
 
-def context_kernel(sg_ref, wo_ref, *rest):
-    out_ref = rest[-1]
+def context_kernel(sg_ref, wo_ref, out_ref):
     out_ref[...] = dot(sg_ref[...], wo_ref[...], 1, 1).astype(BF16)
 
 
-def context_grad(sg, out_weight, first, last, before=()):
+def context_grad(sg, out_weight):
     total, width = sg.shape
     rows = split_rows(total, 720)
-    block = pl.BlockSpec((rows, width), lambda s: (s + first, 0))
+    block = pl.BlockSpec((rows, width), lambda s: (s, 0))
     return pl.pallas_call(
         context_kernel,
-        grid=(last - first,),
-        in_specs=[block, pl.BlockSpec(out_weight.shape, lambda s: (0, 0))] + [ANY] * len(before),
+        grid=(total // rows,),
+        in_specs=[block, pl.BlockSpec(out_weight.shape, lambda s: (0, 0))],
         out_specs=block,
         out_shape=jax.ShapeDtypeStruct(sg.shape, BF16),
-        input_output_aliases={2: 0} if before else {},
         compiler_params=params(),
-        cost_estimate=cost(2 * (last - first) * rows * width * width, 4 * (last - first) * rows * width),
+        cost_estimate=cost(2 * total * width * width, 4 * total * width),
         name="context_grad",
-    )(sg, out_weight, *before)
+    )(sg, out_weight)
 
 
 def split_sum_kernel(inputs, outputs, index_ref, *rest):
@@ -641,17 +638,14 @@
     along = jnp.concatenate([shift_t(mine, k) for k in range(1, nt)] + [rider], axis=0)
     gain2, bias2 = gain.reshape(-1, 128), bias.reshape(-1, 128)
     x = flat(context)
-    blocks = x.shape[0] // split_rows(x.shape[0], 720)
-    forward = functools.partial(student_forward, x, flat(stream), out_weight, gain2, bias2, proj_weight)
-    begun = forward(0, 1)
-    along, far_mine, begun = lax.optimization_barrier((along, far_mine, begun))
+    far_riders = [shift_chip(rider, k) for k in far]
+    along, far_mine, far_riders, forward_gain = lax.optimization_barrier((along, far_mine, far_riders, gain2))
     pieces = [along] + [None] * (chips - 1)
     for k in range(1, chips):
         if k not in far:
             pieces[k] = shift_chip(along, k)
-    for k, other in zip(far, far_mine):
-        received = [shift_t(other, n) for n in range(1, nt)]
-        pieces[k] = jnp.concatenate(received + [shift_chip(rider, k)], axis=0)
+    for k, other, far_rider in zip(far, far_mine, far_riders):
+        pieces[k] = jnp.concatenate([shift_t(other, n) for n in range(1, nt)] + [far_rider], axis=0)
     shifts = jnp.arange(chips, dtype=jnp.int32)
     behind = chip ^ shifts if paired else (chip - shifts) % chips
     piece_rows = jnp.concatenate([behind * CORES + core, behind * CORES + 1 - core]).astype(jnp.int32)
@@ -664,7 +658,9 @@
     qidx = qidx.astype(jnp.int32)
     source = piece_of(jnp.arange(dp, dtype=jnp.int32)).astype(jnp.int32)
 
-    normed, embeds, inverse, turned = forward(1, blocks, begun) if blocks > 1 else begun
+    normed, embeds, inverse, turned = student_forward(
+        x, flat(stream), out_weight, forward_gain, bias2, proj_weight
+    )
     pieces[1:], normed, embeds, inverse, turned, proj_turned = lax.optimization_barrier(
         (pieces[1:], normed, embeds, inverse, turned, proj_weight.T)
     )
@@ -691,17 +687,13 @@
     t_ahead = ((mt + t_shifts) % nt).astype(jnp.int32)
     parts = split_sum([keep, swap_core(send)], ahead, "sum_cores")
     parts, sg = lax.optimization_barrier((parts, sg))
-    most = max(blocks - 1, 1)
-    grad_context = context_grad(sg, out_weight, 0, most)
+    grad_context = context_grad(sg, out_weight)
     parts = [parts[0]] + [shift_chip(parts[k], k) for k in range(1, chips)]
     parts, grad_context = lax.optimization_barrier((parts, grad_context))
     parts = split_sum(parts, t_ahead, "sum_plane")
     parts = [parts[0]] + [shift_t(parts[k], k) for k in range(1, nt)]
     total = plain_sum(parts, "sum_tensor")
     line = jnp.stack([total] + [shift_t(total, k) for k in range(1, nt)])
-    if most < blocks:
-        line, sg, grad_context = lax.optimization_barrier((line, sg, grad_context))
-        grad_context = context_grad(sg, out_weight, most, blocks, (grad_context,))
     plane = [line] + [shift_chip(line, k) for k in range(1, chips)]
     arrays = plane + [swap_core(a) for a in plane]
     base = jnp.concatenate([core * chips + behind, (1 - core) * chips + behind]) * nt

time: 138 us -> 134 us (0.971)
  Pallas kernels: 68.8 us -> 63 us
  starting transfers between devices: 35.2 us -> 38.6 us
  waiting for transfers between devices: 24 us -> 20.7 us
    pallas_call x4 -> x2, Pallas kernels: 25.9 us -> 20.1 us  [the longest x1 12.5 us: student_forward(): pl.pallas_call(forward_kernel, grid=(total // rows,), in_specs=[block(wid...]
    ppermute x12, waiting for transfers between devices: 10 us -> 6.94 us  [shift_t(): return lax.ppermute(x, 'tensor', [(t, (t + k) % nt) for t in range(nt)])]
    ppermute x12, starting transfers between devices: 18.3 us -> 20.6 us  [shift_t(): return lax.ppermute(x, 'tensor', [(t, (t + k) % nt) for t in range(nt)])]
    unnamed x25 -> x23, local copies, waits for them, and re-layouts: 3.49 us -> 4.39 us
  transfers between devices with their start and end apart: 31 -> 31, of which waited for: 15 -> 18; matrix products, arithmetic and copies ran while one was open for 3% -> 4% of each run, Pallas kernels for 22% -> 19%
where the time goes in v9:
time: 134 us; the launch traced here: 133 us
  Pallas kernels  63 us (47%)
  starting transfers between devices  38.6 us (29%)
  waiting for transfers between devices  20.7 us (15%)
  local copies, waits for them, and re-layouts  6.3 us (5%)
  other arithmetic  3.08 us (2%)
    pallas_call x1, Pallas kernels, student_backward(): pl.pallas_call(functools.partial(backward_kernel, tokens, count, blocks),...  22.2 us
    ppermute x12, starting transfers between devices, shift_t(): return lax.ppermute(x, 'tensor', [(t, (t + k) % nt) for t in range(nt)])  20.6 us
    ppermute x9, starting transfers between devices, shift_chip(): lax.ppermute(x, 'dp', [(c * CORES + o, partner(c, k) * CORES + o) for c i...  12.6 us
    pallas_call x1, Pallas kernels, student_forward(): pl.pallas_call(forward_kernel, grid=(total // rows,), in_specs=[block(wid...  12.5 us
    pallas_call x1, Pallas kernels, teacher_maps(): pl.pallas_call(functools.partial(teacher_kernel, parts, count, tokens), i...  11.6 us
    pallas_call x1, Pallas kernels, context_grad(): pl.pallas_call(context_kernel, grid=(total // rows,), in_specs=[block, pl...  7.53 us
    ppermute x12, waiting for transfers between devices, shift_t(): return lax.ppermute(x, 'tensor', [(t, (t + k) % nt) for t in range(nt)])  6.94 us
    ppermute x9, waiting for transfers between devices, shift_chip(): lax.ppermute(x, 'dp', [(c * CORES + o, partner(c, k) * CORES + o) for c i...  6.16 us
  transfers between devices with their start and end apart: 31, of which 18 were waited for; matrix products, arithmetic and copies ran while one was open for 4% of the time, Pallas kernels for 19%

profile of v9, /device:TPU:0, one launch (start us, length us, event | category | flops | bytes accessed | tf_op | source)
XLA Modules:
  0.0 132.8 jit_solution(9421833835490539354)
XLA Ops:
  1.7 3.1 %collective-permute-start = (bf16[2,128,256]{2,1,0:T(8,128)(2,1)S(1)}, bf16[2,128,256]{2,1,0:T(8,128)(2,1)S(1)}, u32[]{:S(2)}, u32[]{:S(2)}) collective-permute-start(bf16[2,128,256]{2,1,0:T(8,128)(2,1)S(1)} %pad_maximum_fusion.3), channel_id=1, source_target_pairs={{0,1},{1,2},{2,3},{3,0},{4,5},{5,6},{6,7},{7,4},{8,9},{9,10},{10,1... | collective-permute-start | bytes 393224 | tf_op jit(solution)/shard_map/ppermute | solution.py:610
  4.7 2.6 %collective-permute-start.1 = (bf16[2,128,256]{2,1,0:T(8,128)(2,1)S(1)}, bf16[2,128,256]{2,1,0:T(8,128)(2,1)S(1)}, u32[]{:S(2)}, u32[]{:S(2)}) collective-permute-start(bf16[2,128,256]{2,1,0:T(8,128)(2,1)S(1)} %pad_maximum_fusion.3), channel_id=1, source_target_pairs={{0,2},{1,3},{2,0},{3,1},{4,6},{5,7},{6,4},{7,5},{8,10},{9,11},{10,... | collective-permute-start | bytes 393224 | tf_op jit(solution)/shard_map/ppermute | solution.py:610
  10.9 2.5 %collective-permute-start.3 = (bf16[1,128,256]{2,1,0:T(8,128)(2,1)S(1)}, bf16[1,128,256]{2,1,0:T(8,128)(2,1)S(1)}, u32[]{:S(2)}, u32[]{:S(2)}) collective-permute-start(bf16[1,128,256]{2,1,0:T(8,128)(2,1)S(1)} %pad_bitcast_fusion), channel_id=1, source_target_pairs={{0,24},{4,28},{8,16},{12,20},{16,8},{20,12},{24,0},{28,4},{1,25},{... | collective-permute-start | bytes 196616 | tf_op jit(solution)/shard_map/ppermute | solution.py:602
  14.0 1.7 %copy.20 = bf16[768,128]{0,1:T(8,128)(2,1)} copy(bf16[768,128]{1,0:T(8,128)(2,1)} %wp_ref.5) | data formatting | bytes 393216 | tf_op args[5]
  16.2 3.2 %collective-permute-start.6 = (bf16[2,128,256]{2,1,0:T(8,128)(2,1)S(1)}, bf16[2,128,256]{2,1,0:T(8,128)(2,1)S(1)}, u32[]{:S(2)}, u32[]{:S(2)}) collective-permute-start(bf16[2,128,256]{2,1,0:T(8,128)(2,1)S(1)} %pad_maximum_fusion.4), channel_id=1, source_target_pairs={{0,1},{1,2},{2,3},{3,0},{4,5},{5,6},{6,7},{7,4},{8,9},{9,10},{10,1... | collective-permute-start | bytes 393224 | tf_op jit(solution)/shard_map/ppermute | solution.py:610
  19.4 1.6 %collective-permute-start.7 = (bf16[2,128,256]{2,1,0:T(8,128)(2,1)S(1)}, bf16[2,128,256]{2,1,0:T(8,128)(2,1)S(1)}, u32[]{:S(2)}, u32[]{:S(2)}) collective-permute-start(bf16[2,128,256]{2,1,0:T(8,128)(2,1)S(1)} %pad_maximum_fusion.4), channel_id=1, source_target_pairs={{0,2},{1,3},{2,0},{3,1},{4,6},{5,7},{6,4},{7,5},{8,10},{9,11},{10,... | collective-permute-start | bytes 393224 | tf_op jit(solution)/shard_map/ppermute | solution.py:610
  21.8 1.5 %collective-permute-start.4 = (bf16[7,128,256]{2,1,0:T(8,128)(2,1)S(1)}, bf16[7,128,256]{2,1,0:T(8,128)(2,1)S(1)}, u32[]{:S(2)}, u32[]{:S(2)}) collective-permute-start(bf16[7,128,256]{2,1,0:T(8,128)(2,1)S(1)} %pad_maximum_fusion.rest_0_), channel_id=1, source_target_pairs={{0,8},{4,12},{8,0},{12,4},{16,24},{20,28},{24,16},{28,20},{1,9},{5... | collective-permute-start | bytes 1376264 | tf_op jit(solution)/shard_map/ppermute | solution.py:602
  23.3 1.5 %collective-permute-start.5 = (bf16[7,128,256]{2,1,0:T(8,128)(2,1)S(1)}, bf16[7,128,256]{2,1,0:T(8,128)(2,1)S(1)}, u32[]{:S(2)}, u32[]{:S(2)}) collective-permute-start(bf16[7,128,256]{2,1,0:T(8,128)(2,1)S(1)} %pad_maximum_fusion.rest_0_), channel_id=1, source_target_pairs={{0,16},{4,20},{8,24},{12,28},{16,0},{20,4},{24,8},{28,12},{1,17},{... | collective-permute-start | bytes 1376264 | tf_op jit(solution)/shard_map/ppermute | solution.py:602
  24.8 12.5 %student_forward.1 = (bf16[2880,768]{1,0:T(8,128)(2,1)}, f32[2880,128]{1,0:T(8,128)}, f32[2880,128]{1,0:T(8,128)}, bf16[4,768,720]{2,1,0:T(8,128)(2,1)}) custom-call(bf16[2880,768]{1,0:T(8,128)(2,1)} %bitcast.61, bf16[2880,768]{1,0:T(8,128)(2,1)} %bitcast.62, bf16[768,768]{1,0:T(8,128)(2,1)} %wo_ref.3, f32[6,128]{1,0:T(8,128)} %bitcast.65, ...), custom_call_target="tpu_custom_call" | custom-call | flops 3963617280 | bytes 17694720 | tf_op jit(solution)/shard_map/student_forward/pallas_call | solution.py:75
  42.8 11.6 %teacher_maps.1 = bf16[16,32,180]{2,1,0:T(8,128)(2,1)} custom-call(s32[8,2]{1,0:T(8,128)} %dynamic-slice_convert_fusion.order_ref, s32[8]{0:T(128)} %get-tuple-element.120.from_ref, s32[8]{0:T(128)} %get-tuple-element.121.rows_ref, bf16[3392,1024]{1,0:T(8,128)(2,1)} %bitcast.60, bf16[1024,256]{1,0:T(8,128)(2,1)} %wq_ref.1, bf16[1024,256]{1,0:T(8,128)(2,1)} %wk_ref.1, ...), custom_call_target="tpu_custom_call" | custom-call | flops 4294967296 | bytes 11141120 | tf_op jit(solution)/shard_map/teacher_maps/pallas_call | solution.py:177
  54.4 3.6 %all-to-all-start = ((bf16[16,32,180]{2,1,0:T(8,128)(2,1)}), bf16[16,32,180]{2,1,0:T(8,128)(2,1)S(1)}, u32[]{:S(2)}, u32[]{:S(2)}) async-start(bf16[16,32,180]{2,1,0:T(8,128)(2,1)} %teacher_maps.1), calls=%async_computation | async-start | bytes 524288 | tf_op jit(solution)/shard_map/all_to_all | solution.py:674
  58.0 5.1 %student_scores.1 = (f32[16,32,180]{2,1,0:T(8,128)}, f32[16,32,180]{2,1,0:T(8,128)}, bf16[16,180,128]{2,1,0:T(8,128)(2,1)}, bf16[8,32,128]{2,1,0:T(8,128)(2,1)},...) custom-call(s32[16]{0:T(128)} %get-tuple-element.108.qidx_ref, s32[16]{0:T(128)} %len_ref.3, ...), custom_call_target="tpu_custom_call" | custom-call | flops 1000000000 | bytes 1474560 | tf_op jit(solution)/shard_map/student_scores/pallas_call | solution.py:259
  63.1 1.6 %all-to-all-done.maps_in = bf16[16,32,180]{2,1,0:T(8,128)(2,1)S(1)} async-done(((bf16[16,32,180]{2,1,0:T(8,128)(2,1)}), bf16[16,32,180]{2,1,0:T(8,128)(2,1)S(1)}, u32[]{:S(2)}, u32[]{:S(2)}) %all-to-all-start) | async-done | bytes 184352 | tf_op jit(solution)/shard_map/all_to_all | solution.py:674
  65.4 22.2 %student_backward.1 = (bf16[2880,768]{1,0:T(8,128)(2,1)}, bf16[16,24,1024]{2,1,0:T(8,128)(2,1)}, bf16[16,24,1024]{2,1,0:T(8,128)(2,1)}) custom-call(s32[16]{0:T(128)} %get-tuple-element.108.qidx_ref, s32[16]{0:T(128)} %copy-done.10, s32[16]{0:T(128)} %len_ref.3, s32[1]{0:T(128)} %bitcast.core_ref, bf16[16,32,180]{2,1,0:T(8,128)(2,1)} %copy-done.9, ...), custom_call_target="tpu_custom_call" | custom-call | flops 4529848320 | bytes 17694720 | tf_op jit(solution)/shard_map/student_backward/pallas_call | solution.py:438
  87.8 2.5 %collective-permute-done.13.rest_1_ = bf16[16,24,1024]{2,1,0:T(8,128)(2,1)S(1)} collective-permute-done((bf16[16,24,1024]{2,1,0:T(8,128)(2,1)}, bf16[16,24,1024]{2,1,0:T(8,128)(2,1)S(1)}, u32[]{:S(2)}, u32[]{:S(2)}) %collective-permute-start.13) | collective-permute-done | bytes 786464 | tf_op jit(solution)/shard_map/ppermute | solution.py:607
  94.0 1.9 %collective-permute-start.16 = (bf16[4,24,1024]{2,1,0:T(8,128)(2,1)S(1)}, bf16[4,24,1024]{2,1,0:T(8,128)(2,1)S(1)}, u32[]{:S(2)}, u32[]{:S(2)}) collective-permute-start(bf16[4,24,1024]{2,1,0:T(8,128)(2,1)S(1)} %get-tuple-element.92), channel_id=1, source_target_pairs={{0,24},{4,28},{8,16},{12,20},{16,8},{20,12},{24,0},{28,4},{1,25},{... | collective-permute-start | bytes 589832 | tf_op jit(solution)/shard_map/ppermute | solution.py:602
  95.9 7.5 %context_grad.1 = bf16[2880,768]{1,0:T(8,128)(2,1)} custom-call(bf16[2880,768]{1,0:T(8,128)(2,1)} %get-tuple-element.93.sg_ref, bf16[768,768]{1,0:T(8,128)(2,1)} %wo_ref.3), custom_call_target="tpu_custom_call" | custom-call | flops 3397386240 | bytes 8847360 | tf_op jit(solution)/shard_map/context_grad/pallas_call | solution.py:475
  108.4 2.2 %collective-permute-done.17.refs_1_ = bf16[24,1024]{1,0:T(8,128)(2,1)S(1)} collective-permute-done((bf16[24,1024]{1,0:T(8,128)(2,1)S(1)}, bf16[24,1024]{1,0:T(8,128)(2,1)S(1)}, u32[]{:S(2)}, u32[]{:S(2)}) %collective-permute-start.17) | collective-permute-done | bytes 49184 | tf_op jit(solution)/shard_map/ppermute | solution.py:610
  113.2 1.8 %collective-permute-start.21 = (bf16[24,1024]{1,0:T(8,128)(2,1)S(1)}, bf16[24,1024]{1,0:T(8,128)(2,1)S(1)}, u32[]{:S(2)}, u32[]{:S(2)}) collective-permute-start(bf16[24,1024]{1,0:T(8,128)(2,1)S(1)} %sum_tensor.1), channel_id=1, source_target_pairs={{0,2},{1,3},{2,0},{3,1},{4,6},{5,7},{6,4},{7,5},{8,10},{9,11},{10,... | collective-permute-start | bytes 147464 | tf_op jit(solution)/shard_map/ppermute | solution.py:610
  115.9 1.9 %collective-permute-done.20 = bf16[24,1024]{1,0:T(8,128)(2,1)S(1)} collective-permute-done((bf16[24,1024]{1,0:T(8,128)(2,1)S(1)}, bf16[24,1024]{1,0:T(8,128)(2,1)S(1)}, u32[]{:S(2)}, u32[]{:S(2)}) %collective-permute-start.20) | collective-permute-done | bytes 49184 | tf_op jit(solution)/shard_map/ppermute | solution.py:610
  119.3 1.5 %collective-permute-start.23 = (bf16[4,24,1024]{2,1,0:T(8,128)(2,1)S(1)}, bf16[4,24,1024]{2,1,0:T(8,128)(2,1)S(1)}, u32[]{:S(2)}, u32[]{:S(2)}) collective-permute-start(bf16[4,24,1024]{2,1,0:T(8,128)(2,1)S(1)} %pad_maximum_fusion.2.rest_0_), channel_id=1, source_target_pairs={{0,8},{4,12},{8,0},{12,4},{16,24},{20,28},{24,16},{28,20},{1,9},{5... | collective-permute-start | bytes 589832 | tf_op jit(solution)/shard_map/ppermute | solution.py:602
  123.0 2.1 %collective-permute-done.23.rest_1_ = bf16[4,24,1024]{2,1,0:T(8,128)(2,1)S(1)} collective-permute-done((bf16[4,24,1024]{2,1,0:T(8,128)(2,1)S(1)}, bf16[4,24,1024]{2,1,0:T(8,128)(2,1)S(1)}, u32[]{:S(2)}, u32[]{:S(2)}) %collective-permute-start.23) | collective-permute-done | bytes 196640 | tf_op jit(solution)/shard_map/ppermute | solution.py:602
  125.1 3.5 %collective-permute-done.24.rest_2_ = bf16[4,24,1024]{2,1,0:T(8,128)(2,1)S(1)} collective-permute-done((bf16[4,24,1024]{2,1,0:T(8,128)(2,1)S(1)}, bf16[4,24,1024]{2,1,0:T(8,128)(2,1)S(1)}, u32[]{:S(2)}, u32[]{:S(2)}) %collective-permute-start.24) | collective-permute-done | bytes 196640 | tf_op jit(solution)/shard_map/ppermute | solution.py:602
  130.3 2.3 %unpack.1 = (f32[32,24,768]{2,1,0:T(8,128)}, f32[32,24,128]{2,1,0:T(8,128)}, f32[6,128]{1,0:T(8,128)}, f32[6,128]{1,0:T(8,128)}, f32[1]{0:T(128)}) custom-call(s32[32]{0:T(128)S(1)} %add.124.index_ref, bf16[4,24,1024]{2,1,0:T(8,128)(2,1)S(1)} %pad_maximum_fusion.2.rest_0_, bf16[4,24,1024]{2,1,0:T(8,128)(2,1)S(1)} %collective-permute-done.23.rest_1_, ...), custom_call_target="tpu_custom_call" | custom-call | tf_op jit(solution)/shard_map/unpack/pallas_call | solution.py:553
  (112 shorter events, 30.1 us)
Async XLA Ops:
  1.7 14.1 %collective-permute-start = (bf16[2,128,256]{2,1,0:T(8,128)(2,1)S(1)}, bf16[2,128,256]{2,1,0:T(8,128)(2,1)S(1)}, u32[]{:S(2)}, u32[]{:S(2)}) collective-permute-start(bf16[2,128,256]{2,1,0:T(8,128)(2,1)S(1)} %pad_maximum_fusion.3), channel_id=1, source_target_pairs={{0,1},{1,2},{2,3},{3,0},{4,5},{5,6},{6,7},{7,4},{8,9},{9,10},{10,1... | collective-permute-start | bytes 393224 | tf_op jit(solution)/shard_map/ppermute | solution.py:610
  4.7 11.2 %collective-permute-start.1 = (bf16[2,128,256]{2,1,0:T(8,128)(2,1)S(1)}, bf16[2,128,256]{2,1,0:T(8,128)(2,1)S(1)}, u32[]{:S(2)}, u32[]{:S(2)}) collective-permute-start(bf16[2,128,256]{2,1,0:T(8,128)(2,1)S(1)} %pad_maximum_fusion.3), channel_id=1, source_target_pairs={{0,2},{1,3},{2,0},{3,1},{4,6},{5,7},{6,4},{7,5},{8,10},{9,11},{10,... | collective-permute-start | bytes 393224 | tf_op jit(solution)/shard_map/ppermute | solution.py:610
  7.3 8.6 %collective-permute-start.2 = (bf16[2,128,256]{2,1,0:T(8,128)(2,1)S(1)}, bf16[2,128,256]{2,1,0:T(8,128)(2,1)S(1)}, u32[]{:S(2)}, u32[]{:S(2)}) collective-permute-start(bf16[2,128,256]{2,1,0:T(8,128)(2,1)S(1)} %pad_maximum_fusion.3), channel_id=1, source_target_pairs={{0,3},{1,0},{2,1},{3,2},{4,7},{5,4},{6,5},{7,6},{8,11},{9,8},{10,9... | collective-permute-start | bytes 393224 | tf_op jit(solution)/shard_map/ppermute | solution.py:610
  10.9 5.2 %collective-permute-start.3 = (bf16[1,128,256]{2,1,0:T(8,128)(2,1)S(1)}, bf16[1,128,256]{2,1,0:T(8,128)(2,1)S(1)}, u32[]{:S(2)}, u32[]{:S(2)}) collective-permute-start(bf16[1,128,256]{2,1,0:T(8,128)(2,1)S(1)} %pad_bitcast_fusion), channel_id=1, source_target_pairs={{0,24},{4,28},{8,16},{12,20},{16,8},{20,12},{24,0},{28,4},{1,25},{... | collective-permute-start | bytes 196616 | tf_op jit(solution)/shard_map/ppermute | solution.py:602
  16.2 21.3 %collective-permute-start.6 = (bf16[2,128,256]{2,1,0:T(8,128)(2,1)S(1)}, bf16[2,128,256]{2,1,0:T(8,128)(2,1)S(1)}, u32[]{:S(2)}, u32[]{:S(2)}) collective-permute-start(bf16[2,128,256]{2,1,0:T(8,128)(2,1)S(1)} %pad_maximum_fusion.4), channel_id=1, source_target_pairs={{0,1},{1,2},{2,3},{3,0},{4,5},{5,6},{6,7},{7,4},{8,9},{9,10},{10,1... | collective-permute-start | bytes 393224 | tf_op jit(solution)/shard_map/ppermute | solution.py:610
  19.4 18.1 %collective-permute-start.7 = (bf16[2,128,256]{2,1,0:T(8,128)(2,1)S(1)}, bf16[2,128,256]{2,1,0:T(8,128)(2,1)S(1)}, u32[]{:S(2)}, u32[]{:S(2)}) collective-permute-start(bf16[2,128,256]{2,1,0:T(8,128)(2,1)S(1)} %pad_maximum_fusion.4), channel_id=1, source_target_pairs={{0,2},{1,3},{2,0},{3,1},{4,6},{5,7},{6,4},{7,5},{8,10},{9,11},{10,... | collective-permute-start | bytes 393224 | tf_op jit(solution)/shard_map/ppermute | solution.py:610
  21.0 16.5 %collective-permute-start.8 = (bf16[2,128,256]{2,1,0:T(8,128)(2,1)S(1)}, bf16[2,128,256]{2,1,0:T(8,128)(2,1)S(1)}, u32[]{:S(2)}, u32[]{:S(2)}) collective-permute-start(bf16[2,128,256]{2,1,0:T(8,128)(2,1)S(1)} %pad_maximum_fusion.4), channel_id=1, source_target_pairs={{0,3},{1,0},{2,1},{3,2},{4,7},{5,4},{6,5},{7,6},{8,11},{9,8},{10,9... | collective-permute-start | bytes 393224 | tf_op jit(solution)/shard_map/ppermute | solution.py:610
  21.8 15.8 %collective-permute-start.4 = (bf16[7,128,256]{2,1,0:T(8,128)(2,1)S(1)}, bf16[7,128,256]{2,1,0:T(8,128)(2,1)S(1)}, u32[]{:S(2)}, u32[]{:S(2)}) collective-permute-start(bf16[7,128,256]{2,1,0:T(8,128)(2,1)S(1)} %pad_maximum_fusion.rest_0_), channel_id=1, source_target_pairs={{0,8},{4,12},{8,0},{12,4},{16,24},{20,28},{24,16},{28,20},{1,9},{5... | collective-permute-start | bytes 1376264 | tf_op jit(solution)/shard_map/ppermute | solution.py:602
  23.3 14.3 %collective-permute-start.5 = (bf16[7,128,256]{2,1,0:T(8,128)(2,1)S(1)}, bf16[7,128,256]{2,1,0:T(8,128)(2,1)S(1)}, u32[]{:S(2)}, u32[]{:S(2)}) collective-permute-start(bf16[7,128,256]{2,1,0:T(8,128)(2,1)S(1)} %pad_maximum_fusion.rest_0_), channel_id=1, source_target_pairs={{0,16},{4,20},{8,24},{12,28},{16,0},{20,4},{24,8},{28,12},{1,17},{... | collective-permute-start | bytes 1376264 | tf_op jit(solution)/shard_map/ppermute | solution.py:602
  54.4 10.3 %all-to-all-start = ((bf16[16,32,180]{2,1,0:T(8,128)(2,1)}), bf16[16,32,180]{2,1,0:T(8,128)(2,1)S(1)}, u32[]{:S(2)}, u32[]{:S(2)}) async-start(bf16[16,32,180]{2,1,0:T(8,128)(2,1)} %teacher_maps.1), calls=%async_computation | async-start | bytes 524288 | tf_op jit(solution)/shard_map/all_to_all | solution.py:674
  92.3 11.1 %collective-permute-start.14 = (bf16[4,24,1024]{2,1,0:T(8,128)(2,1)S(1)}, bf16[4,24,1024]{2,1,0:T(8,128)(2,1)S(1)}, u32[]{:S(2)}, u32[]{:S(2)}) collective-permute-start(bf16[4,24,1024]{2,1,0:T(8,128)(2,1)S(1)} %get-tuple-element.90), channel_id=1, source_target_pairs={{0,8},{4,12},{8,0},{12,4},{16,24},{20,28},{24,16},{28,20},{1,9},{5... | collective-permute-start | bytes 589832 | tf_op jit(solution)/shard_map/ppermute | solution.py:602
  93.0 10.9 %collective-permute-start.15 = (bf16[4,24,1024]{2,1,0:T(8,128)(2,1)S(1)}, bf16[4,24,1024]{2,1,0:T(8,128)(2,1)S(1)}, u32[]{:S(2)}, u32[]{:S(2)}) collective-permute-start(bf16[4,24,1024]{2,1,0:T(8,128)(2,1)S(1)} %get-tuple-element.91), channel_id=1, source_target_pairs={{0,16},{4,20},{8,24},{12,28},{16,0},{20,4},{24,8},{28,12},{1,17},{... | collective-permute-start | bytes 589832 | tf_op jit(solution)/shard_map/ppermute | solution.py:602
  94.0 9.8 %collective-permute-start.16 = (bf16[4,24,1024]{2,1,0:T(8,128)(2,1)S(1)}, bf16[4,24,1024]{2,1,0:T(8,128)(2,1)S(1)}, u32[]{:S(2)}, u32[]{:S(2)}) collective-permute-start(bf16[4,24,1024]{2,1,0:T(8,128)(2,1)S(1)} %get-tuple-element.92), channel_id=1, source_target_pairs={{0,24},{4,28},{8,16},{12,20},{16,8},{20,12},{24,0},{28,4},{1,25},{... | collective-permute-start | bytes 589832 | tf_op jit(solution)/shard_map/ppermute | solution.py:602
  104.6 6.0 %collective-permute-start.17 = (bf16[24,1024]{1,0:T(8,128)(2,1)S(1)}, bf16[24,1024]{1,0:T(8,128)(2,1)S(1)}, u32[]{:S(2)}, u32[]{:S(2)}) collective-permute-start(bf16[24,1024]{1,0:T(8,128)(2,1)S(1)} %get-tuple-element.99), channel_id=1, source_target_pairs={{0,1},{1,2},{2,3},{3,0},{4,5},{5,6},{6,7},{7,4},{8,9},{9,10},{10,1... | collective-permute-start | bytes 147464 | tf_op jit(solution)/shard_map/ppermute | solution.py:610
  105.8 5.9 %collective-permute-start.18 = (bf16[24,1024]{1,0:T(8,128)(2,1)S(1)}, bf16[24,1024]{1,0:T(8,128)(2,1)S(1)}, u32[]{:S(2)}, u32[]{:S(2)}) collective-permute-start(bf16[24,1024]{1,0:T(8,128)(2,1)S(1)} %get-tuple-element.100), channel_id=1, source_target_pairs={{0,2},{1,3},{2,0},{3,1},{4,6},{5,7},{6,4},{7,5},{8,10},{9,11},{10,... | collective-permute-start | bytes 147464 | tf_op jit(solution)/shard_map/ppermute | solution.py:610
  107.1 4.6 %collective-permute-start.19 = (bf16[24,1024]{1,0:T(8,128)(2,1)S(1)}, bf16[24,1024]{1,0:T(8,128)(2,1)S(1)}, u32[]{:S(2)}, u32[]{:S(2)}) collective-permute-start(bf16[24,1024]{1,0:T(8,128)(2,1)S(1)} %get-tuple-element.101), channel_id=1, source_target_pairs={{0,3},{1,0},{2,1},{3,2},{4,7},{5,4},{6,5},{7,6},{8,11},{9,8},{10,9... | collective-permute-start | bytes 147464 | tf_op jit(solution)/shard_map/ppermute | solution.py:610
  111.8 5.9 %collective-permute-start.20 = (bf16[24,1024]{1,0:T(8,128)(2,1)S(1)}, bf16[24,1024]{1,0:T(8,128)(2,1)S(1)}, u32[]{:S(2)}, u32[]{:S(2)}) collective-permute-start(bf16[24,1024]{1,0:T(8,128)(2,1)S(1)} %sum_tensor.1), channel_id=1, source_target_pairs={{0,1},{1,2},{2,3},{3,0},{4,5},{5,6},{6,7},{7,4},{8,9},{9,10},{10,1... | collective-permute-start | bytes 147464 | tf_op jit(solution)/shard_map/ppermute | solution.py:610
  113.2 5.6 %collective-permute-start.21 = (bf16[24,1024]{1,0:T(8,128)(2,1)S(1)}, bf16[24,1024]{1,0:T(8,128)(2,1)S(1)}, u32[]{:S(2)}, u32[]{:S(2)}) collective-permute-start(bf16[24,1024]{1,0:T(8,128)(2,1)S(1)} %sum_tensor.1), channel_id=1, source_target_pairs={{0,2},{1,3},{2,0},{3,1},{4,6},{5,7},{6,4},{7,5},{8,10},{9,11},{10,... | collective-permute-start | bytes 147464 | tf_op jit(solution)/shard_map/ppermute | solution.py:610
  115.0 4.3 %collective-permute-start.22 = (bf16[24,1024]{1,0:T(8,128)(2,1)S(1)}, bf16[24,1024]{1,0:T(8,128)(2,1)S(1)}, u32[]{:S(2)}, u32[]{:S(2)}) collective-permute-start(bf16[24,1024]{1,0:T(8,128)(2,1)S(1)} %sum_tensor.1), channel_id=1, source_target_pairs={{0,3},{1,0},{2,1},{3,2},{4,7},{5,4},{6,5},{7,6},{8,11},{9,8},{10,9... | collective-permute-start | bytes 147464 | tf_op jit(solution)/shard_map/ppermute | solution.py:610
  119.3 5.7 %collective-permute-start.23 = (bf16[4,24,1024]{2,1,0:T(8,128)(2,1)S(1)}, bf16[4,24,1024]{2,1,0:T(8,128)(2,1)S(1)}, u32[]{:S(2)}, u32[]{:S(2)}) collective-permute-start(bf16[4,24,1024]{2,1,0:T(8,128)(2,1)S(1)} %pad_maximum_fusion.2.rest_0_), channel_id=1, source_target_pairs={{0,8},{4,12},{8,0},{12,4},{16,24},{20,28},{24,16},{28,20},{1,9},{5... | collective-permute-start | bytes 589832 | tf_op jit(solution)/shard_map/ppermute | solution.py:602
  120.8 7.8 %collective-permute-start.24 = (bf16[4,24,1024]{2,1,0:T(8,128)(2,1)S(1)}, bf16[4,24,1024]{2,1,0:T(8,128)(2,1)S(1)}, u32[]{:S(2)}, u32[]{:S(2)}) collective-permute-start(bf16[4,24,1024]{2,1,0:T(8,128)(2,1)S(1)} %pad_maximum_fusion.2.rest_0_), channel_id=1, source_target_pairs={{0,16},{4,20},{8,24},{12,28},{16,0},{20,4},{24,8},{28,12},{1,17},{... | collective-permute-start | bytes 589832 | tf_op jit(solution)/shard_map/ppermute | solution.py:602
  121.4 7.2 %collective-permute-start.25 = (bf16[4,24,1024]{2,1,0:T(8,128)(2,1)S(1)}, bf16[4,24,1024]{2,1,0:T(8,128)(2,1)S(1)}, u32[]{:S(2)}, u32[]{:S(2)}) collective-permute-start(bf16[4,24,1024]{2,1,0:T(8,128)(2,1)S(1)} %pad_maximum_fusion.2.rest_0_), channel_id=1, source_target_pairs={{0,24},{4,28},{8,16},{12,20},{16,8},{20,12},{24,0},{28,4},{1,25},{... | collective-permute-start | bytes 589832 | tf_op jit(solution)/shard_map/ppermute | solution.py:602
  123.0 6.3 %collective-permute-start.26 = (bf16[4,24,1024]{2,1,0:T(8,128)(2,1)S(1)}, bf16[4,24,1024]{2,1,0:T(8,128)(2,1)S(1)}, u32[]{:S(2)}, u32[]{:S(2)}) collective-permute-start(bf16[4,24,1024]{2,1,0:T(8,128)(2,1)S(1)} %pad_maximum_fusion.2.rest_0_), channel_id=1, source_target_pairs={{0,4},{4,0},{8,12},{12,8},{16,20},{20,16},{24,28},{28,24},{1,5},{5... | collective-permute-start | bytes 589832 | tf_op jit(solution)/shard_map/ppermute | solution.py:607
  125.1 4.2 %collective-permute-start.27 = (bf16[4,24,1024]{2,1,0:T(8,128)(2,1)S(1)}, bf16[4,24,1024]{2,1,0:T(8,128)(2,1)S(1)}, u32[]{:S(2)}, u32[]{:S(2)}) collective-permute-start(bf16[4,24,1024]{2,1,0:T(8,128)(2,1)S(1)} %collective-permute-done.23.rest_1_), channel_id=1, source_target_pairs={{0,4},{4,0},{8,12},{12,8},{16,20},{20,16},{24,28},{28,24},{1,5},{5... | collective-permute-start | bytes 589832 | tf_op jit(solution)/shard_map/ppermute | solution.py:607
  (18 other events, 90.5 us)

commit v10 on v9

--- a/solution.py
+++ b/solution.py
@@ -126,13 +126,13 @@
     queries.wait()
     for copy in own:
         copy.wait()
-    for copy in keys:
-        copy.start()
     q = q_s[...]
     heads = own_s.shape[2]
     a_s[:, slices * heads :] = dot(q, own_s[0], 1, 0).astype(BF16)
     for copy in gathered:
         copy.wait()
+    for copy in keys:
+        copy.start()
     for k in range(slices):
         a_s[:, k * heads : (k + 1) * heads] = dot(q, w_s[2 * k], 1, 0).astype(BF16)
     keys_weight = jnp.concatenate([w_s[2 * k + 1] for k in range(slices)] + [own_s[1]], axis=1)
@@ -312,15 +312,14 @@
         )
     ]
     first, second = first[:5], first[5:]
-    loads = [
-        [
-            pltpu.make_async_copy(
-                normed_in.at[pl.ds(b * rows, rows)], normed_s.at[pl.ds(b * rows, rows)], block_sem.at[2 * b]
-            ),
+
+    def loads(b):
+        part = pl.ds(pl.multiple_of(b * rows, rows), rows)
+        return (
+            pltpu.make_async_copy(normed_in.at[part], normed_s.at[part], block_sem.at[2 * b]),
             pltpu.make_async_copy(x_in.at[b], x_s.at[b], block_sem.at[2 * b + 1]),
-        ]
-        for b in range(blocks)
-    ]
+        )
+
     last = pltpu.make_async_copy(qs_in, qs_s, last_sem)
     for copy in first:
         copy.start()
@@ -332,10 +331,7 @@
         copy.wait()
     for copy in second:
         copy.start()
-    for pair in loads:
-        for copy in pair:
-            copy.start()
-    last.start()
+    loads(0)[0].start()
 
     spread = jnp.zeros((tokens, 1), F32)
     for r in range(count):
@@ -355,6 +351,10 @@
     total_eg = jnp.zeros((1, emb), F32)
     for copy in second:
         copy.wait()
+    loads(0)[1].start()
+    if blocks > 1:
+        for copy in loads(1):
+            copy.start()
     for b in range(0, total, thin):
         e = emb_s[b : b + thin]
         upstream = up_s[b : b + thin]
@@ -375,7 +375,17 @@
     def wide(b, _):
         base = pl.multiple_of(b * rows, rows)
         part = pl.ds(base, rows)
-        pltpu.make_async_copy(normed_in.at[part], normed_s.at[part], block_sem.at[2 * b]).wait()
+        loads(b)[0].wait()
+
+        @pl.when(b + 2 < blocks)
+        def _():
+            for copy in loads(b + 2):
+                copy.start()
+
+        @pl.when(b == blocks - 1)
+        def _():
+            last.start()
+
         for n in range(0, rows, sub):
             hg_s[n : n + sub] = dot(eg_s[pl.ds(base + n, sub)], wpt_ref[...], 1, 0)
             for c in range(n, n + sub, 16):
@@ -386,7 +396,7 @@
                     normed = normed_s[here, v : v + 128].astype(F32)
                     sg_s[here, v : v + 128] = (inverse * scaled - mean - normed * along).astype(BF16)
         pltpu.make_async_copy(sg_s.at[part], sg_out.at[part], out_sem.at[b]).start()
-        pltpu.make_async_copy(x_in.at[b], x_s.at[b], block_sem.at[2 * b + 1]).wait()
+        loads(b)[1].wait()
         wo_s[...] += dot(x_s[b], sg_s[part], 1, 0)
         nt_s[...] += dot(eg_s[part], normed_s[part], 0, 0)
         return 0

time: 134 us -> 133 us (level)
  no operation moved by 1% of the time
where the time goes in v10:
time: 133 us; the launch traced here: 132 us
  Pallas kernels  62.3 us (47%)
  starting transfers between devices  38.6 us (29%)
  waiting for transfers between devices  20.7 us (16%)
  local copies, waits for them, and re-layouts  6.3 us (5%)
  other arithmetic  3.08 us (2%)
    pallas_call x1, Pallas kernels, student_backward(): pl.pallas_call(functools.partial(backward_kernel, tokens, count, blocks),...  21.4 us
    ppermute x12, starting transfers between devices, shift_t(): return lax.ppermute(x, 'tensor', [(t, (t + k) % nt) for t in range(nt)])  20.6 us
    ppermute x9, starting transfers between devices, shift_chip(): lax.ppermute(x, 'dp', [(c * CORES + o, partner(c, k) * CORES + o) for c i...  12.6 us
    pallas_call x1, Pallas kernels, student_forward(): pl.pallas_call(forward_kernel, grid=(total // rows,), in_specs=[block(wid...  12.5 us
    pallas_call x1, Pallas kernels, teacher_maps(): pl.pallas_call(functools.partial(teacher_kernel, parts, count, tokens), i...  11.6 us
    pallas_call x1, Pallas kernels, context_grad(): pl.pallas_call(context_kernel, grid=(total // rows,), in_specs=[block, pl...  7.53 us
    ppermute x12, waiting for transfers between devices, shift_t(): return lax.ppermute(x, 'tensor', [(t, (t + k) % nt) for t in range(nt)])  6.96 us
    ppermute x9, waiting for transfers between devices, shift_chip(): lax.ppermute(x, 'dp', [(c * CORES + o, partner(c, k) * CORES + o) for c i...  6.16 us
  transfers between devices with their start and end apart: 31, of which 18 were waited for; matrix products, arithmetic and copies ran while one was open for 4% of the time, Pallas kernels for 19%

profile of v10, /device:TPU:0, one launch (start us, length us, event | category | flops | bytes accessed | tf_op | source)
XLA Modules:
  0.0 132.1 jit_solution(13958674546001885462)
XLA Ops:
  1.7 3.1 %collective-permute-start = (bf16[2,128,256]{2,1,0:T(8,128)(2,1)S(1)}, bf16[2,128,256]{2,1,0:T(8,128)(2,1)S(1)}, u32[]{:S(2)}, u32[]{:S(2)}) collective-permute-start(bf16[2,128,256]{2,1,0:T(8,128)(2,1)S(1)} %pad_maximum_fusion.3), channel_id=1, source_target_pairs={{0,1},{1,2},{2,3},{3,0},{4,5},{5,6},{6,7},{7,4},{8,9},{9,10},{10,1... | collective-permute-start | bytes 393224 | tf_op jit(solution)/shard_map/ppermute | solution.py:620
  4.7 2.6 %collective-permute-start.1 = (bf16[2,128,256]{2,1,0:T(8,128)(2,1)S(1)}, bf16[2,128,256]{2,1,0:T(8,128)(2,1)S(1)}, u32[]{:S(2)}, u32[]{:S(2)}) collective-permute-start(bf16[2,128,256]{2,1,0:T(8,128)(2,1)S(1)} %pad_maximum_fusion.3), channel_id=1, source_target_pairs={{0,2},{1,3},{2,0},{3,1},{4,6},{5,7},{6,4},{7,5},{8,10},{9,11},{10,... | collective-permute-start | bytes 393224 | tf_op jit(solution)/shard_map/ppermute | solution.py:620
  10.9 2.5 %collective-permute-start.3 = (bf16[1,128,256]{2,1,0:T(8,128)(2,1)S(1)}, bf16[1,128,256]{2,1,0:T(8,128)(2,1)S(1)}, u32[]{:S(2)}, u32[]{:S(2)}) collective-permute-start(bf16[1,128,256]{2,1,0:T(8,128)(2,1)S(1)} %pad_bitcast_fusion), channel_id=1, source_target_pairs={{0,24},{4,28},{8,16},{12,20},{16,8},{20,12},{24,0},{28,4},{1,25},{... | collective-permute-start | bytes 196616 | tf_op jit(solution)/shard_map/ppermute | solution.py:612
  14.0 1.7 %copy.20 = bf16[768,128]{0,1:T(8,128)(2,1)} copy(bf16[768,128]{1,0:T(8,128)(2,1)} %wp_ref.5) | data formatting | bytes 393216 | tf_op args[5]
  16.2 3.2 %collective-permute-start.6 = (bf16[2,128,256]{2,1,0:T(8,128)(2,1)S(1)}, bf16[2,128,256]{2,1,0:T(8,128)(2,1)S(1)}, u32[]{:S(2)}, u32[]{:S(2)}) collective-permute-start(bf16[2,128,256]{2,1,0:T(8,128)(2,1)S(1)} %pad_maximum_fusion.4), channel_id=1, source_target_pairs={{0,1},{1,2},{2,3},{3,0},{4,5},{5,6},{6,7},{7,4},{8,9},{9,10},{10,1... | collective-permute-start | bytes 393224 | tf_op jit(solution)/shard_map/ppermute | solution.py:620
  19.4 1.6 %collective-permute-start.7 = (bf16[2,128,256]{2,1,0:T(8,128)(2,1)S(1)}, bf16[2,128,256]{2,1,0:T(8,128)(2,1)S(1)}, u32[]{:S(2)}, u32[]{:S(2)}) collective-permute-start(bf16[2,128,256]{2,1,0:T(8,128)(2,1)S(1)} %pad_maximum_fusion.4), channel_id=1, source_target_pairs={{0,2},{1,3},{2,0},{3,1},{4,6},{5,7},{6,4},{7,5},{8,10},{9,11},{10,... | collective-permute-start | bytes 393224 | tf_op jit(solution)/shard_map/ppermute | solution.py:620
  21.8 1.5 %collective-permute-start.4 = (bf16[7,128,256]{2,1,0:T(8,128)(2,1)S(1)}, bf16[7,128,256]{2,1,0:T(8,128)(2,1)S(1)}, u32[]{:S(2)}, u32[]{:S(2)}) collective-permute-start(bf16[7,128,256]{2,1,0:T(8,128)(2,1)S(1)} %pad_maximum_fusion.rest_0_), channel_id=1, source_target_pairs={{0,8},{4,12},{8,0},{12,4},{16,24},{20,28},{24,16},{28,20},{1,9},{5... | collective-permute-start | bytes 1376264 | tf_op jit(solution)/shard_map/ppermute | solution.py:612
  23.3 1.5 %collective-permute-start.5 = (bf16[7,128,256]{2,1,0:T(8,128)(2,1)S(1)}, bf16[7,128,256]{2,1,0:T(8,128)(2,1)S(1)}, u32[]{:S(2)}, u32[]{:S(2)}) collective-permute-start(bf16[7,128,256]{2,1,0:T(8,128)(2,1)S(1)} %pad_maximum_fusion.rest_0_), channel_id=1, source_target_pairs={{0,16},{4,20},{8,24},{12,28},{16,0},{20,4},{24,8},{28,12},{1,17},{... | collective-permute-start | bytes 1376264 | tf_op jit(solution)/shard_map/ppermute | solution.py:612
  24.8 12.5 %student_forward.1 = (bf16[2880,768]{1,0:T(8,128)(2,1)}, f32[2880,128]{1,0:T(8,128)}, f32[2880,128]{1,0:T(8,128)}, bf16[4,768,720]{2,1,0:T(8,128)(2,1)}) custom-call(bf16[2880,768]{1,0:T(8,128)(2,1)} %bitcast.61, bf16[2880,768]{1,0:T(8,128)(2,1)} %bitcast.62, bf16[768,768]{1,0:T(8,128)(2,1)} %wo_ref.3, f32[6,128]{1,0:T(8,128)} %bitcast.65, ...), custom_call_target="tpu_custom_call" | custom-call | flops 3963617280 | bytes 17694720 | tf_op jit(solution)/shard_map/student_forward/pallas_call | solution.py:75
  42.8 11.6 %teacher_maps.1 = bf16[16,32,180]{2,1,0:T(8,128)(2,1)} custom-call(s32[8,2]{1,0:T(8,128)} %dynamic-slice_convert_fusion.order_ref, s32[8]{0:T(128)} %get-tuple-element.120.from_ref, s32[8]{0:T(128)} %get-tuple-element.121.rows_ref, bf16[3392,1024]{1,0:T(8,128)(2,1)} %bitcast.60, bf16[1024,256]{1,0:T(8,128)(2,1)} %wq_ref.1, bf16[1024,256]{1,0:T(8,128)(2,1)} %wk_ref.1, ...), custom_call_target="tpu_custom_call" | custom-call | flops 4294967296 | bytes 11141120 | tf_op jit(solution)/shard_map/teacher_maps/pallas_call | solution.py:177
  54.4 3.6 %all-to-all-start = ((bf16[16,32,180]{2,1,0:T(8,128)(2,1)}), bf16[16,32,180]{2,1,0:T(8,128)(2,1)S(1)}, u32[]{:S(2)}, u32[]{:S(2)}) async-start(bf16[16,32,180]{2,1,0:T(8,128)(2,1)} %teacher_maps.1), calls=%async_computation | async-start | bytes 524288 | tf_op jit(solution)/shard_map/all_to_all | solution.py:684
  58.0 5.1 %student_scores.1 = (f32[16,32,180]{2,1,0:T(8,128)}, f32[16,32,180]{2,1,0:T(8,128)}, bf16[16,180,128]{2,1,0:T(8,128)(2,1)}, bf16[8,32,128]{2,1,0:T(8,128)(2,1)},...) custom-call(s32[16]{0:T(128)} %get-tuple-element.108.qidx_ref, s32[16]{0:T(128)} %len_ref.3, ...), custom_call_target="tpu_custom_call" | custom-call | flops 1000000000 | bytes 1474560 | tf_op jit(solution)/shard_map/student_scores/pallas_call | solution.py:259
  63.1 1.6 %all-to-all-done.maps_in = bf16[16,32,180]{2,1,0:T(8,128)(2,1)S(1)} async-done(((bf16[16,32,180]{2,1,0:T(8,128)(2,1)}), bf16[16,32,180]{2,1,0:T(8,128)(2,1)S(1)}, u32[]{:S(2)}, u32[]{:S(2)}) %all-to-all-start) | async-done | bytes 184352 | tf_op jit(solution)/shard_map/all_to_all | solution.py:684
  65.4 21.4 %student_backward.1 = (bf16[2880,768]{1,0:T(8,128)(2,1)}, bf16[16,24,1024]{2,1,0:T(8,128)(2,1)}, bf16[16,24,1024]{2,1,0:T(8,128)(2,1)}) custom-call(s32[16]{0:T(128)} %get-tuple-element.108.qidx_ref, s32[16]{0:T(128)} %copy-done.10, s32[16]{0:T(128)} %len_ref.3, s32[1]{0:T(128)} %bitcast.core_ref, bf16[16,32,180]{2,1,0:T(8,128)(2,1)} %copy-done.9, ...), custom_call_target="tpu_custom_call" | custom-call | flops 4529848320 | bytes 17694720 | tf_op jit(solution)/shard_map/student_backward/pallas_call | solution.py:448
  87.0 2.5 %collective-permute-done.13.rest_1_ = bf16[16,24,1024]{2,1,0:T(8,128)(2,1)S(1)} collective-permute-done((bf16[16,24,1024]{2,1,0:T(8,128)(2,1)}, bf16[16,24,1024]{2,1,0:T(8,128)(2,1)S(1)}, u32[]{:S(2)}, u32[]{:S(2)}) %collective-permute-start.13) | collective-permute-done | bytes 786464 | tf_op jit(solution)/shard_map/ppermute | solution.py:617
  93.3 1.9 %collective-permute-start.16 = (bf16[4,24,1024]{2,1,0:T(8,128)(2,1)S(1)}, bf16[4,24,1024]{2,1,0:T(8,128)(2,1)S(1)}, u32[]{:S(2)}, u32[]{:S(2)}) collective-permute-start(bf16[4,24,1024]{2,1,0:T(8,128)(2,1)S(1)} %get-tuple-element.92), channel_id=1, source_target_pairs={{0,24},{4,28},{8,16},{12,20},{16,8},{20,12},{24,0},{28,4},{1,25},{... | collective-permute-start | bytes 589832 | tf_op jit(solution)/shard_map/ppermute | solution.py:612
  95.1 7.5 %context_grad.1 = bf16[2880,768]{1,0:T(8,128)(2,1)} custom-call(bf16[2880,768]{1,0:T(8,128)(2,1)} %get-tuple-element.93.sg_ref, bf16[768,768]{1,0:T(8,128)(2,1)} %wo_ref.3), custom_call_target="tpu_custom_call" | custom-call | flops 3397386240 | bytes 8847360 | tf_op jit(solution)/shard_map/context_grad/pallas_call | solution.py:485
  107.7 2.2 %collective-permute-done.17.refs_1_ = bf16[24,1024]{1,0:T(8,128)(2,1)S(1)} collective-permute-done((bf16[24,1024]{1,0:T(8,128)(2,1)S(1)}, bf16[24,1024]{1,0:T(8,128)(2,1)S(1)}, u32[]{:S(2)}, u32[]{:S(2)}) %collective-permute-start.17) | collective-permute-done | bytes 49184 | tf_op jit(solution)/shard_map/ppermute | solution.py:620
  112.4 1.8 %collective-permute-start.21 = (bf16[24,1024]{1,0:T(8,128)(2,1)S(1)}, bf16[24,1024]{1,0:T(8,128)(2,1)S(1)}, u32[]{:S(2)}, u32[]{:S(2)}) collective-permute-start(bf16[24,1024]{1,0:T(8,128)(2,1)S(1)} %sum_tensor.1), channel_id=1, source_target_pairs={{0,2},{1,3},{2,0},{3,1},{4,6},{5,7},{6,4},{7,5},{8,10},{9,11},{10,... | collective-permute-start | bytes 147464 | tf_op jit(solution)/shard_map/ppermute | solution.py:620
  115.1 1.9 %collective-permute-done.20 = bf16[24,1024]{1,0:T(8,128)(2,1)S(1)} collective-permute-done((bf16[24,1024]{1,0:T(8,128)(2,1)S(1)}, bf16[24,1024]{1,0:T(8,128)(2,1)S(1)}, u32[]{:S(2)}, u32[]{:S(2)}) %collective-permute-start.20) | collective-permute-done | bytes 49184 | tf_op jit(solution)/shard_map/ppermute | solution.py:620
  118.6 1.5 %collective-permute-start.23 = (bf16[4,24,1024]{2,1,0:T(8,128)(2,1)S(1)}, bf16[4,24,1024]{2,1,0:T(8,128)(2,1)S(1)}, u32[]{:S(2)}, u32[]{:S(2)}) collective-permute-start(bf16[4,24,1024]{2,1,0:T(8,128)(2,1)S(1)} %pad_maximum_fusion.2.rest_0_), channel_id=1, source_target_pairs={{0,8},{4,12},{8,0},{12,4},{16,24},{20,28},{24,16},{28,20},{1,9},{5... | collective-permute-start | bytes 589832 | tf_op jit(solution)/shard_map/ppermute | solution.py:612
  122.2 2.1 %collective-permute-done.23.rest_1_ = bf16[4,24,1024]{2,1,0:T(8,128)(2,1)S(1)} collective-permute-done((bf16[4,24,1024]{2,1,0:T(8,128)(2,1)S(1)}, bf16[4,24,1024]{2,1,0:T(8,128)(2,1)S(1)}, u32[]{:S(2)}, u32[]{:S(2)}) %collective-permute-start.23) | collective-permute-done | bytes 196640 | tf_op jit(solution)/shard_map/ppermute | solution.py:612
  124.3 3.5 %collective-permute-done.24.rest_2_ = bf16[4,24,1024]{2,1,0:T(8,128)(2,1)S(1)} collective-permute-done((bf16[4,24,1024]{2,1,0:T(8,128)(2,1)S(1)}, bf16[4,24,1024]{2,1,0:T(8,128)(2,1)S(1)}, u32[]{:S(2)}, u32[]{:S(2)}) %collective-permute-start.24) | collective-permute-done | bytes 196640 | tf_op jit(solution)/shard_map/ppermute | solution.py:612
  129.6 2.3 %unpack.1 = (f32[32,24,768]{2,1,0:T(8,128)}, f32[32,24,128]{2,1,0:T(8,128)}, f32[6,128]{1,0:T(8,128)}, f32[6,128]{1,0:T(8,128)}, f32[1]{0:T(128)}) custom-call(s32[32]{0:T(128)S(1)} %add.124.index_ref, bf16[4,24,1024]{2,1,0:T(8,128)(2,1)S(1)} %pad_maximum_fusion.2.rest_0_, bf16[4,24,1024]{2,1,0:T(8,128)(2,1)S(1)} %collective-permute-done.23.rest_1_, ...), custom_call_target="tpu_custom_call" | custom-call | tf_op jit(solution)/shard_map/unpack/pallas_call | solution.py:563
  (112 shorter events, 30.1 us)
Async XLA Ops:
  1.7 14.1 %collective-permute-start = (bf16[2,128,256]{2,1,0:T(8,128)(2,1)S(1)}, bf16[2,128,256]{2,1,0:T(8,128)(2,1)S(1)}, u32[]{:S(2)}, u32[]{:S(2)}) collective-permute-start(bf16[2,128,256]{2,1,0:T(8,128)(2,1)S(1)} %pad_maximum_fusion.3), channel_id=1, source_target_pairs={{0,1},{1,2},{2,3},{3,0},{4,5},{5,6},{6,7},{7,4},{8,9},{9,10},{10,1... | collective-permute-start | bytes 393224 | tf_op jit(solution)/shard_map/ppermute | solution.py:620
  4.7 11.2 %collective-permute-start.1 = (bf16[2,128,256]{2,1,0:T(8,128)(2,1)S(1)}, bf16[2,128,256]{2,1,0:T(8,128)(2,1)S(1)}, u32[]{:S(2)}, u32[]{:S(2)}) collective-permute-start(bf16[2,128,256]{2,1,0:T(8,128)(2,1)S(1)} %pad_maximum_fusion.3), channel_id=1, source_target_pairs={{0,2},{1,3},{2,0},{3,1},{4,6},{5,7},{6,4},{7,5},{8,10},{9,11},{10,... | collective-permute-start | bytes 393224 | tf_op jit(solution)/shard_map/ppermute | solution.py:620
  7.3 8.6 %collective-permute-start.2 = (bf16[2,128,256]{2,1,0:T(8,128)(2,1)S(1)}, bf16[2,128,256]{2,1,0:T(8,128)(2,1)S(1)}, u32[]{:S(2)}, u32[]{:S(2)}) collective-permute-start(bf16[2,128,256]{2,1,0:T(8,128)(2,1)S(1)} %pad_maximum_fusion.3), channel_id=1, source_target_pairs={{0,3},{1,0},{2,1},{3,2},{4,7},{5,4},{6,5},{7,6},{8,11},{9,8},{10,9... | collective-permute-start | bytes 393224 | tf_op jit(solution)/shard_map/ppermute | solution.py:620
  10.9 5.2 %collective-permute-start.3 = (bf16[1,128,256]{2,1,0:T(8,128)(2,1)S(1)}, bf16[1,128,256]{2,1,0:T(8,128)(2,1)S(1)}, u32[]{:S(2)}, u32[]{:S(2)}) collective-permute-start(bf16[1,128,256]{2,1,0:T(8,128)(2,1)S(1)} %pad_bitcast_fusion), channel_id=1, source_target_pairs={{0,24},{4,28},{8,16},{12,20},{16,8},{20,12},{24,0},{28,4},{1,25},{... | collective-permute-start | bytes 196616 | tf_op jit(solution)/shard_map/ppermute | solution.py:612
  16.2 21.3 %collective-permute-start.6 = (bf16[2,128,256]{2,1,0:T(8,128)(2,1)S(1)}, bf16[2,128,256]{2,1,0:T(8,128)(2,1)S(1)}, u32[]{:S(2)}, u32[]{:S(2)}) collective-permute-start(bf16[2,128,256]{2,1,0:T(8,128)(2,1)S(1)} %pad_maximum_fusion.4), channel_id=1, source_target_pairs={{0,1},{1,2},{2,3},{3,0},{4,5},{5,6},{6,7},{7,4},{8,9},{9,10},{10,1... | collective-permute-start | bytes 393224 | tf_op jit(solution)/shard_map/ppermute | solution.py:620
  19.4 18.1 %collective-permute-start.7 = (bf16[2,128,256]{2,1,0:T(8,128)(2,1)S(1)}, bf16[2,128,256]{2,1,0:T(8,128)(2,1)S(1)}, u32[]{:S(2)}, u32[]{:S(2)}) collective-permute-start(bf16[2,128,256]{2,1,0:T(8,128)(2,1)S(1)} %pad_maximum_fusion.4), channel_id=1, source_target_pairs={{0,2},{1,3},{2,0},{3,1},{4,6},{5,7},{6,4},{7,5},{8,10},{9,11},{10,... | collective-permute-start | bytes 393224 | tf_op jit(solution)/shard_map/ppermute | solution.py:620
  21.0 16.5 %collective-permute-start.8 = (bf16[2,128,256]{2,1,0:T(8,128)(2,1)S(1)}, bf16[2,128,256]{2,1,0:T(8,128)(2,1)S(1)}, u32[]{:S(2)}, u32[]{:S(2)}) collective-permute-start(bf16[2,128,256]{2,1,0:T(8,128)(2,1)S(1)} %pad_maximum_fusion.4), channel_id=1, source_target_pairs={{0,3},{1,0},{2,1},{3,2},{4,7},{5,4},{6,5},{7,6},{8,11},{9,8},{10,9... | collective-permute-start | bytes 393224 | tf_op jit(solution)/shard_map/ppermute | solution.py:620
  21.8 15.8 %collective-permute-start.4 = (bf16[7,128,256]{2,1,0:T(8,128)(2,1)S(1)}, bf16[7,128,256]{2,1,0:T(8,128)(2,1)S(1)}, u32[]{:S(2)}, u32[]{:S(2)}) collective-permute-start(bf16[7,128,256]{2,1,0:T(8,128)(2,1)S(1)} %pad_maximum_fusion.rest_0_), channel_id=1, source_target_pairs={{0,8},{4,12},{8,0},{12,4},{16,24},{20,28},{24,16},{28,20},{1,9},{5... | collective-permute-start | bytes 1376264 | tf_op jit(solution)/shard_map/ppermute | solution.py:612
  23.3 14.3 %collective-permute-start.5 = (bf16[7,128,256]{2,1,0:T(8,128)(2,1)S(1)}, bf16[7,128,256]{2,1,0:T(8,128)(2,1)S(1)}, u32[]{:S(2)}, u32[]{:S(2)}) collective-permute-start(bf16[7,128,256]{2,1,0:T(8,128)(2,1)S(1)} %pad_maximum_fusion.rest_0_), channel_id=1, source_target_pairs={{0,16},{4,20},{8,24},{12,28},{16,0},{20,4},{24,8},{28,12},{1,17},{... | collective-permute-start | bytes 1376264 | tf_op jit(solution)/shard_map/ppermute | solution.py:612
  54.4 10.3 %all-to-all-start = ((bf16[16,32,180]{2,1,0:T(8,128)(2,1)}), bf16[16,32,180]{2,1,0:T(8,128)(2,1)S(1)}, u32[]{:S(2)}, u32[]{:S(2)}) async-start(bf16[16,32,180]{2,1,0:T(8,128)(2,1)} %teacher_maps.1), calls=%async_computation | async-start | bytes 524288 | tf_op jit(solution)/shard_map/all_to_all | solution.py:684
  91.6 11.1 %collective-permute-start.14 = (bf16[4,24,1024]{2,1,0:T(8,128)(2,1)S(1)}, bf16[4,24,1024]{2,1,0:T(8,128)(2,1)S(1)}, u32[]{:S(2)}, u32[]{:S(2)}) collective-permute-start(bf16[4,24,1024]{2,1,0:T(8,128)(2,1)S(1)} %get-tuple-element.90), channel_id=1, source_target_pairs={{0,8},{4,12},{8,0},{12,4},{16,24},{20,28},{24,16},{28,20},{1,9},{5... | collective-permute-start | bytes 589832 | tf_op jit(solution)/shard_map/ppermute | solution.py:612
  92.2 10.9 %collective-permute-start.15 = (bf16[4,24,1024]{2,1,0:T(8,128)(2,1)S(1)}, bf16[4,24,1024]{2,1,0:T(8,128)(2,1)S(1)}, u32[]{:S(2)}, u32[]{:S(2)}) collective-permute-start(bf16[4,24,1024]{2,1,0:T(8,128)(2,1)S(1)} %get-tuple-element.91), channel_id=1, source_target_pairs={{0,16},{4,20},{8,24},{12,28},{16,0},{20,4},{24,8},{28,12},{1,17},{... | collective-permute-start | bytes 589832 | tf_op jit(solution)/shard_map/ppermute | solution.py:612
  93.3 9.8 %collective-permute-start.16 = (bf16[4,24,1024]{2,1,0:T(8,128)(2,1)S(1)}, bf16[4,24,1024]{2,1,0:T(8,128)(2,1)S(1)}, u32[]{:S(2)}, u32[]{:S(2)}) collective-permute-start(bf16[4,24,1024]{2,1,0:T(8,128)(2,1)S(1)} %get-tuple-element.92), channel_id=1, source_target_pairs={{0,24},{4,28},{8,16},{12,20},{16,8},{20,12},{24,0},{28,4},{1,25},{... | collective-permute-start | bytes 589832 | tf_op jit(solution)/shard_map/ppermute | solution.py:612
  103.8 6.0 %collective-permute-start.17 = (bf16[24,1024]{1,0:T(8,128)(2,1)S(1)}, bf16[24,1024]{1,0:T(8,128)(2,1)S(1)}, u32[]{:S(2)}, u32[]{:S(2)}) collective-permute-start(bf16[24,1024]{1,0:T(8,128)(2,1)S(1)} %get-tuple-element.99), channel_id=1, source_target_pairs={{0,1},{1,2},{2,3},{3,0},{4,5},{5,6},{6,7},{7,4},{8,9},{9,10},{10,1... | collective-permute-start | bytes 147464 | tf_op jit(solution)/shard_map/ppermute | solution.py:620
  105.1 5.9 %collective-permute-start.18 = (bf16[24,1024]{1,0:T(8,128)(2,1)S(1)}, bf16[24,1024]{1,0:T(8,128)(2,1)S(1)}, u32[]{:S(2)}, u32[]{:S(2)}) collective-permute-start(bf16[24,1024]{1,0:T(8,128)(2,1)S(1)} %get-tuple-element.100), channel_id=1, source_target_pairs={{0,2},{1,3},{2,0},{3,1},{4,6},{5,7},{6,4},{7,5},{8,10},{9,11},{10,... | collective-permute-start | bytes 147464 | tf_op jit(solution)/shard_map/ppermute | solution.py:620
  106.4 4.6 %collective-permute-start.19 = (bf16[24,1024]{1,0:T(8,128)(2,1)S(1)}, bf16[24,1024]{1,0:T(8,128)(2,1)S(1)}, u32[]{:S(2)}, u32[]{:S(2)}) collective-permute-start(bf16[24,1024]{1,0:T(8,128)(2,1)S(1)} %get-tuple-element.101), channel_id=1, source_target_pairs={{0,3},{1,0},{2,1},{3,2},{4,7},{5,4},{6,5},{7,6},{8,11},{9,8},{10,9... | collective-permute-start | bytes 147464 | tf_op jit(solution)/shard_map/ppermute | solution.py:620
  111.0 5.9 %collective-permute-start.20 = (bf16[24,1024]{1,0:T(8,128)(2,1)S(1)}, bf16[24,1024]{1,0:T(8,128)(2,1)S(1)}, u32[]{:S(2)}, u32[]{:S(2)}) collective-permute-start(bf16[24,1024]{1,0:T(8,128)(2,1)S(1)} %sum_tensor.1), channel_id=1, source_target_pairs={{0,1},{1,2},{2,3},{3,0},{4,5},{5,6},{6,7},{7,4},{8,9},{9,10},{10,1... | collective-permute-start | bytes 147464 | tf_op jit(solution)/shard_map/ppermute | solution.py:620
  112.4 5.6 %collective-permute-start.21 = (bf16[24,1024]{1,0:T(8,128)(2,1)S(1)}, bf16[24,1024]{1,0:T(8,128)(2,1)S(1)}, u32[]{:S(2)}, u32[]{:S(2)}) collective-permute-start(bf16[24,1024]{1,0:T(8,128)(2,1)S(1)} %sum_tensor.1), channel_id=1, source_target_pairs={{0,2},{1,3},{2,0},{3,1},{4,6},{5,7},{6,4},{7,5},{8,10},{9,11},{10,... | collective-permute-start | bytes 147464 | tf_op jit(solution)/shard_map/ppermute | solution.py:620
  114.2 4.3 %collective-permute-start.22 = (bf16[24,1024]{1,0:T(8,128)(2,1)S(1)}, bf16[24,1024]{1,0:T(8,128)(2,1)S(1)}, u32[]{:S(2)}, u32[]{:S(2)}) collective-permute-start(bf16[24,1024]{1,0:T(8,128)(2,1)S(1)} %sum_tensor.1), channel_id=1, source_target_pairs={{0,3},{1,0},{2,1},{3,2},{4,7},{5,4},{6,5},{7,6},{8,11},{9,8},{10,9... | collective-permute-start | bytes 147464 | tf_op jit(solution)/shard_map/ppermute | solution.py:620
  118.6 5.7 %collective-permute-start.23 = (bf16[4,24,1024]{2,1,0:T(8,128)(2,1)S(1)}, bf16[4,24,1024]{2,1,0:T(8,128)(2,1)S(1)}, u32[]{:S(2)}, u32[]{:S(2)}) collective-permute-start(bf16[4,24,1024]{2,1,0:T(8,128)(2,1)S(1)} %pad_maximum_fusion.2.rest_0_), channel_id=1, source_target_pairs={{0,8},{4,12},{8,0},{12,4},{16,24},{20,28},{24,16},{28,20},{1,9},{5... | collective-permute-start | bytes 589832 | tf_op jit(solution)/shard_map/ppermute | solution.py:612
  120.1 7.8 %collective-permute-start.24 = (bf16[4,24,1024]{2,1,0:T(8,128)(2,1)S(1)}, bf16[4,24,1024]{2,1,0:T(8,128)(2,1)S(1)}, u32[]{:S(2)}, u32[]{:S(2)}) collective-permute-start(bf16[4,24,1024]{2,1,0:T(8,128)(2,1)S(1)} %pad_maximum_fusion.2.rest_0_), channel_id=1, source_target_pairs={{0,16},{4,20},{8,24},{12,28},{16,0},{20,4},{24,8},{28,12},{1,17},{... | collective-permute-start | bytes 589832 | tf_op jit(solution)/shard_map/ppermute | solution.py:612
  120.7 7.2 %collective-permute-start.25 = (bf16[4,24,1024]{2,1,0:T(8,128)(2,1)S(1)}, bf16[4,24,1024]{2,1,0:T(8,128)(2,1)S(1)}, u32[]{:S(2)}, u32[]{:S(2)}) collective-permute-start(bf16[4,24,1024]{2,1,0:T(8,128)(2,1)S(1)} %pad_maximum_fusion.2.rest_0_), channel_id=1, source_target_pairs={{0,24},{4,28},{8,16},{12,20},{16,8},{20,12},{24,0},{28,4},{1,25},{... | collective-permute-start | bytes 589832 | tf_op jit(solution)/shard_map/ppermute | solution.py:612
  122.2 6.3 %collective-permute-start.26 = (bf16[4,24,1024]{2,1,0:T(8,128)(2,1)S(1)}, bf16[4,24,1024]{2,1,0:T(8,128)(2,1)S(1)}, u32[]{:S(2)}, u32[]{:S(2)}) collective-permute-start(bf16[4,24,1024]{2,1,0:T(8,128)(2,1)S(1)} %pad_maximum_fusion.2.rest_0_), channel_id=1, source_target_pairs={{0,4},{4,0},{8,12},{12,8},{16,20},{20,16},{24,28},{28,24},{1,5},{5... | collective-permute-start | bytes 589832 | tf_op jit(solution)/shard_map/ppermute | solution.py:617
  124.3 4.2 %collective-permute-start.27 = (bf16[4,24,1024]{2,1,0:T(8,128)(2,1)S(1)}, bf16[4,24,1024]{2,1,0:T(8,128)(2,1)S(1)}, u32[]{:S(2)}, u32[]{:S(2)}) collective-permute-start(bf16[4,24,1024]{2,1,0:T(8,128)(2,1)S(1)} %collective-permute-done.23.rest_1_), channel_id=1, source_target_pairs={{0,4},{4,0},{8,12},{12,8},{16,20},{20,16},{24,28},{28,24},{1,5},{5... | collective-permute-start | bytes 589832 | tf_op jit(solution)/shard_map/ppermute | solution.py:617
  (18 other events, 90.5 us)

commit v11 on v10

--- a/solution.py
+++ b/solution.py
@@ -14,6 +14,7 @@
 CORES = 2
 VMEM_LIMIT = 56 * 1024 * 1024
 SMALL_LIMIT = 14 * 1024 * 1024
+TEACHER_LIMIT = 50 * 1024 * 1024
 
 F32 = jnp.float32
 BF16 = jnp.bfloat16
@@ -193,7 +194,7 @@
             pltpu.SemaphoreType.DMA((parts,)),
             pltpu.SemaphoreType.DMA((2,)),
         ],
-        compiler_params=params(),
+        compiler_params=pltpu.CompilerParams(vmem_limit_bytes=TEACHER_LIMIT),
         cost_estimate=cost(8 * count * tokens * depth * depth, 2 * states.size + 4 * depth * depth),
         name="teacher_maps",
     )(order, source, rows, states, wq, wk, *pieces)

time: 133 us -> 132 us (level)
    unnamed x23 -> x25, local copies, waits for them, and re-layouts: 4.39 us -> 5.42 us
  transfers between devices with their start and end apart: 31 -> 31, of which waited for: 18 -> 18; matrix products, arithmetic and copies ran while one was open for 4% -> 3% of each run, Pallas kernels for 19% -> 19%
where the time goes in v11:
time: 132 us
  Pallas kernels  61.3 us (46%)
  starting transfers between devices  38.6 us (29%)
  waiting for transfers between devices  21.1 us (16%)
  local copies, waits for them, and re-layouts  7.32 us (6%)
  other arithmetic  2 us (2%)
    pallas_call x1, Pallas kernels, student_backward(): pl.pallas_call(functools.partial(backward_kernel, tokens, count, blocks),...  21.4 us
    ppermute x12, starting transfers between devices, shift_t(): return lax.ppermute(x, 'tensor', [(t, (t + k) % nt) for t in range(nt)])  20.6 us
    ppermute x9, starting transfers between devices, shift_chip(): lax.ppermute(x, 'dp', [(c * CORES + o, partner(c, k) * CORES + o) for c i...  12.6 us
    pallas_call x1, Pallas kernels, student_forward(): pl.pallas_call(forward_kernel, grid=(total // rows,), in_specs=[block(wid...  12.5 us
    pallas_call x1, Pallas kernels, teacher_maps(): pl.pallas_call(functools.partial(teacher_kernel, parts, count, tokens), i...  10.6 us
    pallas_call x1, Pallas kernels, context_grad(): pl.pallas_call(context_kernel, grid=(total // rows,), in_specs=[block, pl...  7.53 us
    ppermute x12, waiting for transfers between devices, shift_t(): return lax.ppermute(x, 'tensor', [(t, (t + k) % nt) for t in range(nt)])  7.43 us
    ppermute x9, waiting for transfers between devices, shift_chip(): lax.ppermute(x, 'dp', [(c * CORES + o, partner(c, k) * CORES + o) for c i...  6.16 us
  transfers between devices with their start and end apart: 31, of which 18 were waited for; matrix products, arithmetic and copies ran while one was open for 3% of the time, Pallas kernels for 19%

profile of v11, /device:TPU:0, one launch (start us, length us, event | category | flops | bytes accessed | tf_op | source)
XLA Modules:
  0.0 131.5 jit_solution(11275735305586811843)
XLA Ops:
  1.7 3.1 %collective-permute-start = (bf16[2,128,256]{2,1,0:T(8,128)(2,1)S(1)}, bf16[2,128,256]{2,1,0:T(8,128)(2,1)S(1)}, u32[]{:S(2)}, u32[]{:S(2)}) collective-permute-start(bf16[2,128,256]{2,1,0:T(8,128)(2,1)S(1)} %pad_maximum_fusion.3), channel_id=1, source_target_pairs={{0,1},{1,2},{2,3},{3,0},{4,5},{5,6},{6,7},{7,4},{8,9},{9,10},{10,1... | collective-permute-start | bytes 393224 | tf_op jit(solution)/shard_map/ppermute | solution.py:621
  4.7 2.6 %collective-permute-start.1 = (bf16[2,128,256]{2,1,0:T(8,128)(2,1)S(1)}, bf16[2,128,256]{2,1,0:T(8,128)(2,1)S(1)}, u32[]{:S(2)}, u32[]{:S(2)}) collective-permute-start(bf16[2,128,256]{2,1,0:T(8,128)(2,1)S(1)} %pad_maximum_fusion.3), channel_id=1, source_target_pairs={{0,2},{1,3},{2,0},{3,1},{4,6},{5,7},{6,4},{7,5},{8,10},{9,11},{10,... | collective-permute-start | bytes 393224 | tf_op jit(solution)/shard_map/ppermute | solution.py:621
  10.9 2.5 %collective-permute-start.3 = (bf16[1,128,256]{2,1,0:T(8,128)(2,1)S(1)}, bf16[1,128,256]{2,1,0:T(8,128)(2,1)S(1)}, u32[]{:S(2)}, u32[]{:S(2)}) collective-permute-start(bf16[1,128,256]{2,1,0:T(8,128)(2,1)S(1)} %pad_bitcast_fusion), channel_id=1, source_target_pairs={{0,24},{4,28},{8,16},{12,20},{16,8},{20,12},{24,0},{28,4},{1,25},{... | collective-permute-start | bytes 196616 | tf_op jit(solution)/shard_map/ppermute | solution.py:613
  13.5 1.7 %copy.20 = bf16[768,128]{0,1:T(8,128)(2,1)} copy(bf16[768,128]{1,0:T(8,128)(2,1)} %wp_ref.5) | data formatting | bytes 393216 | tf_op args[5]
  16.2 3.2 %collective-permute-start.6 = (bf16[2,128,256]{2,1,0:T(8,128)(2,1)S(1)}, bf16[2,128,256]{2,1,0:T(8,128)(2,1)S(1)}, u32[]{:S(2)}, u32[]{:S(2)}) collective-permute-start(bf16[2,128,256]{2,1,0:T(8,128)(2,1)S(1)} %pad_maximum_fusion.4), channel_id=1, source_target_pairs={{0,1},{1,2},{2,3},{3,0},{4,5},{5,6},{6,7},{7,4},{8,9},{9,10},{10,1... | collective-permute-start | bytes 393224 | tf_op jit(solution)/shard_map/ppermute | solution.py:621
  19.4 1.6 %collective-permute-start.7 = (bf16[2,128,256]{2,1,0:T(8,128)(2,1)S(1)}, bf16[2,128,256]{2,1,0:T(8,128)(2,1)S(1)}, u32[]{:S(2)}, u32[]{:S(2)}) collective-permute-start(bf16[2,128,256]{2,1,0:T(8,128)(2,1)S(1)} %pad_maximum_fusion.4), channel_id=1, source_target_pairs={{0,2},{1,3},{2,0},{3,1},{4,6},{5,7},{6,4},{7,5},{8,10},{9,11},{10,... | collective-permute-start | bytes 393224 | tf_op jit(solution)/shard_map/ppermute | solution.py:621
  21.8 1.5 %collective-permute-start.4 = (bf16[7,128,256]{2,1,0:T(8,128)(2,1)S(1)}, bf16[7,128,256]{2,1,0:T(8,128)(2,1)S(1)}, u32[]{:S(2)}, u32[]{:S(2)}) collective-permute-start(bf16[7,128,256]{2,1,0:T(8,128)(2,1)S(1)} %pad_maximum_fusion.rest_0_), channel_id=1, source_target_pairs={{0,8},{4,12},{8,0},{12,4},{16,24},{20,28},{24,16},{28,20},{1,9},{5... | collective-permute-start | bytes 1376264 | tf_op jit(solution)/shard_map/ppermute | solution.py:613
  23.3 1.5 %collective-permute-start.5 = (bf16[7,128,256]{2,1,0:T(8,128)(2,1)S(1)}, bf16[7,128,256]{2,1,0:T(8,128)(2,1)S(1)}, u32[]{:S(2)}, u32[]{:S(2)}) collective-permute-start(bf16[7,128,256]{2,1,0:T(8,128)(2,1)S(1)} %pad_maximum_fusion.rest_0_), channel_id=1, source_target_pairs={{0,16},{4,20},{8,24},{12,28},{16,0},{20,4},{24,8},{28,12},{1,17},{... | collective-permute-start | bytes 1376264 | tf_op jit(solution)/shard_map/ppermute | solution.py:613
  24.8 12.5 %student_forward.1 = (bf16[2880,768]{1,0:T(8,128)(2,1)}, f32[2880,128]{1,0:T(8,128)}, f32[2880,128]{1,0:T(8,128)}, bf16[4,768,720]{2,1,0:T(8,128)(2,1)}) custom-call(bf16[2880,768]{1,0:T(8,128)(2,1)} %bitcast.61, bf16[2880,768]{1,0:T(8,128)(2,1)} %bitcast.62, bf16[768,768]{1,0:T(8,128)(2,1)} %wo_ref.3, f32[6,128]{1,0:T(8,128)} %bitcast.65, ...), custom_call_target="tpu_custom_call" | custom-call | flops 3963617280 | bytes 17694720 | tf_op jit(solution)/shard_map/student_forward/pallas_call | solution.py:76
  43.2 10.6 %teacher_maps.1 = bf16[16,32,180]{2,1,0:T(8,128)(2,1)} custom-call(s32[8,2]{1,0:T(8,128)S(1)} %dynamic-slice_convert_fusion.order_ref, s32[8]{0:T(128)S(1)} %get-tuple-element.120.from_ref, s32[8]{0:T(128)S(1)} %get-tuple-element.121.rows_ref, bf16[3392,1024]{1,0:T(8,128)(2,1)} %bitcast.60, bf16[1024,256]{1,0:T(8,128)(2,1)} %wq_ref.1, ...), custom_call_target="tpu_custom_call" | custom-call | flops 4294967296 | bytes 11141120 | tf_op jit(solution)/shard_map/teacher_maps/pallas_call | solution.py:178
  53.9 3.6 %all-to-all-start = ((bf16[16,32,180]{2,1,0:T(8,128)(2,1)}), bf16[16,32,180]{2,1,0:T(8,128)(2,1)S(1)}, u32[]{:S(2)}, u32[]{:S(2)}) async-start(bf16[16,32,180]{2,1,0:T(8,128)(2,1)} %teacher_maps.1), calls=%async_computation | async-start | bytes 524288 | tf_op jit(solution)/shard_map/all_to_all | solution.py:685
  57.5 5.1 %student_scores.1 = (f32[16,32,180]{2,1,0:T(8,128)}, f32[16,32,180]{2,1,0:T(8,128)}, bf16[16,180,128]{2,1,0:T(8,128)(2,1)}, bf16[8,32,128]{2,1,0:T(8,128)(2,1)},...) custom-call(s32[16]{0:T(128)} %get-tuple-element.108.qidx_ref, s32[16]{0:T(128)} %len_ref.3, ...), custom_call_target="tpu_custom_call" | custom-call | flops 1000000000 | bytes 1474560 | tf_op jit(solution)/shard_map/student_scores/pallas_call | solution.py:260
  62.6 1.6 %all-to-all-done.maps_in = bf16[16,32,180]{2,1,0:T(8,128)(2,1)S(1)} async-done(((bf16[16,32,180]{2,1,0:T(8,128)(2,1)}), bf16[16,32,180]{2,1,0:T(8,128)(2,1)S(1)}, u32[]{:S(2)}, u32[]{:S(2)}) %all-to-all-start) | async-done | bytes 184352 | tf_op jit(solution)/shard_map/all_to_all | solution.py:685
  64.9 21.4 %student_backward.1 = (bf16[2880,768]{1,0:T(8,128)(2,1)}, bf16[16,24,1024]{2,1,0:T(8,128)(2,1)}, bf16[16,24,1024]{2,1,0:T(8,128)(2,1)}) custom-call(s32[16]{0:T(128)} %get-tuple-element.108.qidx_ref, s32[16]{0:T(128)} %copy-done.11, s32[16]{0:T(128)} %len_ref.3, s32[1]{0:T(128)} %bitcast.core_ref, bf16[16,32,180]{2,1,0:T(8,128)(2,1)} %copy-done.10, ...), custom_call_target="tpu_custom_call" | custom-call | flops 4529848320 | bytes 17694720 | tf_op jit(solution)/shard_map/student_backward/pallas_call | solution.py:449
  86.5 2.5 %collective-permute-done.13.rest_1_ = bf16[16,24,1024]{2,1,0:T(8,128)(2,1)S(1)} collective-permute-done((bf16[16,24,1024]{2,1,0:T(8,128)(2,1)}, bf16[16,24,1024]{2,1,0:T(8,128)(2,1)S(1)}, u32[]{:S(2)}, u32[]{:S(2)}) %collective-permute-start.13) | collective-permute-done | bytes 786464 | tf_op jit(solution)/shard_map/ppermute | solution.py:618
  92.7 1.9 %collective-permute-start.16 = (bf16[4,24,1024]{2,1,0:T(8,128)(2,1)S(1)}, bf16[4,24,1024]{2,1,0:T(8,128)(2,1)S(1)}, u32[]{:S(2)}, u32[]{:S(2)}) collective-permute-start(bf16[4,24,1024]{2,1,0:T(8,128)(2,1)S(1)} %get-tuple-element.92), channel_id=1, source_target_pairs={{0,24},{4,28},{8,16},{12,20},{16,8},{20,12},{24,0},{28,4},{1,25},{... | collective-permute-start | bytes 589832 | tf_op jit(solution)/shard_map/ppermute | solution.py:613
  94.6 7.5 %context_grad.1 = bf16[2880,768]{1,0:T(8,128)(2,1)} custom-call(bf16[2880,768]{1,0:T(8,128)(2,1)} %get-tuple-element.93.sg_ref, bf16[768,768]{1,0:T(8,128)(2,1)} %wo_ref.3), custom_call_target="tpu_custom_call" | custom-call | flops 3397386240 | bytes 8847360 | tf_op jit(solution)/shard_map/context_grad/pallas_call | solution.py:486
  107.1 2.2 %collective-permute-done.17.refs_1_ = bf16[24,1024]{1,0:T(8,128)(2,1)S(1)} collective-permute-done((bf16[24,1024]{1,0:T(8,128)(2,1)S(1)}, bf16[24,1024]{1,0:T(8,128)(2,1)S(1)}, u32[]{:S(2)}, u32[]{:S(2)}) %collective-permute-start.17) | collective-permute-done | bytes 49184 | tf_op jit(solution)/shard_map/ppermute | solution.py:621
  111.9 1.8 %collective-permute-start.21 = (bf16[24,1024]{1,0:T(8,128)(2,1)S(1)}, bf16[24,1024]{1,0:T(8,128)(2,1)S(1)}, u32[]{:S(2)}, u32[]{:S(2)}) collective-permute-start(bf16[24,1024]{1,0:T(8,128)(2,1)S(1)} %sum_tensor.1), channel_id=1, source_target_pairs={{0,2},{1,3},{2,0},{3,1},{4,6},{5,7},{6,4},{7,5},{8,10},{9,11},{10,... | collective-permute-start | bytes 147464 | tf_op jit(solution)/shard_map/ppermute | solution.py:621
  114.6 1.9 %collective-permute-done.20 = bf16[24,1024]{1,0:T(8,128)(2,1)S(1)} collective-permute-done((bf16[24,1024]{1,0:T(8,128)(2,1)S(1)}, bf16[24,1024]{1,0:T(8,128)(2,1)S(1)}, u32[]{:S(2)}, u32[]{:S(2)}) %collective-permute-start.20) | collective-permute-done | bytes 49184 | tf_op jit(solution)/shard_map/ppermute | solution.py:621
  118.0 1.5 %collective-permute-start.23 = (bf16[4,24,1024]{2,1,0:T(8,128)(2,1)S(1)}, bf16[4,24,1024]{2,1,0:T(8,128)(2,1)S(1)}, u32[]{:S(2)}, u32[]{:S(2)}) collective-permute-start(bf16[4,24,1024]{2,1,0:T(8,128)(2,1)S(1)} %pad_maximum_fusion.2.rest_0_), channel_id=1, source_target_pairs={{0,8},{4,12},{8,0},{12,4},{16,24},{20,28},{24,16},{28,20},{1,9},{5... | collective-permute-start | bytes 589832 | tf_op jit(solution)/shard_map/ppermute | solution.py:613
  121.7 2.1 %collective-permute-done.23.rest_1_ = bf16[4,24,1024]{2,1,0:T(8,128)(2,1)S(1)} collective-permute-done((bf16[4,24,1024]{2,1,0:T(8,128)(2,1)S(1)}, bf16[4,24,1024]{2,1,0:T(8,128)(2,1)S(1)}, u32[]{:S(2)}, u32[]{:S(2)}) %collective-permute-start.23) | collective-permute-done | bytes 196640 | tf_op jit(solution)/shard_map/ppermute | solution.py:613
  123.8 3.5 %collective-permute-done.24.rest_2_ = bf16[4,24,1024]{2,1,0:T(8,128)(2,1)S(1)} collective-permute-done((bf16[4,24,1024]{2,1,0:T(8,128)(2,1)S(1)}, bf16[4,24,1024]{2,1,0:T(8,128)(2,1)S(1)}, u32[]{:S(2)}, u32[]{:S(2)}) %collective-permute-start.24) | collective-permute-done | bytes 196640 | tf_op jit(solution)/shard_map/ppermute | solution.py:613
  129.0 2.3 %unpack.1 = (f32[32,24,768]{2,1,0:T(8,128)}, f32[32,24,128]{2,1,0:T(8,128)}, f32[6,128]{1,0:T(8,128)}, f32[6,128]{1,0:T(8,128)}, f32[1]{0:T(128)}) custom-call(s32[32]{0:T(128)S(1)} %add.124.index_ref, bf16[4,24,1024]{2,1,0:T(8,128)(2,1)S(1)} %pad_maximum_fusion.2.rest_0_, bf16[4,24,1024]{2,1,0:T(8,128)(2,1)S(1)} %collective-permute-done.23.rest_1_, ...), custom_call_target="tpu_custom_call" | custom-call | tf_op jit(solution)/shard_map/unpack/pallas_call | solution.py:564
  (114 shorter events, 30.5 us)
Async XLA Ops:
  1.7 13.6 %collective-permute-start = (bf16[2,128,256]{2,1,0:T(8,128)(2,1)S(1)}, bf16[2,128,256]{2,1,0:T(8,128)(2,1)S(1)}, u32[]{:S(2)}, u32[]{:S(2)}) collective-permute-start(bf16[2,128,256]{2,1,0:T(8,128)(2,1)S(1)} %pad_maximum_fusion.3), channel_id=1, source_target_pairs={{0,1},{1,2},{2,3},{3,0},{4,5},{5,6},{6,7},{7,4},{8,9},{9,10},{10,1... | collective-permute-start | bytes 393224 | tf_op jit(solution)/shard_map/ppermute | solution.py:621
  4.7 11.2 %collective-permute-start.1 = (bf16[2,128,256]{2,1,0:T(8,128)(2,1)S(1)}, bf16[2,128,256]{2,1,0:T(8,128)(2,1)S(1)}, u32[]{:S(2)}, u32[]{:S(2)}) collective-permute-start(bf16[2,128,256]{2,1,0:T(8,128)(2,1)S(1)} %pad_maximum_fusion.3), channel_id=1, source_target_pairs={{0,2},{1,3},{2,0},{3,1},{4,6},{5,7},{6,4},{7,5},{8,10},{9,11},{10,... | collective-permute-start | bytes 393224 | tf_op jit(solution)/shard_map/ppermute | solution.py:621
  7.3 8.6 %collective-permute-start.2 = (bf16[2,128,256]{2,1,0:T(8,128)(2,1)S(1)}, bf16[2,128,256]{2,1,0:T(8,128)(2,1)S(1)}, u32[]{:S(2)}, u32[]{:S(2)}) collective-permute-start(bf16[2,128,256]{2,1,0:T(8,128)(2,1)S(1)} %pad_maximum_fusion.3), channel_id=1, source_target_pairs={{0,3},{1,0},{2,1},{3,2},{4,7},{5,4},{6,5},{7,6},{8,11},{9,8},{10,9... | collective-permute-start | bytes 393224 | tf_op jit(solution)/shard_map/ppermute | solution.py:621
  10.9 5.2 %collective-permute-start.3 = (bf16[1,128,256]{2,1,0:T(8,128)(2,1)S(1)}, bf16[1,128,256]{2,1,0:T(8,128)(2,1)S(1)}, u32[]{:S(2)}, u32[]{:S(2)}) collective-permute-start(bf16[1,128,256]{2,1,0:T(8,128)(2,1)S(1)} %pad_bitcast_fusion), channel_id=1, source_target_pairs={{0,24},{4,28},{8,16},{12,20},{16,8},{20,12},{24,0},{28,4},{1,25},{... | collective-permute-start | bytes 196616 | tf_op jit(solution)/shard_map/ppermute | solution.py:613
  16.2 21.2 %collective-permute-start.6 = (bf16[2,128,256]{2,1,0:T(8,128)(2,1)S(1)}, bf16[2,128,256]{2,1,0:T(8,128)(2,1)S(1)}, u32[]{:S(2)}, u32[]{:S(2)}) collective-permute-start(bf16[2,128,256]{2,1,0:T(8,128)(2,1)S(1)} %pad_maximum_fusion.4), channel_id=1, source_target_pairs={{0,1},{1,2},{2,3},{3,0},{4,5},{5,6},{6,7},{7,4},{8,9},{9,10},{10,1... | collective-permute-start | bytes 393224 | tf_op jit(solution)/shard_map/ppermute | solution.py:621
  19.4 18.1 %collective-permute-start.7 = (bf16[2,128,256]{2,1,0:T(8,128)(2,1)S(1)}, bf16[2,128,256]{2,1,0:T(8,128)(2,1)S(1)}, u32[]{:S(2)}, u32[]{:S(2)}) collective-permute-start(bf16[2,128,256]{2,1,0:T(8,128)(2,1)S(1)} %pad_maximum_fusion.4), channel_id=1, source_target_pairs={{0,2},{1,3},{2,0},{3,1},{4,6},{5,7},{6,4},{7,5},{8,10},{9,11},{10,... | collective-permute-start | bytes 393224 | tf_op jit(solution)/shard_map/ppermute | solution.py:621
  21.0 16.5 %collective-permute-start.8 = (bf16[2,128,256]{2,1,0:T(8,128)(2,1)S(1)}, bf16[2,128,256]{2,1,0:T(8,128)(2,1)S(1)}, u32[]{:S(2)}, u32[]{:S(2)}) collective-permute-start(bf16[2,128,256]{2,1,0:T(8,128)(2,1)S(1)} %pad_maximum_fusion.4), channel_id=1, source_target_pairs={{0,3},{1,0},{2,1},{3,2},{4,7},{5,4},{6,5},{7,6},{8,11},{9,8},{10,9... | collective-permute-start | bytes 393224 | tf_op jit(solution)/shard_map/ppermute | solution.py:621
  21.8 15.8 %collective-permute-start.4 = (bf16[7,128,256]{2,1,0:T(8,128)(2,1)S(1)}, bf16[7,128,256]{2,1,0:T(8,128)(2,1)S(1)}, u32[]{:S(2)}, u32[]{:S(2)}) collective-permute-start(bf16[7,128,256]{2,1,0:T(8,128)(2,1)S(1)} %pad_maximum_fusion.rest_0_), channel_id=1, source_target_pairs={{0,8},{4,12},{8,0},{12,4},{16,24},{20,28},{24,16},{28,20},{1,9},{5... | collective-permute-start | bytes 1376264 | tf_op jit(solution)/shard_map/ppermute | solution.py:613
  23.3 14.3 %collective-permute-start.5 = (bf16[7,128,256]{2,1,0:T(8,128)(2,1)S(1)}, bf16[7,128,256]{2,1,0:T(8,128)(2,1)S(1)}, u32[]{:S(2)}, u32[]{:S(2)}) collective-permute-start(bf16[7,128,256]{2,1,0:T(8,128)(2,1)S(1)} %pad_maximum_fusion.rest_0_), channel_id=1, source_target_pairs={{0,16},{4,20},{8,24},{12,28},{16,0},{20,4},{24,8},{28,12},{1,17},{... | collective-permute-start | bytes 1376264 | tf_op jit(solution)/shard_map/ppermute | solution.py:613
  53.9 10.3 %all-to-all-start = ((bf16[16,32,180]{2,1,0:T(8,128)(2,1)}), bf16[16,32,180]{2,1,0:T(8,128)(2,1)S(1)}, u32[]{:S(2)}, u32[]{:S(2)}) async-start(bf16[16,32,180]{2,1,0:T(8,128)(2,1)} %teacher_maps.1), calls=%async_computation | async-start | bytes 524288 | tf_op jit(solution)/shard_map/all_to_all | solution.py:685
  91.0 11.1 %collective-permute-start.14 = (bf16[4,24,1024]{2,1,0:T(8,128)(2,1)S(1)}, bf16[4,24,1024]{2,1,0:T(8,128)(2,1)S(1)}, u32[]{:S(2)}, u32[]{:S(2)}) collective-permute-start(bf16[4,24,1024]{2,1,0:T(8,128)(2,1)S(1)} %get-tuple-element.90), channel_id=1, source_target_pairs={{0,8},{4,12},{8,0},{12,4},{16,24},{20,28},{24,16},{28,20},{1,9},{5... | collective-permute-start | bytes 589832 | tf_op jit(solution)/shard_map/ppermute | solution.py:613
  91.7 10.9 %collective-permute-start.15 = (bf16[4,24,1024]{2,1,0:T(8,128)(2,1)S(1)}, bf16[4,24,1024]{2,1,0:T(8,128)(2,1)S(1)}, u32[]{:S(2)}, u32[]{:S(2)}) collective-permute-start(bf16[4,24,1024]{2,1,0:T(8,128)(2,1)S(1)} %get-tuple-element.91), channel_id=1, source_target_pairs={{0,16},{4,20},{8,24},{12,28},{16,0},{20,4},{24,8},{28,12},{1,17},{... | collective-permute-start | bytes 589832 | tf_op jit(solution)/shard_map/ppermute | solution.py:613
  92.7 9.8 %collective-permute-start.16 = (bf16[4,24,1024]{2,1,0:T(8,128)(2,1)S(1)}, bf16[4,24,1024]{2,1,0:T(8,128)(2,1)S(1)}, u32[]{:S(2)}, u32[]{:S(2)}) collective-permute-start(bf16[4,24,1024]{2,1,0:T(8,128)(2,1)S(1)} %get-tuple-element.92), channel_id=1, source_target_pairs={{0,24},{4,28},{8,16},{12,20},{16,8},{20,12},{24,0},{28,4},{1,25},{... | collective-permute-start | bytes 589832 | tf_op jit(solution)/shard_map/ppermute | solution.py:613
  103.3 6.0 %collective-permute-start.17 = (bf16[24,1024]{1,0:T(8,128)(2,1)S(1)}, bf16[24,1024]{1,0:T(8,128)(2,1)S(1)}, u32[]{:S(2)}, u32[]{:S(2)}) collective-permute-start(bf16[24,1024]{1,0:T(8,128)(2,1)S(1)} %get-tuple-element.99), channel_id=1, source_target_pairs={{0,1},{1,2},{2,3},{3,0},{4,5},{5,6},{6,7},{7,4},{8,9},{9,10},{10,1... | collective-permute-start | bytes 147464 | tf_op jit(solution)/shard_map/ppermute | solution.py:621
  104.5 5.9 %collective-permute-start.18 = (bf16[24,1024]{1,0:T(8,128)(2,1)S(1)}, bf16[24,1024]{1,0:T(8,128)(2,1)S(1)}, u32[]{:S(2)}, u32[]{:S(2)}) collective-permute-start(bf16[24,1024]{1,0:T(8,128)(2,1)S(1)} %get-tuple-element.100), channel_id=1, source_target_pairs={{0,2},{1,3},{2,0},{3,1},{4,6},{5,7},{6,4},{7,5},{8,10},{9,11},{10,... | collective-permute-start | bytes 147464 | tf_op jit(solution)/shard_map/ppermute | solution.py:621
  105.8 4.6 %collective-permute-start.19 = (bf16[24,1024]{1,0:T(8,128)(2,1)S(1)}, bf16[24,1024]{1,0:T(8,128)(2,1)S(1)}, u32[]{:S(2)}, u32[]{:S(2)}) collective-permute-start(bf16[24,1024]{1,0:T(8,128)(2,1)S(1)} %get-tuple-element.101), channel_id=1, source_target_pairs={{0,3},{1,0},{2,1},{3,2},{4,7},{5,4},{6,5},{7,6},{8,11},{9,8},{10,9... | collective-permute-start | bytes 147464 | tf_op jit(solution)/shard_map/ppermute | solution.py:621
  110.5 5.9 %collective-permute-start.20 = (bf16[24,1024]{1,0:T(8,128)(2,1)S(1)}, bf16[24,1024]{1,0:T(8,128)(2,1)S(1)}, u32[]{:S(2)}, u32[]{:S(2)}) collective-permute-start(bf16[24,1024]{1,0:T(8,128)(2,1)S(1)} %sum_tensor.1), channel_id=1, source_target_pairs={{0,1},{1,2},{2,3},{3,0},{4,5},{5,6},{6,7},{7,4},{8,9},{9,10},{10,1... | collective-permute-start | bytes 147464 | tf_op jit(solution)/shard_map/ppermute | solution.py:621
  111.9 5.6 %collective-permute-start.21 = (bf16[24,1024]{1,0:T(8,128)(2,1)S(1)}, bf16[24,1024]{1,0:T(8,128)(2,1)S(1)}, u32[]{:S(2)}, u32[]{:S(2)}) collective-permute-start(bf16[24,1024]{1,0:T(8,128)(2,1)S(1)} %sum_tensor.1), channel_id=1, source_target_pairs={{0,2},{1,3},{2,0},{3,1},{4,6},{5,7},{6,4},{7,5},{8,10},{9,11},{10,... | collective-permute-start | bytes 147464 | tf_op jit(solution)/shard_map/ppermute | solution.py:621
  113.7 4.3 %collective-permute-start.22 = (bf16[24,1024]{1,0:T(8,128)(2,1)S(1)}, bf16[24,1024]{1,0:T(8,128)(2,1)S(1)}, u32[]{:S(2)}, u32[]{:S(2)}) collective-permute-start(bf16[24,1024]{1,0:T(8,128)(2,1)S(1)} %sum_tensor.1), channel_id=1, source_target_pairs={{0,3},{1,0},{2,1},{3,2},{4,7},{5,4},{6,5},{7,6},{8,11},{9,8},{10,9... | collective-permute-start | bytes 147464 | tf_op jit(solution)/shard_map/ppermute | solution.py:621
  118.0 5.7 %collective-permute-start.23 = (bf16[4,24,1024]{2,1,0:T(8,128)(2,1)S(1)}, bf16[4,24,1024]{2,1,0:T(8,128)(2,1)S(1)}, u32[]{:S(2)}, u32[]{:S(2)}) collective-permute-start(bf16[4,24,1024]{2,1,0:T(8,128)(2,1)S(1)} %pad_maximum_fusion.2.rest_0_), channel_id=1, source_target_pairs={{0,8},{4,12},{8,0},{12,4},{16,24},{20,28},{24,16},{28,20},{1,9},{5... | collective-permute-start | bytes 589832 | tf_op jit(solution)/shard_map/ppermute | solution.py:613
  119.5 7.8 %collective-permute-start.24 = (bf16[4,24,1024]{2,1,0:T(8,128)(2,1)S(1)}, bf16[4,24,1024]{2,1,0:T(8,128)(2,1)S(1)}, u32[]{:S(2)}, u32[]{:S(2)}) collective-permute-start(bf16[4,24,1024]{2,1,0:T(8,128)(2,1)S(1)} %pad_maximum_fusion.2.rest_0_), channel_id=1, source_target_pairs={{0,16},{4,20},{8,24},{12,28},{16,0},{20,4},{24,8},{28,12},{1,17},{... | collective-permute-start | bytes 589832 | tf_op jit(solution)/shard_map/ppermute | solution.py:613
  120.1 7.2 %collective-permute-start.25 = (bf16[4,24,1024]{2,1,0:T(8,128)(2,1)S(1)}, bf16[4,24,1024]{2,1,0:T(8,128)(2,1)S(1)}, u32[]{:S(2)}, u32[]{:S(2)}) collective-permute-start(bf16[4,24,1024]{2,1,0:T(8,128)(2,1)S(1)} %pad_maximum_fusion.2.rest_0_), channel_id=1, source_target_pairs={{0,24},{4,28},{8,16},{12,20},{16,8},{20,12},{24,0},{28,4},{1,25},{... | collective-permute-start | bytes 589832 | tf_op jit(solution)/shard_map/ppermute | solution.py:613
  121.7 6.3 %collective-permute-start.26 = (bf16[4,24,1024]{2,1,0:T(8,128)(2,1)S(1)}, bf16[4,24,1024]{2,1,0:T(8,128)(2,1)S(1)}, u32[]{:S(2)}, u32[]{:S(2)}) collective-permute-start(bf16[4,24,1024]{2,1,0:T(8,128)(2,1)S(1)} %pad_maximum_fusion.2.rest_0_), channel_id=1, source_target_pairs={{0,4},{4,0},{8,12},{12,8},{16,20},{20,16},{24,28},{28,24},{1,5},{5... | collective-permute-start | bytes 589832 | tf_op jit(solution)/shard_map/ppermute | solution.py:618
  123.8 4.2 %collective-permute-start.27 = (bf16[4,24,1024]{2,1,0:T(8,128)(2,1)S(1)}, bf16[4,24,1024]{2,1,0:T(8,128)(2,1)S(1)}, u32[]{:S(2)}, u32[]{:S(2)}) collective-permute-start(bf16[4,24,1024]{2,1,0:T(8,128)(2,1)S(1)} %collective-permute-done.23.rest_1_), channel_id=1, source_target_pairs={{0,4},{4,0},{8,12},{12,8},{16,20},{20,16},{24,28},{28,24},{1,5},{5... | collective-permute-start | bytes 589832 | tf_op jit(solution)/shard_map/ppermute | solution.py:618
  (19 other events, 162.9 us)
